TPU v7x, 32 devices: a whole 2x2x4 slice. The times are simulated.
32 devices in a mesh: parts: 2 (over y), rows: 4 (over z), sub: 2 (over x), dim: 2 (over core).
Axes of the slice: x: 2, y: 2, z: 4, core: 2. Of those that a mesh axis runs over, the one named last changes fastest.
Arguments:
- embeddings: bfloat16 [8192, 1024], P(('parts', 'rows', 'sub'), 'dim'), parts along dimension 0, may hold values from -48 to 48
- centroids: bfloat16 [2048, 1024], P('parts'), parts along dimension 0, may hold values from -7 to 7
- cluster_id: int32 [8192, 1], P(('parts', 'rows', 'sub')), parts along dimension 0, may hold values from 0 to 1023; in each aligned block of 512 rows (0 to 511, 512 to 1023, ...) at most 2 rows name the same one
- cluster_place: int32 [1024], replicated, may hold values from 0 to 1023, each once
Outputs:
- new_centroids: float32 [2048, 1024], P(('parts', 'rows', 'sub'), 'dim'), parts along dimension 0
- similarity: bfloat16 [2048, 16, 16], P(('parts', 'rows', 'sub'), 'dim'), parts along dimension 0
There are 2 independent parts, one for each index of `parts`. A program takes and returns all parts, laid end to end along the dimension named above; an argument that names none is the same for every part. Nothing has to cross between parts.
Inputs may be any that keep to these rules, and one draw needn't show every extreme that they name: `cluster_id`: within the documents of one index of rows and sub no cluster appears more than 2 times. `cluster_place`: each position appears once; the owner of position p is p // 128.
All inputs are finite; a program needn't handle non-finite values.
Results may differ from a plain program's by a relative error of at most 0.002.
Values may be sent and summed in bfloat16 or wider, within the bound.
No kernel may reach another device: no remote copies, remote signals or barrier semaphores. Data moves between devices by JAX's collectives and lax.ppermute only.
A program may use at most 64 MiB of HBM per device.

v0:
```python
import jax
import jax.numpy as jnp
from jax import lax
from jax.sharding import PartitionSpec as P

PREFIX = 256
MOST = 2


TEMP = 0.125
SMOOTH = 1.0
EPS = 1e-05


def from_behind(value, axis, steps):
    count = lax.axis_size(axis)
    first, last = (max(0, -steps), min(count, count - steps))
    return lax.ppermute(value, axis, [(source, source + steps) for source in range(first, last)])


def soft_weights(prefix, centre_prefix):
    scores = jnp.dot(prefix, centre_prefix.T, preferred_element_type=jnp.float32) * TEMP
    return jax.nn.softmax(scores, axis=-1).astype(jnp.bfloat16)


def shards(embeddings, centroids, cluster_id, cluster_place):
    row_dev, half_width = embeddings.shape
    clusters, full_width = centroids.shape
    owners = lax.axis_size(("rows", "sub"))
    per_owner = clusters // owners
    per_cluster = MOST
    prefix_width = PREFIX
    dim_index = lax.axis_index("dim")
    owner_index = lax.axis_index(("rows", "sub"))
    centre_prefix = centroids[:, :prefix_width]
    shifted = from_behind(embeddings[:, :prefix_width], "dim", 1)
    prefix = jnp.where(dim_index == 0, embeddings[:, :prefix_width], shifted)
    weights = soft_weights(prefix, centre_prefix)
    centroid_sum = lax.psum_scatter(
        lax.dot_general(
            weights, embeddings, (((0,), (0,)), ((), ())), preferred_element_type=jnp.float32
        ),
        ("rows", "sub"),
        scatter_dimension=0,
        tiled=True,
    )
    cluster_mass = lax.psum_scatter(
        jnp.sum(weights, axis=0, dtype=jnp.float32),
        ("rows", "sub"),
        scatter_dimension=0,
        tiled=True,
    )
    prior_rows = lax.dynamic_slice(
        centroids, (owner_index * per_owner, dim_index * half_width), (per_owner, half_width)
    )
    new_centroids = (centroid_sum + SMOOTH * prior_rows.astype(jnp.float32)) / (
        cluster_mass + SMOOTH
    )[:, None]
    row_cluster = cluster_id[:, 0]
    row_order = jnp.arange(row_dev, dtype=jnp.int32)
    earlier = (row_cluster[:, None] == row_cluster[None, :]) & (
        row_order[None, :] < row_order[:, None]
    )
    within = jnp.sum(earlier, axis=1, dtype=jnp.int32)
    matches = row_cluster[:, None] == jnp.arange(clusters, dtype=jnp.int32)[None, :]
    position = jnp.sum(jnp.where(matches, cluster_place[None, :], 0), axis=1)
    slot = position * per_cluster + within
    outgoing = (
        jnp.zeros((clusters * per_cluster, half_width), jnp.bfloat16).at[slot].set(embeddings)
    )
    present = (
        jnp.zeros((clusters * per_cluster,), jnp.bfloat16)
        .at[slot]
        .set(jnp.ones((row_dev,), jnp.bfloat16))
    )
    arrived, present_in = (
        lax.all_to_all(outgoing, ("rows", "sub"), split_axis=0, concat_axis=0, tiled=True),
        lax.all_to_all(present, ("rows", "sub"), split_axis=0, concat_axis=0, tiled=True),
    )
    slot_count = owners * per_cluster
    arrived = arrived.reshape(owners, per_owner, per_cluster, half_width)
    present_in = present_in.reshape(owners, per_owner, per_cluster)
    members = jnp.transpose(arrived, (1, 0, 2, 3)).reshape(per_owner, slot_count, half_width)
    member_mask = jnp.transpose(present_in, (1, 0, 2)).reshape(per_owner, slot_count)
    targets = owner_index * per_owner + jnp.arange(per_owner, dtype=jnp.int32)
    chooser = (cluster_place[None, :] == targets[:, None]).astype(jnp.bfloat16)
    own_columns = lax.dynamic_slice_in_dim(centroids, dim_index * half_width, half_width, 1)
    centre = jnp.dot(chooser, own_columns, preferred_element_type=jnp.float32)
    centred = (
        (members.astype(jnp.float32) - centre[:, None, :])
        * member_mask.astype(jnp.float32)[:, :, None]
    ).astype(jnp.bfloat16)
    gram_part = jnp.einsum("cse,cte->cst", centred, centred, preferred_element_type=jnp.float32)
    squares = jnp.sum(jnp.square(centred.astype(jnp.float32)), axis=-1)
    slot_norms = lax.psum(squares, "dim")
    shared = lax.psum_scatter(gram_part, "dim", scatter_dimension=1, tiled=True)
    row_scale = lax.rsqrt(slot_norms / full_width + EPS)
    own_scale = lax.dynamic_slice_in_dim(
        row_scale, dim_index * (slot_count // 2), slot_count // 2, 1
    )
    similarity = (shared / full_width * own_scale[:, :, None] * row_scale[:, None, :]).astype(
        jnp.bfloat16
    )
    return (new_centroids, similarity)


def solution(mesh):
    in_specs = (
        P(("parts", "rows", "sub"), "dim"),
        P("parts", None),
        P(("parts", "rows", "sub"), None),
        P(),
    )
    out_specs = (P(("parts", "rows", "sub"), "dim"), P(("parts", "rows", "sub"), "dim", None))
    return jax.shard_map(shards, mesh=mesh, in_specs=in_specs, out_specs=out_specs, check_vma=False)
```

profile of v0, /device:TPU:0, one launch (start us, length us, event | category | flops | bytes accessed | tf_op | source)
XLA Modules:
  0.0 178.8 jit_solution(4476441282126562203)
XLA Ops:
  7.2 1.0 convert_reduce_fusion.1
  8.2 1.1 select_reduce_fusion
  9.3 3.8 %scatter_custom_fusion.1 = bf16[2048]{0:T(1024)(128)(2,1)S(1)} fusion(s32[512]{0:T(512)S(1)} %bitcast.43, bf16[512]{0:T(512)(128)(2,1)S(1)} %broadcast.48, bf16[]{:T(256)} %constant.14.clone.1), kind=kCustom, calls=%fused_computation.40 | custom fusion | bytes 4098 | tf_op jit(solution)/shard_map/scatter | solution.py:74
  13.1 0.5 broadcast.51
  13.6 0.7 reduce.1
  14.3 0.6 reshape.99
  14.9 7.3 %all-to-all-start.1 = ((bf16[8,2,128]{2,1,0:T(2,128)(2,1)}), bf16[8,2,128]{2,1,0:T(2,128)(2,1)S(1)}, u32[]{:S(2)}, u32[]{:S(2)}) async-start(bf16[8,2,128]{2,1,0:T(2,128)(2,1)} %reshape.99), calls=%async_computation.2 | async-start | bytes 8192 | tf_op jit(solution)/shard_map/all_to_all | solution.py:78
  22.2 4.5 %scatter_custom_fusion = bf16[2048,512]{1,0:T(8,128)(2,1)} fusion(s32[512]{0:T(512)S(1)} %bitcast.44, bf16[512,512]{1,0:T(8,128)(2,1)} %param.4, bf16[]{:T(256)} %constant.14.clone.1), kind=kCustom, calls=%fused_computation.24 | custom fusion | bytes 2097664 | tf_op jit(solution)/shard_map/scatter | solution.py:69
  26.7 1.9 %all-to-all-done.1 = bf16[8,2,128]{2,1,0:T(2,128)(2,1)S(1)} async-done(((bf16[8,2,128]{2,1,0:T(2,128)(2,1)}), bf16[8,2,128]{2,1,0:T(2,128)(2,1)S(1)}, u32[]{:S(2)}, u32[]{:S(2)}) %all-to-all-start.1) | async-done | bytes 4128 | tf_op jit(solution)/shard_map/all_to_all | solution.py:78
  28.6 0.0 copy-start
  28.6 0.0 copy-start.2
  28.6 4.6 %all-to-all-start = ((bf16[8,256,512]{2,1,0:T(8,128)(2,1)}), bf16[8,256,512]{2,1,0:T(8,128)(2,1)}, u32[]{:S(2)}, u32[]{:S(2)}) async-start(bf16[8,256,512]{2,1,0:T(8,128)(2,1)} %bitcast.3), calls=%async_computation.1 | async-start | bytes 4194304 | tf_op jit(solution)/shard_map/all_to_all | solution.py:77
  33.2 0.0 reduce-scatter.5.cloned.1.call-start
  33.2 0.0 copy-done
  33.3 1.5 collective-permute-start
  34.8 0.0 copy-done.1
  34.8 0.0 copy-done.2
  34.8 0.4 fusion.8
  35.2 0.1 copy.49
  35.3 0.1 copy.50
  35.4 0.3 collective-permute-done
  35.7 0.6 multiply_reduce_fusion.1
  36.3 0.5 fusion.7
  36.8 0.7 convert_reduce_fusion
  37.5 43.3 %all-to-all-done = bf16[8,256,512]{2,1,0:T(8,128)(2,1)} async-done(((bf16[8,256,512]{2,1,0:T(8,128)(2,1)}), bf16[8,256,512]{2,1,0:T(8,128)(2,1)}, u32[]{:S(2)}, u32[]{:S(2)}) %all-to-all-start) | async-done | bytes 2097184 | tf_op jit(solution)/shard_map/all_to_all | solution.py:77
  80.8 2.9 %fusion.24 = (bf16[8,256,512]{2,0,1:T(8,128)(2,1)S(1)}, f32[128,8,2,512]{3,1,2,0:T(8,128)S(1)}) fusion(bf16[8,256,512]{2,1,0:T(8,128)(2,1)} %all-to-all-done), kind=kLoop, calls=%fused_computation.47 | loop fusion | flops 1048576 | bytes 8388608 | tf_op jit(solution)/shard_map/all_to_all | solution.py:77
  83.7 2.4 %copy.46 = f32[128,8,2,512]{3,0,2,1:T(8,128)S(1)} copy(f32[128,8,2,512]{3,1,2,0:T(8,128)S(1)} %get-tuple-element.17) | data formatting | bytes 8388608 | tf_op jit(solution)/shard_map/convert_element_type | solution.py:90
  86.1 0.6 fusion.4
  86.7 2.3 %fusion.5 = f32[128,16,16]{2,1,0:T(8,128)} fusion(bf16[128,16,512]{2,0,1:T(8,128)(2,1)S(1)} %fusion.4), kind=kOutput, calls=%fused_computation.11 | convolution fusion | flops 33554432 | bytes 2228224 | tf_op jit(solution)/shard_map/cse,cte->cst/dot_general | solution.py:93
  88.9 0.0 reduce-scatter.5.cloned.1.call-update
  89.0 0.0 reduce-scatter.3.cloned.1.call-start
  89.0 0.0 copy-start.3
  89.0 3.1 %fusion.25 = f32[1024,512]{1,0:T(8,128)} fusion(bf16[512,1024]{1,0:T(8,128)(2,1)S(1)} %get-tuple-element.15, bf16[512,512]{1,0:T(8,128)(2,1)} %param.4), kind=kOutput, calls=%fused_computation.48 | convolution fusion | flops 536870912 | bytes 3670016 | tf_op jit(solution)/shard_map/dot_general | solution.py:40
  92.2 0.0 reduce-scatter.3.cloned.1.call-update
  92.2 0.0 copy-done.3
  92.2 0.6 dynamic-slice
  93.5 19.6 %all-reduce = f32[1024]{0:T(1024)S(1)} all-reduce(f32[1024]{0:T(1024)S(1)} %get-tuple-element.14), channel_id=3, replica_groups=mesh['parts'=2,'rows'=4,'sub'=2,'dim'=2] {'rows','sub'}, use_global_device_ids=true, to_apply=%region_4.5.clone | all-reduce | flops 1024 | bytes 8192
  113.0 0.1 dynamic-slice_add_fusion
  113.1 1.1 multiply_reduce_fusion
  114.2 0.1 copy.53
  114.2 2.5 %psum.7 = f32[128,16]{0,1:T(8,128)S(1)} all-reduce(f32[128,16]{0,1:T(8,128)S(1)} %bitcast.37), channel_id=1, replica_groups=mesh['parts'=2,'rows'=4,'sub'=2,'dim'=2] {'dim'}, use_global_device_ids=true, to_apply=%region_11.12 | all-reduce | flops 2048 | bytes 16384 | tf_op jit(solution)/shard_map/psum | solution.py:95
  116.7 0.1 copy.55
  116.8 0.1 copy.54
  117.0 0.0 reduce-scatter.5.cloned.1.call-done
  117.0 1.2 multiply_convert_fusion
  118.2 0.8 copy.56
  119.0 51.1 %reduce-scatter.3.cloned.1.call-done = f32[128,512]{1,0:T(8,128)} async-done(((f32[1024,512]{1,0:T(8,128)}), f32[128,512]{1,0:T(8,128)}) %reduce-scatter.3.cloned.1.call-update) | async-done | bytes 262160 | tf_op jit(solution)/shard_map/reduce_scatter | solution.py:39
  170.2 1.8 add_divide_fusion
  (11 shorter events, 0.1 us)
Async XLA Ops:
  14.9 13.6 %all-to-all-start.1 = ((bf16[8,2,128]{2,1,0:T(2,128)(2,1)}), bf16[8,2,128]{2,1,0:T(2,128)(2,1)S(1)}, u32[]{:S(2)}, u32[]{:S(2)}) async-start(bf16[8,2,128]{2,1,0:T(2,128)(2,1)} %reshape.99), calls=%async_computation.2 | async-start | bytes 8192 | tf_op jit(solution)/shard_map/all_to_all | solution.py:78
  28.6 4.7 %copy-start = (bf16[512,512]{1,0:T(8,128)(2,1)S(1)}, bf16[512,512]{1,0:T(8,128)(2,1)}, u32[]{:S(2)}) copy-start(bf16[512,512]{1,0:T(8,128)(2,1)} %param.4) | copy-start | bytes 1572868
  28.6 6.2 %copy-start.1 = (bf16[1024,1024]{1,0:T(8,128)(2,1)S(1)}, bf16[1024,1024]{1,0:T(8,128)(2,1)}, u32[]{:S(2)}) copy-start(bf16[1024,1024]{1,0:T(8,128)(2,1)} %param.5) | copy-start | bytes 6291460
  28.6 6.2 %copy-start.2 = (s32[1024]{0:T(1024)S(1)}, s32[1024]{0:T(1024)}, u32[]{:S(2)}) copy-start(s32[1024]{0:T(1024)} %param.7) | copy-start | bytes 12292
  28.6 52.2 %all-to-all-start = ((bf16[8,256,512]{2,1,0:T(8,128)(2,1)}), bf16[8,256,512]{2,1,0:T(8,128)(2,1)}, u32[]{:S(2)}, u32[]{:S(2)}) async-start(bf16[8,256,512]{2,1,0:T(8,128)(2,1)} %bitcast.3), calls=%async_computation.1 | async-start | bytes 4194304 | tf_op jit(solution)/shard_map/all_to_all | solution.py:77
  33.2 83.8 %reduce-scatter.5.cloned.1.call-start = ((), (), s32[]{:S(2)}) async-start(), calls=%async_computation.5 | async-start | bytes 1572864 | tf_op jit(solution)/shard_map/reduce_scatter | solution.py:96
  33.3 2.4 %collective-permute-start = (bf16[512,256]{1,0:T(8,128)(2,1)S(1)}, bf16[512,256]{1,0:T(8,128)(2,1)S(1)}, u32[]{:S(2)}, u32[]{:S(2)}) collective-permute-start(bf16[512,256]{1,0:T(8,128)(2,1)S(1)} %slice.7), channel_id=1, source_target_pairs={{0,1},{2,3},{4,5},{6,7},{8,9},{10,11},{12,13},{14,15},{16,17},{18,... | collective-permute-start | bytes 786440 | tf_op jit(solution)/shard_map/ppermute | solution.py:18
  89.0 81.2 %reduce-scatter.3.cloned.1.call-start = ((), (), s32[]{:S(2)}) async-start(), calls=%async_computation.4 | async-start | bytes 2359296 | tf_op jit(solution)/shard_map/reduce_scatter | solution.py:39
  89.0 3.2 %copy-start.3 = (u32[32]{0:T(128)S(1)}, u32[32]{0:T(128)}, u32[]{:S(2)}) copy-start(u32[32]{0:T(128)} %constant.52) | copy-start | bytes 388
Sparse Core Ops, SparseCore 0:
  89.1 7.5 reduce-scatter.4
  100.7 69.4 reduce-scatter.2
where the time goes:
time: 179 us
  waiting for transfers between devices  96.7 us (54%)
  blocking collectives  22 us (12%)
  between operations  14.9 us (8%)
  local copies, waits for them, and re-layouts  13.7 us (8%)
  starting transfers between devices  13.4 us (7%)
  other arithmetic  11.7 us (7%)
  matrix products  6.31 us (4%)
    reduce_scatter x1, waiting for transfers between devices, shards(): lax.psum_scatter(lax.dot_general(weights, embeddings, (((0,), (0,)), ((),...  51.1 us
    all_to_all x1, waiting for transfers between devices, shards(): lax.all_to_all(outgoing, ('rows', 'sub'), split_axis=0, concat_axis=0, ti...  43.3 us
    unnamed x1, blocking collectives  19.6 us
    all_to_all x1, starting transfers between devices, shards(): lax.all_to_all(present, ('rows', 'sub'), split_axis=0, concat_axis=0, til...  7.25 us
    all_to_all x1, starting transfers between devices, shards(): lax.all_to_all(outgoing, ('rows', 'sub'), split_axis=0, concat_axis=0, ti...  4.6 us
    scatter x1, local copies, waits for them, and re-layouts, shards(): jnp.zeros((clusters * per_cluster, half_width), jnp.bfloat16).at[slot]  4.51 us
    scatter x1, local copies, waits for them, and re-layouts, shards(): present = jnp.zeros((clusters * per_cluster,), jnp.bfloat16).at[slot].set...  3.78 us
  transfers between devices with their start and end apart: 5, of which 4 were waited for; matrix products, arithmetic and copies ran while one was open for 8% of the time, Pallas kernels for 0%

commit v1 on v0

v1 whole, which is shorter than its diff:
```python
import functools

import jax
import jax.numpy as jnp
from jax import lax
from jax.experimental import pallas as pl
from jax.experimental.pallas import tpu as pltpu
from jax.sharding import PartitionSpec as P

PREFIX = 256
MOST = 2

TEMP = 0.125
SMOOTH = 1.0
EPS = 1e-05

DIGIT = 32
META = 16
SUBLANES = 8
LANES = 128
F32 = jnp.float32
BF16 = jnp.bfloat16
VMEM_LIMIT = 40 * 1024 * 1024

NT = (((1,), (1,)), ((), ()))


def vmem():
    return pl.BlockSpec(memory_space=pltpu.VMEM)


def params():
    return pltpu.CompilerParams(vmem_limit_bytes=VMEM_LIMIT)


def dot(a, b):
    return jnp.dot(a, b, preferred_element_type=F32)


def dot_nt(a, b):
    return lax.dot_general(a, b, NT, preferred_element_type=F32)


def prep_kernel(subs, per, place_ref, cent_ref, inv_ref, centre_ref, own_prefix_ref, prior_ref):
    clusters = cent_ref.shape[0]
    half = centre_ref.shape[1]
    z, x, h = lax.axis_index("rows"), lax.axis_index("sub"), lax.axis_index("dim")
    row = lax.broadcasted_iota(jnp.int32, (subs * per, clusters), 0)
    ids = lax.broadcasted_iota(jnp.int32, (subs * per, clusters), 1)
    turn, within = row // per, row % per
    target = (z * subs + (x + turn) % subs) * per + within
    chosen = (place_ref[...] == target).astype(F32)
    inv_ref[...] = jnp.sum(chosen * ids.astype(F32), axis=1, keepdims=True)
    columns = cent_ref[:, pl.ds(pl.multiple_of(h * half, LANES), half)]
    centre_ref[...] = dot(chosen.astype(BF16), columns).astype(BF16)
    natural = (ids == target).astype(BF16)
    own_prefix_ref[...] = dot(natural, cent_ref[:, :PREFIX]).astype(BF16)
    prior_ref[...] = dot(natural[:per], columns).astype(BF16)


def block_kernel(first, subs, per, block_ref, near_ref, cent_ref, own_prefix_ref, inv_ref, centre_ref, *refs):
    if first:
        acc_in, (acc_ref, *row_refs) = None, refs
    else:
        acc_in, acc_ref, *row_refs = refs
    docs = block_ref.shape[0] - META
    half = block_ref.shape[1]
    h = lax.axis_index("dim")
    emb = block_ref[:docs, :]
    meta = block_ref[docs:, :].astype(F32)
    cid = ((meta[0:1, :] - 1.0) * DIGIT + meta[1:2, :])[:, :docs]
    prefix = jnp.where(h == 0, emb[:, :PREFIX], near_ref[...])

    scores = dot_nt(cent_ref[:, :PREFIX], prefix) * TEMP
    top = jnp.max(scores, axis=0, keepdims=True)
    scale = 1.0 / jnp.sum(jnp.exp(scores - top), axis=0, keepdims=True)
    own = dot_nt(own_prefix_ref[...], prefix) * TEMP
    weights = jnp.where(cid >= 0.0, jnp.exp(own - top) * scale, 0.0)
    sums = dot(weights.astype(BF16), emb)
    ones = jnp.ones((SUBLANES, docs), BF16)
    for t in range(subs):
        here = slice(t * per, (t + 1) * per)
        mass = dot_nt(ones, weights[here].astype(BF16))
        if first:
            acc_ref[t, :per, :] = sums[here]
            acc_ref[t, per:, :] = jnp.zeros((SUBLANES, half), F32)
            acc_ref[t, per:, :per] = mass
        else:
            acc_ref[t, :per, :] = acc_in[t, :per, :] + sums[here]
            acc_ref[t, per:, :] = acc_in[t, per:, :]
            acc_ref[t, per:, :per] = acc_in[t, per:, :per] + mass

    match = (inv_ref[...] == cid).astype(F32)
    before = lax.broadcasted_iota(jnp.int32, (docs, docs), 0) < lax.broadcasted_iota(jnp.int32, (docs, docs), 1)
    earlier = dot(match.astype(BF16), before.astype(F32).astype(BF16))
    groups = subs * per // SUBLANES
    picks = [jnp.where(earlier == r, match, 0.0).reshape(groups, SUBLANES, docs) for r in range(MOST)]
    pick = jnp.stack(picks, axis=1).reshape(groups * MOST * SUBLANES, docs)
    present = jnp.sum(pick, axis=1, keepdims=True)
    raw = dot(pick.astype(BF16), emb)
    centre = centre_ref[...].astype(F32).reshape(groups, 1, SUBLANES, half)
    centre = jnp.broadcast_to(centre, (groups, MOST, SUBLANES, half)).reshape(raw.shape)
    rows = jnp.where(present > 0.0, raw - centre, 0.0).astype(BF16)
    rows = rows.reshape(subs, per // SUBLANES, MOST * SUBLANES, half)
    for t in range(subs):
        row_refs[t][...] = rows[t]


def gram_kernel(plan, subs, rows, *refs):
    *member_refs, gram_ref, held = refs
    z, x = lax.axis_index("rows"), lax.axis_index("sub")
    owners, groups, packed, half = held.shape
    for t in range(subs):
        for at, (down, up) in enumerate(plan):
            source = jnp.where(z >= down, z - down, z + up) if up else z - down
            if not down and up:
                source = z + up
            valid = (source >= 0) & (source < rows)
            ref = member_refs[t * len(plan) + at]

            @pl.when(valid)
            def _(ref=ref, source=source, t=t):
                held[source * subs + (x - t + subs) % subs] = ref[...]

    size = owners * packed
    slots = size // SUBLANES
    lane = lax.broadcasted_iota(jnp.int32, (1, SUBLANES, size), 2) % SUBLANES
    same = (lane == lax.broadcasted_iota(jnp.int32, (1, SUBLANES, size), 1)).astype(F32)
    tile = min(size, 2 * LANES)
    for g in range(groups):
        mine = held[:, g].reshape(size, half)
        for start in range(0, size, tile):
            part = dot_nt(mine[start : start + tile], mine)
            part = part.reshape(tile // SUBLANES, SUBLANES, size)
            gram_ref[g, start // SUBLANES : (start + tile) // SUBLANES, :] = jnp.sum(part * same, axis=1)


def similarity_kernel(width, mine_ref, other_ref, out_ref):
    groups, slots, size = mine_ref.shape
    kept = out_ref.shape[1]
    h = lax.axis_index("dim")
    start = pl.multiple_of(h * kept, kept)
    row = lax.broadcasted_iota(jnp.int32, (slots, size), 0)
    lane = lax.broadcasted_iota(jnp.int32, (slots, size), 1)
    diagonal = row == lane // SUBLANES
    kept_row = lax.broadcasted_iota(jnp.int32, (kept, size), 0) + start
    kept_lane = lax.broadcasted_iota(jnp.int32, (kept, size), 1)
    kept_diagonal = kept_row == kept_lane // SUBLANES
    for g in range(groups):
        total = mine_ref[g] + other_ref[g]
        norms = jnp.sum(jnp.where(diagonal, total, 0.0), axis=0, keepdims=True)
        scale = lax.rsqrt(norms / width + EPS)
        spread = jnp.where(kept_diagonal, jnp.broadcast_to(scale, (kept, size)), 0.0)
        folded = spread[:, :LANES]
        for at in range(LANES, size, LANES):
            folded = folded + spread[:, at : at + LANES]
        step = SUBLANES
        while step < LANES:
            folded = folded + pltpu.roll(folded, step, 1)
            step *= 2
        row_scale = jnp.concatenate([folded] * (size // LANES), axis=1)
        own = mine_ref[g, pl.ds(start, kept), :] + other_ref[g, pl.ds(start, kept), :]
        out_ref[g] = (own / width * row_scale * scale).astype(BF16)


def centroid_kernel(per, acc_ref, *refs):
    *other_refs, prior_ref, out_ref = refs
    total = acc_ref[0]
    for other in other_refs:
        total = total + other[...]
    mass = jnp.transpose(total[per:, :LANES])[:per, :1]
    out_ref[...] = (total[:per] + SMOOTH * prior_ref[...].astype(F32)) / (mass + SMOOTH)


def shards(embeddings, centroids, cluster_id, cluster_place):
    docs, half = embeddings.shape
    clusters, width = centroids.shape
    rows, subs = lax.axis_size("rows"), lax.axis_size("sub")
    owners = rows * subs
    per = clusters // owners
    groups = per // SUBLANES
    packed = MOST * SUBLANES
    slots = owners * MOST
    z = lax.axis_index("rows")

    cid = cluster_id.reshape(1, docs)
    digits = jnp.concatenate([cid // DIGIT + 1, cid % DIGIT], axis=0).astype(BF16)
    meta = jnp.pad(digits, ((0, META - 2), (0, half - docs)))
    block = jnp.concatenate([embeddings, meta], axis=0)

    def along(value, pairs):
        return lax.ppermute(value, "rows", pairs)

    blocks, plan = [block], [(0, 0)]
    from_below, from_above, merged = block, block, None
    for step in range(1, rows):
        upward = [(i, i + 1) for i in range(step - 1, rows - 1)]
        downward = [(i, i - 1) for i in range(1, rows - step + 1)]
        if merged is not None:
            merged = along(merged, upward + downward)
        else:
            from_below = along(from_below, upward)
            from_above = along(from_above, downward)
            if 2 * step >= rows:
                merged = jnp.where(z >= step, from_below, from_above)
        if merged is None:
            blocks += [from_below, from_above]
            plan += [(step, 0), (0, step)]
        else:
            blocks.append(merged)
            plan.append((step, step))

    inv, centre, own_prefix, prior = pl.pallas_call(
        functools.partial(prep_kernel, subs, per),
        out_shape=(
            jax.ShapeDtypeStruct((subs * per, 1), F32),
            jax.ShapeDtypeStruct((subs * per, half), BF16),
            jax.ShapeDtypeStruct((subs * per, PREFIX), BF16),
            jax.ShapeDtypeStruct((per, half), BF16),
        ),
        in_specs=[vmem()] * 2,
        out_specs=(vmem(),) * 4,
        compiler_params=params(),
        name="prep",
    )(cluster_place.reshape(1, clusters), centroids)

    acc_shape = jax.ShapeDtypeStruct((subs, per + SUBLANES, half), F32)
    row_shape = jax.ShapeDtypeStruct((groups, packed, half), BF16)
    swaps = [[(i, (i + t) % subs) for i in range(subs)] for t in range(subs)]
    members = [[] for _ in range(subs)]
    acc = None
    for block in blocks:
        near = lax.ppermute(block[:docs, :PREFIX], "dim", [(0, 1)])
        first = acc is None
        operands = [block, near, centroids, own_prefix, inv, centre] + ([] if first else [acc])
        acc, *found = pl.pallas_call(
            functools.partial(block_kernel, first, subs, per),
            out_shape=(acc_shape,) + (row_shape,) * subs,
            in_specs=[vmem()] * len(operands),
            out_specs=(vmem(),) * (1 + subs),
            input_output_aliases={} if first else {6: 0},
            compiler_params=params(),
            name="block",
            cost_estimate=pl.CostEstimate(
                flops=2 * docs * (clusters * PREFIX + 4 * subs * per * half),
                bytes_accessed=4 * 1024 * 1024,
                transcendentals=docs * clusters,
            ),
        )(*operands)
        members[0].append(found[0])
        for t in range(1, subs):
            members[t].append(lax.ppermute(found[t], "sub", swaps[t]))

    others = [lax.ppermute(acc[t], "sub", swaps[t]) for t in range(1, subs)]
    new_centroids = pl.pallas_call(
        functools.partial(centroid_kernel, per),
        out_shape=jax.ShapeDtypeStruct((per, half), F32),
        in_specs=[vmem()] * (subs + 1),
        out_specs=vmem(),
        compiler_params=params(),
        name="centroids",
    )(acc, *others, prior)

    gram = pl.pallas_call(
        functools.partial(gram_kernel, plan, subs, rows),
        out_shape=jax.ShapeDtypeStruct((groups, slots, slots * SUBLANES), F32),
        in_specs=[vmem()] * (subs * len(plan)),
        out_specs=vmem(),
        scratch_shapes=[pltpu.VMEM((owners, groups, packed, half), BF16)],
        compiler_params=params(),
        name="gram",
    )(*[ref for column in members for ref in column])
    other_gram = lax.ppermute(gram, "dim", [(0, 1), (1, 0)])
    tiles = pl.pallas_call(
        functools.partial(similarity_kernel, width),
        out_shape=jax.ShapeDtypeStruct((groups, slots // 2, slots * SUBLANES), BF16),
        in_specs=[vmem()] * 2,
        out_specs=vmem(),
        compiler_params=params(),
        name="similarity",
    )(gram, other_gram)
    tiles = tiles.reshape(groups, slots // 2, slots, SUBLANES)
    similarity = jnp.transpose(tiles, (0, 3, 1, 2)).reshape(per, slots // 2, slots)
    return (new_centroids, similarity)


def solution(mesh):
    in_specs = (
        P(("parts", "rows", "sub"), "dim"),
        P("parts", None),
        P(("parts", "rows", "sub"), None),
        P(),
    )
    out_specs = (P(("parts", "rows", "sub"), "dim"), P(("parts", "rows", "sub"), "dim", None))
    return jax.shard_map(shards, mesh=mesh, in_specs=in_specs, out_specs=out_specs, check_vma=False)
```

time: 179 us -> 93.6 us (0.52)
  waiting for transfers between devices: 96.7 us -> 53 us
  blocking collectives: 22 us -> 0 us
  between operations: 14.9 us -> 0.94 us
  Pallas kernels: 0 us -> 13 us
  local copies, waits for them, and re-layouts: 13.7 us -> 1.65 us
  other arithmetic: 11.7 us -> 1.86 us
  starting transfers between devices: 13.4 us -> 22.7 us
  matrix products: 6.31 us -> 0 us
    ppermute x1 -> x17, waiting for transfers between devices: 0.32 us -> 53 us  [the longest x5 33.7 us: along(): return lax.ppermute(value, 'rows', pairs)]
    reduce_scatter x2 -> x0, waiting for transfers between devices: 51.2 us -> none  [the longest x1 51.1 us: shards(): lax.psum_scatter(lax.dot_general(weights, embeddings, (((0,), (0,)), ((),...]
    all_to_all x2 -> x0, waiting for transfers between devices: 45.1 us -> none  [the longest x1 43.3 us: shards(): lax.all_to_all(outgoing, ('rows', 'sub'), split_axis=0, concat_axis=0, ti...]
    ppermute x1 -> x17, starting transfers between devices: 1.49 us -> 22.7 us  [the longest x5 9.77 us: along(): return lax.ppermute(value, 'rows', pairs)]
    unnamed x1 -> x0, blocking collectives: 19.6 us -> none
    pallas_call x0 -> x9, Pallas kernels: none -> 13 us  [the longest x5 10.1 us: shards(): pl.pallas_call(functools.partial(block_kernel, first, subs, per), out_sha...]
    all_to_all x2 -> x0, starting transfers between devices: 11.9 us -> none  [the longest x1 7.25 us: shards(): lax.all_to_all(present, ('rows', 'sub'), split_axis=0, concat_axis=0, til...]
    scatter x2 -> x0, local copies, waits for them, and re-layouts: 8.29 us -> none  [the longest x1 4.51 us: shards(): jnp.zeros((clusters * per_cluster, half_width), jnp.bfloat16).at[slot]]
  transfers between devices with their start and end apart: 5 -> 17, of which waited for: 4 -> 9; matrix products, arithmetic and copies ran while one was open for 8% -> 0% of each run, Pallas kernels for 0% -> 14%
where the time goes in v1:
time: 93.6 us; the launch traced here: 93.2 us
  waiting for transfers between devices  53 us (57%)
  starting transfers between devices  22.7 us (24%)
  Pallas kernels  13 us (14%)
  other arithmetic  1.86 us (2%)
  local copies, waits for them, and re-layouts  1.65 us (2%)
  between operations  0.94 us (1%)
    ppermute x5, waiting for transfers between devices, along(): return lax.ppermute(value, 'rows', pairs)  33.7 us
    ppermute x5, waiting for transfers between devices, shards(): members[t].append(lax.ppermute(found[t], 'sub', swaps[t]))  17.2 us
    pallas_call x5, Pallas kernels, shards(): pl.pallas_call(functools.partial(block_kernel, first, subs, per), out_sha...  10.1 us
    ppermute x5, starting transfers between devices, along(): return lax.ppermute(value, 'rows', pairs)  9.77 us
    ppermute x5, starting transfers between devices, shards(): near = lax.ppermute(block[:docs, :PREFIX], 'dim', [(0, 1)])  6.53 us
    ppermute x5, starting transfers between devices, shards(): members[t].append(lax.ppermute(found[t], 'sub', swaps[t]))  5.8 us
    ppermute x1, waiting for transfers between devices, shards(): others = [lax.ppermute(acc[t], 'sub', swaps[t]) for t in range(1, subs)]  2.06 us
  transfers between devices with their start and end apart: 17, of which 9 were waited for; matrix products, arithmetic and copies ran while one was open for 0% of the time, Pallas kernels for 14%

profile of v1, /device:TPU:0, one launch (start us, length us, event | category | flops | bytes accessed | tf_op | source)
XLA Modules:
  0.0 93.2 jit_solution(11917967843420029021)
XLA Ops:
  0.6 0.7 add_convert_fusion
  1.4 1.1 %pad_maximum_fusion.block_ref = bf16[528,512]{1,0:T(8,128)(2,1)S(1)} fusion(bf16[16,512]{1,0:T(8,128)(2,1)S(1)} %fusion.2, bf16[512,512]{1,0:T(8,128)(2,1)} %param.4), kind=kLoop, calls=%fused_computation | loop fusion | flops 1081344 | bytes 1081344 | tf_op jit(solution)/shard_map/concatenate | solution.py:189
  2.4 0.0 copy-start.2
  2.5 5.1 %collective-permute-start = (bf16[528,512]{1,0:T(8,128)(2,1)S(1)}, bf16[528,512]{1,0:T(8,128)(2,1)S(1)}, u32[]{:S(2)}, u32[]{:S(2)}) collective-permute-start(bf16[528,512]{1,0:T(8,128)(2,1)S(1)} %pad_maximum_fusion.block_ref), channel_id=1, source_target_pairs={{0,4},{4,8},{8,12},{1,5},{5,9},{9,13},{2,6},{6,10},{10,14},{3,7},{... | collective-permute-start | bytes 1622024 | tf_op jit(solution)/shard_map/ppermute | solution.py:192
  7.6 1.3 %collective-permute-start.2 = (bf16[528,512]{1,0:T(8,128)(2,1)S(1)}, bf16[528,512]{1,0:T(8,128)(2,1)S(1)}, u32[]{:S(2)}, u32[]{:S(2)}) collective-permute-start(bf16[528,512]{1,0:T(8,128)(2,1)S(1)} %pad_maximum_fusion.block_ref), channel_id=1, source_target_pairs={{4,0},{8,4},{12,8},{5,1},{9,5},{13,9},{6,2},{10,6},{14,10},{7,3},{... | collective-permute-start | bytes 1622024 | tf_op jit(solution)/shard_map/ppermute | solution.py:192
  8.9 10.2 %collective-permute-done.block_ref = bf16[528,512]{1,0:T(8,128)(2,1)S(1)} collective-permute-done((bf16[528,512]{1,0:T(8,128)(2,1)S(1)}, bf16[528,512]{1,0:T(8,128)(2,1)S(1)}, u32[]{:S(2)}, u32[]{:S(2)}) %collective-permute-start) | collective-permute-done | bytes 540704 | tf_op jit(solution)/shard_map/ppermute | solution.py:192
  19.0 0.7 collective-permute-start.1
  19.7 3.5 %collective-permute-done.2.block_ref = bf16[528,512]{1,0:T(8,128)(2,1)S(1)} collective-permute-done((bf16[528,512]{1,0:T(8,128)(2,1)S(1)}, bf16[528,512]{1,0:T(8,128)(2,1)S(1)}, u32[]{:S(2)}, u32[]{:S(2)}) %collective-permute-start.2) | collective-permute-done | bytes 540704 | tf_op jit(solution)/shard_map/ppermute | solution.py:192
  23.2 1.3 %collective-permute-start.3 = (bf16[528,512]{1,0:T(8,128)(2,1)S(1)}, bf16[528,512]{1,0:T(8,128)(2,1)S(1)}, u32[]{:S(2)}, u32[]{:S(2)}) collective-permute-start(bf16[528,512]{1,0:T(8,128)(2,1)S(1)} %collective-permute-done.2.block_ref), channel_id=1, source_target_pairs={{4,0},{8,4},{5,1},{9,5},{6,2},{10,6},{7,3},{11,7},{20,16},{24,20},... | collective-permute-start | bytes 1622024 | tf_op jit(solution)/shard_map/ppermute | solution.py:192
  24.5 13.6 %collective-permute-done.3 = bf16[528,512]{1,0:T(8,128)(2,1)S(1)} collective-permute-done((bf16[528,512]{1,0:T(8,128)(2,1)S(1)}, bf16[528,512]{1,0:T(8,128)(2,1)S(1)}, u32[]{:S(2)}, u32[]{:S(2)}) %collective-permute-start.3) | collective-permute-done | bytes 540704 | tf_op jit(solution)/shard_map/ppermute | solution.py:192
  38.1 0.1 broadcast_select_fusion.block_ref
  38.1 0.0 copy-start
  38.1 1.4 %collective-permute-start.4 = (bf16[528,512]{1,0:T(8,128)(2,1)S(1)}, bf16[528,512]{1,0:T(8,128)(2,1)S(1)}, u32[]{:S(2)}, u32[]{:S(2)}) collective-permute-start(bf16[528,512]{1,0:T(8,128)(2,1)S(1)} %broadcast_select_fusion.block_ref), channel_id=1, source_target_pairs={{8,12},{4,0},{9,13},{5,1},{10,14},{6,2},{11,15},{7,3},{24,28},{20,... | collective-permute-start | bytes 1622024 | tf_op jit(solution)/shard_map/ppermute | solution.py:192
  39.6 1.3 %collective-permute-start.9 = (bf16[512,256]{1,0:T(8,128)(2,1)S(1)}, bf16[512,256]{1,0:T(8,128)(2,1)S(1)}, u32[]{:S(2)}, u32[]{:S(2)}) collective-permute-start(bf16[512,256]{1,0:T(8,128)(2,1)S(1)} %slice.22), channel_id=1, source_target_pairs={{0,1},{2,3},{4,5},{6,7},{8,9},{10,11},{12,13},{14,15},{16,17},{18,... | collective-permute-start | bytes 786440 | tf_op jit(solution)/shard_map/ppermute | solution.py:233
  41.0 1.3 %collective-permute-start.8 = (bf16[512,256]{1,0:T(8,128)(2,1)S(1)}, bf16[512,256]{1,0:T(8,128)(2,1)S(1)}, u32[]{:S(2)}, u32[]{:S(2)}) collective-permute-start(bf16[512,256]{1,0:T(8,128)(2,1)S(1)} %slice.27), channel_id=1, source_target_pairs={{0,1},{2,3},{4,5},{6,7},{8,9},{10,11},{12,13},{14,15},{16,17},{18,... | collective-permute-start | bytes 786440 | tf_op jit(solution)/shard_map/ppermute | solution.py:233
  42.3 1.3 %collective-permute-start.7 = (bf16[512,256]{1,0:T(8,128)(2,1)S(1)}, bf16[512,256]{1,0:T(8,128)(2,1)S(1)}, u32[]{:S(2)}, u32[]{:S(2)}) collective-permute-start(bf16[512,256]{1,0:T(8,128)(2,1)S(1)} %slice.26), channel_id=1, source_target_pairs={{0,1},{2,3},{4,5},{6,7},{8,9},{10,11},{12,13},{14,15},{16,17},{18,... | collective-permute-start | bytes 786440 | tf_op jit(solution)/shard_map/ppermute | solution.py:233
  43.6 1.3 %collective-permute-start.6 = (bf16[512,256]{1,0:T(8,128)(2,1)S(1)}, bf16[512,256]{1,0:T(8,128)(2,1)S(1)}, u32[]{:S(2)}, u32[]{:S(2)}) collective-permute-start(bf16[512,256]{1,0:T(8,128)(2,1)S(1)} %slice.25), channel_id=1, source_target_pairs={{0,1},{2,3},{4,5},{6,7},{8,9},{10,11},{12,13},{14,15},{16,17},{18,... | collective-permute-start | bytes 786440 | tf_op jit(solution)/shard_map/ppermute | solution.py:233
  45.0 0.8 prep.1
  45.8 6.5 %collective-permute-done.4.block_ref = bf16[528,512]{1,0:T(8,128)(2,1)S(1)} collective-permute-done((bf16[528,512]{1,0:T(8,128)(2,1)S(1)}, bf16[528,512]{1,0:T(8,128)(2,1)S(1)}, u32[]{:S(2)}, u32[]{:S(2)}) %collective-permute-start.4) | collective-permute-done | bytes 540704 | tf_op jit(solution)/shard_map/ppermute | solution.py:192
  52.3 1.3 %collective-permute-start.5 = (bf16[512,256]{1,0:T(8,128)(2,1)S(1)}, bf16[512,256]{1,0:T(8,128)(2,1)S(1)}, u32[]{:S(2)}, u32[]{:S(2)}) collective-permute-start(bf16[512,256]{1,0:T(8,128)(2,1)S(1)} %slice.24), channel_id=1, source_target_pairs={{0,1},{2,3},{4,5},{6,7},{8,9},{10,11},{12,13},{14,15},{16,17},{18,... | collective-permute-start | bytes 786440 | tf_op jit(solution)/shard_map/ppermute | solution.py:233
  53.6 0.0 collective-permute-done.9.near_ref
  53.6 2.0 %block.5 = (f32[2,136,512]{2,1,0:T(8,128)S(1)}, bf16[16,16,512]{2,1,0:T(8,128)(2,1)S(1)}, bf16[16,16,512]{2,1,0:T(8,128)(2,1)S(1)}) custom-call(bf16[528,512]{1,0:T(8,128)(2,1)S(1)} %pad_maximum_fusion.block_ref, bf16[512,256]{1,0:T(8,128)(2,1)S(1)} %collective-permute-done.9.near_ref, bf16[1024,1024]{1,0:T(8,128)(2,1)S(1)} %copy-done, ...), custom_call_target="tpu_custom_call" | custom-call | flops 805306368 | bytes 4194304 | tf_op jit(solution)/shard_map/block/pallas_call | solution.py:236
  55.5 1.6 %collective-permute-start.11 = (bf16[16,16,512]{2,1,0:T(8,128)(2,1)S(1)}, bf16[16,16,512]{2,1,0:T(8,128)(2,1)S(1)}, u32[]{:S(2)}, u32[]{:S(2)}) collective-permute-start(bf16[16,16,512]{2,1,0:T(8,128)(2,1)S(1)} %get-tuple-element.35), channel_id=1, source_target_pairs={{0,2},{2,0},{1,3},{3,1},{4,6},{6,4},{5,7},{7,5},{8,10},{10,8},{9,1... | collective-permute-start | bytes 786440 | tf_op jit(solution)/shard_map/ppermute | solution.py:252
  57.1 2.0 %block.6 = (f32[2,136,512]{2,1,0:T(8,128)S(1)}, bf16[16,16,512]{2,1,0:T(8,128)(2,1)S(1)}, bf16[16,16,512]{2,1,0:T(8,128)(2,1)S(1)}) custom-call(bf16[528,512]{1,0:T(8,128)(2,1)S(1)} %collective-permute-done.block_ref, bf16[512,256]{1,0:T(8,128)(2,1)S(1)} %collective-permute-done.8.near_ref, ...), custom_call_target="tpu_custom_call", output_to_operand_aliasing={{0}: (6, {})} | custom-call | flops 805306368 | bytes 4194304 | tf_op jit(solution)/shard_map/block/pallas_call | solution.py:236
  59.2 0.0 collective-permute-done.7.near_ref
  59.2 2.0 %block.7 = (f32[2,136,512]{2,1,0:T(8,128)S(1)}, bf16[16,16,512]{2,1,0:T(8,128)(2,1)S(1)}, bf16[16,16,512]{2,1,0:T(8,128)(2,1)S(1)}) custom-call(bf16[528,512]{1,0:T(8,128)(2,1)S(1)} %collective-permute-done.2.block_ref, bf16[512,256]{1,0:T(8,128)(2,1)S(1)} %collective-permute-done.7.near_ref, ...), custom_call_target="tpu_custom_call", output_to_operand_aliasing={{0}: (6, {})} | custom-call | flops 805306368 | bytes 4194304 | tf_op jit(solution)/shard_map/block/pallas_call | solution.py:236
  61.2 0.6 collective-permute-start.13
  61.8 1.5 %collective-permute-start.12 = (bf16[16,16,512]{2,1,0:T(8,128)(2,1)S(1)}, bf16[16,16,512]{2,1,0:T(8,128)(2,1)S(1)}, u32[]{:S(2)}, u32[]{:S(2)}) collective-permute-start(bf16[16,16,512]{2,1,0:T(8,128)(2,1)S(1)} %get-tuple-element.36), channel_id=1, source_target_pairs={{0,2},{2,0},{1,3},{3,1},{4,6},{6,4},{5,7},{7,5},{8,10},{10,8},{9,1... | collective-permute-start | bytes 786440 | tf_op jit(solution)/shard_map/ppermute | solution.py:252
  63.3 0.0 collective-permute-done.6.near_ref
  63.3 2.0 %block.8 = (f32[2,136,512]{2,1,0:T(8,128)S(1)}, bf16[16,16,512]{2,1,0:T(8,128)(2,1)S(1)}, bf16[16,16,512]{2,1,0:T(8,128)(2,1)S(1)}) custom-call(bf16[528,512]{1,0:T(8,128)(2,1)S(1)} %broadcast_select_fusion.block_ref, bf16[512,256]{1,0:T(8,128)(2,1)S(1)} %collective-permute-done.6.near_ref, ...), custom_call_target="tpu_custom_call", output_to_operand_aliasing={{0}: (6, {})} | custom-call | flops 805306368 | bytes 4194304 | tf_op jit(solution)/shard_map/block/pallas_call | solution.py:236
  65.3 0.6 collective-permute-start.14
  65.9 0.0 collective-permute-done.5.near_ref
  65.9 2.0 %block.9 = (f32[2,136,512]{2,1,0:T(8,128)S(1)}, bf16[16,16,512]{2,1,0:T(8,128)(2,1)S(1)}, bf16[16,16,512]{2,1,0:T(8,128)(2,1)S(1)}) custom-call(bf16[528,512]{1,0:T(8,128)(2,1)S(1)} %collective-permute-done.4.block_ref, bf16[512,256]{1,0:T(8,128)(2,1)S(1)} %collective-permute-done.5.near_ref, ...), custom_call_target="tpu_custom_call", output_to_operand_aliasing={{0}: (6, {})} | custom-call | flops 805306368 | bytes 4194304 | tf_op jit(solution)/shard_map/block/pallas_call | solution.py:236
  67.9 1.6 %collective-permute-start.15 = (bf16[16,16,512]{2,1,0:T(8,128)(2,1)S(1)}, bf16[16,16,512]{2,1,0:T(8,128)(2,1)S(1)}, u32[]{:S(2)}, u32[]{:S(2)}) collective-permute-start(bf16[16,16,512]{2,1,0:T(8,128)(2,1)S(1)} %get-tuple-element.39), channel_id=1, source_target_pairs={{0,2},{2,0},{1,3},{3,1},{4,6},{6,4},{5,7},{7,5},{8,10},{10,8},{9,1... | collective-permute-start | bytes 786440 | tf_op jit(solution)/shard_map/ppermute | solution.py:252
  69.5 0.0 collective-permute-done.11.refs_5_
  69.5 0.6 collective-permute-start.10
  70.1 0.4 collective-permute-done.13.refs_7_
  70.5 5.6 %collective-permute-done.12.refs_6_ = bf16[16,16,512]{2,1,0:T(8,128)(2,1)S(1)} collective-permute-done((bf16[16,16,512]{2,1,0:T(8,128)(2,1)S(1)}, bf16[16,16,512]{2,1,0:T(8,128)(2,1)S(1)}, u32[]{:S(2)}, u32[]{:S(2)}) %collective-permute-start.12) | collective-permute-done | bytes 262176 | tf_op jit(solution)/shard_map/ppermute | solution.py:252
  76.1 5.6 %collective-permute-done.14.refs_8_ = bf16[16,16,512]{2,1,0:T(8,128)(2,1)S(1)} collective-permute-done((bf16[16,16,512]{2,1,0:T(8,128)(2,1)S(1)}, bf16[16,16,512]{2,1,0:T(8,128)(2,1)S(1)}, u32[]{:S(2)}, u32[]{:S(2)}) %collective-permute-start.14) | collective-permute-done | bytes 262176 | tf_op jit(solution)/shard_map/ppermute | solution.py:252
  81.7 5.6 %collective-permute-done.15.refs_9_ = bf16[16,16,512]{2,1,0:T(8,128)(2,1)S(1)} collective-permute-done((bf16[16,16,512]{2,1,0:T(8,128)(2,1)S(1)}, bf16[16,16,512]{2,1,0:T(8,128)(2,1)S(1)}, u32[]{:S(2)}, u32[]{:S(2)}) %collective-permute-start.15) | collective-permute-done | bytes 262176 | tf_op jit(solution)/shard_map/ppermute | solution.py:252
  87.4 0.9 gram.1.mine_ref
  88.3 0.1 collective-permute-start.16
  88.4 2.1 %collective-permute-done.10.refs_0_ = f32[136,512]{1,0:T(8,128)S(1)} collective-permute-done((f32[136,512]{1,0:T(8,128)S(1)}, f32[136,512]{1,0:T(8,128)S(1)}, u32[]{:S(2)}, u32[]{:S(2)}) %collective-permute-start.10) | collective-permute-done | bytes 278560 | tf_op jit(solution)/shard_map/ppermute | solution.py:254
  90.4 0.9 centroids.1
  91.3 0.3 similarity.1
  91.6 0.2 copy.11
  91.8 0.6 copy.12
  92.4 0.8 copy.13
  (15 shorter events, 0.1 us)
Async XLA Ops:
  2.4 37.1 %copy-start.2 = (bf16[512,512]{1,0:T(8,128)(2,1)S(1)}, bf16[512,512]{1,0:T(8,128)(2,1)}, u32[]{:S(2)}) copy-start(bf16[512,512]{1,0:T(8,128)(2,1)} %param.4) | copy-start | bytes 1572868
  2.5 16.6 %collective-permute-start = (bf16[528,512]{1,0:T(8,128)(2,1)S(1)}, bf16[528,512]{1,0:T(8,128)(2,1)S(1)}, u32[]{:S(2)}, u32[]{:S(2)}) collective-permute-start(bf16[528,512]{1,0:T(8,128)(2,1)S(1)} %pad_maximum_fusion.block_ref), channel_id=1, source_target_pairs={{0,4},{4,8},{8,12},{1,5},{5,9},{9,13},{2,6},{6,10},{10,14},{3,7},{... | collective-permute-start | bytes 1622024 | tf_op jit(solution)/shard_map/ppermute | solution.py:192
  7.6 15.6 %collective-permute-start.2 = (bf16[528,512]{1,0:T(8,128)(2,1)S(1)}, bf16[528,512]{1,0:T(8,128)(2,1)S(1)}, u32[]{:S(2)}, u32[]{:S(2)}) collective-permute-start(bf16[528,512]{1,0:T(8,128)(2,1)S(1)} %pad_maximum_fusion.block_ref), channel_id=1, source_target_pairs={{4,0},{8,4},{12,8},{5,1},{9,5},{13,9},{6,2},{10,6},{14,10},{7,3},{... | collective-permute-start | bytes 1622024 | tf_op jit(solution)/shard_map/ppermute | solution.py:192
  19.0 5.4 %collective-permute-start.1 = (bf16[528,512]{1,0:T(8,128)(2,1)S(1)}, bf16[528,512]{1,0:T(8,128)(2,1)S(1)}, u32[]{:S(2)}, u32[]{:S(2)}) collective-permute-start(bf16[528,512]{1,0:T(8,128)(2,1)S(1)} %collective-permute-done.block_ref), channel_id=1, source_target_pairs={{4,8},{8,12},{5,9},{9,13},{6,10},{10,14},{7,11},{11,15},{20,24},{2... | collective-permute-start | bytes 1622024 | tf_op jit(solution)/shard_map/ppermute | solution.py:192
  23.2 14.9 %collective-permute-start.3 = (bf16[528,512]{1,0:T(8,128)(2,1)S(1)}, bf16[528,512]{1,0:T(8,128)(2,1)S(1)}, u32[]{:S(2)}, u32[]{:S(2)}) collective-permute-start(bf16[528,512]{1,0:T(8,128)(2,1)S(1)} %collective-permute-done.2.block_ref), channel_id=1, source_target_pairs={{4,0},{8,4},{5,1},{9,5},{6,2},{10,6},{7,3},{11,7},{20,16},{24,20},... | collective-permute-start | bytes 1622024 | tf_op jit(solution)/shard_map/ppermute | solution.py:192
  38.1 6.9 %copy-start.1 = (s32[1024]{0:T(1024)S(1)}, s32[1024]{0:T(1024)}, u32[]{:S(2)}) copy-start(s32[1024]{0:T(1024)} %param.7) | copy-start | bytes 12292
  38.1 6.8 %copy-start = (bf16[1024,1024]{1,0:T(8,128)(2,1)S(1)}, bf16[1024,1024]{1,0:T(8,128)(2,1)}, u32[]{:S(2)}) copy-start(bf16[1024,1024]{1,0:T(8,128)(2,1)} %cent_ref.11) | copy-start | bytes 6291460
  38.1 14.1 %collective-permute-start.4 = (bf16[528,512]{1,0:T(8,128)(2,1)S(1)}, bf16[528,512]{1,0:T(8,128)(2,1)S(1)}, u32[]{:S(2)}, u32[]{:S(2)}) collective-permute-start(bf16[528,512]{1,0:T(8,128)(2,1)S(1)} %broadcast_select_fusion.block_ref), channel_id=1, source_target_pairs={{8,12},{4,0},{9,13},{5,1},{10,14},{6,2},{11,15},{7,3},{24,28},{20,... | collective-permute-start | bytes 1622024 | tf_op jit(solution)/shard_map/ppermute | solution.py:192
  39.6 14.0 %collective-permute-start.9 = (bf16[512,256]{1,0:T(8,128)(2,1)S(1)}, bf16[512,256]{1,0:T(8,128)(2,1)S(1)}, u32[]{:S(2)}, u32[]{:S(2)}) collective-permute-start(bf16[512,256]{1,0:T(8,128)(2,1)S(1)} %slice.22), channel_id=1, source_target_pairs={{0,1},{2,3},{4,5},{6,7},{8,9},{10,11},{12,13},{14,15},{16,17},{18,... | collective-permute-start | bytes 786440 | tf_op jit(solution)/shard_map/ppermute | solution.py:233
  41.0 16.2 %collective-permute-start.8 = (bf16[512,256]{1,0:T(8,128)(2,1)S(1)}, bf16[512,256]{1,0:T(8,128)(2,1)S(1)}, u32[]{:S(2)}, u32[]{:S(2)}) collective-permute-start(bf16[512,256]{1,0:T(8,128)(2,1)S(1)} %slice.27), channel_id=1, source_target_pairs={{0,1},{2,3},{4,5},{6,7},{8,9},{10,11},{12,13},{14,15},{16,17},{18,... | collective-permute-start | bytes 786440 | tf_op jit(solution)/shard_map/ppermute | solution.py:233
  42.3 16.9 %collective-permute-start.7 = (bf16[512,256]{1,0:T(8,128)(2,1)S(1)}, bf16[512,256]{1,0:T(8,128)(2,1)S(1)}, u32[]{:S(2)}, u32[]{:S(2)}) collective-permute-start(bf16[512,256]{1,0:T(8,128)(2,1)S(1)} %slice.26), channel_id=1, source_target_pairs={{0,1},{2,3},{4,5},{6,7},{8,9},{10,11},{12,13},{14,15},{16,17},{18,... | collective-permute-start | bytes 786440 | tf_op jit(solution)/shard_map/ppermute | solution.py:233
  43.6 19.7 %collective-permute-start.6 = (bf16[512,256]{1,0:T(8,128)(2,1)S(1)}, bf16[512,256]{1,0:T(8,128)(2,1)S(1)}, u32[]{:S(2)}, u32[]{:S(2)}) collective-permute-start(bf16[512,256]{1,0:T(8,128)(2,1)S(1)} %slice.25), channel_id=1, source_target_pairs={{0,1},{2,3},{4,5},{6,7},{8,9},{10,11},{12,13},{14,15},{16,17},{18,... | collective-permute-start | bytes 786440 | tf_op jit(solution)/shard_map/ppermute | solution.py:233
  52.3 13.6 %collective-permute-start.5 = (bf16[512,256]{1,0:T(8,128)(2,1)S(1)}, bf16[512,256]{1,0:T(8,128)(2,1)S(1)}, u32[]{:S(2)}, u32[]{:S(2)}) collective-permute-start(bf16[512,256]{1,0:T(8,128)(2,1)S(1)} %slice.24), channel_id=1, source_target_pairs={{0,1},{2,3},{4,5},{6,7},{8,9},{10,11},{12,13},{14,15},{16,17},{18,... | collective-permute-start | bytes 786440 | tf_op jit(solution)/shard_map/ppermute | solution.py:233
  55.5 14.0 %collective-permute-start.11 = (bf16[16,16,512]{2,1,0:T(8,128)(2,1)S(1)}, bf16[16,16,512]{2,1,0:T(8,128)(2,1)S(1)}, u32[]{:S(2)}, u32[]{:S(2)}) collective-permute-start(bf16[16,16,512]{2,1,0:T(8,128)(2,1)S(1)} %get-tuple-element.35), channel_id=1, source_target_pairs={{0,2},{2,0},{1,3},{3,1},{4,6},{6,4},{5,7},{7,5},{8,10},{10,8},{9,1... | collective-permute-start | bytes 786440 | tf_op jit(solution)/shard_map/ppermute | solution.py:252
  61.2 9.3 %collective-permute-start.13 = (bf16[16,16,512]{2,1,0:T(8,128)(2,1)S(1)}, bf16[16,16,512]{2,1,0:T(8,128)(2,1)S(1)}, u32[]{:S(2)}, u32[]{:S(2)}) collective-permute-start(bf16[16,16,512]{2,1,0:T(8,128)(2,1)S(1)} %get-tuple-element.37), channel_id=1, source_target_pairs={{0,2},{2,0},{1,3},{3,1},{4,6},{6,4},{5,7},{7,5},{8,10},{10,8},{9,1... | collective-permute-start | bytes 786440 | tf_op jit(solution)/shard_map/ppermute | solution.py:252
  61.8 14.4 %collective-permute-start.12 = (bf16[16,16,512]{2,1,0:T(8,128)(2,1)S(1)}, bf16[16,16,512]{2,1,0:T(8,128)(2,1)S(1)}, u32[]{:S(2)}, u32[]{:S(2)}) collective-permute-start(bf16[16,16,512]{2,1,0:T(8,128)(2,1)S(1)} %get-tuple-element.36), channel_id=1, source_target_pairs={{0,2},{2,0},{1,3},{3,1},{4,6},{6,4},{5,7},{7,5},{8,10},{10,8},{9,1... | collective-permute-start | bytes 786440 | tf_op jit(solution)/shard_map/ppermute | solution.py:252
  65.3 16.4 %collective-permute-start.14 = (bf16[16,16,512]{2,1,0:T(8,128)(2,1)S(1)}, bf16[16,16,512]{2,1,0:T(8,128)(2,1)S(1)}, u32[]{:S(2)}, u32[]{:S(2)}) collective-permute-start(bf16[16,16,512]{2,1,0:T(8,128)(2,1)S(1)} %get-tuple-element.38), channel_id=1, source_target_pairs={{0,2},{2,0},{1,3},{3,1},{4,6},{6,4},{5,7},{7,5},{8,10},{10,8},{9,1... | collective-permute-start | bytes 786440 | tf_op jit(solution)/shard_map/ppermute | solution.py:252
  67.9 19.4 %collective-permute-start.15 = (bf16[16,16,512]{2,1,0:T(8,128)(2,1)S(1)}, bf16[16,16,512]{2,1,0:T(8,128)(2,1)S(1)}, u32[]{:S(2)}, u32[]{:S(2)}) collective-permute-start(bf16[16,16,512]{2,1,0:T(8,128)(2,1)S(1)} %get-tuple-element.39), channel_id=1, source_target_pairs={{0,2},{2,0},{1,3},{3,1},{4,6},{6,4},{5,7},{7,5},{8,10},{10,8},{9,1... | collective-permute-start | bytes 786440 | tf_op jit(solution)/shard_map/ppermute | solution.py:252
  69.5 20.9 %collective-permute-start.10 = (f32[136,512]{1,0:T(8,128)S(1)}, f32[136,512]{1,0:T(8,128)S(1)}, u32[]{:S(2)}, u32[]{:S(2)}) collective-permute-start(f32[136,512]{1,0:T(8,128)S(1)} %slice_bitcast_fusion), channel_id=1, source_target_pairs={{0,2},{2,0},{1,3},{3,1},{4,6},{6,4},{5,7},{7,5},{8,10},{10,8},{9,1... | collective-permute-start | bytes 835592 | tf_op jit(solution)/shard_map/ppermute | solution.py:254
  88.3 3.0 %collective-permute-start.16 = (f32[16,16,128]{2,1,0:T(8,128)S(1)}, f32[16,16,128]{2,1,0:T(8,128)S(1)}, u32[]{:S(2)}, u32[]{:S(2)}) collective-permute-start(f32[16,16,128]{2,1,0:T(8,128)S(1)} %gram.1.mine_ref), channel_id=1, source_target_pairs={{0,1},{1,0},{2,3},{3,2},{4,5},{5,4},{6,7},{7,6},{8,9},{9,8},{10,11... | collective-permute-start | bytes 393224 | tf_op jit(solution)/shard_map/ppermute | solution.py:273

commit v2 on v1

v2 whole, which is shorter than its diff:
```python
import functools

import jax
import jax.numpy as jnp
from jax import lax
from jax.experimental import pallas as pl
from jax.experimental.pallas import tpu as pltpu
from jax.sharding import PartitionSpec as P

PREFIX = 256
MOST = 2

TEMP = 0.125
SMOOTH = 1.0
EPS = 1e-05

DIGIT = 32
META = 16
SUBLANES = 8
LANES = 128
F32 = jnp.float32
BF16 = jnp.bfloat16
VMEM_LIMIT = 40 * 1024 * 1024

NT = (((1,), (1,)), ((), ()))


def call(kernel, name, out_shape, operands, aliases=None, scratch=(), flops=0, transcendentals=0):
    def whole():
        return pl.BlockSpec(memory_space=pltpu.VMEM)

    return pl.pallas_call(
        kernel,
        out_shape=tuple(out_shape),
        in_specs=[whole() for _ in operands],
        out_specs=tuple(whole() for _ in out_shape),
        input_output_aliases=aliases or {},
        scratch_shapes=list(scratch),
        compiler_params=pltpu.CompilerParams(vmem_limit_bytes=VMEM_LIMIT),
        cost_estimate=pl.CostEstimate(flops=flops, bytes_accessed=1024 * 1024, transcendentals=transcendentals),
        name=name,
    )(*operands)


def dot(a, b):
    return jnp.dot(a, b, preferred_element_type=F32)


def dot_nt(a, b):
    return lax.dot_general(a, b, NT, preferred_element_type=F32)


def tied(values, *others):
    leaves, tree = jax.tree.flatten(values)
    kept = lax.optimization_barrier(tuple(leaves) + tuple(jax.tree.leaves(others)))
    return jax.tree.unflatten(tree, kept[: len(leaves)])


def arrivals(rows):
    table = []
    for k in range(rows):
        line = []
        for z in range(rows):
            below, above = z, rows - 1 - z
            both = min(below, above)
            if k == 0:
                line.append((0, z))
            elif k <= 2 * both:
                step = (k + 1) // 2
                line.append((step, z - step if k % 2 else z + step))
            else:
                step = k - both
                line.append((step, z - step if below > above else z + step))
        table.append(line)
    return table


def pack_kernel(emb_ref, cid_ref, lead_ref, rest_ref):
    docs = emb_ref.shape[0]
    lead_ref[:docs, :] = emb_ref[:, :PREFIX]
    rest_ref[...] = emb_ref[:, PREFIX:]
    cid = cid_ref[...]
    high, low = (cid // DIGIT + 1).astype(F32), (cid % DIGIT).astype(F32)
    rows = []
    for digit in (high, low):
        rows += [digit[:, at : at + PREFIX] for at in range(0, docs, PREFIX)]
    rows.append(jnp.zeros((META - len(rows), PREFIX), F32))
    lead_ref[docs:, :] = jnp.concatenate(rows, axis=0).astype(BF16)


def ids_of(lead_ref):
    docs = lead_ref.shape[0] - META
    meta = lead_ref[docs:, :].astype(F32)
    parts = docs // PREFIX
    high = jnp.concatenate([meta[i : i + 1] for i in range(parts)], axis=1)
    low = jnp.concatenate([meta[parts + i : parts + i + 1] for i in range(parts)], axis=1)
    return (high - 1.0) * DIGIT + low


def prep_kernel(subs, per, place_ref, cent_ref, inv_ref, centre_ref, own_prefix_ref, prior_ref):
    clusters = cent_ref.shape[0]
    half = centre_ref.shape[1]
    z, x, h = lax.axis_index("rows"), lax.axis_index("sub"), lax.axis_index("dim")
    row = lax.broadcasted_iota(jnp.int32, (subs * per, clusters), 0)
    ids = lax.broadcasted_iota(jnp.int32, (subs * per, clusters), 1)
    turn, within = row // per, row % per
    target = (z * subs + (x + turn) % subs) * per + within
    chosen = (place_ref[...] == target).astype(F32)
    inv_ref[...] = jnp.sum(chosen * ids.astype(F32), axis=1, keepdims=True)
    columns = cent_ref[:, pl.ds(pl.multiple_of(h * half, LANES), half)]
    centre_ref[...] = dot(chosen.astype(BF16), columns).astype(BF16)
    natural = (ids == target).astype(BF16)
    own_prefix_ref[...] = dot(natural, cent_ref[:, :PREFIX]).astype(BF16)
    prior_ref[...] = dot(natural[:per], columns).astype(BF16)


def centred(pick, centre, columns):
    slots = pick.shape[0]
    groups = slots // (MOST * SUBLANES)
    width = columns.shape[1]
    present = jnp.sum(pick.astype(F32), axis=1, keepdims=True)
    raw = dot(pick, columns)
    middle = centre.astype(F32).reshape(groups, 1, SUBLANES, width)
    middle = jnp.broadcast_to(middle, (groups, MOST, SUBLANES, width)).reshape(slots, width)
    return jnp.where(present > 0.0, raw - middle, 0.0).astype(BF16)


def picked(lead_ref, inv_ref):
    cid = ids_of(lead_ref)
    docs = cid.shape[1]
    groups = inv_ref.shape[0] // SUBLANES
    match = (inv_ref[...] == cid).astype(F32)
    before = lax.broadcasted_iota(jnp.int32, (docs, docs), 0) < lax.broadcasted_iota(jnp.int32, (docs, docs), 1)
    earlier = dot(match.astype(BF16), before.astype(F32).astype(BF16))
    ranked = [jnp.where(earlier == r, match, 0.0).reshape(groups, SUBLANES, docs) for r in range(MOST)]
    return jnp.stack(ranked, axis=1).reshape(groups * MOST * SUBLANES, docs).astype(BF16)


def select_kernel(lead_ref, rest_ref, inv_ref, centre_ref, *row_refs):
    docs = rest_ref.shape[0]
    pick = picked(lead_ref, inv_ref)
    groups, packed, _ = row_refs[0].shape
    for columns, at in ((lead_ref[:docs, :], 0), (rest_ref[...], PREFIX)):
        width = columns.shape[1]
        rows = centred(pick, centre_ref[:, at : at + width], columns)
        rows = rows.reshape(len(row_refs), groups, packed, width)
        for t, ref in enumerate(row_refs):
            ref[:, :, at : at + width] = rows[t]


def select_lead_kernel(lead_ref, inv_ref, centre_ref, pick_ref, *row_refs):
    docs = lead_ref.shape[0] - META
    pick = picked(lead_ref, inv_ref)
    pick_ref[...] = pick
    rows = centred(pick, centre_ref[:, :PREFIX], lead_ref[:docs, :])
    rows = rows.reshape((len(row_refs),) + row_refs[0].shape)
    for t, ref in enumerate(row_refs):
        ref[...] = rows[t]


def select_rest_kernel(pick_ref, rest_ref, centre_ref, *row_refs):
    rows = centred(pick_ref[...], centre_ref[:, PREFIX:], rest_ref[...])
    rows = rows.reshape((len(row_refs),) + row_refs[0].shape)
    for t, ref in enumerate(row_refs):
        ref[...] = rows[t]


def soft_weights(lead_ref, near_ref, cent_ref, own_prefix_ref):
    docs = lead_ref.shape[0] - META
    h = lax.axis_index("dim")
    prefix = jnp.where(h == 0, lead_ref[:docs, :], near_ref[:docs, :])
    scores = dot_nt(cent_ref[:, :PREFIX], prefix) * TEMP
    top = jnp.max(scores, axis=0, keepdims=True)
    scale = 1.0 / jnp.sum(jnp.exp(scores - top), axis=0, keepdims=True)
    own = dot_nt(own_prefix_ref[...], prefix) * TEMP
    return jnp.where(ids_of(lead_ref) >= 0.0, jnp.exp(own - top) * scale, 0.0)


def add_lead(weights, lead_ref, old_refs, new_refs):
    docs = lead_ref.shape[0] - META
    per = new_refs[0].shape[0] - SUBLANES
    sums = dot(weights.astype(BF16), lead_ref[:docs, :])
    ones = jnp.ones((SUBLANES, docs), BF16)
    for t, new in enumerate(new_refs):
        here = slice(t * per, (t + 1) * per)
        mass = dot_nt(ones, weights[here].astype(BF16))
        if old_refs:
            old = old_refs[t]
            new[:per, :] = old[:per, :] + sums[here]
            new[per:, :] = old[per:, :]
            new[per:, :per] = old[per:, :per] + mass
        else:
            new[:per, :] = sums[here]
            new[per:, :] = jnp.zeros((SUBLANES, new.shape[1]), F32)
            new[per:, :per] = mass


def add_rest(weights, rest_ref, old_refs, new_refs):
    per = new_refs[0].shape[0]
    sums = dot(weights, rest_ref[...])
    for t, new in enumerate(new_refs):
        part = sums[t * per : (t + 1) * per]
        new[...] = old_refs[t][...] + part if old_refs else part


def sums_kernel(subs, lead_ref, rest_ref, near_ref, cent_ref, own_prefix_ref, *refs):
    old, new = refs[: -2 * subs], refs[-2 * subs :]
    weights = soft_weights(lead_ref, near_ref, cent_ref, own_prefix_ref)
    add_lead(weights, lead_ref, old[:subs], new[:subs])
    add_rest(weights.astype(BF16), rest_ref, old[subs:], new[subs:])


def sums_lead_kernel(subs, lead_ref, near_ref, cent_ref, own_prefix_ref, *refs):
    old, weights_ref, new = refs[:subs], refs[subs], refs[subs + 1 :]
    weights = soft_weights(lead_ref, near_ref, cent_ref, own_prefix_ref)
    weights_ref[...] = weights.astype(BF16)
    add_lead(weights, lead_ref, old, new)


def sums_rest_kernel(subs, weights_ref, rest_ref, *refs):
    add_rest(weights_ref[...], rest_ref, refs[:subs], refs[subs:])


def gram_kernel(table, subs, *refs):
    *member_refs, gram_ref, held = refs
    z, x = lax.axis_index("rows"), lax.axis_index("sub")
    owners, groups, packed, half = held.shape
    each = len(member_refs) // subs
    for t in range(subs):
        column = member_refs[t * each : (t + 1) * each]
        for k, line in enumerate(table):
            source = sum(jnp.where(z == i, at, 0) for i, (_, at) in enumerate(line))
            row = source * subs + (x - t + subs) % subs
            if k < len(table) - 1:
                held[row] = column[k][...]
            else:
                held[row, :, :, :PREFIX] = column[k][...]
                held[row, :, :, PREFIX:] = column[k + 1][...]

    size = owners * packed
    lane = lax.broadcasted_iota(jnp.int32, (1, SUBLANES, size), 2) % SUBLANES
    same = (lane == lax.broadcasted_iota(jnp.int32, (1, SUBLANES, size), 1)).astype(F32)
    tile = min(size, 2 * LANES)
    for g in range(groups):
        mine = held[:, g].reshape(size, half)
        for start in range(0, size, tile):
            part = dot_nt(mine[start : start + tile], mine)
            part = part.reshape(tile // SUBLANES, SUBLANES, size)
            gram_ref[g, start // SUBLANES : (start + tile) // SUBLANES, :] = jnp.sum(part * same, axis=1)


def similarity_kernel(width, mine_ref, other_ref, out_ref):
    groups, slots, size = mine_ref.shape
    kept = out_ref.shape[1]
    h = lax.axis_index("dim")
    start = pl.multiple_of(h * kept, kept)
    row = lax.broadcasted_iota(jnp.int32, (slots, size), 0)
    lane = lax.broadcasted_iota(jnp.int32, (slots, size), 1)
    diagonal = row == lane // SUBLANES
    kept_row = lax.broadcasted_iota(jnp.int32, (kept, size), 0) + start
    kept_lane = lax.broadcasted_iota(jnp.int32, (kept, size), 1)
    kept_diagonal = kept_row == kept_lane // SUBLANES
    for g in range(groups):
        total = mine_ref[g] + other_ref[g]
        norms = jnp.sum(jnp.where(diagonal, total, 0.0), axis=0, keepdims=True)
        scale = lax.rsqrt(norms / width + EPS)
        spread = jnp.where(kept_diagonal, jnp.broadcast_to(scale, (kept, size)), 0.0)
        folded = spread[:, :LANES]
        for at in range(LANES, size, LANES):
            folded = folded + spread[:, at : at + LANES]
        step = SUBLANES
        while step < LANES:
            folded = folded + pltpu.roll(folded, step, 1)
            step *= 2
        row_scale = jnp.concatenate([folded] * (size // LANES), axis=1)
        own = mine_ref[g, pl.ds(start, kept), :] + other_ref[g, pl.ds(start, kept), :]
        out_ref[g] = (own / width * row_scale * scale).astype(BF16)


def centroid_kernel(*refs):
    *part_refs, prior_ref, out_ref = refs
    subs = len(part_refs) // 2
    lead = sum(ref[...] for ref in part_refs[1:subs]) + part_refs[0][...]
    rest = sum(ref[...] for ref in part_refs[subs + 1 :]) + part_refs[subs][...]
    per = rest.shape[0]
    mass = jnp.transpose(lead[per:, :LANES])[:per, :1] + SMOOTH
    prior = SMOOTH * prior_ref[...].astype(F32)
    out_ref[:, :PREFIX] = (lead[:per] + prior[:, :PREFIX]) / mass
    out_ref[:, PREFIX:] = (rest + prior[:, PREFIX:]) / mass


def shards(embeddings, centroids, cluster_id, cluster_place):
    docs, half = embeddings.shape
    clusters, width = centroids.shape
    rows, subs = lax.axis_size("rows"), lax.axis_size("sub")
    owners = rows * subs
    per = clusters // owners
    groups = per // SUBLANES
    packed = MOST * SUBLANES
    slots = owners * MOST
    table = arrivals(rows)
    z = lax.axis_index("rows")
    shape = jax.ShapeDtypeStruct

    def along(value, pairs):
        return lax.ppermute(value, "rows", pairs)

    def across(values):
        got = [values[0]]
        for t in range(1, subs):
            got.append(lax.ppermute(values[t], "sub", [(i, (i + t) % subs) for i in range(subs)]))
        return got

    def near(value):
        return lax.ppermute(value, "dim", [(0, 1), (1, 0)])

    def upward(step):
        return [(i, i + 1) for i in range(step - 1, rows - 1)]

    def downward(step):
        return [(i, i - 1) for i in range(1, rows - step + 1)]

    def send(step, held):
        if len(held) == 1:
            return (along(held[0], upward(step) + downward(step)),)
        return (along(held[0], upward(step)), along(held[1], downward(step)))

    def merged(step, held):
        if len(held) == 2 and 2 * step >= rows:
            return (jnp.where(z >= step, held[0], held[1]),)
        return held

    def slot_block(k, history):
        kinds = {}
        for i, (step, source) in enumerate(table[k]):
            side = 0 if source < i or len(history[step]) == 1 else 1
            kinds.setdefault((step, side), []).append(i)
        (step, side), *others = sorted(kinds, key=lambda kind: -len(kinds[kind]))
        value = history[step][side]
        for kind in others:
            here = functools.reduce(jnp.logical_or, [z == i for i in kinds[kind]])
            value = jnp.where(here, history[kind[0]][kind[1]], value)
        return value

    lead, rest = call(
        pack_kernel,
        "pack",
        [shape((docs + META, PREFIX), BF16), shape((docs, half - PREFIX), BF16)],
        [embeddings, cluster_id.reshape(1, docs)],
    )
    leads, rests = {0: (lead,)}, {0: (rest,)}
    sending_lead = send(1, (lead, lead))
    sending_rest = send(1, (rest, rest))

    inv, centre, own_prefix, prior = call(
        functools.partial(prep_kernel, subs, per),
        "prep",
        [
            shape((subs * per, 1), F32),
            shape((subs * per, half), BF16),
            shape((subs * per, PREFIX), BF16),
            shape((per, half), BF16),
        ],
        [cluster_place.reshape(1, clusters), centroids],
    )

    lead_sum, rest_sum = shape((per + SUBLANES, PREFIX), F32), shape((per, half - PREFIX), F32)
    sum_shapes = [lead_sum] * subs + [rest_sum] * subs
    score_flops = 2 * docs * clusters * PREFIX
    pick_flops = 2 * docs * MOST * subs * per * half

    def select(lead, rest):
        found = call(
            select_kernel, "select", [shape((groups, packed, half), BF16)] * subs, [lead, rest, inv, centre],
            flops=pick_flops,
        )
        return list(found)

    def add(lead, rest, prefix, sums):
        operands = [lead, rest, prefix, centroids, own_prefix] + sums
        return list(
            call(
                functools.partial(sums_kernel, subs), "sums", sum_shapes, operands,
                aliases={5 + i: i for i in range(len(sums))},
                flops=score_flops, transcendentals=docs * clusters,
            )
        )

    members = [[] for _ in range(subs)]

    def keep(found):
        for column, value in zip(members, found):
            column.append(value)

    prefix = near(lead)
    found = select(lead, rest)
    got = across(found)
    keep(got)
    sums = add(lead, rest, prefix, [])
    for step in range(1, rows):
        last = step == rows - 1
        leads[step] = merged(step, sending_lead)
        if not last:
            leads[step] = tied(leads[step], found)
            sending_lead = send(step + 1, leads[step])
        else:
            leads[step] = tied(leads[step], found, sums)
        lead = slot_block(step, leads)
        prefix = near(lead)
        if last:
            break
        rests[step] = merged(step, sending_rest)
        rests[step] = tied(rests[step], sums, got)
        sending_rest = send(step + 1, rests[step])
        rest = slot_block(step, rests)
        found = select(lead, rest)
        got = across(found)
        keep(got)
        sums = add(lead, rest, prefix, sums)

    half_rows = [shape((groups, packed, PREFIX), BF16)] * subs
    pick, *found = call(
        select_lead_kernel, "select_lead", [shape((subs * per * MOST, docs), BF16)] + half_rows, [lead, inv, centre],
        flops=pick_flops // 2,
    )
    keep(across(found))
    weights, *lead_sums = call(
        functools.partial(sums_lead_kernel, subs), "sums_lead", [shape((subs * per, docs), BF16)] + [lead_sum] * subs,
        [lead, prefix, centroids, own_prefix] + sums[:subs],
        aliases={4 + i: 1 + i for i in range(subs)},
        flops=score_flops, transcendentals=docs * clusters,
    )
    lead_sums = across(lead_sums)
    rests[rows - 1] = tied(merged(rows - 1, sending_rest), weights, found, pick)
    rest = slot_block(rows - 1, rests)
    half_rows = [shape((groups, packed, half - PREFIX), BF16)] * subs
    found = call(select_rest_kernel, "select_rest", half_rows, [pick, rest, centre], flops=pick_flops // 2)
    keep(across(found))
    rest_sums = call(
        functools.partial(sums_rest_kernel, subs), "sums_rest", [rest_sum] * subs, [weights, rest] + sums[subs:],
        aliases={2 + i: i for i in range(subs)},
    )
    rest_sums = across(rest_sums)

    (gram,) = call(
        functools.partial(gram_kernel, table, subs),
        "gram",
        [shape((groups, slots, slots * SUBLANES), F32)],
        [ref for column in members for ref in column],
        scratch=[pltpu.VMEM((owners, groups, packed, half), BF16)],
    )
    (tiles,) = call(
        functools.partial(similarity_kernel, width),
        "similarity",
        [shape((groups, slots // 2, slots * SUBLANES), BF16)],
        [gram, near(gram)],
    )
    tiles = tiles.reshape(groups, slots // 2, slots, SUBLANES)
    similarity = jnp.transpose(tiles, (0, 3, 1, 2)).reshape(per, slots // 2, slots)
    (new_centroids,) = call(centroid_kernel, "centroids", [shape((per, half), F32)], lead_sums + rest_sums + [prior])
    return (new_centroids, similarity)


def solution(mesh):
    in_specs = (
        P(("parts", "rows", "sub"), "dim"),
        P("parts", None),
        P(("parts", "rows", "sub"), None),
        P(),
    )
    out_specs = (P(("parts", "rows", "sub"), "dim"), P(("parts", "rows", "sub"), "dim", None))
    return jax.shard_map(shards, mesh=mesh, in_specs=in_specs, out_specs=out_specs, check_vma=False)
```

time: 93.6 us -> 74.4 us (0.79)
  waiting for transfers between devices: 53 us -> 27.1 us
  starting transfers between devices: 22.7 us -> 28.4 us
  local copies, waits for them, and re-layouts: 1.65 us -> 5.52 us
  other arithmetic: 1.86 us -> 0.27 us
  Pallas kernels: 13 us -> 11.6 us
    ppermute x5 -> x10, waiting for transfers between devices: 33.7 us -> 17.2 us  [along(): return lax.ppermute(value, 'rows', pairs)]
    ppermute x5 -> x10, starting transfers between devices: 9.77 us -> 19.2 us  [along(): return lax.ppermute(value, 'rows', pairs)]
    ppermute x12, waiting for transfers between devices: 19.3 us -> 9.94 us  [the longest x7 9.93 us: across(): lax.ppermute(values[t], 'sub', [(i, (i + t) % subs) for i in range(subs)])]
    unnamed x7 -> x11, local copies, waits for them, and re-layouts: 0.81 us -> 4.78 us
    ppermute x12, starting transfers between devices: 13 us -> 9.18 us  [the longest x7 8.83 us: across(): lax.ppermute(values[t], 'sub', [(i, (i + t) % subs) for i in range(subs)])]
    pallas_call x9 -> x15, Pallas kernels: 13 us -> 11.6 us  [call(): pl.pallas_call(kernel, out_shape=tuple(out_shape), in_specs=[whole() for...]
    concatenate x2 -> x0, other arithmetic: 1.09 us -> none  [the longest x1 1.08 us: shards(): block = jnp.concatenate([embeddings, meta], axis=0)]
  transfers between devices with their start and end apart: 17 -> 22, of which waited for: 9 -> 6; matrix products, arithmetic and copies ran while one was open for 0% -> 0% of each run, Pallas kernels for 14% -> 15%
where the time goes in v2:
time: 74.4 us; the launch traced here: 73.9 us
  starting transfers between devices  28.4 us (38%)
  waiting for transfers between devices  27.1 us (36%)
  Pallas kernels  11.6 us (16%)
  local copies, waits for them, and re-layouts  5.52 us (7%)
  between operations  1.01 us (1%)
    ppermute x10, starting transfers between devices, along(): return lax.ppermute(value, 'rows', pairs)  19.2 us
    ppermute x10, waiting for transfers between devices, along(): return lax.ppermute(value, 'rows', pairs)  17.2 us
    pallas_call x15, Pallas kernels, call(): pl.pallas_call(kernel, out_shape=tuple(out_shape), in_specs=[whole() for...  11.6 us
    ppermute x7, waiting for transfers between devices, across(): lax.ppermute(values[t], 'sub', [(i, (i + t) % subs) for i in range(subs)])  9.93 us
    ppermute x7, starting transfers between devices, across(): lax.ppermute(values[t], 'sub', [(i, (i + t) % subs) for i in range(subs)])  8.83 us
    unnamed x11, local copies, waits for them, and re-layouts  4.78 us
  transfers between devices with their start and end apart: 22, of which 6 were waited for; matrix products, arithmetic and copies ran while one was open for 0% of the time, Pallas kernels for 15%

profile of v2, /device:TPU:0, one launch (start us, length us, event | category | flops | bytes accessed | tf_op | source)
XLA Modules:
  0.0 73.9 jit_solution(7251306128375083557)
XLA Ops:
  0.6 1.0 %copy-done.2 = bf16[512,512]{1,0:T(8,128)(2,1)S(1)} copy-done((bf16[512,512]{1,0:T(8,128)(2,1)S(1)}, bf16[512,512]{1,0:T(8,128)(2,1)}, u32[]{:S(2)}) %copy-start.2) | copy-done | bytes 524312
  1.7 0.7 copy-done.4
  2.4 1.3 %collective-permute-start.1 = (bf16[528,256]{1,0:T(8,128)(2,1)S(1)}, bf16[528,256]{1,0:T(8,128)(2,1)S(1)}, u32[]{:S(2)}, u32[]{:S(2)}) collective-permute-start(bf16[528,256]{1,0:T(8,128)(2,1)S(1)} %get-tuple-element.44.lead_ref), channel_id=1, source_target_pairs={{4,0},{8,4},{12,8},{5,1},{9,5},{13,9},{6,2},{10,6},{14,10},{7,3},{... | collective-permute-start | bytes 811016 | tf_op jit(solution)/shard_map/ppermute | solution.py:306
  3.7 5.6 %collective-permute-start = (bf16[528,256]{1,0:T(8,128)(2,1)S(1)}, bf16[528,256]{1,0:T(8,128)(2,1)S(1)}, u32[]{:S(2)}, u32[]{:S(2)}) collective-permute-start(bf16[528,256]{1,0:T(8,128)(2,1)S(1)} %get-tuple-element.44.lead_ref), channel_id=1, source_target_pairs={{0,4},{4,8},{8,12},{1,5},{5,9},{9,13},{2,6},{6,10},{10,14},{3,7},{... | collective-permute-start | bytes 811016 | tf_op jit(solution)/shard_map/ppermute | solution.py:306
  9.3 0.1 collective-permute-start.6
  9.4 1.3 %collective-permute-start.5 = (bf16[512,256]{1,0:T(8,128)(2,1)S(1)}, bf16[512,256]{1,0:T(8,128)(2,1)S(1)}, u32[]{:S(2)}, u32[]{:S(2)}) collective-permute-start(bf16[512,256]{1,0:T(8,128)(2,1)S(1)} %get-tuple-element.45.rest_ref), channel_id=1, source_target_pairs={{4,0},{8,4},{12,8},{5,1},{9,5},{13,9},{6,2},{10,6},{14,10},{7,3},{... | collective-permute-start | bytes 786440 | tf_op jit(solution)/shard_map/ppermute | solution.py:306
  10.7 4.6 %collective-permute-start.4 = (bf16[512,256]{1,0:T(8,128)(2,1)S(1)}, bf16[512,256]{1,0:T(8,128)(2,1)S(1)}, u32[]{:S(2)}, u32[]{:S(2)}) collective-permute-start(bf16[512,256]{1,0:T(8,128)(2,1)S(1)} %get-tuple-element.45.rest_ref), channel_id=1, source_target_pairs={{0,4},{4,8},{8,12},{1,5},{5,9},{9,13},{2,6},{6,10},{10,14},{3,7},{... | collective-permute-start | bytes 786440 | tf_op jit(solution)/shard_map/ppermute | solution.py:306
  15.3 1.6 %copy-done = bf16[1024,1024]{1,0:T(8,128)(2,1)S(1)} copy-done((bf16[1024,1024]{1,0:T(8,128)(2,1)S(1)}, bf16[1024,1024]{1,0:T(8,128)(2,1)}, u32[]{:S(2)}) %copy-start) | copy-done | bytes 2097176
  16.8 0.7 copy-done.3
  17.5 0.8 %prep.1 = (f32[256,1]{1,0:T(8,128)S(1)}, bf16[256,512]{1,0:T(8,128)(2,1)S(1)}, bf16[256,256]{1,0:T(8,128)(2,1)S(1)}, bf16[128,512]{1,0:T(8,128)(2,1)S(1)}) custom-call(s32[1,1024]{1,0:T(1,128)S(1)} %bitcast.6, bf16[1024,1024]{1,0:T(8,128)(2,1)S(1)} %copy-done), custom_call_target="tpu_custom_call" | custom-call | bytes 1048576 | tf_op jit(solution)/shard_map/prep/pallas_call | solution.py:32
  18.3 0.7 select.3
  19.1 2.0 %collective-permute-start.7 = (bf16[16,16,512]{2,1,0:T(8,128)(2,1)S(1)}, bf16[16,16,512]{2,1,0:T(8,128)(2,1)S(1)}, u32[]{:S(2)}, u32[]{:S(2)}) collective-permute-start(bf16[16,16,512]{2,1,0:T(8,128)(2,1)S(1)} %get-tuple-element.49), channel_id=1, source_target_pairs={{0,2},{2,0},{1,3},{3,1},{4,6},{6,4},{5,7},{7,5},{8,10},{10,8},{9,1... | collective-permute-start | bytes 786440 | tf_op jit(solution)/shard_map/ppermute | solution.py:311
  21.1 0.7 collective-permute-start.2
  21.8 1.3 %collective-permute-start.3 = (bf16[528,256]{1,0:T(8,128)(2,1)S(1)}, bf16[528,256]{1,0:T(8,128)(2,1)S(1)}, u32[]{:S(2)}, u32[]{:S(2)}) collective-permute-start(bf16[528,256]{1,0:T(8,128)(2,1)S(1)} %collective-permute-done.1), channel_id=1, source_target_pairs={{4,0},{8,4},{5,1},{9,5},{6,2},{10,6},{7,3},{11,7},{20,16},{24,20},... | collective-permute-start | bytes 811016 | tf_op jit(solution)/shard_map/ppermute | solution.py:306
  23.1 1.3 %sums.3 = (f32[136,256]{1,0:T(8,128)S(1)}, f32[136,256]{1,0:T(8,128)S(1)}, f32[128,256]{1,0:T(8,128)S(1)}, f32[128,256]{1,0:T(8,128)S(1)}) custom-call(bf16[528,256]{1,0:T(8,128)(2,1)S(1)} %get-tuple-element.44.lead_ref, bf16[512,256]{1,0:T(8,128)(2,1)S(1)} %get-tuple-element.45.rest_ref, bf16[528,256]{1,0:T(8,128)(2,1)S(1)} %collective-permute-done.6.near_ref, ...), custom_call_target="tpu_custom_call" | custom-call | flops 268435456 | bytes 1048576 | tf_op jit(solution)/shard_map/sums/pallas_call | solution.py:32
  24.5 3.1 %collective-permute-done.7.refs_5_ = bf16[16,16,512]{2,1,0:T(8,128)(2,1)S(1)} collective-permute-done((bf16[16,16,512]{2,1,0:T(8,128)(2,1)S(1)}, bf16[16,16,512]{2,1,0:T(8,128)(2,1)S(1)}, u32[]{:S(2)}, u32[]{:S(2)}) %collective-permute-start.7) | collective-permute-done | bytes 262176 | tf_op jit(solution)/shard_map/ppermute | solution.py:311
  27.6 0.7 collective-permute-start.9
  28.2 1.3 %collective-permute-start.10 = (bf16[512,256]{1,0:T(8,128)(2,1)S(1)}, bf16[512,256]{1,0:T(8,128)(2,1)S(1)}, u32[]{:S(2)}, u32[]{:S(2)}) collective-permute-start(bf16[512,256]{1,0:T(8,128)(2,1)S(1)} %collective-permute-done.5), channel_id=1, source_target_pairs={{4,0},{8,4},{5,1},{9,5},{6,2},{10,6},{7,3},{11,7},{20,16},{24,20},... | collective-permute-start | bytes 786440 | tf_op jit(solution)/shard_map/ppermute | solution.py:306
  29.6 0.1 collective-permute-start.11
  29.6 0.7 select.4
  30.4 1.7 %collective-permute-start.12 = (bf16[16,16,512]{2,1,0:T(8,128)(2,1)S(1)}, bf16[16,16,512]{2,1,0:T(8,128)(2,1)S(1)}, u32[]{:S(2)}, u32[]{:S(2)}) collective-permute-start(bf16[16,16,512]{2,1,0:T(8,128)(2,1)S(1)} %get-tuple-element.60), channel_id=1, source_target_pairs={{0,2},{2,0},{1,3},{3,1},{4,6},{6,4},{5,7},{7,5},{8,10},{10,8},{9,1... | collective-permute-start | bytes 786440 | tf_op jit(solution)/shard_map/ppermute | solution.py:311
  32.1 8.5 %collective-permute-done.10 = bf16[512,256]{1,0:T(8,128)(2,1)S(1)} collective-permute-done((bf16[512,256]{1,0:T(8,128)(2,1)S(1)}, bf16[512,256]{1,0:T(8,128)(2,1)S(1)}, u32[]{:S(2)}, u32[]{:S(2)}) %collective-permute-start.10) | collective-permute-done | bytes 262176 | tf_op jit(solution)/shard_map/ppermute | solution.py:306
  40.7 1.3 %collective-permute-start.8 = (bf16[528,256]{1,0:T(8,128)(2,1)S(1)}, bf16[528,256]{1,0:T(8,128)(2,1)S(1)}, u32[]{:S(2)}, u32[]{:S(2)}) collective-permute-start(bf16[528,256]{1,0:T(8,128)(2,1)S(1)} %broadcast_select_fusion.1), channel_id=1, source_target_pairs={{8,12},{4,0},{9,13},{5,1},{10,14},{6,2},{11,15},{7,3},{24,28},{20,... | collective-permute-start | bytes 811016 | tf_op jit(solution)/shard_map/ppermute | solution.py:306
  42.1 0.1 collective-permute-start.13
  42.2 1.3 %sums.4 = (f32[136,256]{1,0:T(8,128)S(1)}, f32[136,256]{1,0:T(8,128)S(1)}, f32[128,256]{1,0:T(8,128)S(1)}, f32[128,256]{1,0:T(8,128)S(1)}) custom-call(bf16[528,256]{1,0:T(8,128)(2,1)S(1)} %broadcast_select_fusion.lead_ref, ...), custom_call_target="tpu_custom_call", output_to_operand_aliasing={{0}: (5, {}), {1}: (6, {}), {2}: (7, {}), {3}: (8, {})} | custom-call | flops 268435456 | bytes 1048576 | tf_op jit(solution)/shard_map/sums/pallas_call | solution.py:32
  43.5 0.7 select.5
  44.3 1.3 %sums.5 = (f32[136,256]{1,0:T(8,128)S(1)}, f32[136,256]{1,0:T(8,128)S(1)}, f32[128,256]{1,0:T(8,128)S(1)}, f32[128,256]{1,0:T(8,128)S(1)}) custom-call(bf16[528,256]{1,0:T(8,128)(2,1)S(1)} %broadcast_select_fusion.3.lead_ref, ...), custom_call_target="tpu_custom_call", output_to_operand_aliasing={{0}: (5, {}), {1}: (6, {}), {2}: (7, {}), {3}: (8, {})} | custom-call | flops 268435456 | bytes 1048576 | tf_op jit(solution)/shard_map/sums/pallas_call | solution.py:32
  45.6 3.5 %collective-permute-done.8 = bf16[528,256]{1,0:T(8,128)(2,1)S(1)} collective-permute-done((bf16[528,256]{1,0:T(8,128)(2,1)S(1)}, bf16[528,256]{1,0:T(8,128)(2,1)S(1)}, u32[]{:S(2)}, u32[]{:S(2)}) %collective-permute-start.8) | collective-permute-done | bytes 270368 | tf_op jit(solution)/shard_map/ppermute | solution.py:306
  49.2 0.1 collective-permute-start.14
  49.3 1.3 %collective-permute-start.16 = (bf16[512,256]{1,0:T(8,128)(2,1)S(1)}, bf16[512,256]{1,0:T(8,128)(2,1)S(1)}, u32[]{:S(2)}, u32[]{:S(2)}) collective-permute-start(bf16[512,256]{1,0:T(8,128)(2,1)S(1)} %broadcast_select_fusion.4), channel_id=1, source_target_pairs={{8,12},{4,0},{9,13},{5,1},{10,14},{6,2},{11,15},{7,3},{24,28},{20,... | collective-permute-start | bytes 786440 | tf_op jit(solution)/shard_map/ppermute | solution.py:306
  50.6 0.9 %collective-permute-start.18 = (bf16[16,16,512]{2,1,0:T(8,128)(2,1)S(1)}, bf16[16,16,512]{2,1,0:T(8,128)(2,1)S(1)}, u32[]{:S(2)}, u32[]{:S(2)}) collective-permute-start(bf16[16,16,512]{2,1,0:T(8,128)(2,1)S(1)} %get-tuple-element.68), channel_id=1, source_target_pairs={{0,2},{2,0},{1,3},{3,1},{4,6},{6,4},{5,7},{7,5},{8,10},{10,8},{9,1... | collective-permute-start | bytes 786440 | tf_op jit(solution)/shard_map/ppermute | solution.py:311
  51.4 0.6 select_lead.1
  52.0 1.3 %collective-permute-start.19 = (bf16[16,16,256]{2,1,0:T(8,128)(2,1)S(1)}, bf16[16,16,256]{2,1,0:T(8,128)(2,1)S(1)}, u32[]{:S(2)}, u32[]{:S(2)}) collective-permute-start(bf16[16,16,256]{2,1,0:T(8,128)(2,1)S(1)} %get-tuple-element.78), channel_id=1, source_target_pairs={{0,2},{2,0},{1,3},{3,1},{4,6},{6,4},{5,7},{7,5},{8,10},{10,8},{9,1... | collective-permute-start | bytes 393224 | tf_op jit(solution)/shard_map/ppermute | solution.py:311
  53.3 1.4 %sums_lead.1 = (bf16[256,512]{1,0:T(8,128)(2,1)S(1)}, f32[136,256]{1,0:T(8,128)S(1)}, f32[136,256]{1,0:T(8,128)S(1)}) custom-call(bf16[528,256]{1,0:T(8,128)(2,1)S(1)} %broadcast_select_fusion.2.lead_ref, bf16[528,256]{1,0:T(8,128)(2,1)S(1)} %collective-permute-done.14.near_ref, ...), custom_call_target="tpu_custom_call", output_to_operand_aliasing={{1}: (4, {}), {2}: (5, {})} | custom-call | flops 268435456 | bytes 1048576 | tf_op jit(solution)/shard_map/sums_lead/pallas_call | solution.py:32
  54.7 5.1 %collective-permute-done.16 = bf16[512,256]{1,0:T(8,128)(2,1)S(1)} collective-permute-done((bf16[512,256]{1,0:T(8,128)(2,1)S(1)}, bf16[512,256]{1,0:T(8,128)(2,1)S(1)}, u32[]{:S(2)}, u32[]{:S(2)}) %collective-permute-start.16) | collective-permute-done | bytes 262176 | tf_op jit(solution)/shard_map/ppermute | solution.py:306
  59.9 0.3 select_rest.1
  60.2 0.9 %collective-permute-start.20 = (bf16[16,16,256]{2,1,0:T(8,128)(2,1)S(1)}, bf16[16,16,256]{2,1,0:T(8,128)(2,1)S(1)}, u32[]{:S(2)}, u32[]{:S(2)}) collective-permute-start(bf16[16,16,256]{2,1,0:T(8,128)(2,1)S(1)} %get-tuple-element.85), channel_id=1, source_target_pairs={{0,2},{2,0},{1,3},{3,1},{4,6},{6,4},{5,7},{7,5},{8,10},{10,8},{9,1... | collective-permute-start | bytes 393224 | tf_op jit(solution)/shard_map/ppermute | solution.py:311
  61.1 1.2 %collective-permute-start.15 = (f32[136,256]{1,0:T(8,128)S(1)}, f32[136,256]{1,0:T(8,128)S(1)}, u32[]{:S(2)}, u32[]{:S(2)}) collective-permute-start(f32[136,256]{1,0:T(8,128)S(1)} %get-tuple-element.75), channel_id=1, source_target_pairs={{0,2},{2,0},{1,3},{3,1},{4,6},{6,4},{5,7},{7,5},{8,10},{10,8},{9,1... | collective-permute-start | bytes 417800 | tf_op jit(solution)/shard_map/ppermute | solution.py:311
  62.3 0.2 sums_rest.1
  62.6 0.9 %collective-permute-start.17 = (f32[128,256]{1,0:T(8,128)S(1)}, f32[128,256]{1,0:T(8,128)S(1)}, u32[]{:S(2)}, u32[]{:S(2)}) collective-permute-start(f32[128,256]{1,0:T(8,128)S(1)} %get-tuple-element.82), channel_id=1, source_target_pairs={{0,2},{2,0},{1,3},{3,1},{4,6},{6,4},{5,7},{7,5},{8,10},{10,8},{9,1... | collective-permute-start | bytes 393224 | tf_op jit(solution)/shard_map/ppermute | solution.py:311
  63.4 3.3 %collective-permute-done.20.refs_9_ = bf16[16,16,256]{2,1,0:T(8,128)(2,1)S(1)} collective-permute-done((bf16[16,16,256]{2,1,0:T(8,128)(2,1)S(1)}, bf16[16,16,256]{2,1,0:T(8,128)(2,1)S(1)}, u32[]{:S(2)}, u32[]{:S(2)}) %collective-permute-start.20) | collective-permute-done | bytes 131104 | tf_op jit(solution)/shard_map/ppermute | solution.py:311
  66.7 0.9 %gram.1.mine_ref = f32[16,16,128]{2,1,0:T(8,128)S(1)} custom-call(bf16[16,16,512]{2,1,0:T(8,128)(2,1)S(1)} %get-tuple-element.48.refs_0_, bf16[16,16,512]{2,1,0:T(8,128)(2,1)S(1)} %get-tuple-element.59.refs_1_, bf16[16,16,512]{2,1,0:T(8,128)(2,1)S(1)} %get-tuple-element.67.refs_2_, bf16[16,16,256]{2,1,0:T(8,128)(2,1)S(1)} %get-tuple-element.77.refs_3_, ...), custom_call_target="tpu_custom_call" | custom-call | bytes 1048576 | tf_op jit(solution)/shard_map/gram/pallas_call | solution.py:32
  67.6 3.6 %collective-permute-done.17.refs_3_ = f32[128,256]{1,0:T(8,128)S(1)} collective-permute-done((f32[128,256]{1,0:T(8,128)S(1)}, f32[128,256]{1,0:T(8,128)S(1)}, u32[]{:S(2)}, u32[]{:S(2)}) %collective-permute-start.17) | collective-permute-done | bytes 131104 | tf_op jit(solution)/shard_map/ppermute | solution.py:311
  71.2 0.9 %centroids.1 = f32[128,512]{1,0:T(8,128)} custom-call(f32[136,256]{1,0:T(8,128)S(1)} %get-tuple-element.74.refs_0_, f32[136,256]{1,0:T(8,128)S(1)} %collective-permute-done.15.refs_1_, f32[128,256]{1,0:T(8,128)S(1)} %get-tuple-element.81.refs_2_, f32[128,256]{1,0:T(8,128)S(1)} %collective-permute-done.17.refs_3_, bf16[128,512]{1,0:T(8,128)(2,1)S(1)} %get-tuple-element.83.refs_4_), custom_call_target="tpu_custom_call" | custom-call | bytes 1048576 | tf_op jit(solution)/shard_map/centroids/pallas_call | solution.py:32
  72.1 0.3 similarity.1
  72.4 0.2 copy.19
  72.6 0.6 copy.20
  73.2 0.8 %copy.21 = bf16[128,8,16]{0,2,1:T(8,128)(2,1)} copy(bf16[128,8,16]{2,1,0:T(8,128)(2,1)S(1)} %bitcast.9) | data formatting | bytes 65536
  (32 shorter events, 0.4 us)
Async XLA Ops:
  0.6 1.0 %copy-start.2 = (bf16[512,512]{1,0:T(8,128)(2,1)S(1)}, bf16[512,512]{1,0:T(8,128)(2,1)}, u32[]{:S(2)}) copy-start(bf16[512,512]{1,0:T(8,128)(2,1)} %emb_ref.1) | copy-start | bytes 1572868
  1.7 0.7 copy-start.4
  2.4 16.7 %collective-permute-start.1 = (bf16[528,256]{1,0:T(8,128)(2,1)S(1)}, bf16[528,256]{1,0:T(8,128)(2,1)S(1)}, u32[]{:S(2)}, u32[]{:S(2)}) collective-permute-start(bf16[528,256]{1,0:T(8,128)(2,1)S(1)} %get-tuple-element.44.lead_ref), channel_id=1, source_target_pairs={{4,0},{8,4},{12,8},{5,1},{9,5},{13,9},{6,2},{10,6},{14,10},{7,3},{... | collective-permute-start | bytes 811016 | tf_op jit(solution)/shard_map/ppermute | solution.py:306
  3.7 17.4 %collective-permute-start = (bf16[528,256]{1,0:T(8,128)(2,1)S(1)}, bf16[528,256]{1,0:T(8,128)(2,1)S(1)}, u32[]{:S(2)}, u32[]{:S(2)}) collective-permute-start(bf16[528,256]{1,0:T(8,128)(2,1)S(1)} %get-tuple-element.44.lead_ref), channel_id=1, source_target_pairs={{0,4},{4,8},{8,12},{1,5},{5,9},{9,13},{2,6},{6,10},{10,14},{3,7},{... | collective-permute-start | bytes 811016 | tf_op jit(solution)/shard_map/ppermute | solution.py:306
  9.3 12.5 %collective-permute-start.6 = (bf16[528,256]{1,0:T(8,128)(2,1)S(1)}, bf16[528,256]{1,0:T(8,128)(2,1)S(1)}, u32[]{:S(2)}, u32[]{:S(2)}) collective-permute-start(bf16[528,256]{1,0:T(8,128)(2,1)S(1)} %get-tuple-element.44.lead_ref), channel_id=1, source_target_pairs={{0,1},{1,0},{2,3},{3,2},{4,5},{5,4},{6,7},{7,6},{8,9},{9,8},{10,11... | collective-permute-start | bytes 811016 | tf_op jit(solution)/shard_map/ppermute | solution.py:315
  9.4 15.1 %collective-permute-start.5 = (bf16[512,256]{1,0:T(8,128)(2,1)S(1)}, bf16[512,256]{1,0:T(8,128)(2,1)S(1)}, u32[]{:S(2)}, u32[]{:S(2)}) collective-permute-start(bf16[512,256]{1,0:T(8,128)(2,1)S(1)} %get-tuple-element.45.rest_ref), channel_id=1, source_target_pairs={{4,0},{8,4},{12,8},{5,1},{9,5},{13,9},{6,2},{10,6},{14,10},{7,3},{... | collective-permute-start | bytes 786440 | tf_op jit(solution)/shard_map/ppermute | solution.py:306
  10.7 13.8 %collective-permute-start.4 = (bf16[512,256]{1,0:T(8,128)(2,1)S(1)}, bf16[512,256]{1,0:T(8,128)(2,1)S(1)}, u32[]{:S(2)}, u32[]{:S(2)}) collective-permute-start(bf16[512,256]{1,0:T(8,128)(2,1)S(1)} %get-tuple-element.45.rest_ref), channel_id=1, source_target_pairs={{0,4},{4,8},{8,12},{1,5},{5,9},{9,13},{2,6},{6,10},{10,14},{3,7},{... | collective-permute-start | bytes 786440 | tf_op jit(solution)/shard_map/ppermute | solution.py:306
  15.2 1.6 %copy-start = (bf16[1024,1024]{1,0:T(8,128)(2,1)S(1)}, bf16[1024,1024]{1,0:T(8,128)(2,1)}, u32[]{:S(2)}) copy-start(bf16[1024,1024]{1,0:T(8,128)(2,1)} %cent_ref.9) | copy-start | bytes 6291460
  16.8 0.7 copy-start.3
  17.5 5.5 %copy-start.1 = (bf16[1024,1024]{1,0:T(8,128)(2,1)S(1)}, bf16[1024,1024]{1,0:T(8,128)(2,1)}, u32[]{:S(2)}) copy-start(bf16[1024,1024]{1,0:T(8,128)(2,1)} %cent_ref.9) | copy-start | bytes 6291460
  19.1 8.5 %collective-permute-start.7 = (bf16[16,16,512]{2,1,0:T(8,128)(2,1)S(1)}, bf16[16,16,512]{2,1,0:T(8,128)(2,1)S(1)}, u32[]{:S(2)}, u32[]{:S(2)}) collective-permute-start(bf16[16,16,512]{2,1,0:T(8,128)(2,1)S(1)} %get-tuple-element.49), channel_id=1, source_target_pairs={{0,2},{2,0},{1,3},{3,1},{4,6},{6,4},{5,7},{7,5},{8,10},{10,8},{9,1... | collective-permute-start | bytes 786440 | tf_op jit(solution)/shard_map/ppermute | solution.py:311
  21.1 19.6 %collective-permute-start.2 = (bf16[528,256]{1,0:T(8,128)(2,1)S(1)}, bf16[528,256]{1,0:T(8,128)(2,1)S(1)}, u32[]{:S(2)}, u32[]{:S(2)}) collective-permute-start(bf16[528,256]{1,0:T(8,128)(2,1)S(1)} %collective-permute-done), channel_id=1, source_target_pairs={{4,8},{8,12},{5,9},{9,13},{6,10},{10,14},{7,11},{11,15},{20,24},{2... | collective-permute-start | bytes 811016 | tf_op jit(solution)/shard_map/ppermute | solution.py:306
  21.8 18.9 %collective-permute-start.3 = (bf16[528,256]{1,0:T(8,128)(2,1)S(1)}, bf16[528,256]{1,0:T(8,128)(2,1)S(1)}, u32[]{:S(2)}, u32[]{:S(2)}) collective-permute-start(bf16[528,256]{1,0:T(8,128)(2,1)S(1)} %collective-permute-done.1), channel_id=1, source_target_pairs={{4,0},{8,4},{5,1},{9,5},{6,2},{10,6},{7,3},{11,7},{20,16},{24,20},... | collective-permute-start | bytes 811016 | tf_op jit(solution)/shard_map/ppermute | solution.py:306
  27.6 2.8 %collective-permute-start.9 = (bf16[512,256]{1,0:T(8,128)(2,1)S(1)}, bf16[512,256]{1,0:T(8,128)(2,1)S(1)}, u32[]{:S(2)}, u32[]{:S(2)}) collective-permute-start(bf16[512,256]{1,0:T(8,128)(2,1)S(1)} %collective-permute-done.4), channel_id=1, source_target_pairs={{4,8},{8,12},{5,9},{9,13},{6,10},{10,14},{7,11},{11,15},{20,24},{2... | collective-permute-start | bytes 786440 | tf_op jit(solution)/shard_map/ppermute | solution.py:306
  28.2 12.4 %collective-permute-start.10 = (bf16[512,256]{1,0:T(8,128)(2,1)S(1)}, bf16[512,256]{1,0:T(8,128)(2,1)S(1)}, u32[]{:S(2)}, u32[]{:S(2)}) collective-permute-start(bf16[512,256]{1,0:T(8,128)(2,1)S(1)} %collective-permute-done.5), channel_id=1, source_target_pairs={{4,0},{8,4},{5,1},{9,5},{6,2},{10,6},{7,3},{11,7},{20,16},{24,20},... | collective-permute-start | bytes 786440 | tf_op jit(solution)/shard_map/ppermute | solution.py:306
  29.6 12.6 %collective-permute-start.11 = (bf16[528,256]{1,0:T(8,128)(2,1)S(1)}, bf16[528,256]{1,0:T(8,128)(2,1)S(1)}, u32[]{:S(2)}, u32[]{:S(2)}) collective-permute-start(bf16[528,256]{1,0:T(8,128)(2,1)S(1)} %broadcast_select_fusion.lead_ref), channel_id=1, source_target_pairs={{0,1},{1,0},{2,3},{3,2},{4,5},{5,4},{6,7},{7,6},{8,9},{9,8},{10,11... | collective-permute-start | bytes 811016 | tf_op jit(solution)/shard_map/ppermute | solution.py:315
  30.4 13.1 %collective-permute-start.12 = (bf16[16,16,512]{2,1,0:T(8,128)(2,1)S(1)}, bf16[16,16,512]{2,1,0:T(8,128)(2,1)S(1)}, u32[]{:S(2)}, u32[]{:S(2)}) collective-permute-start(bf16[16,16,512]{2,1,0:T(8,128)(2,1)S(1)} %get-tuple-element.60), channel_id=1, source_target_pairs={{0,2},{2,0},{1,3},{3,1},{4,6},{6,4},{5,7},{7,5},{8,10},{10,8},{9,1... | collective-permute-start | bytes 786440 | tf_op jit(solution)/shard_map/ppermute | solution.py:311
  40.7 8.4 %collective-permute-start.8 = (bf16[528,256]{1,0:T(8,128)(2,1)S(1)}, bf16[528,256]{1,0:T(8,128)(2,1)S(1)}, u32[]{:S(2)}, u32[]{:S(2)}) collective-permute-start(bf16[528,256]{1,0:T(8,128)(2,1)S(1)} %broadcast_select_fusion.1), channel_id=1, source_target_pairs={{8,12},{4,0},{9,13},{5,1},{10,14},{6,2},{11,15},{7,3},{24,28},{20,... | collective-permute-start | bytes 811016 | tf_op jit(solution)/shard_map/ppermute | solution.py:306
  42.1 2.2 %collective-permute-start.13 = (bf16[528,256]{1,0:T(8,128)(2,1)S(1)}, bf16[528,256]{1,0:T(8,128)(2,1)S(1)}, u32[]{:S(2)}, u32[]{:S(2)}) collective-permute-start(bf16[528,256]{1,0:T(8,128)(2,1)S(1)} %broadcast_select_fusion.3.lead_ref), channel_id=1, source_target_pairs={{0,1},{1,0},{2,3},{3,2},{4,5},{5,4},{6,7},{7,6},{8,9},{9,8},{10,11... | collective-permute-start | bytes 811016 | tf_op jit(solution)/shard_map/ppermute | solution.py:315
  49.2 4.1 %collective-permute-start.14 = (bf16[528,256]{1,0:T(8,128)(2,1)S(1)}, bf16[528,256]{1,0:T(8,128)(2,1)S(1)}, u32[]{:S(2)}, u32[]{:S(2)}) collective-permute-start(bf16[528,256]{1,0:T(8,128)(2,1)S(1)} %broadcast_select_fusion.2.lead_ref), channel_id=1, source_target_pairs={{0,1},{1,0},{2,3},{3,2},{4,5},{5,4},{6,7},{7,6},{8,9},{9,8},{10,11... | collective-permute-start | bytes 811016 | tf_op jit(solution)/shard_map/ppermute | solution.py:315
  49.3 10.6 %collective-permute-start.16 = (bf16[512,256]{1,0:T(8,128)(2,1)S(1)}, bf16[512,256]{1,0:T(8,128)(2,1)S(1)}, u32[]{:S(2)}, u32[]{:S(2)}) collective-permute-start(bf16[512,256]{1,0:T(8,128)(2,1)S(1)} %broadcast_select_fusion.4), channel_id=1, source_target_pairs={{8,12},{4,0},{9,13},{5,1},{10,14},{6,2},{11,15},{7,3},{24,28},{20,... | collective-permute-start | bytes 786440 | tf_op jit(solution)/shard_map/ppermute | solution.py:306
  50.6 12.8 %collective-permute-start.18 = (bf16[16,16,512]{2,1,0:T(8,128)(2,1)S(1)}, bf16[16,16,512]{2,1,0:T(8,128)(2,1)S(1)}, u32[]{:S(2)}, u32[]{:S(2)}) collective-permute-start(bf16[16,16,512]{2,1,0:T(8,128)(2,1)S(1)} %get-tuple-element.68), channel_id=1, source_target_pairs={{0,2},{2,0},{1,3},{3,1},{4,6},{6,4},{5,7},{7,5},{8,10},{10,8},{9,1... | collective-permute-start | bytes 786440 | tf_op jit(solution)/shard_map/ppermute | solution.py:311
  52.0 11.4 %collective-permute-start.19 = (bf16[16,16,256]{2,1,0:T(8,128)(2,1)S(1)}, bf16[16,16,256]{2,1,0:T(8,128)(2,1)S(1)}, u32[]{:S(2)}, u32[]{:S(2)}) collective-permute-start(bf16[16,16,256]{2,1,0:T(8,128)(2,1)S(1)} %get-tuple-element.78), channel_id=1, source_target_pairs={{0,2},{2,0},{1,3},{3,1},{4,6},{6,4},{5,7},{7,5},{8,10},{10,8},{9,1... | collective-permute-start | bytes 393224 | tf_op jit(solution)/shard_map/ppermute | solution.py:311
  60.2 6.5 %collective-permute-start.20 = (bf16[16,16,256]{2,1,0:T(8,128)(2,1)S(1)}, bf16[16,16,256]{2,1,0:T(8,128)(2,1)S(1)}, u32[]{:S(2)}, u32[]{:S(2)}) collective-permute-start(bf16[16,16,256]{2,1,0:T(8,128)(2,1)S(1)} %get-tuple-element.85), channel_id=1, source_target_pairs={{0,2},{2,0},{1,3},{3,1},{4,6},{6,4},{5,7},{7,5},{8,10},{10,8},{9,1... | collective-permute-start | bytes 393224 | tf_op jit(solution)/shard_map/ppermute | solution.py:311
  61.1 10.1 %collective-permute-start.15 = (f32[136,256]{1,0:T(8,128)S(1)}, f32[136,256]{1,0:T(8,128)S(1)}, u32[]{:S(2)}, u32[]{:S(2)}) collective-permute-start(f32[136,256]{1,0:T(8,128)S(1)} %get-tuple-element.75), channel_id=1, source_target_pairs={{0,2},{2,0},{1,3},{3,1},{4,6},{6,4},{5,7},{7,5},{8,10},{10,8},{9,1... | collective-permute-start | bytes 417800 | tf_op jit(solution)/shard_map/ppermute | solution.py:311
  62.6 8.6 %collective-permute-start.17 = (f32[128,256]{1,0:T(8,128)S(1)}, f32[128,256]{1,0:T(8,128)S(1)}, u32[]{:S(2)}, u32[]{:S(2)}) collective-permute-start(f32[128,256]{1,0:T(8,128)S(1)} %get-tuple-element.82), channel_id=1, source_target_pairs={{0,2},{2,0},{1,3},{3,1},{4,6},{6,4},{5,7},{7,5},{8,10},{10,8},{9,1... | collective-permute-start | bytes 393224 | tf_op jit(solution)/shard_map/ppermute | solution.py:311
  67.6 4.5 %collective-permute-start.21 = (f32[16,16,128]{2,1,0:T(8,128)S(1)}, f32[16,16,128]{2,1,0:T(8,128)S(1)}, u32[]{:S(2)}, u32[]{:S(2)}) collective-permute-start(f32[16,16,128]{2,1,0:T(8,128)S(1)} %gram.1.mine_ref), channel_id=1, source_target_pairs={{0,1},{1,0},{2,3},{3,2},{4,5},{5,4},{6,7},{7,6},{8,9},{9,8},{10,11... | collective-permute-start | bytes 393224 | tf_op jit(solution)/shard_map/ppermute | solution.py:315

commit v3 on v2

--- a/solution.py
+++ b/solution.py
@@ -25,19 +25,19 @@
 NT = (((1,), (1,)), ((), ()))
 
 
-def call(kernel, name, out_shape, operands, aliases=None, scratch=(), flops=0, transcendentals=0):
-    def whole():
-        return pl.BlockSpec(memory_space=pltpu.VMEM)
+def call(kernel, name, out_shape, operands, aliases=None, scratch=(), far=0, cost=0):
+    def place(at):
+        return pl.BlockSpec(memory_space=pltpu.HBM if at < far else pltpu.VMEM)
 
     return pl.pallas_call(
         kernel,
         out_shape=tuple(out_shape),
-        in_specs=[whole() for _ in operands],
-        out_specs=tuple(whole() for _ in out_shape),
+        in_specs=[place(at) for at in range(len(operands))],
+        out_specs=tuple(pl.BlockSpec(memory_space=pltpu.VMEM) for _ in out_shape),
         input_output_aliases=aliases or {},
         scratch_shapes=list(scratch),
         compiler_params=pltpu.CompilerParams(vmem_limit_bytes=VMEM_LIMIT),
-        cost_estimate=pl.CostEstimate(flops=flops, bytes_accessed=1024 * 1024, transcendentals=transcendentals),
+        cost_estimate=pl.CostEstimate(flops=50 * cost, bytes_accessed=cost, transcendentals=0),
         name=name,
     )(*operands)
 
@@ -58,34 +58,43 @@
 
 def arrivals(rows):
     table = []
-    for k in range(rows):
-        line = []
-        for z in range(rows):
-            below, above = z, rows - 1 - z
-            both = min(below, above)
-            if k == 0:
-                line.append((0, z))
-            elif k <= 2 * both:
-                step = (k + 1) // 2
-                line.append((step, z - step if k % 2 else z + step))
-            else:
-                step = k - both
-                line.append((step, z - step if below > above else z + step))
+    for z in range(rows):
+        line = [(0, 0, z)]
+        for step in range(1, rows):
+            for kind in range(2):
+                source = z + step if z % 2 == kind else z - step
+                if 0 <= source < rows:
+                    line.append((step, kind, source))
         table.append(line)
-    return table
-
-
-def pack_kernel(emb_ref, cid_ref, lead_ref, rest_ref):
+    return [[table[z][k] for z in range(rows)] for k in range(rows)]
+
+
+def pairs_of(rows, kind):
+    other = list(range(rows))
+    for i in range(kind, rows - 1, 2):
+        other[i], other[i + 1] = i + 1, i
+    return list(enumerate(other))
+
+
+def pack_kernel(emb_ref, cid_ref, lead_ref, rest_ref, cid_held, sems):
     docs = emb_ref.shape[0]
-    lead_ref[:docs, :] = emb_ref[:, :PREFIX]
-    rest_ref[...] = emb_ref[:, PREFIX:]
-    cid = cid_ref[...]
+    copies = [
+        pltpu.make_async_copy(cid_ref, cid_held, sems.at[0]),
+        pltpu.make_async_copy(emb_ref.at[:, :PREFIX], lead_ref.at[:docs, :], sems.at[1]),
+        pltpu.make_async_copy(emb_ref.at[:, PREFIX:], rest_ref, sems.at[2]),
+    ]
+    for copy in copies:
+        copy.start()
+    copies[0].wait()
+    cid = cid_held[...]
     high, low = (cid // DIGIT + 1).astype(F32), (cid % DIGIT).astype(F32)
     rows = []
     for digit in (high, low):
         rows += [digit[:, at : at + PREFIX] for at in range(0, docs, PREFIX)]
     rows.append(jnp.zeros((META - len(rows), PREFIX), F32))
     lead_ref[docs:, :] = jnp.concatenate(rows, axis=0).astype(BF16)
+    for copy in copies[1:]:
+        copy.wait()
 
 
 def ids_of(lead_ref):
@@ -97,21 +106,33 @@
     return (high - 1.0) * DIGIT + low
 
 
-def prep_kernel(subs, per, place_ref, cent_ref, inv_ref, centre_ref, own_prefix_ref, prior_ref):
+def prep_kernel(
+    subs, per, place_ref, cent_ref, inv_ref, centre_ref, own_prefix_ref, prior_ref, prefix_ref, place_held, columns_held, sems
+):
     clusters = cent_ref.shape[0]
     half = centre_ref.shape[1]
     z, x, h = lax.axis_index("rows"), lax.axis_index("sub"), lax.axis_index("dim")
+    copies = [
+        pltpu.make_async_copy(place_ref, place_held, sems.at[0]),
+        pltpu.make_async_copy(cent_ref.at[:, pl.ds(pl.multiple_of(h * half, LANES), half)], columns_held, sems.at[1]),
+        pltpu.make_async_copy(cent_ref.at[:, :PREFIX], prefix_ref, sems.at[2]),
+    ]
+    for copy in copies:
+        copy.start()
     row = lax.broadcasted_iota(jnp.int32, (subs * per, clusters), 0)
     ids = lax.broadcasted_iota(jnp.int32, (subs * per, clusters), 1)
     turn, within = row // per, row % per
     target = (z * subs + (x + turn) % subs) * per + within
-    chosen = (place_ref[...] == target).astype(F32)
+    natural = (ids == target).astype(BF16)
+    copies[0].wait()
+    chosen = (place_held[...] == target).astype(F32)
     inv_ref[...] = jnp.sum(chosen * ids.astype(F32), axis=1, keepdims=True)
-    columns = cent_ref[:, pl.ds(pl.multiple_of(h * half, LANES), half)]
+    copies[1].wait()
+    columns = columns_held[...]
     centre_ref[...] = dot(chosen.astype(BF16), columns).astype(BF16)
-    natural = (ids == target).astype(BF16)
-    own_prefix_ref[...] = dot(natural, cent_ref[:, :PREFIX]).astype(BF16)
     prior_ref[...] = dot(natural[:per], columns).astype(BF16)
+    copies[2].wait()
+    own_prefix_ref[...] = dot(natural, prefix_ref[...]).astype(BF16)
 
 
 def centred(pick, centre, columns):
@@ -169,7 +190,7 @@
     docs = lead_ref.shape[0] - META
     h = lax.axis_index("dim")
     prefix = jnp.where(h == 0, lead_ref[:docs, :], near_ref[:docs, :])
-    scores = dot_nt(cent_ref[:, :PREFIX], prefix) * TEMP
+    scores = dot_nt(cent_ref[...], prefix) * TEMP
     top = jnp.max(scores, axis=0, keepdims=True)
     scale = 1.0 / jnp.sum(jnp.exp(scores - top), axis=0, keepdims=True)
     own = dot_nt(own_prefix_ref[...], prefix) * TEMP
@@ -229,7 +250,7 @@
     for t in range(subs):
         column = member_refs[t * each : (t + 1) * each]
         for k, line in enumerate(table):
-            source = sum(jnp.where(z == i, at, 0) for i, (_, at) in enumerate(line))
+            source = sum(jnp.where(z == i, at, 0) for i, (_, _, at) in enumerate(line))
             row = source * subs + (x - t + subs) % subs
             if k < len(table) - 1:
                 held[row] = column[k][...]
@@ -249,9 +270,9 @@
             gram_ref[g, start // SUBLANES : (start + tile) // SUBLANES, :] = jnp.sum(part * same, axis=1)
 
 
-def similarity_kernel(width, mine_ref, other_ref, out_ref):
+def scaled_tiles(width, mine_ref, other_ref, scaled_ref):
     groups, slots, size = mine_ref.shape
-    kept = out_ref.shape[1]
+    kept = scaled_ref.shape[1]
     h = lax.axis_index("dim")
     start = pl.multiple_of(h * kept, kept)
     row = lax.broadcasted_iota(jnp.int32, (slots, size), 0)
@@ -274,19 +295,46 @@
             step *= 2
         row_scale = jnp.concatenate([folded] * (size // LANES), axis=1)
         own = mine_ref[g, pl.ds(start, kept), :] + other_ref[g, pl.ds(start, kept), :]
-        out_ref[g] = (own / width * row_scale * scale).astype(BF16)
-
-
-def centroid_kernel(*refs):
-    *part_refs, prior_ref, out_ref = refs
+        scaled_ref[g] = own / width * row_scale * scale
+
+
+def finish_kernel(width, mine_ref, other_ref, *refs):
+    *part_refs, prior_ref, new_ref, tile_ref, scaled_ref = refs
     subs = len(part_refs) // 2
     lead = sum(ref[...] for ref in part_refs[1:subs]) + part_refs[0][...]
     rest = sum(ref[...] for ref in part_refs[subs + 1 :]) + part_refs[subs][...]
     per = rest.shape[0]
     mass = jnp.transpose(lead[per:, :LANES])[:per, :1] + SMOOTH
     prior = SMOOTH * prior_ref[...].astype(F32)
-    out_ref[:, :PREFIX] = (lead[:per] + prior[:, :PREFIX]) / mass
-    out_ref[:, PREFIX:] = (rest + prior[:, PREFIX:]) / mass
+    new_ref[:, :PREFIX] = (lead[:per] + prior[:, :PREFIX]) / mass
+    new_ref[:, PREFIX:] = (rest + prior[:, PREFIX:]) / mass
+
+    scaled_tiles(width, mine_ref, other_ref, scaled_ref)
+    groups, kept, size = scaled_ref.shape
+    slots = size // SUBLANES
+    at = lax.broadcasted_iota(jnp.int32, (groups * size, per), 0)
+    to = lax.broadcasted_iota(jnp.int32, (groups * size, per), 1)
+    move = ((at // size == to // SUBLANES) & (at % SUBLANES == to % SUBLANES)).astype(F32).astype(BF16)
+    row = lax.broadcasted_iota(jnp.int32, (slots, size), 0)
+    lane = lax.broadcasted_iota(jnp.int32, (slots, size), 1)
+    here = row == lane // SUBLANES
+    batch = max(1, LANES // slots)
+
+    def some(step, carry):
+        spread = []
+        for b in range(batch):
+            i = step * batch + b
+            lines = [jnp.broadcast_to(scaled_ref[g, pl.ds(i, 1), :], (slots, size)) for g in range(groups)]
+            spread.append(jnp.concatenate([jnp.where(here, line, 0.0) for line in lines], axis=1))
+        moved = dot(jnp.concatenate(spread, axis=0).astype(BF16), move).astype(BF16)
+        for b in range(batch):
+            tile_ref[step * batch + b] = moved[b * slots : (b + 1) * slots]
+        return carry
+
+    if kept == batch:
+        some(0, 0)
+    else:
+        lax.fori_loop(0, kept // batch, some, 0)
 
 
 def shards(embeddings, centroids, cluster_id, cluster_place):
@@ -302,9 +350,6 @@
     z = lax.axis_index("rows")
     shape = jax.ShapeDtypeStruct
 
-    def along(value, pairs):
-        return lax.ppermute(value, "rows", pairs)
-
     def across(values):
         got = [values[0]]
         for t in range(1, subs):
@@ -314,32 +359,23 @@
     def near(value):
         return lax.ppermute(value, "dim", [(0, 1), (1, 0)])
 
-    def upward(step):
-        return [(i, i + 1) for i in range(step - 1, rows - 1)]
-
-    def downward(step):
-        return [(i, i - 1) for i in range(1, rows - step + 1)]
-
-    def send(step, held):
-        if len(held) == 1:
-            return (along(held[0], upward(step) + downward(step)),)
-        return (along(held[0], upward(step)), along(held[1], downward(step)))
-
-    def merged(step, held):
-        if len(held) == 2 and 2 * step >= rows:
-            return (jnp.where(z >= step, held[0], held[1]),)
-        return held
+    def needed(step, kind):
+        return any((step, kind) in [entry[:2] for entry in line] for line in table)
+
+    def swap(step, held):
+        return [
+            lax.ppermute(held[1 - kind], "rows", pairs_of(rows, kind)) if needed(step, kind) else None for kind in range(2)
+        ]
 
     def slot_block(k, history):
         kinds = {}
-        for i, (step, source) in enumerate(table[k]):
-            side = 0 if source < i or len(history[step]) == 1 else 1
-            kinds.setdefault((step, side), []).append(i)
-        (step, side), *others = sorted(kinds, key=lambda kind: -len(kinds[kind]))
-        value = history[step][side]
-        for kind in others:
-            here = functools.reduce(jnp.logical_or, [z == i for i in kinds[kind]])
-            value = jnp.where(here, history[kind[0]][kind[1]], value)
+        for i, (step, kind, _) in enumerate(table[k]):
+            kinds.setdefault((step, kind), []).append(i)
+        (step, kind), *others = sorted(kinds, key=lambda key: (-len(kinds[key]), key))
+        value = history[step][kind]
+        for step, kind in others:
+            here = functools.reduce(jnp.logical_or, [z == i for i in kinds[step, kind]])
+            value = jnp.where(here, history[step][kind], value)
         return value
 
     lead, rest = call(
@@ -347,12 +383,14 @@
         "pack",
         [shape((docs + META, PREFIX), BF16), shape((docs, half - PREFIX), BF16)],
         [embeddings, cluster_id.reshape(1, docs)],
-    )
-    leads, rests = {0: (lead,)}, {0: (rest,)}
-    sending_lead = send(1, (lead, lead))
-    sending_rest = send(1, (rest, rest))
-
-    inv, centre, own_prefix, prior = call(
+        scratch=[pltpu.VMEM((1, docs), jnp.int32), pltpu.SemaphoreType.DMA((3,))],
+        far=2,
+    )
+    leads, rests = {0: [lead, lead]}, {0: [rest, rest]}
+    sending_lead = swap(1, leads[0])
+    sending_rest = swap(1, rests[0])
+
+    inv, centre, own_prefix, prior, cent_prefix = call(
         functools.partial(prep_kernel, subs, per),
         "prep",
         [
@@ -360,85 +398,80 @@
             shape((subs * per, half), BF16),
             shape((subs * per, PREFIX), BF16),
             shape((per, half), BF16),
+            shape((clusters, PREFIX), BF16),
         ],
         [cluster_place.reshape(1, clusters), centroids],
+        scratch=[
+            pltpu.VMEM((1, clusters), jnp.int32),
+            pltpu.VMEM((clusters, half), BF16),
+            pltpu.SemaphoreType.DMA((3,)),
+        ],
+        far=2,
+        cost=4 * 1024 * 1024,
     )
 
     lead_sum, rest_sum = shape((per + SUBLANES, PREFIX), F32), shape((per, half - PREFIX), F32)
     sum_shapes = [lead_sum] * subs + [rest_sum] * subs
-    score_flops = 2 * docs * clusters * PREFIX
-    pick_flops = 2 * docs * MOST * subs * per * half
-
-    def select(lead, rest):
-        found = call(
-            select_kernel, "select", [shape((groups, packed, half), BF16)] * subs, [lead, rest, inv, centre],
-            flops=pick_flops,
-        )
+    own_cost, other_cost = 2 * 1024 * 1024, 128 * 1024
+
+    def select(lead, rest, cost):
+        found = call(select_kernel, "select", [shape((groups, packed, half), BF16)] * subs, [lead, rest, inv, centre], cost=cost)
         return list(found)
 
-    def add(lead, rest, prefix, sums):
-        operands = [lead, rest, prefix, centroids, own_prefix] + sums
-        return list(
-            call(
-                functools.partial(sums_kernel, subs), "sums", sum_shapes, operands,
-                aliases={5 + i: i for i in range(len(sums))},
-                flops=score_flops, transcendentals=docs * clusters,
-            )
-        )
-
-    members = [[] for _ in range(subs)]
-
-    def keep(found):
-        for column, value in zip(members, found):
-            column.append(value)
+    def add(lead, rest, prefix, sums, cost):
+        operands = [lead, rest, prefix, cent_prefix, own_prefix] + sums
+        aliases = {5 + i: i for i in range(len(sums))}
+        return list(call(functools.partial(sums_kernel, subs), "sums", sum_shapes, operands, aliases, cost=cost))
+
+    members = []
 
     prefix = near(lead)
-    found = select(lead, rest)
-    got = across(found)
-    keep(got)
-    sums = add(lead, rest, prefix, [])
+    found = select(lead, rest, own_cost)
+    members.append(across(found))
+    sums = add(lead, rest, prefix, [], own_cost)
     for step in range(1, rows):
         last = step == rows - 1
-        leads[step] = merged(step, sending_lead)
+        leads[step] = tied(sending_lead, found, members[: step - 1], *([sums] if last else []))
         if not last:
-            leads[step] = tied(leads[step], found)
-            sending_lead = send(step + 1, leads[step])
-        else:
-            leads[step] = tied(leads[step], found, sums)
+            sending_lead = swap(step + 1, leads[step])
         lead = slot_block(step, leads)
         prefix = near(lead)
         if last:
             break
-        rests[step] = merged(step, sending_rest)
-        rests[step] = tied(rests[step], sums, got)
-        sending_rest = send(step + 1, rests[step])
+        rests[step] = tied(sending_rest, sums)
+        sending_rest = swap(step + 1, rests[step])
         rest = slot_block(step, rests)
-        found = select(lead, rest)
-        got = across(found)
-        keep(got)
-        sums = add(lead, rest, prefix, sums)
+        found = select(lead, rest, own_cost)
+        members.append(across(found))
+        sums = add(lead, rest, prefix, sums, other_cost)
 
     half_rows = [shape((groups, packed, PREFIX), BF16)] * subs
     pick, *found = call(
         select_lead_kernel, "select_lead", [shape((subs * per * MOST, docs), BF16)] + half_rows, [lead, inv, centre],
-        flops=pick_flops // 2,
-    )
-    keep(across(found))
+        cost=other_cost,
+    )
+    lead_found = found
     weights, *lead_sums = call(
-        functools.partial(sums_lead_kernel, subs), "sums_lead", [shape((subs * per, docs), BF16)] + [lead_sum] * subs,
-        [lead, prefix, centroids, own_prefix] + sums[:subs],
-        aliases={4 + i: 1 + i for i in range(subs)},
-        flops=score_flops, transcendentals=docs * clusters,
-    )
+        functools.partial(sums_lead_kernel, subs),
+        "sums_lead",
+        [shape((subs * per, docs), BF16)] + [lead_sum] * subs,
+        [lead, prefix, cent_prefix, own_prefix] + sums[:subs],
+        {4 + i: 1 + i for i in range(subs)},
+        cost=other_cost,
+    )
+    members.append(across(tied(lead_found, members[: rows - 1])))
     lead_sums = across(lead_sums)
-    rests[rows - 1] = tied(merged(rows - 1, sending_rest), weights, found, pick)
+    rests[rows - 1] = tied(sending_rest, weights, found, pick, members[: rows - 1])
     rest = slot_block(rows - 1, rests)
     half_rows = [shape((groups, packed, half - PREFIX), BF16)] * subs
-    found = call(select_rest_kernel, "select_rest", half_rows, [pick, rest, centre], flops=pick_flops // 2)
-    keep(across(found))
+    found = call(select_rest_kernel, "select_rest", half_rows, [pick, rest, centre], cost=other_cost)
+    members.append(across(found))
     rest_sums = call(
-        functools.partial(sums_rest_kernel, subs), "sums_rest", [rest_sum] * subs, [weights, rest] + sums[subs:],
-        aliases={2 + i: i for i in range(subs)},
+        functools.partial(sums_rest_kernel, subs),
+        "sums_rest",
+        [rest_sum] * subs,
+        [weights, rest] + sums[subs:],
+        {2 + i: i for i in range(subs)},
     )
     rest_sums = across(rest_sums)
 
@@ -446,19 +479,17 @@
         functools.partial(gram_kernel, table, subs),
         "gram",
         [shape((groups, slots, slots * SUBLANES), F32)],
-        [ref for column in members for ref in column],
+        [arrays[t] for t in range(subs) for arrays in members],
         scratch=[pltpu.VMEM((owners, groups, packed, half), BF16)],
     )
-    (tiles,) = call(
-        functools.partial(similarity_kernel, width),
-        "similarity",
-        [shape((groups, slots // 2, slots * SUBLANES), BF16)],
-        [gram, near(gram)],
-    )
-    tiles = tiles.reshape(groups, slots // 2, slots, SUBLANES)
-    similarity = jnp.transpose(tiles, (0, 3, 1, 2)).reshape(per, slots // 2, slots)
-    (new_centroids,) = call(centroid_kernel, "centroids", [shape((per, half), F32)], lead_sums + rest_sums + [prior])
-    return (new_centroids, similarity)
+    new_centroids, tiles = call(
+        functools.partial(finish_kernel, width),
+        "finish",
+        [shape((per, half), F32), shape((slots // 2, slots, per), BF16)],
+        [gram, near(gram)] + lead_sums + rest_sums + [prior],
+        scratch=[pltpu.VMEM((groups, slots // 2, slots * SUBLANES), F32)],
+    )
+    return (new_centroids, jnp.transpose(tiles, (2, 0, 1)))
 
 
 def solution(mesh):

time: 74.4 us -> 66.6 us (0.90)
  waiting for transfers between devices: 27.1 us -> 20.9 us
  starting transfers between devices: 28.4 us -> 26.6 us
  local copies, waits for them, and re-layouts: 5.52 us -> 3.99 us
  Pallas kernels: 11.6 us -> 12.7 us
  other arithmetic: 0.27 us -> 1.1 us
    ppermute x10, waiting for transfers between devices: 17.2 us -> 3.49 us  [swap(): lax.ppermute(held[1 - kind], 'rows', pairs_of(rows, kind))]
    ppermute x7, waiting for transfers between devices: 9.93 us -> 17.4 us  [across(): lax.ppermute(values[t], 'sub', [(i, (i + t) % subs) for i in range(subs)])]
    ppermute x7, starting transfers between devices: 8.83 us -> 6.87 us  [across(): lax.ppermute(values[t], 'sub', [(i, (i + t) % subs) for i in range(subs)])]
    pallas_call x15 -> x14, Pallas kernels: 11.6 us -> 12.7 us  [call(): pl.pallas_call(kernel, out_shape=tuple(out_shape), in_specs=[place(at) fo...]
    select_n x8 -> x4, other arithmetic: 0.27 us -> 1.1 us  [slot_block(): value = jnp.where(here, history[step][kind], value)]
    unnamed x11 -> x8, local copies, waits for them, and re-layouts: 4.78 us -> 3.99 us
  transfers between devices with their start and end apart: 22 -> 22, of which waited for: 6 -> 6; matrix products, arithmetic and copies ran while one was open for 0% -> 2% of each run, Pallas kernels for 15% -> 17%
where the time goes in v3:
time: 66.6 us; the launch traced here: 66.2 us
  starting transfers between devices  26.6 us (40%)
  waiting for transfers between devices  20.9 us (31%)
  Pallas kernels  12.7 us (19%)
  local copies, waits for them, and re-layouts  3.99 us (6%)
  other arithmetic  1.1 us (2%)
  between operations  0.86 us (1%)
    ppermute x10, starting transfers between devices, swap(): lax.ppermute(held[1 - kind], 'rows', pairs_of(rows, kind))  19.5 us
    ppermute x7, waiting for transfers between devices, across(): lax.ppermute(values[t], 'sub', [(i, (i + t) % subs) for i in range(subs)])  17.4 us
    pallas_call x14, Pallas kernels, call(): pl.pallas_call(kernel, out_shape=tuple(out_shape), in_specs=[place(at) fo...  12.7 us
    ppermute x7, starting transfers between devices, across(): lax.ppermute(values[t], 'sub', [(i, (i + t) % subs) for i in range(subs)])  6.87 us
    unnamed x8, local copies, waits for them, and re-layouts  3.99 us
    ppermute x10, waiting for transfers between devices, swap(): lax.ppermute(held[1 - kind], 'rows', pairs_of(rows, kind))  3.49 us
  transfers between devices with their start and end apart: 22, of which 6 were waited for; matrix products, arithmetic and copies ran while one was open for 2% of the time, Pallas kernels for 17%

profile of v3, /device:TPU:0, one launch (start us, length us, event | category | flops | bytes accessed | tf_op | source)
XLA Modules:
  0.0 66.2 jit_solution(10471919031323506046)
XLA Ops:
  0.6 1.0 %copy-done.1 = bf16[512,512]{1,0:T(8,128)(2,1)S(1)} copy-done((bf16[512,512]{1,0:T(8,128)(2,1)S(1)}, bf16[512,512]{1,0:T(8,128)(2,1)}, u32[]{:S(2)}) %copy-start.1) | copy-done | bytes 524312
  1.7 0.7 %copy-done.3 = s32[512,1]{0,1:T(1,128)S(1)} copy-done((s32[512,1]{0,1:T(1,128)S(1)}, s32[512,1]{0,1:T(1,128)}, u32[]{:S(2)}) %copy-start.3) | copy-done | bytes 2072
  2.4 0.1 pack.1
  2.4 3.1 %collective-permute-start = (bf16[528,256]{1,0:T(8,128)(2,1)S(1)}, bf16[528,256]{1,0:T(8,128)(2,1)S(1)}, u32[]{:S(2)}, u32[]{:S(2)}) collective-permute-start(bf16[528,256]{1,0:T(8,128)(2,1)S(1)} %get-tuple-element.51.lead_ref), channel_id=1, source_target_pairs={{0,4},{4,0},{8,12},{12,8},{1,5},{5,1},{9,13},{13,9},{2,6},{6,2},{1... | collective-permute-start | bytes 811016 | tf_op jit(solution)/shard_map/ppermute | solution.py:367
  5.5 1.3 %collective-permute-start.1 = (bf16[528,256]{1,0:T(8,128)(2,1)S(1)}, bf16[528,256]{1,0:T(8,128)(2,1)}, u32[]{:S(2)}, u32[]{:S(2)}) collective-permute-start(bf16[528,256]{1,0:T(8,128)(2,1)S(1)} %get-tuple-element.51.lead_ref), channel_id=1, source_target_pairs={{0,0},{4,8},{8,4},{12,12},{1,1},{5,9},{9,5},{13,13},{2,2},{6,10},{... | collective-permute-start | bytes 811016 | tf_op jit(solution)/shard_map/ppermute | solution.py:367
  6.9 3.8 %collective-permute-start.2 = (bf16[512,256]{1,0:T(8,128)(2,1)S(1)}, bf16[512,256]{1,0:T(8,128)(2,1)S(1)}, u32[]{:S(2)}, u32[]{:S(2)}) collective-permute-start(bf16[512,256]{1,0:T(8,128)(2,1)S(1)} %get-tuple-element.52.rest_ref), channel_id=1, source_target_pairs={{0,4},{4,0},{8,12},{12,8},{1,5},{5,1},{9,13},{13,9},{2,6},{6,2},{1... | collective-permute-start | bytes 786440 | tf_op jit(solution)/shard_map/ppermute | solution.py:367
  10.7 1.3 %collective-permute-start.3 = (bf16[512,256]{1,0:T(8,128)(2,1)S(1)}, bf16[512,256]{1,0:T(8,128)(2,1)}, u32[]{:S(2)}, u32[]{:S(2)}) collective-permute-start(bf16[512,256]{1,0:T(8,128)(2,1)S(1)} %get-tuple-element.52.rest_ref), channel_id=1, source_target_pairs={{0,0},{4,8},{8,4},{12,12},{1,1},{5,9},{9,5},{13,13},{2,2},{6,10},{... | collective-permute-start | bytes 786440 | tf_op jit(solution)/shard_map/ppermute | solution.py:367
  12.0 1.6 %copy-done = bf16[1024,1024]{1,0:T(8,128)(2,1)S(1)} copy-done((bf16[1024,1024]{1,0:T(8,128)(2,1)S(1)}, bf16[1024,1024]{1,0:T(8,128)(2,1)}, u32[]{:S(2)}) %copy-start) | copy-done | bytes 2097176
  13.6 0.7 %copy-done.2 = s32[1024]{0:T(1024)S(1)} copy-done((s32[1024]{0:T(1024)S(1)}, s32[1024]{0:T(1024)}, u32[]{:S(2)}) %copy-start.2) | copy-done | bytes 4120
  14.3 1.8 %prep.1 = (f32[256,1]{1,0:T(8,128)S(1)}, bf16[256,512]{1,0:T(8,128)(2,1)S(1)}, bf16[256,256]{1,0:T(8,128)(2,1)S(1)}, bf16[128,512]{1,0:T(8,128)(2,1)S(1)}, bf16[1024,256]{1,0:T(8,128)(2,1)S(1)}) custom-call(s32[1,1024]{1,0:T(1,128)S(1)} %bitcast.3, bf16[1024,1024]{1,0:T(8,128)(2,1)S(1)} %copy-done), custom_call_target="tpu_custom_call" | custom-call | flops 209715200 | bytes 4194304 | tf_op jit(solution)/shard_map/prep/pallas_call | solution.py:32
  16.1 0.7 %select.3 = (bf16[16,16,512]{2,1,0:T(8,128)(2,1)S(1)}, bf16[16,16,512]{2,1,0:T(8,128)(2,1)S(1)}) custom-call(bf16[528,256]{1,0:T(8,128)(2,1)S(1)} %get-tuple-element.51.lead_ref, bf16[512,256]{1,0:T(8,128)(2,1)S(1)} %get-tuple-element.52.rest_ref, f32[256,1]{1,0:T(8,128)S(1)} %get-tuple-element.53.inv_ref, bf16[256,512]{1,0:T(8,128)(2,1)S(1)} %get-tuple-element.54.centre_ref), custom_call_target="tpu_custom_call" | custom-call | flops 104857600 | bytes 2097152 | tf_op jit(solution)/shard_map/select/pallas_call | solution.py:32
  16.9 0.0 collective-permute-done.lead_ref
  16.9 1.6 %collective-permute-start.7 = (bf16[16,16,512]{2,1,0:T(8,128)(2,1)S(1)}, bf16[16,16,512]{2,1,0:T(8,128)(2,1)S(1)}, u32[]{:S(2)}, u32[]{:S(2)}) collective-permute-start(bf16[16,16,512]{2,1,0:T(8,128)(2,1)S(1)} %get-tuple-element.56), channel_id=1, source_target_pairs={{0,2},{2,0},{1,3},{3,1},{4,6},{6,4},{5,7},{7,5},{8,10},{10,8},{9,1... | collective-permute-start | bytes 786440 | tf_op jit(solution)/shard_map/ppermute | solution.py:356
  18.4 0.0 collective-permute-done.1
  18.4 1.3 %collective-permute-start.6 = (bf16[528,256]{1,0:T(8,128)(2,1)S(1)}, bf16[528,256]{1,0:T(8,128)(2,1)}, u32[]{:S(2)}, u32[]{:S(2)}) collective-permute-start(bf16[528,256]{1,0:T(8,128)(2,1)S(1)} %collective-permute-done.lead_ref), channel_id=1, source_target_pairs={{0,0},{4,8},{8,4},{12,12},{1,1},{5,9},{9,5},{13,13},{2,2},{6,10},{... | collective-permute-start | bytes 811016 | tf_op jit(solution)/shard_map/ppermute | solution.py:367
  19.8 0.0 collective-permute-done.2.rest_ref
  19.8 3.3 %collective-permute-start.5 = (bf16[528,256]{1,0:T(8,128)(2,1)}, bf16[528,256]{1,0:T(8,128)(2,1)}, u32[]{:S(2)}, u32[]{:S(2)}) collective-permute-start(bf16[528,256]{1,0:T(8,128)(2,1)} %collective-permute-done.1), channel_id=1, source_target_pairs={{0,4},{4,0},{8,12},{12,8},{1,5},{5,1},{9,13},{13,9},{2,6},{6,2},{1... | collective-permute-start | bytes 811016 | tf_op jit(solution)/shard_map/ppermute | solution.py:367
  23.1 1.3 %sums.3 = (f32[136,256]{1,0:T(8,128)S(1)}, f32[136,256]{1,0:T(8,128)S(1)}, f32[128,256]{1,0:T(8,128)S(1)}, f32[128,256]{1,0:T(8,128)S(1)}) custom-call(bf16[528,256]{1,0:T(8,128)(2,1)S(1)} %get-tuple-element.51.lead_ref, bf16[512,256]{1,0:T(8,128)(2,1)S(1)} %get-tuple-element.52.rest_ref, bf16[528,256]{1,0:T(8,128)(2,1)S(1)} %collective-permute-done.4.near_ref, ...), custom_call_target="tpu_custom_call" | custom-call | flops 104857600 | bytes 2097152 | tf_op jit(solution)/shard_map/sums/pallas_call | solution.py:32
  24.4 0.7 %collective-permute-start.9 = (bf16[512,256]{1,0:T(8,128)(2,1)S(1)}, bf16[512,256]{1,0:T(8,128)(2,1)S(1)}, u32[]{:S(2)}, u32[]{:S(2)}) collective-permute-start(bf16[512,256]{1,0:T(8,128)(2,1)S(1)} %collective-permute-done.2.rest_ref), channel_id=1, source_target_pairs={{0,0},{4,8},{8,4},{12,12},{1,1},{5,9},{9,5},{13,13},{2,2},{6,10},{... | collective-permute-start | bytes 786440 | tf_op jit(solution)/shard_map/ppermute | solution.py:367
  25.1 0.5 collective-permute-done.7.refs_5_
  25.7 0.9 %collective-permute-start.8 = (bf16[512,256]{1,0:T(8,128)(2,1)}, bf16[512,256]{1,0:T(8,128)(2,1)S(1)}, u32[]{:S(2)}, u32[]{:S(2)}) collective-permute-start(bf16[512,256]{1,0:T(8,128)(2,1)} %collective-permute-done.3), channel_id=1, source_target_pairs={{0,4},{4,0},{8,12},{12,8},{1,5},{5,1},{9,13},{13,9},{2,6},{6,2},{1... | collective-permute-start | bytes 786440 | tf_op jit(solution)/shard_map/ppermute | solution.py:367
  26.6 0.7 %select.4 = (bf16[16,16,512]{2,1,0:T(8,128)(2,1)S(1)}, bf16[16,16,512]{2,1,0:T(8,128)(2,1)S(1)}) custom-call(bf16[528,256]{1,0:T(8,128)(2,1)S(1)} %collective-permute-done.lead_ref, bf16[512,256]{1,0:T(8,128)(2,1)S(1)} %collective-permute-done.2.rest_ref, f32[256,1]{1,0:T(8,128)S(1)} %get-tuple-element.53.inv_ref, ...), custom_call_target="tpu_custom_call" | custom-call | flops 104857600 | bytes 2097152 | tf_op jit(solution)/shard_map/select/pallas_call | solution.py:32
  27.3 3.5 %collective-permute-done.5 = bf16[528,256]{1,0:T(8,128)(2,1)} collective-permute-done((bf16[528,256]{1,0:T(8,128)(2,1)}, bf16[528,256]{1,0:T(8,128)(2,1)}, u32[]{:S(2)}, u32[]{:S(2)}) %collective-permute-start.5) | collective-permute-done | bytes 270368 | tf_op jit(solution)/shard_map/ppermute | solution.py:367
  30.8 1.0 %broadcast_select_fusion.1.lead_ref = bf16[528,256]{1,0:T(8,128)(2,1)S(1)} fusion(bf16[528,256]{1,0:T(8,128)(2,1)} %collective-permute-done.5, bf16[528,256]{1,0:T(8,128)(2,1)} %collective-permute-done.1, pred[]{:T(512)S(6)} %or.2), kind=kLoop, calls=%fused_computation.1 | loop fusion | flops 135168 | bytes 811009 | tf_op jit(solution)/shard_map/jit(_where)/select_n | solution.py:378
  31.8 0.1 collective-permute-start.13
  31.8 2.1 %collective-permute-start.11 = (bf16[528,256]{1,0:T(8,128)(2,1)}, bf16[528,256]{1,0:T(8,128)(2,1)S(1)}, u32[]{:S(2)}, u32[]{:S(2)}) collective-permute-start(bf16[528,256]{1,0:T(8,128)(2,1)} %collective-permute-done.6), channel_id=1, source_target_pairs={{0,4},{4,0},{8,12},{12,8},{1,5},{5,1},{9,13},{13,9},{2,6},{6,2},{1... | collective-permute-start | bytes 811016 | tf_op jit(solution)/shard_map/ppermute | solution.py:367
  34.0 0.5 collective-permute-start.12
  34.5 1.3 %sums.4 = (f32[136,256]{1,0:T(8,128)S(1)}, f32[136,256]{1,0:T(8,128)S(1)}, f32[128,256]{1,0:T(8,128)S(1)}, f32[128,256]{1,0:T(8,128)S(1)}) custom-call(bf16[528,256]{1,0:T(8,128)(2,1)S(1)} %collective-permute-done.lead_ref, ...), custom_call_target="tpu_custom_call", output_to_operand_aliasing={{0}: (5, {}), {1}: (6, {}), {2}: (7, {}), {3}: (8, {})} | custom-call | flops 6553600 | bytes 131072 | tf_op jit(solution)/shard_map/sums/pallas_call | solution.py:32
  35.9 0.7 %select.5 = (bf16[16,16,512]{2,1,0:T(8,128)(2,1)S(1)}, bf16[16,16,512]{2,1,0:T(8,128)(2,1)S(1)}) custom-call(bf16[528,256]{1,0:T(8,128)(2,1)S(1)} %broadcast_select_fusion.1.lead_ref, bf16[512,256]{1,0:T(8,128)(2,1)S(1)} %broadcast_select_fusion.3.rest_ref, f32[256,1]{1,0:T(8,128)S(1)} %get-tuple-element.53.inv_ref, ...), custom_call_target="tpu_custom_call" | custom-call | flops 104857600 | bytes 2097152 | tf_op jit(solution)/shard_map/select/pallas_call | solution.py:32
  36.6 1.3 %sums.5 = (f32[136,256]{1,0:T(8,128)S(1)}, f32[136,256]{1,0:T(8,128)S(1)}, f32[128,256]{1,0:T(8,128)S(1)}, f32[128,256]{1,0:T(8,128)S(1)}) custom-call(bf16[528,256]{1,0:T(8,128)(2,1)S(1)} %broadcast_select_fusion.1.lead_ref, ...), custom_call_target="tpu_custom_call", output_to_operand_aliasing={{0}: (5, {}), {1}: (6, {}), {2}: (7, {}), {3}: (8, {})} | custom-call | flops 6553600 | bytes 131072 | tf_op jit(solution)/shard_map/sums/pallas_call | solution.py:32
  38.0 4.4 %collective-permute-done.12.refs_6_ = bf16[16,16,512]{2,1,0:T(8,128)(2,1)S(1)} collective-permute-done((bf16[16,16,512]{2,1,0:T(8,128)(2,1)S(1)}, bf16[16,16,512]{2,1,0:T(8,128)(2,1)S(1)}, u32[]{:S(2)}, u32[]{:S(2)}) %collective-permute-start.12) | collective-permute-done | bytes 262176 | tf_op jit(solution)/shard_map/ppermute | solution.py:356
  42.4 0.1 collective-permute-start.16
  42.5 0.6 collective-permute-start.14
  43.1 1.6 %collective-permute-start.15 = (bf16[512,256]{1,0:T(8,128)(2,1)S(1)}, bf16[512,256]{1,0:T(8,128)(2,1)S(1)}, u32[]{:S(2)}, u32[]{:S(2)}) collective-permute-start(bf16[512,256]{1,0:T(8,128)(2,1)S(1)} %collective-permute-done.9), channel_id=1, source_target_pairs={{0,4},{4,0},{8,12},{12,8},{1,5},{5,1},{9,13},{13,9},{2,6},{6,2},{1... | collective-permute-start | bytes 786440 | tf_op jit(solution)/shard_map/ppermute | solution.py:367
  44.7 0.6 select_lead.1
  45.3 5.9 %collective-permute-done.14.refs_7_ = bf16[16,16,512]{2,1,0:T(8,128)(2,1)S(1)} collective-permute-done((bf16[16,16,512]{2,1,0:T(8,128)(2,1)S(1)}, bf16[16,16,512]{2,1,0:T(8,128)(2,1)S(1)}, u32[]{:S(2)}, u32[]{:S(2)}) %collective-permute-start.14) | collective-permute-done | bytes 262176 | tf_op jit(solution)/shard_map/ppermute | solution.py:356
  51.2 0.5 collective-permute-start.17
  51.7 1.4 %sums_lead.1 = (bf16[256,512]{1,0:T(8,128)(2,1)S(1)}, f32[136,256]{1,0:T(8,128)S(1)}, f32[136,256]{1,0:T(8,128)S(1)}) custom-call(bf16[528,256]{1,0:T(8,128)(2,1)S(1)} %broadcast_select_fusion.lead_ref, bf16[528,256]{1,0:T(8,128)(2,1)S(1)} %collective-permute-done.16.near_ref, ...), custom_call_target="tpu_custom_call", output_to_operand_aliasing={{1}: (4, {}), {2}: (5, {})} | custom-call | flops 6553600 | bytes 131072 | tf_op jit(solution)/shard_map/sums_lead/pallas_call | solution.py:32
  53.1 0.3 select_rest.1
  53.4 1.6 %collective-permute-start.18 = (bf16[16,16,256]{2,1,0:T(8,128)(2,1)S(1)}, bf16[16,16,256]{2,1,0:T(8,128)(2,1)S(1)}, u32[]{:S(2)}, u32[]{:S(2)}) collective-permute-start(bf16[16,16,256]{2,1,0:T(8,128)(2,1)S(1)} %get-tuple-element.92), channel_id=1, source_target_pairs={{0,2},{2,0},{1,3},{3,1},{4,6},{6,4},{5,7},{7,5},{8,10},{10,8},{9,1... | collective-permute-start | bytes 393224 | tf_op jit(solution)/shard_map/ppermute | solution.py:356
  55.0 0.5 collective-permute-start.20
  55.5 0.2 sums_rest.1
  55.8 1.6 %collective-permute-start.21 = (f32[128,256]{1,0:T(8,128)S(1)}, f32[128,256]{1,0:T(8,128)S(1)}, u32[]{:S(2)}, u32[]{:S(2)}) collective-permute-start(f32[128,256]{1,0:T(8,128)S(1)} %get-tuple-element.96), channel_id=1, source_target_pairs={{0,2},{2,0},{1,3},{3,1},{4,6},{6,4},{5,7},{7,5},{8,10},{10,8},{9,1... | collective-permute-start | bytes 393224 | tf_op jit(solution)/shard_map/ppermute | solution.py:356
  57.3 2.6 %collective-permute-done.18.refs_9_ = bf16[16,16,256]{2,1,0:T(8,128)(2,1)S(1)} collective-permute-done((bf16[16,16,256]{2,1,0:T(8,128)(2,1)S(1)}, bf16[16,16,256]{2,1,0:T(8,128)(2,1)S(1)}, u32[]{:S(2)}, u32[]{:S(2)}) %collective-permute-start.18) | collective-permute-done | bytes 131104 | tf_op jit(solution)/shard_map/ppermute | solution.py:356
  59.9 0.9 %gram.1.mine_ref = f32[16,16,128]{2,1,0:T(8,128)S(1)} custom-call(bf16[16,16,512]{2,1,0:T(8,128)(2,1)S(1)} %get-tuple-element.55.refs_0_, bf16[16,16,512]{2,1,0:T(8,128)(2,1)S(1)} %get-tuple-element.65.refs_1_, bf16[16,16,512]{2,1,0:T(8,128)(2,1)S(1)} %get-tuple-element.75.refs_2_, bf16[16,16,256]{2,1,0:T(8,128)(2,1)S(1)} %get-tuple-element.85.refs_3_, ...), custom_call_target="tpu_custom_call" | custom-call | tf_op jit(solution)/shard_map/gram/pallas_call | solution.py:32
  60.8 0.1 collective-permute-start.19
  60.9 3.9 %collective-permute-done.21.refs_3_ = f32[128,256]{1,0:T(8,128)S(1)} collective-permute-done((f32[128,256]{1,0:T(8,128)S(1)}, f32[128,256]{1,0:T(8,128)S(1)}, u32[]{:S(2)}, u32[]{:S(2)}) %collective-permute-start.21) | collective-permute-done | bytes 131104 | tf_op jit(solution)/shard_map/ppermute | solution.py:356
  64.9 1.4 %finish.1 = (f32[128,512]{1,0:T(8,128)}, bf16[8,16,128]{2,1,0:T(8,128)(2,1)}) custom-call(f32[16,16,128]{2,1,0:T(8,128)S(1)} %gram.1.mine_ref, f32[16,16,128]{2,1,0:T(8,128)S(1)} %collective-permute-done.19.other_ref, f32[136,256]{1,0:T(8,128)S(1)} %get-tuple-element.93.refs_0_, f32[136,256]{1,0:T(8,128)S(1)} %collective-permute-done.20.refs_1_, ...), custom_call_target="tpu_custom_call" | custom-call | tf_op jit(solution)/shard_map/finish/pallas_call | solution.py:32
  (22 shorter events, 0.2 us)
Async XLA Ops:
  0.6 1.0 %copy-start.1 = (bf16[512,512]{1,0:T(8,128)(2,1)S(1)}, bf16[512,512]{1,0:T(8,128)(2,1)}, u32[]{:S(2)}) copy-start(bf16[512,512]{1,0:T(8,128)(2,1)} %emb_ref.1) | copy-start | bytes 1572868
  1.7 0.7 %copy-start.3 = (s32[512,1]{0,1:T(1,128)S(1)}, s32[512,1]{0,1:T(1,128)}, u32[]{:S(2)}) copy-start(s32[512,1]{0,1:T(1,128)} %param.6) | copy-start | bytes 6148
  2.4 14.4 %collective-permute-start = (bf16[528,256]{1,0:T(8,128)(2,1)S(1)}, bf16[528,256]{1,0:T(8,128)(2,1)S(1)}, u32[]{:S(2)}, u32[]{:S(2)}) collective-permute-start(bf16[528,256]{1,0:T(8,128)(2,1)S(1)} %get-tuple-element.51.lead_ref), channel_id=1, source_target_pairs={{0,4},{4,0},{8,12},{12,8},{1,5},{5,1},{9,13},{13,9},{2,6},{6,2},{1... | collective-permute-start | bytes 811016 | tf_op jit(solution)/shard_map/ppermute | solution.py:367
  5.5 12.9 %collective-permute-start.1 = (bf16[528,256]{1,0:T(8,128)(2,1)S(1)}, bf16[528,256]{1,0:T(8,128)(2,1)}, u32[]{:S(2)}, u32[]{:S(2)}) collective-permute-start(bf16[528,256]{1,0:T(8,128)(2,1)S(1)} %get-tuple-element.51.lead_ref), channel_id=1, source_target_pairs={{0,0},{4,8},{8,4},{12,12},{1,1},{5,9},{9,5},{13,13},{2,2},{6,10},{... | collective-permute-start | bytes 811016 | tf_op jit(solution)/shard_map/ppermute | solution.py:367
  6.9 12.9 %collective-permute-start.2 = (bf16[512,256]{1,0:T(8,128)(2,1)S(1)}, bf16[512,256]{1,0:T(8,128)(2,1)S(1)}, u32[]{:S(2)}, u32[]{:S(2)}) collective-permute-start(bf16[512,256]{1,0:T(8,128)(2,1)S(1)} %get-tuple-element.52.rest_ref), channel_id=1, source_target_pairs={{0,4},{4,0},{8,12},{12,8},{1,5},{5,1},{9,13},{13,9},{2,6},{6,2},{1... | collective-permute-start | bytes 786440 | tf_op jit(solution)/shard_map/ppermute | solution.py:367
  10.7 12.5 %collective-permute-start.4 = (bf16[528,256]{1,0:T(8,128)(2,1)S(1)}, bf16[528,256]{1,0:T(8,128)(2,1)S(1)}, u32[]{:S(2)}, u32[]{:S(2)}) collective-permute-start(bf16[528,256]{1,0:T(8,128)(2,1)S(1)} %get-tuple-element.51.lead_ref), channel_id=1, source_target_pairs={{0,1},{1,0},{2,3},{3,2},{4,5},{5,4},{6,7},{7,6},{8,9},{9,8},{10,11... | collective-permute-start | bytes 811016 | tf_op jit(solution)/shard_map/ppermute | solution.py:360
  10.7 13.8 %collective-permute-start.3 = (bf16[512,256]{1,0:T(8,128)(2,1)S(1)}, bf16[512,256]{1,0:T(8,128)(2,1)}, u32[]{:S(2)}, u32[]{:S(2)}) collective-permute-start(bf16[512,256]{1,0:T(8,128)(2,1)S(1)} %get-tuple-element.52.rest_ref), channel_id=1, source_target_pairs={{0,0},{4,8},{8,4},{12,12},{1,1},{5,9},{9,5},{13,13},{2,2},{6,10},{... | collective-permute-start | bytes 786440 | tf_op jit(solution)/shard_map/ppermute | solution.py:367
  12.0 1.6 %copy-start = (bf16[1024,1024]{1,0:T(8,128)(2,1)S(1)}, bf16[1024,1024]{1,0:T(8,128)(2,1)}, u32[]{:S(2)}) copy-start(bf16[1024,1024]{1,0:T(8,128)(2,1)} %cent_ref.1) | copy-start | bytes 6291460
  13.6 0.7 %copy-start.2 = (s32[1024]{0:T(1024)S(1)}, s32[1024]{0:T(1024)}, u32[]{:S(2)}) copy-start(s32[1024]{0:T(1024)} %param.7) | copy-start | bytes 12292
  16.9 8.8 %collective-permute-start.7 = (bf16[16,16,512]{2,1,0:T(8,128)(2,1)S(1)}, bf16[16,16,512]{2,1,0:T(8,128)(2,1)S(1)}, u32[]{:S(2)}, u32[]{:S(2)}) collective-permute-start(bf16[16,16,512]{2,1,0:T(8,128)(2,1)S(1)} %get-tuple-element.56), channel_id=1, source_target_pairs={{0,2},{2,0},{1,3},{3,1},{4,6},{6,4},{5,7},{7,5},{8,10},{10,8},{9,1... | collective-permute-start | bytes 786440 | tf_op jit(solution)/shard_map/ppermute | solution.py:356
  18.4 8.9 %collective-permute-start.6 = (bf16[528,256]{1,0:T(8,128)(2,1)S(1)}, bf16[528,256]{1,0:T(8,128)(2,1)}, u32[]{:S(2)}, u32[]{:S(2)}) collective-permute-start(bf16[528,256]{1,0:T(8,128)(2,1)S(1)} %collective-permute-done.lead_ref), channel_id=1, source_target_pairs={{0,0},{4,8},{8,4},{12,12},{1,1},{5,9},{9,5},{13,13},{2,2},{6,10},{... | collective-permute-start | bytes 811016 | tf_op jit(solution)/shard_map/ppermute | solution.py:367
  19.8 11.0 %collective-permute-start.5 = (bf16[528,256]{1,0:T(8,128)(2,1)}, bf16[528,256]{1,0:T(8,128)(2,1)}, u32[]{:S(2)}, u32[]{:S(2)}) collective-permute-start(bf16[528,256]{1,0:T(8,128)(2,1)} %collective-permute-done.1), channel_id=1, source_target_pairs={{0,4},{4,0},{8,12},{12,8},{1,5},{5,1},{9,13},{13,9},{2,6},{6,2},{1... | collective-permute-start | bytes 811016 | tf_op jit(solution)/shard_map/ppermute | solution.py:367
  23.1 10.8 %collective-permute-start.10 = (bf16[528,256]{1,0:T(8,128)(2,1)S(1)}, bf16[528,256]{1,0:T(8,128)(2,1)S(1)}, u32[]{:S(2)}, u32[]{:S(2)}) collective-permute-start(bf16[528,256]{1,0:T(8,128)(2,1)S(1)} %collective-permute-done.lead_ref), channel_id=1, source_target_pairs={{0,1},{1,0},{2,3},{3,2},{4,5},{5,4},{6,7},{7,6},{8,9},{9,8},{10,11... | collective-permute-start | bytes 811016 | tf_op jit(solution)/shard_map/ppermute | solution.py:360
  24.4 11.4 %collective-permute-start.9 = (bf16[512,256]{1,0:T(8,128)(2,1)S(1)}, bf16[512,256]{1,0:T(8,128)(2,1)S(1)}, u32[]{:S(2)}, u32[]{:S(2)}) collective-permute-start(bf16[512,256]{1,0:T(8,128)(2,1)S(1)} %collective-permute-done.2.rest_ref), channel_id=1, source_target_pairs={{0,0},{4,8},{8,4},{12,12},{1,1},{5,9},{9,5},{13,13},{2,2},{6,10},{... | collective-permute-start | bytes 786440 | tf_op jit(solution)/shard_map/ppermute | solution.py:367
  25.7 10.2 %collective-permute-start.8 = (bf16[512,256]{1,0:T(8,128)(2,1)}, bf16[512,256]{1,0:T(8,128)(2,1)S(1)}, u32[]{:S(2)}, u32[]{:S(2)}) collective-permute-start(bf16[512,256]{1,0:T(8,128)(2,1)} %collective-permute-done.3), channel_id=1, source_target_pairs={{0,4},{4,0},{8,12},{12,8},{1,5},{5,1},{9,13},{13,9},{2,6},{6,2},{1... | collective-permute-start | bytes 786440 | tf_op jit(solution)/shard_map/ppermute | solution.py:367
  31.8 4.9 %collective-permute-start.13 = (bf16[528,256]{1,0:T(8,128)(2,1)S(1)}, bf16[528,256]{1,0:T(8,128)(2,1)S(1)}, u32[]{:S(2)}, u32[]{:S(2)}) collective-permute-start(bf16[528,256]{1,0:T(8,128)(2,1)S(1)} %broadcast_select_fusion.1.lead_ref), channel_id=1, source_target_pairs={{0,1},{1,0},{2,3},{3,2},{4,5},{5,4},{6,7},{7,6},{8,9},{9,8},{10,11... | collective-permute-start | bytes 811016 | tf_op jit(solution)/shard_map/ppermute | solution.py:360
  31.8 10.5 %collective-permute-start.11 = (bf16[528,256]{1,0:T(8,128)(2,1)}, bf16[528,256]{1,0:T(8,128)(2,1)S(1)}, u32[]{:S(2)}, u32[]{:S(2)}) collective-permute-start(bf16[528,256]{1,0:T(8,128)(2,1)} %collective-permute-done.6), channel_id=1, source_target_pairs={{0,4},{4,0},{8,12},{12,8},{1,5},{5,1},{9,13},{13,9},{2,6},{6,2},{1... | collective-permute-start | bytes 811016 | tf_op jit(solution)/shard_map/ppermute | solution.py:367
  34.0 8.4 %collective-permute-start.12 = (bf16[16,16,512]{2,1,0:T(8,128)(2,1)S(1)}, bf16[16,16,512]{2,1,0:T(8,128)(2,1)S(1)}, u32[]{:S(2)}, u32[]{:S(2)}) collective-permute-start(bf16[16,16,512]{2,1,0:T(8,128)(2,1)S(1)} %get-tuple-element.67), channel_id=1, source_target_pairs={{0,2},{2,0},{1,3},{3,1},{4,6},{6,4},{5,7},{7,5},{8,10},{10,8},{9,1... | collective-permute-start | bytes 786440 | tf_op jit(solution)/shard_map/ppermute | solution.py:356
  42.4 9.3 %collective-permute-start.16 = (bf16[528,256]{1,0:T(8,128)(2,1)S(1)}, bf16[528,256]{1,0:T(8,128)(2,1)S(1)}, u32[]{:S(2)}, u32[]{:S(2)}) collective-permute-start(bf16[528,256]{1,0:T(8,128)(2,1)S(1)} %broadcast_select_fusion.lead_ref), channel_id=1, source_target_pairs={{0,1},{1,0},{2,3},{3,2},{4,5},{5,4},{6,7},{7,6},{8,9},{9,8},{10,11... | collective-permute-start | bytes 811016 | tf_op jit(solution)/shard_map/ppermute | solution.py:360
  42.5 8.7 %collective-permute-start.14 = (bf16[16,16,512]{2,1,0:T(8,128)(2,1)S(1)}, bf16[16,16,512]{2,1,0:T(8,128)(2,1)S(1)}, u32[]{:S(2)}, u32[]{:S(2)}) collective-permute-start(bf16[16,16,512]{2,1,0:T(8,128)(2,1)S(1)} %get-tuple-element.77), channel_id=1, source_target_pairs={{0,2},{2,0},{1,3},{3,1},{4,6},{6,4},{5,7},{7,5},{8,10},{10,8},{9,1... | collective-permute-start | bytes 786440 | tf_op jit(solution)/shard_map/ppermute | solution.py:356
  43.1 10.0 %collective-permute-start.15 = (bf16[512,256]{1,0:T(8,128)(2,1)S(1)}, bf16[512,256]{1,0:T(8,128)(2,1)S(1)}, u32[]{:S(2)}, u32[]{:S(2)}) collective-permute-start(bf16[512,256]{1,0:T(8,128)(2,1)S(1)} %collective-permute-done.9), channel_id=1, source_target_pairs={{0,4},{4,0},{8,12},{12,8},{1,5},{5,1},{9,13},{13,9},{2,6},{6,2},{1... | collective-permute-start | bytes 786440 | tf_op jit(solution)/shard_map/ppermute | solution.py:367
  51.2 6.2 %collective-permute-start.17 = (bf16[16,16,256]{2,1,0:T(8,128)(2,1)S(1)}, bf16[16,16,256]{2,1,0:T(8,128)(2,1)S(1)}, u32[]{:S(2)}, u32[]{:S(2)}) collective-permute-start(bf16[16,16,256]{2,1,0:T(8,128)(2,1)S(1)} %get-tuple-element.91), channel_id=1, source_target_pairs={{0,2},{2,0},{1,3},{3,1},{4,6},{6,4},{5,7},{7,5},{8,10},{10,8},{9,1... | collective-permute-start | bytes 393224 | tf_op jit(solution)/shard_map/ppermute | solution.py:356
  53.4 6.5 %collective-permute-start.18 = (bf16[16,16,256]{2,1,0:T(8,128)(2,1)S(1)}, bf16[16,16,256]{2,1,0:T(8,128)(2,1)S(1)}, u32[]{:S(2)}, u32[]{:S(2)}) collective-permute-start(bf16[16,16,256]{2,1,0:T(8,128)(2,1)S(1)} %get-tuple-element.92), channel_id=1, source_target_pairs={{0,2},{2,0},{1,3},{3,1},{4,6},{6,4},{5,7},{7,5},{8,10},{10,8},{9,1... | collective-permute-start | bytes 393224 | tf_op jit(solution)/shard_map/ppermute | solution.py:356
  55.0 9.8 %collective-permute-start.20 = (f32[136,256]{1,0:T(8,128)S(1)}, f32[136,256]{1,0:T(8,128)S(1)}, u32[]{:S(2)}, u32[]{:S(2)}) collective-permute-start(f32[136,256]{1,0:T(8,128)S(1)} %get-tuple-element.94), channel_id=1, source_target_pairs={{0,2},{2,0},{1,3},{3,1},{4,6},{6,4},{5,7},{7,5},{8,10},{10,8},{9,1... | collective-permute-start | bytes 417800 | tf_op jit(solution)/shard_map/ppermute | solution.py:356
  55.8 9.1 %collective-permute-start.21 = (f32[128,256]{1,0:T(8,128)S(1)}, f32[128,256]{1,0:T(8,128)S(1)}, u32[]{:S(2)}, u32[]{:S(2)}) collective-permute-start(f32[128,256]{1,0:T(8,128)S(1)} %get-tuple-element.96), channel_id=1, source_target_pairs={{0,2},{2,0},{1,3},{3,1},{4,6},{6,4},{5,7},{7,5},{8,10},{10,8},{9,1... | collective-permute-start | bytes 393224 | tf_op jit(solution)/shard_map/ppermute | solution.py:356
  60.8 4.0 %collective-permute-start.19 = (f32[16,16,128]{2,1,0:T(8,128)S(1)}, f32[16,16,128]{2,1,0:T(8,128)S(1)}, u32[]{:S(2)}, u32[]{:S(2)}) collective-permute-start(f32[16,16,128]{2,1,0:T(8,128)S(1)} %gram.1.mine_ref), channel_id=1, source_target_pairs={{0,1},{1,0},{2,3},{3,2},{4,5},{5,4},{6,7},{7,6},{8,9},{9,8},{10,11... | collective-permute-start | bytes 393224 | tf_op jit(solution)/shard_map/ppermute | solution.py:360

commit v4 on v3

--- a/solution.py
+++ b/solution.py
@@ -76,62 +76,43 @@
     return list(enumerate(other))
 
 
-def pack_kernel(emb_ref, cid_ref, lead_ref, rest_ref, cid_held, sems):
-    docs = emb_ref.shape[0]
-    copies = [
-        pltpu.make_async_copy(cid_ref, cid_held, sems.at[0]),
-        pltpu.make_async_copy(emb_ref.at[:, :PREFIX], lead_ref.at[:docs, :], sems.at[1]),
-        pltpu.make_async_copy(emb_ref.at[:, PREFIX:], rest_ref, sems.at[2]),
-    ]
-    for copy in copies:
-        copy.start()
-    copies[0].wait()
-    cid = cid_held[...]
+def pack_kernel(emb_ref, cid_ref, block_ref):
+    docs, half = emb_ref.shape
+    block_ref[:docs, :] = emb_ref[...]
+    cid = cid_ref[...]
     high, low = (cid // DIGIT + 1).astype(F32), (cid % DIGIT).astype(F32)
     rows = []
     for digit in (high, low):
         rows += [digit[:, at : at + PREFIX] for at in range(0, docs, PREFIX)]
     rows.append(jnp.zeros((META - len(rows), PREFIX), F32))
-    lead_ref[docs:, :] = jnp.concatenate(rows, axis=0).astype(BF16)
-    for copy in copies[1:]:
-        copy.wait()
+    block_ref[docs:, :PREFIX] = jnp.concatenate(rows, axis=0).astype(BF16)
+    block_ref[docs:, PREFIX:] = jnp.zeros((META, half - PREFIX), BF16)
 
 
 def ids_of(lead_ref):
     docs = lead_ref.shape[0] - META
-    meta = lead_ref[docs:, :].astype(F32)
+    meta = lead_ref[docs:, :PREFIX].astype(F32)
     parts = docs // PREFIX
     high = jnp.concatenate([meta[i : i + 1] for i in range(parts)], axis=1)
     low = jnp.concatenate([meta[parts + i : parts + i + 1] for i in range(parts)], axis=1)
     return (high - 1.0) * DIGIT + low
 
 
-def prep_kernel(
-    subs, per, place_ref, cent_ref, inv_ref, centre_ref, own_prefix_ref, prior_ref, prefix_ref, place_held, columns_held, sems
-):
+def prep_kernel(subs, per, place_ref, cent_ref, inv_ref, centre_ref, own_prefix_ref, prior_ref, prefix_ref):
     clusters = cent_ref.shape[0]
     half = centre_ref.shape[1]
     z, x, h = lax.axis_index("rows"), lax.axis_index("sub"), lax.axis_index("dim")
-    copies = [
-        pltpu.make_async_copy(place_ref, place_held, sems.at[0]),
-        pltpu.make_async_copy(cent_ref.at[:, pl.ds(pl.multiple_of(h * half, LANES), half)], columns_held, sems.at[1]),
-        pltpu.make_async_copy(cent_ref.at[:, :PREFIX], prefix_ref, sems.at[2]),
-    ]
-    for copy in copies:
-        copy.start()
     row = lax.broadcasted_iota(jnp.int32, (subs * per, clusters), 0)
     ids = lax.broadcasted_iota(jnp.int32, (subs * per, clusters), 1)
     turn, within = row // per, row % per
     target = (z * subs + (x + turn) % subs) * per + within
+    chosen = (place_ref[...] == target).astype(F32)
+    inv_ref[...] = jnp.sum(chosen * ids.astype(F32), axis=1, keepdims=True)
+    columns = cent_ref[:, pl.ds(pl.multiple_of(h * half, LANES), half)]
+    centre_ref[...] = dot(chosen.astype(BF16), columns).astype(BF16)
     natural = (ids == target).astype(BF16)
-    copies[0].wait()
-    chosen = (place_held[...] == target).astype(F32)
-    inv_ref[...] = jnp.sum(chosen * ids.astype(F32), axis=1, keepdims=True)
-    copies[1].wait()
-    columns = columns_held[...]
-    centre_ref[...] = dot(chosen.astype(BF16), columns).astype(BF16)
     prior_ref[...] = dot(natural[:per], columns).astype(BF16)
-    copies[2].wait()
+    prefix_ref[...] = cent_ref[:, :PREFIX]
     own_prefix_ref[...] = dot(natural, prefix_ref[...]).astype(BF16)
 
 
@@ -157,16 +138,12 @@
     return jnp.stack(ranked, axis=1).reshape(groups * MOST * SUBLANES, docs).astype(BF16)
 
 
-def select_kernel(lead_ref, rest_ref, inv_ref, centre_ref, *row_refs):
-    docs = rest_ref.shape[0]
-    pick = picked(lead_ref, inv_ref)
-    groups, packed, _ = row_refs[0].shape
-    for columns, at in ((lead_ref[:docs, :], 0), (rest_ref[...], PREFIX)):
-        width = columns.shape[1]
-        rows = centred(pick, centre_ref[:, at : at + width], columns)
-        rows = rows.reshape(len(row_refs), groups, packed, width)
-        for t, ref in enumerate(row_refs):
-            ref[:, :, at : at + width] = rows[t]
+def select_kernel(block_ref, inv_ref, centre_ref, *row_refs):
+    docs = block_ref.shape[0] - META
+    rows = centred(picked(block_ref, inv_ref), centre_ref[...], block_ref[:docs, :])
+    rows = rows.reshape((len(row_refs),) + row_refs[0].shape)
+    for t, ref in enumerate(row_refs):
+        ref[...] = rows[t]
 
 
 def select_lead_kernel(lead_ref, inv_ref, centre_ref, pick_ref, *row_refs):
@@ -189,7 +166,7 @@
 def soft_weights(lead_ref, near_ref, cent_ref, own_prefix_ref):
     docs = lead_ref.shape[0] - META
     h = lax.axis_index("dim")
-    prefix = jnp.where(h == 0, lead_ref[:docs, :], near_ref[:docs, :])
+    prefix = jnp.where(h == 0, lead_ref[:docs, :PREFIX], near_ref[...])
     scores = dot_nt(cent_ref[...], prefix) * TEMP
     top = jnp.max(scores, axis=0, keepdims=True)
     scale = 1.0 / jnp.sum(jnp.exp(scores - top), axis=0, keepdims=True)
@@ -200,7 +177,7 @@
 def add_lead(weights, lead_ref, old_refs, new_refs):
     docs = lead_ref.shape[0] - META
     per = new_refs[0].shape[0] - SUBLANES
-    sums = dot(weights.astype(BF16), lead_ref[:docs, :])
+    sums = dot(weights.astype(BF16), lead_ref[:docs, :PREFIX])
     ones = jnp.ones((SUBLANES, docs), BF16)
     for t, new in enumerate(new_refs):
         here = slice(t * per, (t + 1) * per)
@@ -216,19 +193,20 @@
             new[per:, :per] = mass
 
 
-def add_rest(weights, rest_ref, old_refs, new_refs):
+def add_rest(weights, rest, old_refs, new_refs):
     per = new_refs[0].shape[0]
-    sums = dot(weights, rest_ref[...])
+    sums = dot(weights, rest)
     for t, new in enumerate(new_refs):
         part = sums[t * per : (t + 1) * per]
         new[...] = old_refs[t][...] + part if old_refs else part
 
 
-def sums_kernel(subs, lead_ref, rest_ref, near_ref, cent_ref, own_prefix_ref, *refs):
+def sums_kernel(subs, block_ref, near_ref, cent_ref, own_prefix_ref, *refs):
     old, new = refs[: -2 * subs], refs[-2 * subs :]
-    weights = soft_weights(lead_ref, near_ref, cent_ref, own_prefix_ref)
-    add_lead(weights, lead_ref, old[:subs], new[:subs])
-    add_rest(weights.astype(BF16), rest_ref, old[subs:], new[subs:])
+    docs = block_ref.shape[0] - META
+    weights = soft_weights(block_ref, near_ref, cent_ref, own_prefix_ref)
+    add_lead(weights, block_ref, old[:subs], new[:subs])
+    add_rest(weights.astype(BF16), block_ref[:docs, PREFIX:], old[subs:], new[subs:])
 
 
 def sums_lead_kernel(subs, lead_ref, near_ref, cent_ref, own_prefix_ref, *refs):
@@ -239,7 +217,7 @@
 
 
 def sums_rest_kernel(subs, weights_ref, rest_ref, *refs):
-    add_rest(weights_ref[...], rest_ref, refs[:subs], refs[subs:])
+    add_rest(weights_ref[...], rest_ref[...], refs[:subs], refs[subs:])
 
 
 def gram_kernel(table, subs, *refs):
@@ -362,33 +340,39 @@
     def needed(step, kind):
         return any((step, kind) in [entry[:2] for entry in line] for line in table)
 
-    def swap(step, held):
-        return [
-            lax.ppermute(held[1 - kind], "rows", pairs_of(rows, kind)) if needed(step, kind) else None for kind in range(2)
-        ]
-
-    def slot_block(k, history):
+    def swap(step, held, cut=lambda value: value):
+        return {
+            kind: lax.ppermute(cut(held[1 - kind]), "rows", pairs_of(rows, kind))
+            for kind in (1, 0)
+            if needed(step, kind)
+        }
+
+    def lead_of(block):
+        return block[:, :PREFIX]
+
+    def rest_of(block):
+        return block[:docs, PREFIX:]
+
+    def slot_block(k, history, cut=lambda value: value):
+        def part(step, kind):
+            block = history[step][kind]
+            return block if step == rows - 1 else cut(block)
+
         kinds = {}
         for i, (step, kind, _) in enumerate(table[k]):
             kinds.setdefault((step, kind), []).append(i)
         (step, kind), *others = sorted(kinds, key=lambda key: (-len(kinds[key]), key))
-        value = history[step][kind]
+        value = part(step, kind)
         for step, kind in others:
             here = functools.reduce(jnp.logical_or, [z == i for i in kinds[step, kind]])
-            value = jnp.where(here, history[step][kind], value)
+            value = jnp.where(here, part(step, kind), value)
         return value
 
-    lead, rest = call(
-        pack_kernel,
-        "pack",
-        [shape((docs + META, PREFIX), BF16), shape((docs, half - PREFIX), BF16)],
-        [embeddings, cluster_id.reshape(1, docs)],
-        scratch=[pltpu.VMEM((1, docs), jnp.int32), pltpu.SemaphoreType.DMA((3,))],
-        far=2,
-    )
-    leads, rests = {0: [lead, lead]}, {0: [rest, rest]}
-    sending_lead = swap(1, leads[0])
-    sending_rest = swap(1, rests[0])
+    (block,) = call(
+        pack_kernel, "pack", [shape((docs + META, half), BF16)], [embeddings, cluster_id.reshape(1, docs)]
+    )
+    history = {0: {0: block, 1: block}}
+    coming = swap(1, history[0])
 
     inv, centre, own_prefix, prior, cent_prefix = call(
         functools.partial(prep_kernel, subs, per),
@@ -401,12 +385,6 @@
             shape((clusters, PREFIX), BF16),
         ],
         [cluster_place.reshape(1, clusters), centroids],
-        scratch=[
-            pltpu.VMEM((1, clusters), jnp.int32),
-            pltpu.VMEM((clusters, half), BF16),
-            pltpu.SemaphoreType.DMA((3,)),
-        ],
-        far=2,
         cost=4 * 1024 * 1024,
     )
 
@@ -414,43 +392,45 @@
     sum_shapes = [lead_sum] * subs + [rest_sum] * subs
     own_cost, other_cost = 2 * 1024 * 1024, 128 * 1024
 
-    def select(lead, rest, cost):
-        found = call(select_kernel, "select", [shape((groups, packed, half), BF16)] * subs, [lead, rest, inv, centre], cost=cost)
-        return list(found)
-
-    def add(lead, rest, prefix, sums, cost):
-        operands = [lead, rest, prefix, cent_prefix, own_prefix] + sums
-        aliases = {5 + i: i for i in range(len(sums))}
+    def select(block, cost):
+        row_shapes = [shape((groups, packed, half), BF16)] * subs
+        return list(call(select_kernel, "select", row_shapes, [block, inv, centre], cost=cost))
+
+    def add(block, prefix, sums, cost):
+        operands = [block, prefix, cent_prefix, own_prefix] + sums
+        aliases = {4 + i: i for i in range(len(sums))}
         return list(call(functools.partial(sums_kernel, subs), "sums", sum_shapes, operands, aliases, cost=cost))
 
     members = []
-
-    prefix = near(lead)
-    found = select(lead, rest, own_cost)
+    prefix = near(block[:docs, :PREFIX])
+    found = select(block, own_cost)
     members.append(across(found))
-    sums = add(lead, rest, prefix, [], own_cost)
-    for step in range(1, rows):
-        last = step == rows - 1
-        leads[step] = tied(sending_lead, found, members[: step - 1], *([sums] if last else []))
-        if not last:
-            sending_lead = swap(step + 1, leads[step])
-        lead = slot_block(step, leads)
-        prefix = near(lead)
-        if last:
-            break
-        rests[step] = tied(sending_rest, sums)
-        sending_rest = swap(step + 1, rests[step])
-        rest = slot_block(step, rests)
-        found = select(lead, rest, own_cost)
+    sums = add(block, prefix, [], own_cost)
+    for step in range(1, rows - 1):
+        history[step] = tied(coming, found, sums, members[: step - 1])
+        if step == rows - 2:
+            coming = swap(step + 1, history[step], lead_of)
+            coming_rest = swap(step + 1, history[step], rest_of)
+        else:
+            coming = swap(step + 1, history[step])
+        block = slot_block(step, history)
+        prefix = near(block[:docs, :PREFIX])
+        found = select(block, other_cost)
         members.append(across(found))
-        sums = add(lead, rest, prefix, sums, other_cost)
-
+        sums = add(block, prefix, sums, other_cost)
+
+    history[rows - 1] = tied(coming, found, sums, members)
+    lead = slot_block(rows - 1, history, lead_of)
+    prefix = near(lead[:docs])
     half_rows = [shape((groups, packed, PREFIX), BF16)] * subs
-    pick, *found = call(
-        select_lead_kernel, "select_lead", [shape((subs * per * MOST, docs), BF16)] + half_rows, [lead, inv, centre],
+    pick, *lead_found = call(
+        select_lead_kernel,
+        "select_lead",
+        [shape((subs * per * MOST, docs), BF16)] + half_rows,
+        [lead, inv, centre],
         cost=other_cost,
     )
-    lead_found = found
+    members.append(across(lead_found))
     weights, *lead_sums = call(
         functools.partial(sums_lead_kernel, subs),
         "sums_lead",
@@ -459,10 +439,9 @@
         {4 + i: 1 + i for i in range(subs)},
         cost=other_cost,
     )
-    members.append(across(tied(lead_found, members[: rows - 1])))
     lead_sums = across(lead_sums)
-    rests[rows - 1] = tied(sending_rest, weights, found, pick, members[: rows - 1])
-    rest = slot_block(rows - 1, rests)
+    history[rows - 1] = tied(coming_rest, prefix)
+    rest = slot_block(rows - 1, history, rest_of)
     half_rows = [shape((groups, packed, half - PREFIX), BF16)] * subs
     found = call(select_rest_kernel, "select_rest", half_rows, [pick, rest, centre], cost=other_cost)
     members.append(across(found))

time: 66.6 us -> 67.6 us (1.015)
  starting transfers between devices: 26.6 us -> 23 us
  local copies, waits for them, and re-layouts: 3.99 us -> 6.7 us
  other arithmetic: 1.1 us -> 3.08 us
  waiting for transfers between devices: 20.9 us -> 21.8 us
  Pallas kernels: 12.7 us -> 11.8 us
    ppermute x10 -> x6, starting transfers between devices: 19.5 us -> 14.4 us  [swap(): lax.ppermute(cut(held[1 - kind]), 'rows', pairs_of(rows, kind))]
    slice x0 -> x6, local copies, waits for them, and re-layouts: none -> 2.71 us  [the longest x1 0.97 us: lead_of(): return block[:, :PREFIX]]
    ppermute x10 -> x6, waiting for transfers between devices: 3.49 us -> 5.97 us  [swap(): lax.ppermute(cut(held[1 - kind]), 'rows', pairs_of(rows, kind))]
    select_n x4 -> x3, other arithmetic: 1.1 us -> 3.08 us  [slot_block(): value = jnp.where(here, part(step, kind), value)]
    ppermute x7, waiting for transfers between devices: 17.4 us -> 15.8 us  [across(): lax.ppermute(values[t], 'sub', [(i, (i + t) % subs) for i in range(subs)])]
    ppermute x7, starting transfers between devices: 6.87 us -> 8.29 us  [across(): lax.ppermute(values[t], 'sub', [(i, (i + t) % subs) for i in range(subs)])]
    pallas_call x14, Pallas kernels: 12.7 us -> 11.8 us  [call(): pl.pallas_call(kernel, out_shape=tuple(out_shape), in_specs=[place(at) fo...]
  transfers between devices with their start and end apart: 22 -> 18, of which waited for: 6 -> 6; matrix products, arithmetic and copies ran while one was open for 2% -> 9% of each run, Pallas kernels for 17% -> 15%
where the time goes in v4:
time: 67.6 us; the launch traced here: 67.1 us
  starting transfers between devices  23 us (34%)
  waiting for transfers between devices  21.8 us (32%)
  Pallas kernels  11.8 us (17%)
  local copies, waits for them, and re-layouts  6.7 us (10%)
  other arithmetic  3.08 us (5%)
  between operations  0.83 us (1%)
    ppermute x7, waiting for transfers between devices, across(): lax.ppermute(values[t], 'sub', [(i, (i + t) % subs) for i in range(subs)])  15.8 us
    ppermute x6, starting transfers between devices, swap(): lax.ppermute(cut(held[1 - kind]), 'rows', pairs_of(rows, kind))  14.4 us
    pallas_call x14, Pallas kernels, call(): pl.pallas_call(kernel, out_shape=tuple(out_shape), in_specs=[place(at) fo...  11.8 us
    ppermute x7, starting transfers between devices, across(): lax.ppermute(values[t], 'sub', [(i, (i + t) % subs) for i in range(subs)])  8.29 us
    ppermute x6, waiting for transfers between devices, swap(): lax.ppermute(cut(held[1 - kind]), 'rows', pairs_of(rows, kind))  5.97 us
    unnamed x8, local copies, waits for them, and re-layouts  3.99 us
    select_n x3, other arithmetic, slot_block(): value = jnp.where(here, part(step, kind), value)  3.08 us
  transfers between devices with their start and end apart: 18, of which 6 were waited for; matrix products, arithmetic and copies ran while one was open for 9% of the time, Pallas kernels for 15%

profile of v4, /device:TPU:0, one launch (start us, length us, event | category | flops | bytes accessed | tf_op | source)
XLA Modules:
  0.0 67.1 jit_solution(9717096202923803935)
XLA Ops:
  0.6 1.0 %copy-done.1 = bf16[512,512]{1,0:T(8,128)(2,1)S(1)} copy-done((bf16[512,512]{1,0:T(8,128)(2,1)S(1)}, bf16[512,512]{1,0:T(8,128)(2,1)}, u32[]{:S(2)}) %copy-start.1) | copy-done | bytes 524312
  1.7 0.7 %copy-done.3 = s32[512,1]{0,1:T(1,128)S(1)} copy-done((s32[512,1]{0,1:T(1,128)S(1)}, s32[512,1]{0,1:T(1,128)}, u32[]{:S(2)}) %copy-start.3) | copy-done | bytes 2072
  2.4 3.1 %collective-permute-start = (bf16[528,512]{1,0:T(8,128)(2,1)S(1)}, bf16[528,512]{1,0:T(8,128)(2,1)S(1)}, u32[]{:S(2)}, u32[]{:S(2)}) collective-permute-start(bf16[528,512]{1,0:T(8,128)(2,1)S(1)} %pack.1.block_ref), channel_id=1, source_target_pairs={{0,4},{4,0},{8,12},{12,8},{1,5},{5,1},{9,13},{13,9},{2,6},{6,2},{1... | collective-permute-start | bytes 1622024 | tf_op jit(solution)/shard_map/ppermute | solution.py:345
  5.5 1.4 %collective-permute-start.1 = (bf16[528,512]{1,0:T(8,128)(2,1)S(1)}, bf16[528,512]{1,0:T(8,128)(2,1)}, u32[]{:S(2)}, u32[]{:S(2)}) collective-permute-start(bf16[528,512]{1,0:T(8,128)(2,1)S(1)} %pack.1.block_ref), channel_id=1, source_target_pairs={{0,0},{4,8},{8,4},{12,12},{1,1},{5,9},{9,5},{13,13},{2,2},{6,10},{... | collective-permute-start | bytes 1622024 | tf_op jit(solution)/shard_map/ppermute | solution.py:345
  7.0 0.1 collective-permute-start.2
  7.0 0.0 copy-start
  7.0 1.6 %copy-done = bf16[1024,1024]{1,0:T(8,128)(2,1)S(1)} copy-done((bf16[1024,1024]{1,0:T(8,128)(2,1)S(1)}, bf16[1024,1024]{1,0:T(8,128)(2,1)}, u32[]{:S(2)}) %copy-start) | copy-done | bytes 2097176
  8.6 0.7 %copy-done.2 = s32[1024]{0:T(1024)S(1)} copy-done((s32[1024]{0:T(1024)S(1)}, s32[1024]{0:T(1024)}, u32[]{:S(2)}) %copy-start.2) | copy-done | bytes 4120
  9.3 0.8 %prep.1 = (f32[256,1]{1,0:T(8,128)S(1)}, bf16[256,512]{1,0:T(8,128)(2,1)S(1)}, bf16[256,256]{1,0:T(8,128)(2,1)S(1)}, bf16[128,512]{1,0:T(8,128)(2,1)S(1)}, bf16[1024,256]{1,0:T(8,128)(2,1)S(1)}) custom-call(s32[1,1024]{1,0:T(1,128)S(1)} %bitcast.3, bf16[1024,1024]{1,0:T(8,128)(2,1)S(1)} %copy-done), custom_call_target="tpu_custom_call" | custom-call | flops 209715200 | bytes 4194304 | tf_op jit(solution)/shard_map/prep/pallas_call | solution.py:32
  10.2 0.8 %select.3 = (bf16[16,16,512]{2,1,0:T(8,128)(2,1)S(1)}, bf16[16,16,512]{2,1,0:T(8,128)(2,1)S(1)}) custom-call(bf16[528,512]{1,0:T(8,128)(2,1)S(1)} %pack.1.block_ref, f32[256,1]{1,0:T(8,128)S(1)} %get-tuple-element.43.inv_ref, bf16[256,512]{1,0:T(8,128)(2,1)S(1)} %get-tuple-element.44.centre_ref), custom_call_target="tpu_custom_call" | custom-call | flops 104857600 | bytes 2097152 | tf_op jit(solution)/shard_map/select/pallas_call | solution.py:32
  10.9 1.3 %sums.3 = (f32[136,256]{1,0:T(8,128)S(1)}, f32[136,256]{1,0:T(8,128)S(1)}, f32[128,256]{1,0:T(8,128)S(1)}, f32[128,256]{1,0:T(8,128)S(1)}) custom-call(bf16[528,512]{1,0:T(8,128)(2,1)S(1)} %pack.1.block_ref, bf16[512,256]{1,0:T(8,128)(2,1)S(1)} %collective-permute-done.2.near_ref, bf16[1024,256]{1,0:T(8,128)(2,1)S(1)} %get-tuple-element.47.cent_ref, ...), custom_call_target="tpu_custom_call" | custom-call | flops 104857600 | bytes 2097152 | tf_op jit(solution)/shard_map/sums/pallas_call | solution.py:32
  12.3 5.5 %collective-permute-done.block_ref = bf16[528,512]{1,0:T(8,128)(2,1)S(1)} collective-permute-done((bf16[528,512]{1,0:T(8,128)(2,1)S(1)}, bf16[528,512]{1,0:T(8,128)(2,1)S(1)}, u32[]{:S(2)}, u32[]{:S(2)}) %collective-permute-start) | collective-permute-done | bytes 540704 | tf_op jit(solution)/shard_map/ppermute | solution.py:345
  17.8 4.9 %collective-permute-start.3 = (bf16[528,512]{1,0:T(8,128)(2,1)}, bf16[528,512]{1,0:T(8,128)(2,1)}, u32[]{:S(2)}, u32[]{:S(2)}) collective-permute-start(bf16[528,512]{1,0:T(8,128)(2,1)} %collective-permute-done.1), channel_id=1, source_target_pairs={{0,4},{4,0},{8,12},{12,8},{1,5},{5,1},{9,13},{13,9},{2,6},{6,2},{1... | collective-permute-start | bytes 1622024 | tf_op jit(solution)/shard_map/ppermute | solution.py:345
  22.6 1.4 %collective-permute-start.4 = (bf16[528,512]{1,0:T(8,128)(2,1)S(1)}, bf16[528,512]{1,0:T(8,128)(2,1)}, u32[]{:S(2)}, u32[]{:S(2)}) collective-permute-start(bf16[528,512]{1,0:T(8,128)(2,1)S(1)} %collective-permute-done.block_ref), channel_id=1, source_target_pairs={{0,0},{4,8},{8,4},{12,12},{1,1},{5,9},{9,5},{13,13},{2,2},{6,10},{... | collective-permute-start | bytes 1622024 | tf_op jit(solution)/shard_map/ppermute | solution.py:345
  24.1 0.7 %slice.21 = bf16[512,256]{1,0:T(8,128)(2,1)} slice(bf16[528,512]{1,0:T(8,128)(2,1)S(1)} %collective-permute-done.block_ref), slice={[0:512], [0:256]} | slice | bytes 524288 | tf_op jit(solution)/shard_map/slice | solution.py:417
  24.8 0.0 collective-permute-start.5
  24.8 1.5 %collective-permute-start.6 = (bf16[16,16,512]{2,1,0:T(8,128)(2,1)S(1)}, bf16[16,16,512]{2,1,0:T(8,128)(2,1)S(1)}, u32[]{:S(2)}, u32[]{:S(2)}) collective-permute-start(bf16[16,16,512]{2,1,0:T(8,128)(2,1)S(1)} %get-tuple-element.46), channel_id=1, source_target_pairs={{0,2},{2,0},{1,3},{3,1},{4,6},{6,4},{5,7},{7,5},{8,10},{10,8},{9,1... | collective-permute-start | bytes 786440 | tf_op jit(solution)/shard_map/ppermute | solution.py:334
  26.3 0.7 %select.4 = (bf16[16,16,512]{2,1,0:T(8,128)(2,1)S(1)}, bf16[16,16,512]{2,1,0:T(8,128)(2,1)S(1)}) custom-call(bf16[528,512]{1,0:T(8,128)(2,1)S(1)} %collective-permute-done.block_ref, f32[256,1]{1,0:T(8,128)S(1)} %get-tuple-element.43.inv_ref, bf16[256,512]{1,0:T(8,128)(2,1)S(1)} %get-tuple-element.44.centre_ref), custom_call_target="tpu_custom_call" | custom-call | flops 6553600 | bytes 131072 | tf_op jit(solution)/shard_map/select/pallas_call | solution.py:32
  27.0 0.6 collective-permute-start.9
  27.6 1.3 %sums.4 = (f32[136,256]{1,0:T(8,128)S(1)}, f32[136,256]{1,0:T(8,128)S(1)}, f32[128,256]{1,0:T(8,128)S(1)}, f32[128,256]{1,0:T(8,128)S(1)}) custom-call(bf16[528,512]{1,0:T(8,128)(2,1)S(1)} %collective-permute-done.block_ref, ...), custom_call_target="tpu_custom_call", output_to_operand_aliasing={{0}: (4, {}), {1}: (5, {}), {2}: (6, {}), {3}: (7, {})} | custom-call | flops 6553600 | bytes 131072 | tf_op jit(solution)/shard_map/sums/pallas_call | solution.py:32
  28.9 5.0 %collective-permute-done.6.refs_5_ = bf16[16,16,512]{2,1,0:T(8,128)(2,1)S(1)} collective-permute-done((bf16[16,16,512]{2,1,0:T(8,128)(2,1)S(1)}, bf16[16,16,512]{2,1,0:T(8,128)(2,1)S(1)}, u32[]{:S(2)}, u32[]{:S(2)}) %collective-permute-start.6) | collective-permute-done | bytes 262176 | tf_op jit(solution)/shard_map/ppermute | solution.py:334
  33.9 0.5 collective-permute-done.3
  34.4 1.0 %slice.22 = bf16[528,256]{1,0:T(8,128)(2,1)S(1)} slice(bf16[528,512]{1,0:T(8,128)(2,1)} %collective-permute-done.4), slice={[0:528], [0:256]} | slice | bytes 540672 | tf_op jit(solution)/shard_map/slice | solution.py:351
  35.3 3.5 %collective-permute-start.7 = (bf16[528,256]{1,0:T(8,128)(2,1)S(1)}, bf16[528,256]{1,0:T(8,128)(2,1)S(1)}, u32[]{:S(2)}, u32[]{:S(2)}) collective-permute-start(bf16[528,256]{1,0:T(8,128)(2,1)S(1)} %slice.22), channel_id=1, source_target_pairs={{0,4},{4,0},{8,12},{12,8},{1,5},{5,1},{9,13},{13,9},{2,6},{6,2},{1... | collective-permute-start | bytes 811016 | tf_op jit(solution)/shard_map/ppermute | solution.py:345
  38.8 1.1 %broadcast_select_fusion.block_ref = bf16[528,512]{1,0:T(8,128)(2,1)S(1)} fusion(bf16[528,512]{1,0:T(8,128)(2,1)} %collective-permute-done.3, bf16[528,512]{1,0:T(8,128)(2,1)} %collective-permute-done.1, pred[]{:T(512)S(6)} %or.2), kind=kLoop, calls=%fused_computation | loop fusion | flops 270336 | bytes 1622017 | tf_op jit(solution)/shard_map/jit(_where)/select_n | solution.py:368
  39.9 0.1 collective-permute-start.8
  40.0 0.7 %select.5 = (bf16[16,16,512]{2,1,0:T(8,128)(2,1)S(1)}, bf16[16,16,512]{2,1,0:T(8,128)(2,1)S(1)}) custom-call(bf16[528,512]{1,0:T(8,128)(2,1)S(1)} %broadcast_select_fusion.block_ref, f32[256,1]{1,0:T(8,128)S(1)} %get-tuple-element.43.inv_ref, bf16[256,512]{1,0:T(8,128)(2,1)S(1)} %get-tuple-element.44.centre_ref), custom_call_target="tpu_custom_call" | custom-call | flops 6553600 | bytes 131072 | tf_op jit(solution)/shard_map/select/pallas_call | solution.py:32
  40.8 1.6 %collective-permute-start.10 = (bf16[16,16,512]{2,1,0:T(8,128)(2,1)S(1)}, bf16[16,16,512]{2,1,0:T(8,128)(2,1)S(1)}, u32[]{:S(2)}, u32[]{:S(2)}) collective-permute-start(bf16[16,16,512]{2,1,0:T(8,128)(2,1)S(1)} %get-tuple-element.64), channel_id=1, source_target_pairs={{0,2},{2,0},{1,3},{3,1},{4,6},{6,4},{5,7},{7,5},{8,10},{10,8},{9,1... | collective-permute-start | bytes 786440 | tf_op jit(solution)/shard_map/ppermute | solution.py:334
  42.3 1.0 %slice.24 = bf16[512,256]{1,0:T(8,128)(2,1)S(1)} slice(bf16[528,512]{1,0:T(8,128)(2,1)} %collective-permute-done.4), slice={[0:512], [256:512]} | slice | bytes 524288 | tf_op jit(solution)/shard_map/slice | solution.py:354
  43.3 0.1 collective-permute-start.11
  43.4 1.3 %sums.5 = (f32[136,256]{1,0:T(8,128)S(1)}, f32[136,256]{1,0:T(8,128)S(1)}, f32[128,256]{1,0:T(8,128)S(1)}, f32[128,256]{1,0:T(8,128)S(1)}) custom-call(bf16[528,512]{1,0:T(8,128)(2,1)S(1)} %broadcast_select_fusion.block_ref, ...), custom_call_target="tpu_custom_call", output_to_operand_aliasing={{0}: (4, {}), {1}: (5, {}), {2}: (6, {}), {3}: (7, {})} | custom-call | flops 6553600 | bytes 131072 | tf_op jit(solution)/shard_map/sums/pallas_call | solution.py:32
  44.7 4.8 %collective-permute-done.10.refs_7_ = bf16[16,16,512]{2,1,0:T(8,128)(2,1)S(1)} collective-permute-done((bf16[16,16,512]{2,1,0:T(8,128)(2,1)S(1)}, bf16[16,16,512]{2,1,0:T(8,128)(2,1)S(1)}, u32[]{:S(2)}, u32[]{:S(2)}) %collective-permute-start.10) | collective-permute-done | bytes 262176 | tf_op jit(solution)/shard_map/ppermute | solution.py:334
  49.5 1.0 %broadcast_select_fusion.1.lead_ref = bf16[528,256]{1,0:T(8,128)(2,1)S(1)} fusion(bf16[528,256]{1,0:T(8,128)(2,1)S(1)} %collective-permute-done.7, pred[]{:T(512)S(6)} %or.2, bf16[528,512]{1,0:T(8,128)(2,1)} %collective-permute-done.4), kind=kLoop, calls=%fused_computation.1 | loop fusion | flops 135168 | bytes 811009 | tf_op jit(solution)/shard_map/jit(_where)/select_n | solution.py:368
  50.6 0.1 collective-permute-start.12
  50.6 0.6 select_lead.1
  51.2 1.6 %collective-permute-start.13 = (bf16[16,16,256]{2,1,0:T(8,128)(2,1)S(1)}, bf16[16,16,256]{2,1,0:T(8,128)(2,1)S(1)}, u32[]{:S(2)}, u32[]{:S(2)}) collective-permute-start(bf16[16,16,256]{2,1,0:T(8,128)(2,1)S(1)} %get-tuple-element.74), channel_id=1, source_target_pairs={{0,2},{2,0},{1,3},{3,1},{4,6},{6,4},{5,7},{7,5},{8,10},{10,8},{9,1... | collective-permute-start | bytes 393224 | tf_op jit(solution)/shard_map/ppermute | solution.py:334
  52.8 1.0 %broadcast_select_fusion.2.rest_ref = bf16[512,256]{1,0:T(8,128)(2,1)S(1)} fusion(bf16[512,256]{1,0:T(8,128)(2,1)S(1)} %collective-permute-done.11, pred[]{:T(512)S(6)} %or.2, bf16[528,512]{1,0:T(8,128)(2,1)} %collective-permute-done.4), kind=kLoop, calls=%fused_computation.2 | loop fusion | flops 131072 | bytes 786433 | tf_op jit(solution)/shard_map/jit(_where)/select_n | solution.py:368
  53.8 0.3 select_rest.1
  54.1 0.9 %collective-permute-start.14 = (bf16[16,16,256]{2,1,0:T(8,128)(2,1)S(1)}, bf16[16,16,256]{2,1,0:T(8,128)(2,1)S(1)}, u32[]{:S(2)}, u32[]{:S(2)}) collective-permute-start(bf16[16,16,256]{2,1,0:T(8,128)(2,1)S(1)} %get-tuple-element.75), channel_id=1, source_target_pairs={{0,2},{2,0},{1,3},{3,1},{4,6},{6,4},{5,7},{7,5},{8,10},{10,8},{9,1... | collective-permute-start | bytes 393224 | tf_op jit(solution)/shard_map/ppermute | solution.py:334
  55.0 1.4 %sums_lead.1 = (bf16[256,512]{1,0:T(8,128)(2,1)S(1)}, f32[136,256]{1,0:T(8,128)S(1)}, f32[136,256]{1,0:T(8,128)S(1)}) custom-call(bf16[528,256]{1,0:T(8,128)(2,1)S(1)} %broadcast_select_fusion.1.lead_ref, bf16[512,256]{1,0:T(8,128)(2,1)S(1)} %collective-permute-done.12.near_ref, ...), custom_call_target="tpu_custom_call", output_to_operand_aliasing={{1}: (4, {}), {2}: (5, {})} | custom-call | flops 6553600 | bytes 131072 | tf_op jit(solution)/shard_map/sums_lead/pallas_call | solution.py:32
  56.4 1.2 %collective-permute-start.16 = (f32[136,256]{1,0:T(8,128)S(1)}, f32[136,256]{1,0:T(8,128)S(1)}, u32[]{:S(2)}, u32[]{:S(2)}) collective-permute-start(f32[136,256]{1,0:T(8,128)S(1)} %get-tuple-element.77), channel_id=1, source_target_pairs={{0,2},{2,0},{1,3},{3,1},{4,6},{6,4},{5,7},{7,5},{8,10},{10,8},{9,1... | collective-permute-start | bytes 417800 | tf_op jit(solution)/shard_map/ppermute | solution.py:334
  57.6 0.2 sums_rest.1
  57.9 0.9 %collective-permute-start.17 = (f32[128,256]{1,0:T(8,128)S(1)}, f32[128,256]{1,0:T(8,128)S(1)}, u32[]{:S(2)}, u32[]{:S(2)}) collective-permute-start(f32[128,256]{1,0:T(8,128)S(1)} %get-tuple-element.80), channel_id=1, source_target_pairs={{0,2},{2,0},{1,3},{3,1},{4,6},{6,4},{5,7},{7,5},{8,10},{10,8},{9,1... | collective-permute-start | bytes 393224 | tf_op jit(solution)/shard_map/ppermute | solution.py:334
  58.8 1.7 %collective-permute-done.14.refs_9_ = bf16[16,16,256]{2,1,0:T(8,128)(2,1)S(1)} collective-permute-done((bf16[16,16,256]{2,1,0:T(8,128)(2,1)S(1)}, bf16[16,16,256]{2,1,0:T(8,128)(2,1)S(1)}, u32[]{:S(2)}, u32[]{:S(2)}) %collective-permute-start.14) | collective-permute-done | bytes 131104 | tf_op jit(solution)/shard_map/ppermute | solution.py:334
  60.5 0.9 %gram.1.mine_ref = f32[16,16,128]{2,1,0:T(8,128)S(1)} custom-call(bf16[16,16,512]{2,1,0:T(8,128)(2,1)S(1)} %get-tuple-element.45.refs_0_, bf16[16,16,512]{2,1,0:T(8,128)(2,1)S(1)} %get-tuple-element.54.refs_1_, bf16[16,16,512]{2,1,0:T(8,128)(2,1)S(1)} %get-tuple-element.62.refs_2_, bf16[16,16,256]{2,1,0:T(8,128)(2,1)S(1)} %get-tuple-element.70.refs_3_, ...), custom_call_target="tpu_custom_call" | custom-call | tf_op jit(solution)/shard_map/gram/pallas_call | solution.py:32
  61.4 0.1 collective-permute-start.15
  61.4 4.4 %collective-permute-done.17.refs_3_ = f32[128,256]{1,0:T(8,128)S(1)} collective-permute-done((f32[128,256]{1,0:T(8,128)S(1)}, f32[128,256]{1,0:T(8,128)S(1)}, u32[]{:S(2)}, u32[]{:S(2)}) %collective-permute-start.17) | collective-permute-done | bytes 131104 | tf_op jit(solution)/shard_map/ppermute | solution.py:334
  65.8 1.4 %finish.1 = (f32[128,512]{1,0:T(8,128)}, bf16[8,16,128]{2,1,0:T(8,128)(2,1)}) custom-call(f32[16,16,128]{2,1,0:T(8,128)S(1)} %gram.1.mine_ref, f32[16,16,128]{2,1,0:T(8,128)S(1)} %collective-permute-done.15.other_ref, f32[136,256]{1,0:T(8,128)S(1)} %get-tuple-element.76.refs_0_, f32[136,256]{1,0:T(8,128)S(1)} %collective-permute-done.16.refs_1_, ...), custom_call_target="tpu_custom_call" | custom-call | tf_op jit(solution)/shard_map/finish/pallas_call | solution.py:32
  (19 shorter events, 0.1 us)
Async XLA Ops:
  0.6 1.0 %copy-start.1 = (bf16[512,512]{1,0:T(8,128)(2,1)S(1)}, bf16[512,512]{1,0:T(8,128)(2,1)}, u32[]{:S(2)}) copy-start(bf16[512,512]{1,0:T(8,128)(2,1)} %emb_ref.1) | copy-start | bytes 1572868
  1.7 0.7 %copy-start.3 = (s32[512,1]{0,1:T(1,128)S(1)}, s32[512,1]{0,1:T(1,128)}, u32[]{:S(2)}) copy-start(s32[512,1]{0,1:T(1,128)} %param.6) | copy-start | bytes 6148
  2.4 15.4 %collective-permute-start = (bf16[528,512]{1,0:T(8,128)(2,1)S(1)}, bf16[528,512]{1,0:T(8,128)(2,1)S(1)}, u32[]{:S(2)}, u32[]{:S(2)}) collective-permute-start(bf16[528,512]{1,0:T(8,128)(2,1)S(1)} %pack.1.block_ref), channel_id=1, source_target_pairs={{0,4},{4,0},{8,12},{12,8},{1,5},{5,1},{9,13},{13,9},{2,6},{6,2},{1... | collective-permute-start | bytes 1622024 | tf_op jit(solution)/shard_map/ppermute | solution.py:345
  5.5 12.3 %collective-permute-start.1 = (bf16[528,512]{1,0:T(8,128)(2,1)S(1)}, bf16[528,512]{1,0:T(8,128)(2,1)}, u32[]{:S(2)}, u32[]{:S(2)}) collective-permute-start(bf16[528,512]{1,0:T(8,128)(2,1)S(1)} %pack.1.block_ref), channel_id=1, source_target_pairs={{0,0},{4,8},{8,4},{12,12},{1,1},{5,9},{9,5},{13,13},{2,2},{6,10},{... | collective-permute-start | bytes 1622024 | tf_op jit(solution)/shard_map/ppermute | solution.py:345
  7.0 4.0 %collective-permute-start.2 = (bf16[512,256]{1,0:T(8,128)(2,1)S(1)}, bf16[512,256]{1,0:T(8,128)(2,1)S(1)}, u32[]{:S(2)}, u32[]{:S(2)}) collective-permute-start(bf16[512,256]{1,0:T(8,128)(2,1)S(1)} %slice.26), channel_id=1, source_target_pairs={{0,1},{1,0},{2,3},{3,2},{4,5},{5,4},{6,7},{7,6},{8,9},{9,8},{10,11... | collective-permute-start | bytes 786440 | tf_op jit(solution)/shard_map/ppermute | solution.py:338
  7.0 1.6 %copy-start = (bf16[1024,1024]{1,0:T(8,128)(2,1)S(1)}, bf16[1024,1024]{1,0:T(8,128)(2,1)}, u32[]{:S(2)}) copy-start(bf16[1024,1024]{1,0:T(8,128)(2,1)} %cent_ref.1) | copy-start | bytes 6291460
  8.6 0.7 %copy-start.2 = (s32[1024]{0:T(1024)S(1)}, s32[1024]{0:T(1024)}, u32[]{:S(2)}) copy-start(s32[1024]{0:T(1024)} %param.7) | copy-start | bytes 12292
  17.8 16.6 %collective-permute-start.3 = (bf16[528,512]{1,0:T(8,128)(2,1)}, bf16[528,512]{1,0:T(8,128)(2,1)}, u32[]{:S(2)}, u32[]{:S(2)}) collective-permute-start(bf16[528,512]{1,0:T(8,128)(2,1)} %collective-permute-done.1), channel_id=1, source_target_pairs={{0,4},{4,0},{8,12},{12,8},{1,5},{5,1},{9,13},{13,9},{2,6},{6,2},{1... | collective-permute-start | bytes 1622024 | tf_op jit(solution)/shard_map/ppermute | solution.py:345
  22.6 11.7 %collective-permute-start.4 = (bf16[528,512]{1,0:T(8,128)(2,1)S(1)}, bf16[528,512]{1,0:T(8,128)(2,1)}, u32[]{:S(2)}, u32[]{:S(2)}) collective-permute-start(bf16[528,512]{1,0:T(8,128)(2,1)S(1)} %collective-permute-done.block_ref), channel_id=1, source_target_pairs={{0,0},{4,8},{8,4},{12,12},{1,1},{5,9},{9,5},{13,13},{2,2},{6,10},{... | collective-permute-start | bytes 1622024 | tf_op jit(solution)/shard_map/ppermute | solution.py:345
  24.8 2.8 %collective-permute-start.5 = (bf16[512,256]{1,0:T(8,128)(2,1)}, bf16[512,256]{1,0:T(8,128)(2,1)S(1)}, u32[]{:S(2)}, u32[]{:S(2)}) collective-permute-start(bf16[512,256]{1,0:T(8,128)(2,1)} %slice.21), channel_id=1, source_target_pairs={{0,1},{1,0},{2,3},{3,2},{4,5},{5,4},{6,7},{7,6},{8,9},{9,8},{10,11... | collective-permute-start | bytes 786440 | tf_op jit(solution)/shard_map/ppermute | solution.py:338
  24.8 9.1 %collective-permute-start.6 = (bf16[16,16,512]{2,1,0:T(8,128)(2,1)S(1)}, bf16[16,16,512]{2,1,0:T(8,128)(2,1)S(1)}, u32[]{:S(2)}, u32[]{:S(2)}) collective-permute-start(bf16[16,16,512]{2,1,0:T(8,128)(2,1)S(1)} %get-tuple-element.46), channel_id=1, source_target_pairs={{0,2},{2,0},{1,3},{3,1},{4,6},{6,4},{5,7},{7,5},{8,10},{10,8},{9,1... | collective-permute-start | bytes 786440 | tf_op jit(solution)/shard_map/ppermute | solution.py:334
  27.0 17.7 %collective-permute-start.9 = (bf16[16,16,512]{2,1,0:T(8,128)(2,1)S(1)}, bf16[16,16,512]{2,1,0:T(8,128)(2,1)S(1)}, u32[]{:S(2)}, u32[]{:S(2)}) collective-permute-start(bf16[16,16,512]{2,1,0:T(8,128)(2,1)S(1)} %get-tuple-element.56), channel_id=1, source_target_pairs={{0,2},{2,0},{1,3},{3,1},{4,6},{6,4},{5,7},{7,5},{8,10},{10,8},{9,1... | collective-permute-start | bytes 786440 | tf_op jit(solution)/shard_map/ppermute | solution.py:334
  35.3 14.2 %collective-permute-start.7 = (bf16[528,256]{1,0:T(8,128)(2,1)S(1)}, bf16[528,256]{1,0:T(8,128)(2,1)S(1)}, u32[]{:S(2)}, u32[]{:S(2)}) collective-permute-start(bf16[528,256]{1,0:T(8,128)(2,1)S(1)} %slice.22), channel_id=1, source_target_pairs={{0,4},{4,0},{8,12},{12,8},{1,5},{5,1},{9,13},{13,9},{2,6},{6,2},{1... | collective-permute-start | bytes 811016 | tf_op jit(solution)/shard_map/ppermute | solution.py:345
  39.9 3.4 %collective-permute-start.8 = (bf16[512,256]{1,0:T(8,128)(2,1)S(1)}, bf16[512,256]{1,0:T(8,128)(2,1)S(1)}, u32[]{:S(2)}, u32[]{:S(2)}) collective-permute-start(bf16[512,256]{1,0:T(8,128)(2,1)S(1)} %slice.27), channel_id=1, source_target_pairs={{0,1},{1,0},{2,3},{3,2},{4,5},{5,4},{6,7},{7,6},{8,9},{9,8},{10,11... | collective-permute-start | bytes 786440 | tf_op jit(solution)/shard_map/ppermute | solution.py:338
  40.8 8.8 %collective-permute-start.10 = (bf16[16,16,512]{2,1,0:T(8,128)(2,1)S(1)}, bf16[16,16,512]{2,1,0:T(8,128)(2,1)S(1)}, u32[]{:S(2)}, u32[]{:S(2)}) collective-permute-start(bf16[16,16,512]{2,1,0:T(8,128)(2,1)S(1)} %get-tuple-element.64), channel_id=1, source_target_pairs={{0,2},{2,0},{1,3},{3,1},{4,6},{6,4},{5,7},{7,5},{8,10},{10,8},{9,1... | collective-permute-start | bytes 786440 | tf_op jit(solution)/shard_map/ppermute | solution.py:334
  43.3 9.5 %collective-permute-start.11 = (bf16[512,256]{1,0:T(8,128)(2,1)S(1)}, bf16[512,256]{1,0:T(8,128)(2,1)S(1)}, u32[]{:S(2)}, u32[]{:S(2)}) collective-permute-start(bf16[512,256]{1,0:T(8,128)(2,1)S(1)} %slice.24), channel_id=1, source_target_pairs={{0,4},{4,0},{8,12},{12,8},{1,5},{5,1},{9,13},{13,9},{2,6},{6,2},{1... | collective-permute-start | bytes 786440 | tf_op jit(solution)/shard_map/ppermute | solution.py:345
  50.6 2.2 %collective-permute-start.12 = (bf16[512,256]{1,0:T(8,128)(2,1)S(1)}, bf16[512,256]{1,0:T(8,128)(2,1)S(1)}, u32[]{:S(2)}, u32[]{:S(2)}) collective-permute-start(bf16[512,256]{1,0:T(8,128)(2,1)S(1)} %slice.28), channel_id=1, source_target_pairs={{0,1},{1,0},{2,3},{3,2},{4,5},{5,4},{6,7},{7,6},{8,9},{9,8},{10,11... | collective-permute-start | bytes 786440 | tf_op jit(solution)/shard_map/ppermute | solution.py:338
  51.2 7.6 %collective-permute-start.13 = (bf16[16,16,256]{2,1,0:T(8,128)(2,1)S(1)}, bf16[16,16,256]{2,1,0:T(8,128)(2,1)S(1)}, u32[]{:S(2)}, u32[]{:S(2)}) collective-permute-start(bf16[16,16,256]{2,1,0:T(8,128)(2,1)S(1)} %get-tuple-element.74), channel_id=1, source_target_pairs={{0,2},{2,0},{1,3},{3,1},{4,6},{6,4},{5,7},{7,5},{8,10},{10,8},{9,1... | collective-permute-start | bytes 393224 | tf_op jit(solution)/shard_map/ppermute | solution.py:334
  54.1 6.4 %collective-permute-start.14 = (bf16[16,16,256]{2,1,0:T(8,128)(2,1)S(1)}, bf16[16,16,256]{2,1,0:T(8,128)(2,1)S(1)}, u32[]{:S(2)}, u32[]{:S(2)}) collective-permute-start(bf16[16,16,256]{2,1,0:T(8,128)(2,1)S(1)} %get-tuple-element.75), channel_id=1, source_target_pairs={{0,2},{2,0},{1,3},{3,1},{4,6},{6,4},{5,7},{7,5},{8,10},{10,8},{9,1... | collective-permute-start | bytes 393224 | tf_op jit(solution)/shard_map/ppermute | solution.py:334
  56.4 9.4 %collective-permute-start.16 = (f32[136,256]{1,0:T(8,128)S(1)}, f32[136,256]{1,0:T(8,128)S(1)}, u32[]{:S(2)}, u32[]{:S(2)}) collective-permute-start(f32[136,256]{1,0:T(8,128)S(1)} %get-tuple-element.77), channel_id=1, source_target_pairs={{0,2},{2,0},{1,3},{3,1},{4,6},{6,4},{5,7},{7,5},{8,10},{10,8},{9,1... | collective-permute-start | bytes 417800 | tf_op jit(solution)/shard_map/ppermute | solution.py:334
  57.9 7.9 %collective-permute-start.17 = (f32[128,256]{1,0:T(8,128)S(1)}, f32[128,256]{1,0:T(8,128)S(1)}, u32[]{:S(2)}, u32[]{:S(2)}) collective-permute-start(f32[128,256]{1,0:T(8,128)S(1)} %get-tuple-element.80), channel_id=1, source_target_pairs={{0,2},{2,0},{1,3},{3,1},{4,6},{6,4},{5,7},{7,5},{8,10},{10,8},{9,1... | collective-permute-start | bytes 393224 | tf_op jit(solution)/shard_map/ppermute | solution.py:334
  61.4 4.4 %collective-permute-start.15 = (f32[16,16,128]{2,1,0:T(8,128)S(1)}, f32[16,16,128]{2,1,0:T(8,128)S(1)}, u32[]{:S(2)}, u32[]{:S(2)}) collective-permute-start(f32[16,16,128]{2,1,0:T(8,128)S(1)} %gram.1.mine_ref), channel_id=1, source_target_pairs={{0,1},{1,0},{2,3},{3,2},{4,5},{5,4},{6,7},{7,6},{8,9},{9,8},{10,11... | collective-permute-start | bytes 393224 | tf_op jit(solution)/shard_map/ppermute | solution.py:338

commit v5 on v4

--- a/solution.py
+++ b/solution.py
@@ -56,24 +56,8 @@
     return jax.tree.unflatten(tree, kept[: len(leaves)])
 
 
-def arrivals(rows):
-    table = []
-    for z in range(rows):
-        line = [(0, 0, z)]
-        for step in range(1, rows):
-            for kind in range(2):
-                source = z + step if z % 2 == kind else z - step
-                if 0 <= source < rows:
-                    line.append((step, kind, source))
-        table.append(line)
-    return [[table[z][k] for z in range(rows)] for k in range(rows)]
-
-
-def pairs_of(rows, kind):
-    other = list(range(rows))
-    for i in range(kind, rows - 1, 2):
-        other[i], other[i + 1] = i + 1, i
-    return list(enumerate(other))
+def slots_order(rows):
+    return sorted(range(rows), key=lambda bits: (bits.bit_count(), bits))
 
 
 def pack_kernel(emb_ref, cid_ref, block_ref):
@@ -220,17 +204,16 @@
     add_rest(weights_ref[...], rest_ref[...], refs[:subs], refs[subs:])
 
 
-def gram_kernel(table, subs, *refs):
+def gram_kernel(order, subs, *refs):
     *member_refs, gram_ref, held = refs
     z, x = lax.axis_index("rows"), lax.axis_index("sub")
     owners, groups, packed, half = held.shape
     each = len(member_refs) // subs
     for t in range(subs):
         column = member_refs[t * each : (t + 1) * each]
-        for k, line in enumerate(table):
-            source = sum(jnp.where(z == i, at, 0) for i, (_, _, at) in enumerate(line))
-            row = source * subs + (x - t + subs) % subs
-            if k < len(table) - 1:
+        for k, bits in enumerate(order):
+            row = (z ^ bits) * subs + (x - t + subs) % subs
+            if k < len(order) - 1:
                 held[row] = column[k][...]
             else:
                 held[row, :, :, :PREFIX] = column[k][...]
@@ -324,8 +307,7 @@
     groups = per // SUBLANES
     packed = MOST * SUBLANES
     slots = owners * MOST
-    table = arrivals(rows)
-    z = lax.axis_index("rows")
+    order = slots_order(rows)
     shape = jax.ShapeDtypeStruct
 
     def across(values):
@@ -337,42 +319,22 @@
     def near(value):
         return lax.ppermute(value, "dim", [(0, 1), (1, 0)])
 
-    def needed(step, kind):
-        return any((step, kind) in [entry[:2] for entry in line] for line in table)
-
-    def swap(step, held, cut=lambda value: value):
-        return {
-            kind: lax.ppermute(cut(held[1 - kind]), "rows", pairs_of(rows, kind))
-            for kind in (1, 0)
-            if needed(step, kind)
-        }
-
-    def lead_of(block):
-        return block[:, :PREFIX]
-
-    def rest_of(block):
-        return block[:docs, PREFIX:]
-
-    def slot_block(k, history, cut=lambda value: value):
-        def part(step, kind):
-            block = history[step][kind]
-            return block if step == rows - 1 else cut(block)
-
-        kinds = {}
-        for i, (step, kind, _) in enumerate(table[k]):
-            kinds.setdefault((step, kind), []).append(i)
-        (step, kind), *others = sorted(kinds, key=lambda key: (-len(kinds[key]), key))
-        value = part(step, kind)
-        for step, kind in others:
-            here = functools.reduce(jnp.logical_or, [z == i for i in kinds[step, kind]])
-            value = jnp.where(here, part(step, kind), value)
-        return value
+    def swap(value, bit):
+        return lax.ppermute(value, "rows", [(i, i ^ bit) for i in range(rows)])
 
     (block,) = call(
         pack_kernel, "pack", [shape((docs + META, half), BF16)], [embeddings, cluster_id.reshape(1, docs)]
     )
-    history = {0: {0: block, 1: block}}
-    coming = swap(1, history[0])
+    blocks = {0: block}
+
+    def send(bits):
+        bit = (bits & -bits or rows) // 2
+        while bit:
+            if bits | bit != rows - 1:
+                blocks[bits | bit] = swap(blocks[bits], bit)
+            bit //= 2
+
+    send(0)
 
     inv, centre, own_prefix, prior, cent_prefix = call(
         functools.partial(prep_kernel, subs, per),
@@ -406,21 +368,17 @@
     found = select(block, own_cost)
     members.append(across(found))
     sums = add(block, prefix, [], own_cost)
-    for step in range(1, rows - 1):
-        history[step] = tied(coming, found, sums, members[: step - 1])
-        if step == rows - 2:
-            coming = swap(step + 1, history[step], lead_of)
-            coming_rest = swap(step + 1, history[step], rest_of)
-        else:
-            coming = swap(step + 1, history[step])
-        block = slot_block(step, history)
+    for k, bits in enumerate(order[1:-1], 1):
+        block = blocks[bits] = tied(blocks[bits], found, sums, members[: k - 1])
+        send(bits)
+        if bits == rows - 2:
+            coming, coming_rest = swap(block[:, :PREFIX], 1), swap(block[:docs, PREFIX:], 1)
         prefix = near(block[:docs, :PREFIX])
         found = select(block, other_cost)
         members.append(across(found))
         sums = add(block, prefix, sums, other_cost)
 
-    history[rows - 1] = tied(coming, found, sums, members)
-    lead = slot_block(rows - 1, history, lead_of)
+    lead = tied(coming, found, sums, members)
     prefix = near(lead[:docs])
     half_rows = [shape((groups, packed, PREFIX), BF16)] * subs
     pick, *lead_found = call(
@@ -440,8 +398,7 @@
         cost=other_cost,
     )
     lead_sums = across(lead_sums)
-    history[rows - 1] = tied(coming_rest, prefix)
-    rest = slot_block(rows - 1, history, rest_of)
+    rest = tied(coming_rest, prefix)
     half_rows = [shape((groups, packed, half - PREFIX), BF16)] * subs
     found = call(select_rest_kernel, "select_rest", half_rows, [pick, rest, centre], cost=other_cost)
     members.append(across(found))
@@ -455,7 +412,7 @@
     rest_sums = across(rest_sums)
 
     (gram,) = call(
-        functools.partial(gram_kernel, table, subs),
+        functools.partial(gram_kernel, order, subs),
         "gram",
         [shape((groups, slots, slots * SUBLANES), F32)],
         [arrays[t] for t in range(subs) for arrays in members],

time: 67.6 us -> 66.2 us (0.979)
  waiting for transfers between devices: 21.8 us -> 31.6 us
  starting transfers between devices: 23 us -> 17.6 us
  other arithmetic: 3.08 us -> 0 us
  local copies, waits for them, and re-layouts: 6.7 us -> 4.1 us
    ppermute x6 -> x4, waiting for transfers between devices: 5.97 us -> 16 us  [swap(): return lax.ppermute(value, 'rows', [(i, i ^ bit) for i in range(rows)])]
    ppermute x6 -> x4, starting transfers between devices: 14.4 us -> 7.75 us  [swap(): return lax.ppermute(value, 'rows', [(i, i ^ bit) for i in range(rows)])]
    select_n x3 -> x0, other arithmetic: 3.08 us -> none  [slot_block(): value = jnp.where(here, part(step, kind), value)]
    slice x2, local copies, waits for them, and re-layouts: 1.94 us -> 0.05 us  [the longest x1 0.04 us: shards(): block[:docs, PREFIX:]]
    ppermute x7, starting transfers between devices: 8.29 us -> 9.47 us  [across(): lax.ppermute(values[t], 'sub', [(i, (i + t) % subs) for i in range(subs)])]
    slice x3 -> x2, local copies, waits for them, and re-layouts: 0.76 us -> 0.04 us  [shards(): prefix = near(block[:docs, :PREFIX])]
  transfers between devices with their start and end apart: 18 -> 16, of which waited for: 6 -> 6; matrix products, arithmetic and copies ran while one was open for 9% -> 0% of each run, Pallas kernels for 15% -> 16%
where the time goes in v5:
time: 66.2 us; the launch traced here: 65.9 us
  waiting for transfers between devices  31.6 us (48%)
  starting transfers between devices  17.6 us (27%)
  Pallas kernels  11.8 us (18%)
  local copies, waits for them, and re-layouts  4.1 us (6%)
  between operations  0.84 us (1%)
    ppermute x4, waiting for transfers between devices, swap(): return lax.ppermute(value, 'rows', [(i, i ^ bit) for i in range(rows)])  16 us
    ppermute x7, waiting for transfers between devices, across(): lax.ppermute(values[t], 'sub', [(i, (i + t) % subs) for i in range(subs)])  15.6 us
    pallas_call x14, Pallas kernels, call(): pl.pallas_call(kernel, out_shape=tuple(out_shape), in_specs=[place(at) fo...  11.8 us
    ppermute x7, starting transfers between devices, across(): lax.ppermute(values[t], 'sub', [(i, (i + t) % subs) for i in range(subs)])  9.47 us
    ppermute x4, starting transfers between devices, swap(): return lax.ppermute(value, 'rows', [(i, i ^ bit) for i in range(rows)])  7.75 us
    unnamed x8, local copies, waits for them, and re-layouts  3.99 us
  transfers between devices with their start and end apart: 16, of which 6 were waited for; matrix products, arithmetic and copies ran while one was open for 0% of the time, Pallas kernels for 16%

profile of v5, /device:TPU:0, one launch (start us, length us, event | category | flops | bytes accessed | tf_op | source)
XLA Modules:
  0.0 65.9 jit_solution(13026749184832687529)
XLA Ops:
  0.6 1.0 %copy-done.1 = bf16[512,512]{1,0:T(8,128)(2,1)S(1)} copy-done((bf16[512,512]{1,0:T(8,128)(2,1)S(1)}, bf16[512,512]{1,0:T(8,128)(2,1)}, u32[]{:S(2)}) %copy-start.1) | copy-done | bytes 524312
  1.7 0.7 %copy-done.3 = s32[512,1]{0,1:T(1,128)S(1)} copy-done((s32[512,1]{0,1:T(1,128)S(1)}, s32[512,1]{0,1:T(1,128)}, u32[]{:S(2)}) %copy-start.3) | copy-done | bytes 2072
  2.4 3.1 %collective-permute-start = (bf16[528,512]{1,0:T(8,128)(2,1)S(1)}, bf16[528,512]{1,0:T(8,128)(2,1)S(1)}, u32[]{:S(2)}, u32[]{:S(2)}) collective-permute-start(bf16[528,512]{1,0:T(8,128)(2,1)S(1)} %pack.1.block_ref), channel_id=1, source_target_pairs={{0,4},{4,0},{8,12},{12,8},{1,5},{5,1},{9,13},{13,9},{2,6},{6,2},{1... | collective-permute-start | bytes 1622024 | tf_op jit(solution)/shard_map/ppermute | solution.py:323
  5.5 2.6 %collective-permute-start.2 = (bf16[528,512]{1,0:T(8,128)(2,1)S(1)}, bf16[528,512]{1,0:T(8,128)(2,1)S(1)}, u32[]{:S(2)}, u32[]{:S(2)}) collective-permute-start(bf16[528,512]{1,0:T(8,128)(2,1)S(1)} %pack.1.block_ref), channel_id=1, source_target_pairs={{0,8},{4,12},{8,0},{12,4},{1,9},{5,13},{9,1},{13,5},{2,10},{6,14},... | collective-permute-start | bytes 1622024 | tf_op jit(solution)/shard_map/ppermute | solution.py:323
  8.1 0.1 collective-permute-start.1
  8.2 0.0 copy-start
  8.2 1.6 %copy-done = bf16[1024,1024]{1,0:T(8,128)(2,1)S(1)} copy-done((bf16[1024,1024]{1,0:T(8,128)(2,1)S(1)}, bf16[1024,1024]{1,0:T(8,128)(2,1)}, u32[]{:S(2)}) %copy-start) | copy-done | bytes 2097176
  9.8 0.7 %copy-done.2 = s32[1024]{0:T(1024)S(1)} copy-done((s32[1024]{0:T(1024)S(1)}, s32[1024]{0:T(1024)}, u32[]{:S(2)}) %copy-start.2) | copy-done | bytes 4120
  10.5 0.8 %prep.1 = (f32[256,1]{1,0:T(8,128)S(1)}, bf16[256,512]{1,0:T(8,128)(2,1)S(1)}, bf16[256,256]{1,0:T(8,128)(2,1)S(1)}, bf16[128,512]{1,0:T(8,128)(2,1)S(1)}, bf16[1024,256]{1,0:T(8,128)(2,1)S(1)}) custom-call(s32[1,1024]{1,0:T(1,128)S(1)} %bitcast.3, bf16[1024,1024]{1,0:T(8,128)(2,1)S(1)} %copy-done), custom_call_target="tpu_custom_call" | custom-call | flops 209715200 | bytes 4194304 | tf_op jit(solution)/shard_map/prep/pallas_call | solution.py:32
  11.3 0.7 %select.3 = (bf16[16,16,512]{2,1,0:T(8,128)(2,1)S(1)}, bf16[16,16,512]{2,1,0:T(8,128)(2,1)S(1)}) custom-call(bf16[528,512]{1,0:T(8,128)(2,1)S(1)} %pack.1.block_ref, f32[256,1]{1,0:T(8,128)S(1)} %get-tuple-element.41.inv_ref, bf16[256,512]{1,0:T(8,128)(2,1)S(1)} %get-tuple-element.42.centre_ref), custom_call_target="tpu_custom_call" | custom-call | flops 104857600 | bytes 2097152 | tf_op jit(solution)/shard_map/select/pallas_call | solution.py:32
  12.0 0.0 collective-permute-done.1.near_ref
  12.1 1.3 %sums.3 = (f32[136,256]{1,0:T(8,128)S(1)}, f32[136,256]{1,0:T(8,128)S(1)}, f32[128,256]{1,0:T(8,128)S(1)}, f32[128,256]{1,0:T(8,128)S(1)}) custom-call(bf16[528,512]{1,0:T(8,128)(2,1)S(1)} %pack.1.block_ref, bf16[512,256]{1,0:T(8,128)(2,1)S(1)} %collective-permute-done.1.near_ref, bf16[1024,256]{1,0:T(8,128)(2,1)S(1)} %get-tuple-element.45.cent_ref, ...), custom_call_target="tpu_custom_call" | custom-call | flops 104857600 | bytes 2097152 | tf_op jit(solution)/shard_map/sums/pallas_call | solution.py:32
  13.4 15.9 %collective-permute-done.block_ref = bf16[528,512]{1,0:T(8,128)(2,1)S(1)} collective-permute-done((bf16[528,512]{1,0:T(8,128)(2,1)S(1)}, bf16[528,512]{1,0:T(8,128)(2,1)S(1)}, u32[]{:S(2)}, u32[]{:S(2)}) %collective-permute-start) | collective-permute-done | bytes 540704 | tf_op jit(solution)/shard_map/ppermute | solution.py:323
  29.3 0.1 collective-permute-start.3
  29.3 1.7 %collective-permute-start.4 = (bf16[16,16,512]{2,1,0:T(8,128)(2,1)S(1)}, bf16[16,16,512]{2,1,0:T(8,128)(2,1)S(1)}, u32[]{:S(2)}, u32[]{:S(2)}) collective-permute-start(bf16[16,16,512]{2,1,0:T(8,128)(2,1)S(1)} %get-tuple-element.44), channel_id=1, source_target_pairs={{0,2},{2,0},{1,3},{3,1},{4,6},{6,4},{5,7},{7,5},{8,10},{10,8},{9,1... | collective-permute-start | bytes 786440 | tf_op jit(solution)/shard_map/ppermute | solution.py:316
  31.1 0.7 %select.4 = (bf16[16,16,512]{2,1,0:T(8,128)(2,1)S(1)}, bf16[16,16,512]{2,1,0:T(8,128)(2,1)S(1)}) custom-call(bf16[528,512]{1,0:T(8,128)(2,1)S(1)} %collective-permute-done.block_ref, f32[256,1]{1,0:T(8,128)S(1)} %get-tuple-element.41.inv_ref, bf16[256,512]{1,0:T(8,128)(2,1)S(1)} %get-tuple-element.42.centre_ref), custom_call_target="tpu_custom_call" | custom-call | flops 6553600 | bytes 131072 | tf_op jit(solution)/shard_map/select/pallas_call | solution.py:32
  31.8 0.4 collective-permute-start.7
  32.2 0.0 collective-permute-done.3.near_ref
  32.2 1.3 %sums.4 = (f32[136,256]{1,0:T(8,128)S(1)}, f32[136,256]{1,0:T(8,128)S(1)}, f32[128,256]{1,0:T(8,128)S(1)}, f32[128,256]{1,0:T(8,128)S(1)}) custom-call(bf16[528,512]{1,0:T(8,128)(2,1)S(1)} %collective-permute-done.block_ref, ...), custom_call_target="tpu_custom_call", output_to_operand_aliasing={{0}: (4, {}), {1}: (5, {}), {2}: (6, {}), {3}: (7, {})} | custom-call | flops 6553600 | bytes 131072 | tf_op jit(solution)/shard_map/sums/pallas_call | solution.py:32
  33.6 4.9 %collective-permute-done.4.refs_5_ = bf16[16,16,512]{2,1,0:T(8,128)(2,1)S(1)} collective-permute-done((bf16[16,16,512]{2,1,0:T(8,128)(2,1)S(1)}, bf16[16,16,512]{2,1,0:T(8,128)(2,1)S(1)}, u32[]{:S(2)}, u32[]{:S(2)}) %collective-permute-start.4) | collective-permute-done | bytes 262176 | tf_op jit(solution)/shard_map/ppermute | solution.py:316
  38.5 0.0 collective-permute-done.2.block_ref
  38.5 0.1 collective-permute-start.5
  38.7 0.1 collective-permute-start.6
  38.7 0.7 %select.5 = (bf16[16,16,512]{2,1,0:T(8,128)(2,1)S(1)}, bf16[16,16,512]{2,1,0:T(8,128)(2,1)S(1)}) custom-call(bf16[528,512]{1,0:T(8,128)(2,1)S(1)} %collective-permute-done.2.block_ref, f32[256,1]{1,0:T(8,128)S(1)} %get-tuple-element.41.inv_ref, bf16[256,512]{1,0:T(8,128)(2,1)S(1)} %get-tuple-element.42.centre_ref), custom_call_target="tpu_custom_call" | custom-call | flops 6553600 | bytes 131072 | tf_op jit(solution)/shard_map/select/pallas_call | solution.py:32
  39.5 1.7 %collective-permute-start.8 = (bf16[16,16,512]{2,1,0:T(8,128)(2,1)S(1)}, bf16[16,16,512]{2,1,0:T(8,128)(2,1)S(1)}, u32[]{:S(2)}, u32[]{:S(2)}) collective-permute-start(bf16[16,16,512]{2,1,0:T(8,128)(2,1)S(1)} %get-tuple-element.60), channel_id=1, source_target_pairs={{0,2},{2,0},{1,3},{3,1},{4,6},{6,4},{5,7},{7,5},{8,10},{10,8},{9,1... | collective-permute-start | bytes 786440 | tf_op jit(solution)/shard_map/ppermute | solution.py:316
  41.2 2.0 %collective-permute-start.9 = (bf16[512,256]{1,0:T(8,128)(2,1)S(1)}, bf16[512,256]{1,0:T(8,128)(2,1)S(1)}, u32[]{:S(2)}, u32[]{:S(2)}) collective-permute-start(bf16[512,256]{1,0:T(8,128)(2,1)S(1)} %get-tuple-element.80), channel_id=1, source_target_pairs={{0,4},{4,0},{8,12},{12,8},{1,5},{5,1},{9,13},{13,9},{2,6},{6,2},{1... | collective-permute-start | bytes 786440 | tf_op jit(solution)/shard_map/ppermute | solution.py:323
  43.2 0.0 collective-permute-done.6.near_ref
  43.2 1.3 %sums.5 = (f32[136,256]{1,0:T(8,128)S(1)}, f32[136,256]{1,0:T(8,128)S(1)}, f32[128,256]{1,0:T(8,128)S(1)}, f32[128,256]{1,0:T(8,128)S(1)}) custom-call(bf16[528,512]{1,0:T(8,128)(2,1)S(1)} %collective-permute-done.2.block_ref, ...), custom_call_target="tpu_custom_call", output_to_operand_aliasing={{0}: (4, {}), {1}: (5, {}), {2}: (6, {}), {3}: (7, {})} | custom-call | flops 6553600 | bytes 131072 | tf_op jit(solution)/shard_map/sums/pallas_call | solution.py:32
  44.5 0.0 collective-permute-done.7.refs_6_
  44.6 4.7 %collective-permute-done.8.refs_7_ = bf16[16,16,512]{2,1,0:T(8,128)(2,1)S(1)} collective-permute-done((bf16[16,16,512]{2,1,0:T(8,128)(2,1)S(1)}, bf16[16,16,512]{2,1,0:T(8,128)(2,1)S(1)}, u32[]{:S(2)}, u32[]{:S(2)}) %collective-permute-start.8) | collective-permute-done | bytes 262176 | tf_op jit(solution)/shard_map/ppermute | solution.py:316
  49.3 0.1 collective-permute-start.10
  49.4 0.6 select_lead.1
  50.0 1.7 %collective-permute-start.11 = (bf16[16,16,256]{2,1,0:T(8,128)(2,1)S(1)}, bf16[16,16,256]{2,1,0:T(8,128)(2,1)S(1)}, u32[]{:S(2)}, u32[]{:S(2)}) collective-permute-start(bf16[16,16,256]{2,1,0:T(8,128)(2,1)S(1)} %get-tuple-element.70), channel_id=1, source_target_pairs={{0,2},{2,0},{1,3},{3,1},{4,6},{6,4},{5,7},{7,5},{8,10},{10,8},{9,1... | collective-permute-start | bytes 393224 | tf_op jit(solution)/shard_map/ppermute | solution.py:316
  51.7 0.1 collective-permute-done.9.rest_ref
  51.8 0.0 collective-permute-done.10.near_ref
  51.8 0.3 select_rest.1
  52.1 1.7 %collective-permute-start.12 = (bf16[16,16,256]{2,1,0:T(8,128)(2,1)S(1)}, bf16[16,16,256]{2,1,0:T(8,128)(2,1)S(1)}, u32[]{:S(2)}, u32[]{:S(2)}) collective-permute-start(bf16[16,16,256]{2,1,0:T(8,128)(2,1)S(1)} %get-tuple-element.71), channel_id=1, source_target_pairs={{0,2},{2,0},{1,3},{3,1},{4,6},{6,4},{5,7},{7,5},{8,10},{10,8},{9,1... | collective-permute-start | bytes 393224 | tf_op jit(solution)/shard_map/ppermute | solution.py:316
  53.9 1.4 %sums_lead.1 = (bf16[256,512]{1,0:T(8,128)(2,1)S(1)}, f32[136,256]{1,0:T(8,128)S(1)}, f32[136,256]{1,0:T(8,128)S(1)}) custom-call(bf16[528,256]{1,0:T(8,128)(2,1)S(1)} %collective-permute-done.5.lead_ref, bf16[512,256]{1,0:T(8,128)(2,1)S(1)} %collective-permute-done.10.near_ref, ...), custom_call_target="tpu_custom_call", output_to_operand_aliasing={{1}: (4, {}), {2}: (5, {})} | custom-call | flops 6553600 | bytes 131072 | tf_op jit(solution)/shard_map/sums_lead/pallas_call | solution.py:32
  55.2 0.4 collective-permute-start.14
  55.7 0.2 sums_rest.1
  55.9 1.7 %collective-permute-start.15 = (f32[128,256]{1,0:T(8,128)S(1)}, f32[128,256]{1,0:T(8,128)S(1)}, u32[]{:S(2)}, u32[]{:S(2)}) collective-permute-start(f32[128,256]{1,0:T(8,128)S(1)} %get-tuple-element.76), channel_id=1, source_target_pairs={{0,2},{2,0},{1,3},{3,1},{4,6},{6,4},{5,7},{7,5},{8,10},{10,8},{9,1... | collective-permute-start | bytes 393224 | tf_op jit(solution)/shard_map/ppermute | solution.py:316
  57.6 0.0 collective-permute-done.11.refs_8_
  57.6 1.5 %collective-permute-done.12.refs_9_ = bf16[16,16,256]{2,1,0:T(8,128)(2,1)S(1)} collective-permute-done((bf16[16,16,256]{2,1,0:T(8,128)(2,1)S(1)}, bf16[16,16,256]{2,1,0:T(8,128)(2,1)S(1)}, u32[]{:S(2)}, u32[]{:S(2)}) %collective-permute-start.12) | collective-permute-done | bytes 131104 | tf_op jit(solution)/shard_map/ppermute | solution.py:316
  59.2 0.9 %gram.1.mine_ref = f32[16,16,128]{2,1,0:T(8,128)S(1)} custom-call(bf16[16,16,512]{2,1,0:T(8,128)(2,1)S(1)} %get-tuple-element.43.refs_0_, bf16[16,16,512]{2,1,0:T(8,128)(2,1)S(1)} %get-tuple-element.52.refs_1_, bf16[16,16,512]{2,1,0:T(8,128)(2,1)S(1)} %get-tuple-element.59.refs_2_, bf16[16,16,256]{2,1,0:T(8,128)(2,1)S(1)} %get-tuple-element.66.refs_3_, ...), custom_call_target="tpu_custom_call" | custom-call | tf_op jit(solution)/shard_map/gram/pallas_call | solution.py:32
  60.0 0.1 collective-permute-start.13
  60.1 4.4 %collective-permute-done.15.refs_3_ = f32[128,256]{1,0:T(8,128)S(1)} collective-permute-done((f32[128,256]{1,0:T(8,128)S(1)}, f32[128,256]{1,0:T(8,128)S(1)}, u32[]{:S(2)}, u32[]{:S(2)}) %collective-permute-start.15) | collective-permute-done | bytes 131104 | tf_op jit(solution)/shard_map/ppermute | solution.py:316
  64.6 0.0 collective-permute-done.13.other_ref
  64.6 1.4 %finish.1 = (f32[128,512]{1,0:T(8,128)}, bf16[8,16,128]{2,1,0:T(8,128)(2,1)}) custom-call(f32[16,16,128]{2,1,0:T(8,128)S(1)} %gram.1.mine_ref, f32[16,16,128]{2,1,0:T(8,128)S(1)} %collective-permute-done.13.other_ref, f32[136,256]{1,0:T(8,128)S(1)} %get-tuple-element.72.refs_0_, f32[136,256]{1,0:T(8,128)S(1)} %collective-permute-done.14.refs_1_, ...), custom_call_target="tpu_custom_call" | custom-call | tf_op jit(solution)/shard_map/finish/pallas_call | solution.py:32
  (11 shorter events, 0.2 us)
Async XLA Ops:
  0.6 1.0 %copy-start.1 = (bf16[512,512]{1,0:T(8,128)(2,1)S(1)}, bf16[512,512]{1,0:T(8,128)(2,1)}, u32[]{:S(2)}) copy-start(bf16[512,512]{1,0:T(8,128)(2,1)} %emb_ref.1) | copy-start | bytes 1572868
  1.7 0.7 %copy-start.3 = (s32[512,1]{0,1:T(1,128)S(1)}, s32[512,1]{0,1:T(1,128)}, u32[]{:S(2)}) copy-start(s32[512,1]{0,1:T(1,128)} %param.6) | copy-start | bytes 6148
  2.4 26.8 %collective-permute-start = (bf16[528,512]{1,0:T(8,128)(2,1)S(1)}, bf16[528,512]{1,0:T(8,128)(2,1)S(1)}, u32[]{:S(2)}, u32[]{:S(2)}) collective-permute-start(bf16[528,512]{1,0:T(8,128)(2,1)S(1)} %pack.1.block_ref), channel_id=1, source_target_pairs={{0,4},{4,0},{8,12},{12,8},{1,5},{5,1},{9,13},{13,9},{2,6},{6,2},{1... | collective-permute-start | bytes 1622024 | tf_op jit(solution)/shard_map/ppermute | solution.py:323
  5.5 33.0 %collective-permute-start.2 = (bf16[528,512]{1,0:T(8,128)(2,1)S(1)}, bf16[528,512]{1,0:T(8,128)(2,1)S(1)}, u32[]{:S(2)}, u32[]{:S(2)}) collective-permute-start(bf16[528,512]{1,0:T(8,128)(2,1)S(1)} %pack.1.block_ref), channel_id=1, source_target_pairs={{0,8},{4,12},{8,0},{12,4},{1,9},{5,13},{9,1},{13,5},{2,10},{6,14},... | collective-permute-start | bytes 1622024 | tf_op jit(solution)/shard_map/ppermute | solution.py:323
  8.1 3.9 %collective-permute-start.1 = (bf16[512,256]{1,0:T(8,128)(2,1)S(1)}, bf16[512,256]{1,0:T(8,128)(2,1)S(1)}, u32[]{:S(2)}, u32[]{:S(2)}) collective-permute-start(bf16[512,256]{1,0:T(8,128)(2,1)S(1)} %slice.24), channel_id=1, source_target_pairs={{0,1},{1,0},{2,3},{3,2},{4,5},{5,4},{6,7},{7,6},{8,9},{9,8},{10,11... | collective-permute-start | bytes 786440 | tf_op jit(solution)/shard_map/ppermute | solution.py:320
  8.2 1.6 %copy-start = (bf16[1024,1024]{1,0:T(8,128)(2,1)S(1)}, bf16[1024,1024]{1,0:T(8,128)(2,1)}, u32[]{:S(2)}) copy-start(bf16[1024,1024]{1,0:T(8,128)(2,1)} %cent_ref.1) | copy-start | bytes 6291460
  9.8 0.7 %copy-start.2 = (s32[1024]{0:T(1024)S(1)}, s32[1024]{0:T(1024)}, u32[]{:S(2)}) copy-start(s32[1024]{0:T(1024)} %param.7) | copy-start | bytes 12292
  29.3 3.0 %collective-permute-start.3 = (bf16[512,256]{1,0:T(8,128)(2,1)S(1)}, bf16[512,256]{1,0:T(8,128)(2,1)S(1)}, u32[]{:S(2)}, u32[]{:S(2)}) collective-permute-start(bf16[512,256]{1,0:T(8,128)(2,1)S(1)} %slice.19), channel_id=1, source_target_pairs={{0,1},{1,0},{2,3},{3,2},{4,5},{5,4},{6,7},{7,6},{8,9},{9,8},{10,11... | collective-permute-start | bytes 786440 | tf_op jit(solution)/shard_map/ppermute | solution.py:320
  29.3 9.2 %collective-permute-start.4 = (bf16[16,16,512]{2,1,0:T(8,128)(2,1)S(1)}, bf16[16,16,512]{2,1,0:T(8,128)(2,1)S(1)}, u32[]{:S(2)}, u32[]{:S(2)}) collective-permute-start(bf16[16,16,512]{2,1,0:T(8,128)(2,1)S(1)} %get-tuple-element.44), channel_id=1, source_target_pairs={{0,2},{2,0},{1,3},{3,1},{4,6},{6,4},{5,7},{7,5},{8,10},{10,8},{9,1... | collective-permute-start | bytes 786440 | tf_op jit(solution)/shard_map/ppermute | solution.py:316
  31.8 12.8 %collective-permute-start.7 = (bf16[16,16,512]{2,1,0:T(8,128)(2,1)S(1)}, bf16[16,16,512]{2,1,0:T(8,128)(2,1)S(1)}, u32[]{:S(2)}, u32[]{:S(2)}) collective-permute-start(bf16[16,16,512]{2,1,0:T(8,128)(2,1)S(1)} %get-tuple-element.53), channel_id=1, source_target_pairs={{0,2},{2,0},{1,3},{3,1},{4,6},{6,4},{5,7},{7,5},{8,10},{10,8},{9,1... | collective-permute-start | bytes 786440 | tf_op jit(solution)/shard_map/ppermute | solution.py:316
  38.5 10.8 %collective-permute-start.5 = (bf16[528,256]{1,0:T(8,128)(2,1)S(1)}, bf16[528,256]{1,0:T(8,128)(2,1)S(1)}, u32[]{:S(2)}, u32[]{:S(2)}) collective-permute-start(bf16[528,256]{1,0:T(8,128)(2,1)S(1)} %slice.20), channel_id=1, source_target_pairs={{0,4},{4,0},{8,12},{12,8},{1,5},{5,1},{9,13},{13,9},{2,6},{6,2},{1... | collective-permute-start | bytes 811016 | tf_op jit(solution)/shard_map/ppermute | solution.py:323
  38.7 4.5 %collective-permute-start.6 = (bf16[512,256]{1,0:T(8,128)(2,1)S(1)}, bf16[512,256]{1,0:T(8,128)(2,1)S(1)}, u32[]{:S(2)}, u32[]{:S(2)}) collective-permute-start(bf16[512,256]{1,0:T(8,128)(2,1)S(1)} %get-tuple-element.81), channel_id=1, source_target_pairs={{0,1},{1,0},{2,3},{3,2},{4,5},{5,4},{6,7},{7,6},{8,9},{9,8},{10,11... | collective-permute-start | bytes 786440 | tf_op jit(solution)/shard_map/ppermute | solution.py:320
  39.5 9.8 %collective-permute-start.8 = (bf16[16,16,512]{2,1,0:T(8,128)(2,1)S(1)}, bf16[16,16,512]{2,1,0:T(8,128)(2,1)S(1)}, u32[]{:S(2)}, u32[]{:S(2)}) collective-permute-start(bf16[16,16,512]{2,1,0:T(8,128)(2,1)S(1)} %get-tuple-element.60), channel_id=1, source_target_pairs={{0,2},{2,0},{1,3},{3,1},{4,6},{6,4},{5,7},{7,5},{8,10},{10,8},{9,1... | collective-permute-start | bytes 786440 | tf_op jit(solution)/shard_map/ppermute | solution.py:316
  41.2 10.6 %collective-permute-start.9 = (bf16[512,256]{1,0:T(8,128)(2,1)S(1)}, bf16[512,256]{1,0:T(8,128)(2,1)S(1)}, u32[]{:S(2)}, u32[]{:S(2)}) collective-permute-start(bf16[512,256]{1,0:T(8,128)(2,1)S(1)} %get-tuple-element.80), channel_id=1, source_target_pairs={{0,4},{4,0},{8,12},{12,8},{1,5},{5,1},{9,13},{13,9},{2,6},{6,2},{1... | collective-permute-start | bytes 786440 | tf_op jit(solution)/shard_map/ppermute | solution.py:323
  49.3 2.5 %collective-permute-start.10 = (bf16[512,256]{1,0:T(8,128)(2,1)S(1)}, bf16[512,256]{1,0:T(8,128)(2,1)S(1)}, u32[]{:S(2)}, u32[]{:S(2)}) collective-permute-start(bf16[512,256]{1,0:T(8,128)(2,1)S(1)} %slice.23), channel_id=1, source_target_pairs={{0,1},{1,0},{2,3},{3,2},{4,5},{5,4},{6,7},{7,6},{8,9},{9,8},{10,11... | collective-permute-start | bytes 786440 | tf_op jit(solution)/shard_map/ppermute | solution.py:320
  50.0 7.6 %collective-permute-start.11 = (bf16[16,16,256]{2,1,0:T(8,128)(2,1)S(1)}, bf16[16,16,256]{2,1,0:T(8,128)(2,1)S(1)}, u32[]{:S(2)}, u32[]{:S(2)}) collective-permute-start(bf16[16,16,256]{2,1,0:T(8,128)(2,1)S(1)} %get-tuple-element.70), channel_id=1, source_target_pairs={{0,2},{2,0},{1,3},{3,1},{4,6},{6,4},{5,7},{7,5},{8,10},{10,8},{9,1... | collective-permute-start | bytes 393224 | tf_op jit(solution)/shard_map/ppermute | solution.py:316
  52.1 7.0 %collective-permute-start.12 = (bf16[16,16,256]{2,1,0:T(8,128)(2,1)S(1)}, bf16[16,16,256]{2,1,0:T(8,128)(2,1)S(1)}, u32[]{:S(2)}, u32[]{:S(2)}) collective-permute-start(bf16[16,16,256]{2,1,0:T(8,128)(2,1)S(1)} %get-tuple-element.71), channel_id=1, source_target_pairs={{0,2},{2,0},{1,3},{3,1},{4,6},{6,4},{5,7},{7,5},{8,10},{10,8},{9,1... | collective-permute-start | bytes 393224 | tf_op jit(solution)/shard_map/ppermute | solution.py:316
  55.2 9.3 %collective-permute-start.14 = (f32[136,256]{1,0:T(8,128)S(1)}, f32[136,256]{1,0:T(8,128)S(1)}, u32[]{:S(2)}, u32[]{:S(2)}) collective-permute-start(f32[136,256]{1,0:T(8,128)S(1)} %get-tuple-element.73), channel_id=1, source_target_pairs={{0,2},{2,0},{1,3},{3,1},{4,6},{6,4},{5,7},{7,5},{8,10},{10,8},{9,1... | collective-permute-start | bytes 417800 | tf_op jit(solution)/shard_map/ppermute | solution.py:316
  55.9 8.6 %collective-permute-start.15 = (f32[128,256]{1,0:T(8,128)S(1)}, f32[128,256]{1,0:T(8,128)S(1)}, u32[]{:S(2)}, u32[]{:S(2)}) collective-permute-start(f32[128,256]{1,0:T(8,128)S(1)} %get-tuple-element.76), channel_id=1, source_target_pairs={{0,2},{2,0},{1,3},{3,1},{4,6},{6,4},{5,7},{7,5},{8,10},{10,8},{9,1... | collective-permute-start | bytes 393224 | tf_op jit(solution)/shard_map/ppermute | solution.py:316
  60.0 4.5 %collective-permute-start.13 = (f32[16,16,128]{2,1,0:T(8,128)S(1)}, f32[16,16,128]{2,1,0:T(8,128)S(1)}, u32[]{:S(2)}, u32[]{:S(2)}) collective-permute-start(f32[16,16,128]{2,1,0:T(8,128)S(1)} %gram.1.mine_ref), channel_id=1, source_target_pairs={{0,1},{1,0},{2,3},{3,2},{4,5},{5,4},{6,7},{7,6},{8,9},{9,8},{10,11... | collective-permute-start | bytes 393224 | tf_op jit(solution)/shard_map/ppermute | solution.py:320

commit v6 on v5

--- a/solution.py
+++ b/solution.py
@@ -150,7 +150,7 @@
 def soft_weights(lead_ref, near_ref, cent_ref, own_prefix_ref):
     docs = lead_ref.shape[0] - META
     h = lax.axis_index("dim")
-    prefix = jnp.where(h == 0, lead_ref[:docs, :PREFIX], near_ref[...])
+    prefix = jnp.where(h == 0, lead_ref[:docs, :PREFIX], near_ref[:docs, :PREFIX])
     scores = dot_nt(cent_ref[...], prefix) * TEMP
     top = jnp.max(scores, axis=0, keepdims=True)
     scale = 1.0 / jnp.sum(jnp.exp(scores - top), axis=0, keepdims=True)
@@ -364,22 +364,26 @@
         return list(call(functools.partial(sums_kernel, subs), "sums", sum_shapes, operands, aliases, cost=cost))
 
     members = []
-    prefix = near(block[:docs, :PREFIX])
+    prefix = near(block)
     found = select(block, own_cost)
     members.append(across(found))
     sums = add(block, prefix, [], own_cost)
-    for k, bits in enumerate(order[1:-1], 1):
-        block = blocks[bits] = tied(blocks[bits], found, sums, members[: k - 1])
-        send(bits)
-        if bits == rows - 2:
-            coming, coming_rest = swap(block[:, :PREFIX], 1), swap(block[:docs, PREFIX:], 1)
-        prefix = near(block[:docs, :PREFIX])
-        found = select(block, other_cost)
-        members.append(across(found))
-        sums = add(block, prefix, sums, other_cost)
-
-    lead = tied(coming, found, sums, members)
-    prefix = near(lead[:docs])
+    for depth in range(1, (rows - 1).bit_count()):
+        group = [bits for bits in order if bits.bit_count() == depth]
+        arrived = tied([blocks[bits] for bits in group], found, sums, members)
+        blocks.update(zip(group, arrived))
+        for bits in group:
+            send(bits)
+            if bits == rows - 2:
+                coming, coming_rest = swap(blocks[bits][:, :PREFIX], 1), swap(blocks[bits][:docs, PREFIX:], 1)
+        for bits in group:
+            prefix = near(blocks[bits])
+            found = select(blocks[bits], other_cost)
+            members.append(across(found))
+            sums = add(blocks[bits], prefix, sums, other_cost)
+
+    lead = tied(coming, found, sums, members[:-1])
+    prefix = near(lead)
     half_rows = [shape((groups, packed, PREFIX), BF16)] * subs
     pick, *lead_found = call(
         select_lead_kernel,
@@ -398,7 +402,7 @@
         cost=other_cost,
     )
     lead_sums = across(lead_sums)
-    rest = tied(coming_rest, prefix)
+    rest = tied(coming_rest, prefix, members[: rows - 1])
     half_rows = [shape((groups, packed, half - PREFIX), BF16)] * subs
     found = call(select_rest_kernel, "select_rest", half_rows, [pick, rest, centre], cost=other_cost)
     members.append(across(found))

time: 66.2 us -> 65 us (0.982)
  starting transfers between devices: 17.6 us -> 16.4 us
    ppermute x7, waiting for transfers between devices: 15.6 us -> 18.5 us  [across(): lax.ppermute(values[t], 'sub', [(i, (i + t) % subs) for i in range(subs)])]
    ppermute x4, waiting for transfers between devices: 16 us -> 13.2 us  [swap(): return lax.ppermute(value, 'rows', [(i, i ^ bit) for i in range(rows)])]
    ppermute x7, starting transfers between devices: 9.47 us -> 7.95 us  [across(): lax.ppermute(values[t], 'sub', [(i, (i + t) % subs) for i in range(subs)])]
    ppermute x5, starting transfers between devices: 0.36 us -> 1.1 us  [near(): return lax.ppermute(value, 'dim', [(0, 1), (1, 0)])]
  transfers between devices with their start and end apart: 16 -> 16, of which waited for: 6 -> 8; matrix products, arithmetic and copies ran while one was open for 0% -> 0% of each run, Pallas kernels for 16% -> 16%
where the time goes in v6:
time: 65 us; the launch traced here: 64.8 us
  waiting for transfers between devices  31.7 us (49%)
  starting transfers between devices  16.4 us (25%)
  Pallas kernels  11.8 us (18%)
  local copies, waits for them, and re-layouts  4.03 us (6%)
  between operations  0.77 us (1%)
    ppermute x7, waiting for transfers between devices, across(): lax.ppermute(values[t], 'sub', [(i, (i + t) % subs) for i in range(subs)])  18.5 us
    ppermute x4, waiting for transfers between devices, swap(): return lax.ppermute(value, 'rows', [(i, i ^ bit) for i in range(rows)])  13.2 us
    pallas_call x14, Pallas kernels, call(): pl.pallas_call(kernel, out_shape=tuple(out_shape), in_specs=[place(at) fo...  11.8 us
    ppermute x7, starting transfers between devices, across(): lax.ppermute(values[t], 'sub', [(i, (i + t) % subs) for i in range(subs)])  7.95 us
    ppermute x4, starting transfers between devices, swap(): return lax.ppermute(value, 'rows', [(i, i ^ bit) for i in range(rows)])  7.39 us
    unnamed x8, local copies, waits for them, and re-layouts  3.99 us
  transfers between devices with their start and end apart: 16, of which 8 were waited for; matrix products, arithmetic and copies ran while one was open for 0% of the time, Pallas kernels for 16%

profile of v6, /device:TPU:0, one launch (start us, length us, event | category | flops | bytes accessed | tf_op | source)
XLA Modules:
  0.0 64.8 jit_solution(9355158059211525683)
XLA Ops:
  0.6 1.0 %copy-done.1 = bf16[512,512]{1,0:T(8,128)(2,1)S(1)} copy-done((bf16[512,512]{1,0:T(8,128)(2,1)S(1)}, bf16[512,512]{1,0:T(8,128)(2,1)}, u32[]{:S(2)}) %copy-start.1) | copy-done | bytes 524312
  1.7 0.7 %copy-done.3 = s32[512,1]{0,1:T(1,128)S(1)} copy-done((s32[512,1]{0,1:T(1,128)S(1)}, s32[512,1]{0,1:T(1,128)}, u32[]{:S(2)}) %copy-start.3) | copy-done | bytes 2072
  2.4 0.5 collective-permute-start.2
  2.9 2.6 %collective-permute-start = (bf16[528,512]{1,0:T(8,128)(2,1)S(1)}, bf16[528,512]{1,0:T(8,128)(2,1)S(1)}, u32[]{:S(2)}, u32[]{:S(2)}) collective-permute-start(bf16[528,512]{1,0:T(8,128)(2,1)S(1)} %pack.1.block_ref), channel_id=1, source_target_pairs={{0,4},{4,0},{8,12},{12,8},{1,5},{5,1},{9,13},{13,9},{2,6},{6,2},{1... | collective-permute-start | bytes 1622024 | tf_op jit(solution)/shard_map/ppermute | solution.py:323
  5.6 2.6 %collective-permute-start.1 = (bf16[528,512]{1,0:T(8,128)(2,1)S(1)}, bf16[528,512]{1,0:T(8,128)(2,1)S(1)}, u32[]{:S(2)}, u32[]{:S(2)}) collective-permute-start(bf16[528,512]{1,0:T(8,128)(2,1)S(1)} %pack.1.block_ref), channel_id=1, source_target_pairs={{0,8},{4,12},{8,0},{12,4},{1,9},{5,13},{9,1},{13,5},{2,10},{6,14},... | collective-permute-start | bytes 1622024 | tf_op jit(solution)/shard_map/ppermute | solution.py:323
  8.2 1.6 %copy-done = bf16[1024,1024]{1,0:T(8,128)(2,1)S(1)} copy-done((bf16[1024,1024]{1,0:T(8,128)(2,1)S(1)}, bf16[1024,1024]{1,0:T(8,128)(2,1)}, u32[]{:S(2)}) %copy-start) | copy-done | bytes 2097176
  9.8 0.7 %copy-done.2 = s32[1024]{0:T(1024)S(1)} copy-done((s32[1024]{0:T(1024)S(1)}, s32[1024]{0:T(1024)}, u32[]{:S(2)}) %copy-start.2) | copy-done | bytes 4120
  10.4 0.8 %prep.1 = (f32[256,1]{1,0:T(8,128)S(1)}, bf16[256,512]{1,0:T(8,128)(2,1)S(1)}, bf16[256,256]{1,0:T(8,128)(2,1)S(1)}, bf16[128,512]{1,0:T(8,128)(2,1)S(1)}, bf16[1024,256]{1,0:T(8,128)(2,1)S(1)}) custom-call(s32[1,1024]{1,0:T(1,128)S(1)} %bitcast.3, bf16[1024,1024]{1,0:T(8,128)(2,1)S(1)} %copy-done), custom_call_target="tpu_custom_call" | custom-call | flops 209715200 | bytes 4194304 | tf_op jit(solution)/shard_map/prep/pallas_call | solution.py:32
  11.3 0.8 %select.3 = (bf16[16,16,512]{2,1,0:T(8,128)(2,1)S(1)}, bf16[16,16,512]{2,1,0:T(8,128)(2,1)S(1)}) custom-call(bf16[528,512]{1,0:T(8,128)(2,1)S(1)} %pack.1.block_ref, f32[256,1]{1,0:T(8,128)S(1)} %get-tuple-element.41.inv_ref, bf16[256,512]{1,0:T(8,128)(2,1)S(1)} %get-tuple-element.42.centre_ref), custom_call_target="tpu_custom_call" | custom-call | flops 104857600 | bytes 2097152 | tf_op jit(solution)/shard_map/select/pallas_call | solution.py:32
  12.0 1.5 %collective-permute-start.3 = (bf16[16,16,512]{2,1,0:T(8,128)(2,1)S(1)}, bf16[16,16,512]{2,1,0:T(8,128)(2,1)S(1)}, u32[]{:S(2)}, u32[]{:S(2)}) collective-permute-start(bf16[16,16,512]{2,1,0:T(8,128)(2,1)S(1)} %get-tuple-element.44), channel_id=1, source_target_pairs={{0,2},{2,0},{1,3},{3,1},{4,6},{6,4},{5,7},{7,5},{8,10},{10,8},{9,1... | collective-permute-start | bytes 786440 | tf_op jit(solution)/shard_map/ppermute | solution.py:316
  13.6 0.0 collective-permute-done.2.near_ref
  13.6 1.3 %sums.3 = (f32[136,256]{1,0:T(8,128)S(1)}, f32[136,256]{1,0:T(8,128)S(1)}, f32[128,256]{1,0:T(8,128)S(1)}, f32[128,256]{1,0:T(8,128)S(1)}) custom-call(bf16[528,512]{1,0:T(8,128)(2,1)S(1)} %pack.1.block_ref, bf16[528,512]{1,0:T(8,128)(2,1)S(1)} %collective-permute-done.2.near_ref, bf16[1024,256]{1,0:T(8,128)(2,1)S(1)} %get-tuple-element.45.cent_ref, ...), custom_call_target="tpu_custom_call" | custom-call | flops 104857600 | bytes 2097152 | tf_op jit(solution)/shard_map/sums/pallas_call | solution.py:32
  14.9 5.3 %collective-permute-done.3.refs_5_ = bf16[16,16,512]{2,1,0:T(8,128)(2,1)S(1)} collective-permute-done((bf16[16,16,512]{2,1,0:T(8,128)(2,1)S(1)}, bf16[16,16,512]{2,1,0:T(8,128)(2,1)S(1)}, u32[]{:S(2)}, u32[]{:S(2)}) %collective-permute-start.3) | collective-permute-done | bytes 262176 | tf_op jit(solution)/shard_map/ppermute | solution.py:316
  20.2 9.7 %collective-permute-done.block_ref = bf16[528,512]{1,0:T(8,128)(2,1)S(1)} collective-permute-done((bf16[528,512]{1,0:T(8,128)(2,1)S(1)}, bf16[528,512]{1,0:T(8,128)(2,1)S(1)}, u32[]{:S(2)}, u32[]{:S(2)}) %collective-permute-start) | collective-permute-done | bytes 540704 | tf_op jit(solution)/shard_map/ppermute | solution.py:323
  29.9 2.5 %collective-permute-done.1.block_ref = bf16[528,512]{1,0:T(8,128)(2,1)S(1)} collective-permute-done((bf16[528,512]{1,0:T(8,128)(2,1)S(1)}, bf16[528,512]{1,0:T(8,128)(2,1)S(1)}, u32[]{:S(2)}, u32[]{:S(2)}) %collective-permute-start.1) | collective-permute-done | bytes 540704 | tf_op jit(solution)/shard_map/ppermute | solution.py:323
  32.5 0.0 collective-permute-start.6
  32.5 0.5 collective-permute-start.5
  33.0 0.5 collective-permute-start.4
  33.5 0.7 %select.4 = (bf16[16,16,512]{2,1,0:T(8,128)(2,1)S(1)}, bf16[16,16,512]{2,1,0:T(8,128)(2,1)S(1)}) custom-call(bf16[528,512]{1,0:T(8,128)(2,1)S(1)} %collective-permute-done.block_ref, f32[256,1]{1,0:T(8,128)S(1)} %get-tuple-element.41.inv_ref, bf16[256,512]{1,0:T(8,128)(2,1)S(1)} %get-tuple-element.42.centre_ref), custom_call_target="tpu_custom_call" | custom-call | flops 6553600 | bytes 131072 | tf_op jit(solution)/shard_map/select/pallas_call | solution.py:32
  34.3 1.5 %collective-permute-start.7 = (bf16[16,16,512]{2,1,0:T(8,128)(2,1)S(1)}, bf16[16,16,512]{2,1,0:T(8,128)(2,1)S(1)}, u32[]{:S(2)}, u32[]{:S(2)}) collective-permute-start(bf16[16,16,512]{2,1,0:T(8,128)(2,1)S(1)} %get-tuple-element.64), channel_id=1, source_target_pairs={{0,2},{2,0},{1,3},{3,1},{4,6},{6,4},{5,7},{7,5},{8,10},{10,8},{9,1... | collective-permute-start | bytes 786440 | tf_op jit(solution)/shard_map/ppermute | solution.py:316
  35.8 0.7 %select.5 = (bf16[16,16,512]{2,1,0:T(8,128)(2,1)S(1)}, bf16[16,16,512]{2,1,0:T(8,128)(2,1)S(1)}) custom-call(bf16[528,512]{1,0:T(8,128)(2,1)S(1)} %collective-permute-done.1.block_ref, f32[256,1]{1,0:T(8,128)S(1)} %get-tuple-element.41.inv_ref, bf16[256,512]{1,0:T(8,128)(2,1)S(1)} %get-tuple-element.42.centre_ref), custom_call_target="tpu_custom_call" | custom-call | flops 6553600 | bytes 131072 | tf_op jit(solution)/shard_map/select/pallas_call | solution.py:32
  36.5 0.0 collective-permute-done.6.near_ref
  36.5 1.3 %sums.4 = (f32[136,256]{1,0:T(8,128)S(1)}, f32[136,256]{1,0:T(8,128)S(1)}, f32[128,256]{1,0:T(8,128)S(1)}, f32[128,256]{1,0:T(8,128)S(1)}) custom-call(bf16[528,512]{1,0:T(8,128)(2,1)S(1)} %collective-permute-done.block_ref, ...), custom_call_target="tpu_custom_call", output_to_operand_aliasing={{0}: (4, {}), {1}: (5, {}), {2}: (6, {}), {3}: (7, {})} | custom-call | flops 6553600 | bytes 131072 | tf_op jit(solution)/shard_map/sums/pallas_call | solution.py:32
  37.9 0.0 collective-permute-done.5.near_ref
  37.9 1.3 %sums.5 = (f32[136,256]{1,0:T(8,128)S(1)}, f32[136,256]{1,0:T(8,128)S(1)}, f32[128,256]{1,0:T(8,128)S(1)}, f32[128,256]{1,0:T(8,128)S(1)}) custom-call(bf16[528,512]{1,0:T(8,128)(2,1)S(1)} %collective-permute-done.1.block_ref, ...), custom_call_target="tpu_custom_call", output_to_operand_aliasing={{0}: (4, {}), {1}: (5, {}), {2}: (6, {}), {3}: (7, {})} | custom-call | flops 6553600 | bytes 131072 | tf_op jit(solution)/shard_map/sums/pallas_call | solution.py:32
  39.2 3.0 %collective-permute-done.7.refs_6_ = bf16[16,16,512]{2,1,0:T(8,128)(2,1)S(1)} collective-permute-done((bf16[16,16,512]{2,1,0:T(8,128)(2,1)S(1)}, bf16[16,16,512]{2,1,0:T(8,128)(2,1)S(1)}, u32[]{:S(2)}, u32[]{:S(2)}) %collective-permute-start.7) | collective-permute-done | bytes 262176 | tf_op jit(solution)/shard_map/ppermute | solution.py:316
  42.2 0.0 collective-permute-done.4.lead_ref
  42.2 0.0 collective-permute-start.9
  42.2 1.5 %collective-permute-start.10 = (bf16[16,16,512]{2,1,0:T(8,128)(2,1)S(1)}, bf16[16,16,512]{2,1,0:T(8,128)(2,1)S(1)}, u32[]{:S(2)}, u32[]{:S(2)}) collective-permute-start(bf16[16,16,512]{2,1,0:T(8,128)(2,1)S(1)} %get-tuple-element.55), channel_id=1, source_target_pairs={{0,2},{2,0},{1,3},{3,1},{4,6},{6,4},{5,7},{7,5},{8,10},{10,8},{9,1... | collective-permute-start | bytes 786440 | tf_op jit(solution)/shard_map/ppermute | solution.py:316
  43.8 1.6 %collective-permute-start.8 = (bf16[512,256]{1,0:T(8,128)(2,1)S(1)}, bf16[512,256]{1,0:T(8,128)(2,1)S(1)}, u32[]{:S(2)}, u32[]{:S(2)}) collective-permute-start(bf16[512,256]{1,0:T(8,128)(2,1)S(1)} %slice.7), channel_id=1, source_target_pairs={{0,4},{4,0},{8,12},{12,8},{1,5},{5,1},{9,13},{13,9},{2,6},{6,2},{1... | collective-permute-start | bytes 786440 | tf_op jit(solution)/shard_map/ppermute | solution.py:323
  45.4 0.6 select_lead.1
  46.0 0.6 collective-permute-start.11
  46.6 4.8 %collective-permute-done.10.refs_7_ = bf16[16,16,512]{2,1,0:T(8,128)(2,1)S(1)} collective-permute-done((bf16[16,16,512]{2,1,0:T(8,128)(2,1)S(1)}, bf16[16,16,512]{2,1,0:T(8,128)(2,1)S(1)}, u32[]{:S(2)}, u32[]{:S(2)}) %collective-permute-start.10) | collective-permute-done | bytes 262176 | tf_op jit(solution)/shard_map/ppermute | solution.py:316
  51.3 0.9 %collective-permute-done.8.rest_ref = bf16[512,256]{1,0:T(8,128)(2,1)S(1)} collective-permute-done((bf16[512,256]{1,0:T(8,128)(2,1)S(1)}, bf16[512,256]{1,0:T(8,128)(2,1)S(1)}, u32[]{:S(2)}, u32[]{:S(2)}) %collective-permute-start.8) | collective-permute-done | bytes 262176 | tf_op jit(solution)/shard_map/ppermute | solution.py:323
  52.3 0.0 collective-permute-done.9.near_ref
  52.3 0.3 select_rest.1
  52.6 0.6 %collective-permute-start.12 = (bf16[16,16,256]{2,1,0:T(8,128)(2,1)S(1)}, bf16[16,16,256]{2,1,0:T(8,128)(2,1)S(1)}, u32[]{:S(2)}, u32[]{:S(2)}) collective-permute-start(bf16[16,16,256]{2,1,0:T(8,128)(2,1)S(1)} %get-tuple-element.71), channel_id=1, source_target_pairs={{0,2},{2,0},{1,3},{3,1},{4,6},{6,4},{5,7},{7,5},{8,10},{10,8},{9,1... | collective-permute-start | bytes 393224 | tf_op jit(solution)/shard_map/ppermute | solution.py:316
  53.2 1.4 %sums_lead.1 = (bf16[256,512]{1,0:T(8,128)(2,1)S(1)}, f32[136,256]{1,0:T(8,128)S(1)}, f32[136,256]{1,0:T(8,128)S(1)}) custom-call(bf16[528,256]{1,0:T(8,128)(2,1)S(1)} %collective-permute-done.4.lead_ref, bf16[528,256]{1,0:T(8,128)(2,1)S(1)} %collective-permute-done.9.near_ref, ...), custom_call_target="tpu_custom_call", output_to_operand_aliasing={{1}: (4, {}), {2}: (5, {})} | custom-call | flops 6553600 | bytes 131072 | tf_op jit(solution)/shard_map/sums_lead/pallas_call | solution.py:32
  54.6 1.5 %collective-permute-start.14 = (f32[136,256]{1,0:T(8,128)S(1)}, f32[136,256]{1,0:T(8,128)S(1)}, u32[]{:S(2)}, u32[]{:S(2)}) collective-permute-start(f32[136,256]{1,0:T(8,128)S(1)} %get-tuple-element.73), channel_id=1, source_target_pairs={{0,2},{2,0},{1,3},{3,1},{4,6},{6,4},{5,7},{7,5},{8,10},{10,8},{9,1... | collective-permute-start | bytes 417800 | tf_op jit(solution)/shard_map/ppermute | solution.py:316
  56.1 0.2 sums_rest.1
  56.4 0.6 collective-permute-start.15
  57.0 0.0 collective-permute-done.11.refs_8_
  57.0 1.9 %collective-permute-done.12.refs_9_ = bf16[16,16,256]{2,1,0:T(8,128)(2,1)S(1)} collective-permute-done((bf16[16,16,256]{2,1,0:T(8,128)(2,1)S(1)}, bf16[16,16,256]{2,1,0:T(8,128)(2,1)S(1)}, u32[]{:S(2)}, u32[]{:S(2)}) %collective-permute-start.12) | collective-permute-done | bytes 131104 | tf_op jit(solution)/shard_map/ppermute | solution.py:316
  58.9 0.9 %gram.1.mine_ref = f32[16,16,128]{2,1,0:T(8,128)S(1)} custom-call(bf16[16,16,512]{2,1,0:T(8,128)(2,1)S(1)} %get-tuple-element.43.refs_0_, bf16[16,16,512]{2,1,0:T(8,128)(2,1)S(1)} %get-tuple-element.52.refs_1_, bf16[16,16,512]{2,1,0:T(8,128)(2,1)S(1)} %get-tuple-element.54.refs_2_, bf16[16,16,256]{2,1,0:T(8,128)(2,1)S(1)} %get-tuple-element.66.refs_3_, ...), custom_call_target="tpu_custom_call" | custom-call | tf_op jit(solution)/shard_map/gram/pallas_call | solution.py:32
  59.8 0.1 collective-permute-start.13
  59.8 3.6 %collective-permute-done.15.refs_3_ = f32[128,256]{1,0:T(8,128)S(1)} collective-permute-done((f32[128,256]{1,0:T(8,128)S(1)}, f32[128,256]{1,0:T(8,128)S(1)}, u32[]{:S(2)}, u32[]{:S(2)}) %collective-permute-start.15) | collective-permute-done | bytes 131104 | tf_op jit(solution)/shard_map/ppermute | solution.py:316
  63.4 0.0 collective-permute-done.14.refs_1_
  63.4 1.4 %finish.1 = (f32[128,512]{1,0:T(8,128)}, bf16[8,16,128]{2,1,0:T(8,128)(2,1)}) custom-call(f32[16,16,128]{2,1,0:T(8,128)S(1)} %gram.1.mine_ref, f32[16,16,128]{2,1,0:T(8,128)S(1)} %collective-permute-done.13.other_ref, f32[136,256]{1,0:T(8,128)S(1)} %get-tuple-element.72.refs_0_, f32[136,256]{1,0:T(8,128)S(1)} %collective-permute-done.14.refs_1_, ...), custom_call_target="tpu_custom_call" | custom-call | tf_op jit(solution)/shard_map/finish/pallas_call | solution.py:32
  (8 shorter events, 0.1 us)
Async XLA Ops:
  0.6 1.0 %copy-start.1 = (bf16[512,512]{1,0:T(8,128)(2,1)S(1)}, bf16[512,512]{1,0:T(8,128)(2,1)}, u32[]{:S(2)}) copy-start(bf16[512,512]{1,0:T(8,128)(2,1)} %emb_ref.1) | copy-start | bytes 1572868
  1.7 0.7 %copy-start.3 = (s32[512,1]{0,1:T(1,128)S(1)}, s32[512,1]{0,1:T(1,128)}, u32[]{:S(2)}) copy-start(s32[512,1]{0,1:T(1,128)} %param.6) | copy-start | bytes 6148
  2.4 11.2 %collective-permute-start.2 = (bf16[528,512]{1,0:T(8,128)(2,1)S(1)}, bf16[528,512]{1,0:T(8,128)(2,1)S(1)}, u32[]{:S(2)}, u32[]{:S(2)}) collective-permute-start(bf16[528,512]{1,0:T(8,128)(2,1)S(1)} %pack.1.block_ref), channel_id=1, source_target_pairs={{0,1},{1,0},{2,3},{3,2},{4,5},{5,4},{6,7},{7,6},{8,9},{9,8},{10,11... | collective-permute-start | bytes 1622024 | tf_op jit(solution)/shard_map/ppermute | solution.py:320
  2.9 27.0 %collective-permute-start = (bf16[528,512]{1,0:T(8,128)(2,1)S(1)}, bf16[528,512]{1,0:T(8,128)(2,1)S(1)}, u32[]{:S(2)}, u32[]{:S(2)}) collective-permute-start(bf16[528,512]{1,0:T(8,128)(2,1)S(1)} %pack.1.block_ref), channel_id=1, source_target_pairs={{0,4},{4,0},{8,12},{12,8},{1,5},{5,1},{9,13},{13,9},{2,6},{6,2},{1... | collective-permute-start | bytes 1622024 | tf_op jit(solution)/shard_map/ppermute | solution.py:323
  5.6 26.9 %collective-permute-start.1 = (bf16[528,512]{1,0:T(8,128)(2,1)S(1)}, bf16[528,512]{1,0:T(8,128)(2,1)S(1)}, u32[]{:S(2)}, u32[]{:S(2)}) collective-permute-start(bf16[528,512]{1,0:T(8,128)(2,1)S(1)} %pack.1.block_ref), channel_id=1, source_target_pairs={{0,8},{4,12},{8,0},{12,4},{1,9},{5,13},{9,1},{13,5},{2,10},{6,14},... | collective-permute-start | bytes 1622024 | tf_op jit(solution)/shard_map/ppermute | solution.py:323
  8.2 1.6 %copy-start = (bf16[1024,1024]{1,0:T(8,128)(2,1)S(1)}, bf16[1024,1024]{1,0:T(8,128)(2,1)}, u32[]{:S(2)}) copy-start(bf16[1024,1024]{1,0:T(8,128)(2,1)} %cent_ref.1) | copy-start | bytes 6291460
  9.8 0.7 %copy-start.2 = (s32[1024]{0:T(1024)S(1)}, s32[1024]{0:T(1024)}, u32[]{:S(2)}) copy-start(s32[1024]{0:T(1024)} %param.7) | copy-start | bytes 12292
  12.0 8.1 %collective-permute-start.3 = (bf16[16,16,512]{2,1,0:T(8,128)(2,1)S(1)}, bf16[16,16,512]{2,1,0:T(8,128)(2,1)S(1)}, u32[]{:S(2)}, u32[]{:S(2)}) collective-permute-start(bf16[16,16,512]{2,1,0:T(8,128)(2,1)S(1)} %get-tuple-element.44), channel_id=1, source_target_pairs={{0,2},{2,0},{1,3},{3,1},{4,6},{6,4},{5,7},{7,5},{8,10},{10,8},{9,1... | collective-permute-start | bytes 786440 | tf_op jit(solution)/shard_map/ppermute | solution.py:316
  32.5 4.1 %collective-permute-start.6 = (bf16[528,512]{1,0:T(8,128)(2,1)S(1)}, bf16[528,512]{1,0:T(8,128)(2,1)S(1)}, u32[]{:S(2)}, u32[]{:S(2)}) collective-permute-start(bf16[528,512]{1,0:T(8,128)(2,1)S(1)} %collective-permute-done.block_ref), channel_id=1, source_target_pairs={{0,1},{1,0},{2,3},{3,2},{4,5},{5,4},{6,7},{7,6},{8,9},{9,8},{10,11... | collective-permute-start | bytes 1622024 | tf_op jit(solution)/shard_map/ppermute | solution.py:320
  32.5 5.4 %collective-permute-start.5 = (bf16[528,512]{1,0:T(8,128)(2,1)S(1)}, bf16[528,512]{1,0:T(8,128)(2,1)S(1)}, u32[]{:S(2)}, u32[]{:S(2)}) collective-permute-start(bf16[528,512]{1,0:T(8,128)(2,1)S(1)} %collective-permute-done.1.block_ref), channel_id=1, source_target_pairs={{0,1},{1,0},{2,3},{3,2},{4,5},{5,4},{6,7},{7,6},{8,9},{9,8},{10,11... | collective-permute-start | bytes 1622024 | tf_op jit(solution)/shard_map/ppermute | solution.py:320
  33.0 9.3 %collective-permute-start.4 = (bf16[528,256]{1,0:T(8,128)(2,1)S(1)}, bf16[528,256]{1,0:T(8,128)(2,1)S(1)}, u32[]{:S(2)}, u32[]{:S(2)}) collective-permute-start(bf16[528,256]{1,0:T(8,128)(2,1)S(1)} %slice.6), channel_id=1, source_target_pairs={{0,4},{4,0},{8,12},{12,8},{1,5},{5,1},{9,13},{13,9},{2,6},{6,2},{1... | collective-permute-start | bytes 811016 | tf_op jit(solution)/shard_map/ppermute | solution.py:323
  34.3 8.0 %collective-permute-start.7 = (bf16[16,16,512]{2,1,0:T(8,128)(2,1)S(1)}, bf16[16,16,512]{2,1,0:T(8,128)(2,1)S(1)}, u32[]{:S(2)}, u32[]{:S(2)}) collective-permute-start(bf16[16,16,512]{2,1,0:T(8,128)(2,1)S(1)} %get-tuple-element.64), channel_id=1, source_target_pairs={{0,2},{2,0},{1,3},{3,1},{4,6},{6,4},{5,7},{7,5},{8,10},{10,8},{9,1... | collective-permute-start | bytes 786440 | tf_op jit(solution)/shard_map/ppermute | solution.py:316
  42.2 10.0 %collective-permute-start.9 = (bf16[528,256]{1,0:T(8,128)(2,1)S(1)}, bf16[528,256]{1,0:T(8,128)(2,1)S(1)}, u32[]{:S(2)}, u32[]{:S(2)}) collective-permute-start(bf16[528,256]{1,0:T(8,128)(2,1)S(1)} %collective-permute-done.4.lead_ref), channel_id=1, source_target_pairs={{0,1},{1,0},{2,3},{3,2},{4,5},{5,4},{6,7},{7,6},{8,9},{9,8},{10,11... | collective-permute-start | bytes 811016 | tf_op jit(solution)/shard_map/ppermute | solution.py:320
  42.2 9.1 %collective-permute-start.10 = (bf16[16,16,512]{2,1,0:T(8,128)(2,1)S(1)}, bf16[16,16,512]{2,1,0:T(8,128)(2,1)S(1)}, u32[]{:S(2)}, u32[]{:S(2)}) collective-permute-start(bf16[16,16,512]{2,1,0:T(8,128)(2,1)S(1)} %get-tuple-element.55), channel_id=1, source_target_pairs={{0,2},{2,0},{1,3},{3,1},{4,6},{6,4},{5,7},{7,5},{8,10},{10,8},{9,1... | collective-permute-start | bytes 786440 | tf_op jit(solution)/shard_map/ppermute | solution.py:316
  43.8 8.5 %collective-permute-start.8 = (bf16[512,256]{1,0:T(8,128)(2,1)S(1)}, bf16[512,256]{1,0:T(8,128)(2,1)S(1)}, u32[]{:S(2)}, u32[]{:S(2)}) collective-permute-start(bf16[512,256]{1,0:T(8,128)(2,1)S(1)} %slice.7), channel_id=1, source_target_pairs={{0,4},{4,0},{8,12},{12,8},{1,5},{5,1},{9,13},{13,9},{2,6},{6,2},{1... | collective-permute-start | bytes 786440 | tf_op jit(solution)/shard_map/ppermute | solution.py:323
  46.0 11.0 %collective-permute-start.11 = (bf16[16,16,256]{2,1,0:T(8,128)(2,1)S(1)}, bf16[16,16,256]{2,1,0:T(8,128)(2,1)S(1)}, u32[]{:S(2)}, u32[]{:S(2)}) collective-permute-start(bf16[16,16,256]{2,1,0:T(8,128)(2,1)S(1)} %get-tuple-element.70), channel_id=1, source_target_pairs={{0,2},{2,0},{1,3},{3,1},{4,6},{6,4},{5,7},{7,5},{8,10},{10,8},{9,1... | collective-permute-start | bytes 393224 | tf_op jit(solution)/shard_map/ppermute | solution.py:316
  52.6 6.3 %collective-permute-start.12 = (bf16[16,16,256]{2,1,0:T(8,128)(2,1)S(1)}, bf16[16,16,256]{2,1,0:T(8,128)(2,1)S(1)}, u32[]{:S(2)}, u32[]{:S(2)}) collective-permute-start(bf16[16,16,256]{2,1,0:T(8,128)(2,1)S(1)} %get-tuple-element.71), channel_id=1, source_target_pairs={{0,2},{2,0},{1,3},{3,1},{4,6},{6,4},{5,7},{7,5},{8,10},{10,8},{9,1... | collective-permute-start | bytes 393224 | tf_op jit(solution)/shard_map/ppermute | solution.py:316
  54.6 8.8 %collective-permute-start.14 = (f32[136,256]{1,0:T(8,128)S(1)}, f32[136,256]{1,0:T(8,128)S(1)}, u32[]{:S(2)}, u32[]{:S(2)}) collective-permute-start(f32[136,256]{1,0:T(8,128)S(1)} %get-tuple-element.73), channel_id=1, source_target_pairs={{0,2},{2,0},{1,3},{3,1},{4,6},{6,4},{5,7},{7,5},{8,10},{10,8},{9,1... | collective-permute-start | bytes 417800 | tf_op jit(solution)/shard_map/ppermute | solution.py:316
  56.4 7.0 %collective-permute-start.15 = (f32[128,256]{1,0:T(8,128)S(1)}, f32[128,256]{1,0:T(8,128)S(1)}, u32[]{:S(2)}, u32[]{:S(2)}) collective-permute-start(f32[128,256]{1,0:T(8,128)S(1)} %get-tuple-element.76), channel_id=1, source_target_pairs={{0,2},{2,0},{1,3},{3,1},{4,6},{6,4},{5,7},{7,5},{8,10},{10,8},{9,1... | collective-permute-start | bytes 393224 | tf_op jit(solution)/shard_map/ppermute | solution.py:316
  59.8 3.6 %collective-permute-start.13 = (f32[16,16,128]{2,1,0:T(8,128)S(1)}, f32[16,16,128]{2,1,0:T(8,128)S(1)}, u32[]{:S(2)}, u32[]{:S(2)}) collective-permute-start(f32[16,16,128]{2,1,0:T(8,128)S(1)} %gram.1.mine_ref), channel_id=1, source_target_pairs={{0,1},{1,0},{2,3},{3,2},{4,5},{5,4},{6,7},{7,6},{8,9},{9,8},{10,11... | collective-permute-start | bytes 393224 | tf_op jit(solution)/shard_map/ppermute | solution.py:320

commit v7 on v5

--- a/solution.py
+++ b/solution.py
@@ -56,26 +56,26 @@
     return jax.tree.unflatten(tree, kept[: len(leaves)])
 
 
-def slots_order(rows):
-    return sorted(range(rows), key=lambda bits: (bits.bit_count(), bits))
-
-
-def pack_kernel(emb_ref, cid_ref, block_ref):
-    docs, half = emb_ref.shape
-    block_ref[:docs, :] = emb_ref[...]
+def bits_by_count(rows):
+    return [[bits for bits in range(rows) if bits.bit_count() == n] for n in range(1, (rows - 1).bit_count() + 1)]
+
+
+def pack_kernel(emb_ref, cid_ref, lead_ref, rest_ref):
+    docs = emb_ref.shape[0]
+    lead_ref[:docs, :] = emb_ref[:, :PREFIX]
+    rest_ref[...] = emb_ref[:, PREFIX:]
     cid = cid_ref[...]
     high, low = (cid // DIGIT + 1).astype(F32), (cid % DIGIT).astype(F32)
     rows = []
     for digit in (high, low):
         rows += [digit[:, at : at + PREFIX] for at in range(0, docs, PREFIX)]
     rows.append(jnp.zeros((META - len(rows), PREFIX), F32))
-    block_ref[docs:, :PREFIX] = jnp.concatenate(rows, axis=0).astype(BF16)
-    block_ref[docs:, PREFIX:] = jnp.zeros((META, half - PREFIX), BF16)
+    lead_ref[docs:, :] = jnp.concatenate(rows, axis=0).astype(BF16)
 
 
 def ids_of(lead_ref):
     docs = lead_ref.shape[0] - META
-    meta = lead_ref[docs:, :PREFIX].astype(F32)
+    meta = lead_ref[docs:, :].astype(F32)
     parts = docs // PREFIX
     high = jnp.concatenate([meta[i : i + 1] for i in range(parts)], axis=1)
     low = jnp.concatenate([meta[parts + i : parts + i + 1] for i in range(parts)], axis=1)
@@ -122,35 +122,43 @@
     return jnp.stack(ranked, axis=1).reshape(groups * MOST * SUBLANES, docs).astype(BF16)
 
 
-def select_kernel(block_ref, inv_ref, centre_ref, *row_refs):
-    docs = block_ref.shape[0] - META
-    rows = centred(picked(block_ref, inv_ref), centre_ref[...], block_ref[:docs, :])
-    rows = rows.reshape((len(row_refs),) + row_refs[0].shape)
-    for t, ref in enumerate(row_refs):
-        ref[...] = rows[t]
-
-
-def select_lead_kernel(lead_ref, inv_ref, centre_ref, pick_ref, *row_refs):
-    docs = lead_ref.shape[0] - META
+def select_kernel(lead_ref, rest_ref, inv_ref, centre_ref, *row_refs):
+    docs = rest_ref.shape[0]
     pick = picked(lead_ref, inv_ref)
-    pick_ref[...] = pick
-    rows = centred(pick, centre_ref[:, :PREFIX], lead_ref[:docs, :])
-    rows = rows.reshape((len(row_refs),) + row_refs[0].shape)
-    for t, ref in enumerate(row_refs):
-        ref[...] = rows[t]
-
-
-def select_rest_kernel(pick_ref, rest_ref, centre_ref, *row_refs):
-    rows = centred(pick_ref[...], centre_ref[:, PREFIX:], rest_ref[...])
-    rows = rows.reshape((len(row_refs),) + row_refs[0].shape)
-    for t, ref in enumerate(row_refs):
-        ref[...] = rows[t]
+    groups, packed, _ = row_refs[0].shape
+    for columns, at in ((lead_ref[:docs, :], 0), (rest_ref[...], PREFIX)):
+        width = columns.shape[1]
+        rows = centred(pick, centre_ref[:, at : at + width], columns)
+        rows = rows.reshape(len(row_refs), groups, packed, width)
+        for t, ref in enumerate(row_refs):
+            ref[:, :, at : at + width] = rows[t]
+
+
+def select_lead_kernel(count, subs, inv_ref, centre_ref, *refs):
+    lead_refs, pick_refs, row_refs = refs[:count], refs[count : 2 * count], refs[2 * count :]
+    for i in range(count):
+        docs = lead_refs[i].shape[0] - META
+        pick = picked(lead_refs[i], inv_ref)
+        pick_refs[i][...] = pick
+        rows = centred(pick, centre_ref[:, :PREFIX], lead_refs[i][:docs, :])
+        rows = rows.reshape((subs,) + row_refs[0].shape[1:])
+        for t in range(subs):
+            row_refs[t][i] = rows[t]
+
+
+def select_rest_kernel(count, subs, centre_ref, *refs):
+    pick_refs, rest_refs, row_refs = refs[:count], refs[count : 2 * count], refs[2 * count :]
+    for i in range(count):
+        rows = centred(pick_refs[i][...], centre_ref[:, PREFIX:], rest_refs[i][...])
+        rows = rows.reshape((subs,) + row_refs[0].shape[1:])
+        for t in range(subs):
+            row_refs[t][i] = rows[t]
 
 
 def soft_weights(lead_ref, near_ref, cent_ref, own_prefix_ref):
     docs = lead_ref.shape[0] - META
     h = lax.axis_index("dim")
-    prefix = jnp.where(h == 0, lead_ref[:docs, :PREFIX], near_ref[...])
+    prefix = jnp.where(h == 0, lead_ref[:docs, :], near_ref[:docs, :])
     scores = dot_nt(cent_ref[...], prefix) * TEMP
     top = jnp.max(scores, axis=0, keepdims=True)
     scale = 1.0 / jnp.sum(jnp.exp(scores - top), axis=0, keepdims=True)
@@ -161,7 +169,7 @@
 def add_lead(weights, lead_ref, old_refs, new_refs):
     docs = lead_ref.shape[0] - META
     per = new_refs[0].shape[0] - SUBLANES
-    sums = dot(weights.astype(BF16), lead_ref[:docs, :PREFIX])
+    sums = dot(weights.astype(BF16), lead_ref[:docs, :])
     ones = jnp.ones((SUBLANES, docs), BF16)
     for t, new in enumerate(new_refs):
         here = slice(t * per, (t + 1) * per)
@@ -185,12 +193,10 @@
         new[...] = old_refs[t][...] + part if old_refs else part
 
 
-def sums_kernel(subs, block_ref, near_ref, cent_ref, own_prefix_ref, *refs):
-    old, new = refs[: -2 * subs], refs[-2 * subs :]
-    docs = block_ref.shape[0] - META
-    weights = soft_weights(block_ref, near_ref, cent_ref, own_prefix_ref)
-    add_lead(weights, block_ref, old[:subs], new[:subs])
-    add_rest(weights.astype(BF16), block_ref[:docs, PREFIX:], old[subs:], new[subs:])
+def sums_kernel(subs, lead_ref, rest_ref, near_ref, cent_ref, own_prefix_ref, *new):
+    weights = soft_weights(lead_ref, near_ref, cent_ref, own_prefix_ref)
+    add_lead(weights, lead_ref, (), new[:subs])
+    add_rest(weights.astype(BF16), rest_ref[...], (), new[subs:])
 
 
 def sums_lead_kernel(subs, lead_ref, near_ref, cent_ref, own_prefix_ref, *refs):
@@ -200,24 +206,28 @@
     add_lead(weights, lead_ref, old, new)
 
 
-def sums_rest_kernel(subs, weights_ref, rest_ref, *refs):
-    add_rest(weights_ref[...], rest_ref[...], refs[:subs], refs[subs:])
-
-
-def gram_kernel(order, subs, *refs):
+def sums_rest_kernel(count, subs, *refs):
+    weights_refs, rest_refs, old, new = refs[:count], refs[count : 2 * count], refs[-2 * subs : -subs], refs[-subs:]
+    total = sum(dot(w[...], rest[...]) for w, rest in zip(weights_refs, rest_refs))
+    per = new[0].shape[0]
+    for t in range(subs):
+        new[t][...] = old[t][...] + total[t * per : (t + 1) * per]
+
+
+def gram_kernel(groups_of_bits, subs, *refs):
     *member_refs, gram_ref, held = refs
     z, x = lax.axis_index("rows"), lax.axis_index("sub")
     owners, groups, packed, half = held.shape
     each = len(member_refs) // subs
     for t in range(subs):
-        column = member_refs[t * each : (t + 1) * each]
-        for k, bits in enumerate(order):
-            row = (z ^ bits) * subs + (x - t + subs) % subs
-            if k < len(order) - 1:
-                held[row] = column[k][...]
-            else:
-                held[row, :, :, :PREFIX] = column[k][...]
-                held[row, :, :, PREFIX:] = column[k + 1][...]
+        own, *chunks = member_refs[t * each : (t + 1) * each]
+        column = (x - t + subs) % subs
+        held[z * subs + column] = own[...]
+        for k, group in enumerate(groups_of_bits):
+            for i, bits in enumerate(group):
+                row = (z ^ bits) * subs + column
+                held[row, :, :, :PREFIX] = chunks[2 * k][i]
+                held[row, :, :, PREFIX:] = chunks[2 * k + 1][i]
 
     size = owners * packed
     lane = lax.broadcasted_iota(jnp.int32, (1, SUBLANES, size), 2) % SUBLANES
@@ -307,7 +317,7 @@
     groups = per // SUBLANES
     packed = MOST * SUBLANES
     slots = owners * MOST
-    order = slots_order(rows)
+    groups_of_bits = bits_by_count(rows)
     shape = jax.ShapeDtypeStruct
 
     def across(values):
@@ -322,19 +332,20 @@
     def swap(value, bit):
         return lax.ppermute(value, "rows", [(i, i ^ bit) for i in range(rows)])
 
-    (block,) = call(
-        pack_kernel, "pack", [shape((docs + META, half), BF16)], [embeddings, cluster_id.reshape(1, docs)]
-    )
-    blocks = {0: block}
-
-    def send(bits):
+    def send(blocks, bits):
         bit = (bits & -bits or rows) // 2
         while bit:
-            if bits | bit != rows - 1:
-                blocks[bits | bit] = swap(blocks[bits], bit)
+            blocks[bits | bit] = swap(blocks[bits], bit)
             bit //= 2
 
-    send(0)
+    lead, rest = call(
+        pack_kernel,
+        "pack",
+        [shape((docs + META, PREFIX), BF16), shape((docs, half - PREFIX), BF16)],
+        [embeddings, cluster_id.reshape(1, docs)],
+    )
+    leads, rests = {0: lead}, {0: rest}
+    send(leads, 0)
 
     inv, centre, own_prefix, prior, cent_prefix = call(
         functools.partial(prep_kernel, subs, per),
@@ -354,65 +365,80 @@
     sum_shapes = [lead_sum] * subs + [rest_sum] * subs
     own_cost, other_cost = 2 * 1024 * 1024, 128 * 1024
 
-    def select(block, cost):
-        row_shapes = [shape((groups, packed, half), BF16)] * subs
-        return list(call(select_kernel, "select", row_shapes, [block, inv, centre], cost=cost))
-
-    def add(block, prefix, sums, cost):
-        operands = [block, prefix, cent_prefix, own_prefix] + sums
-        aliases = {4 + i: i for i in range(len(sums))}
-        return list(call(functools.partial(sums_kernel, subs), "sums", sum_shapes, operands, aliases, cost=cost))
-
-    members = []
-    prefix = near(block[:docs, :PREFIX])
-    found = select(block, own_cost)
-    members.append(across(found))
-    sums = add(block, prefix, [], own_cost)
-    for k, bits in enumerate(order[1:-1], 1):
-        block = blocks[bits] = tied(blocks[bits], found, sums, members[: k - 1])
-        send(bits)
-        if bits == rows - 2:
-            coming, coming_rest = swap(block[:, :PREFIX], 1), swap(block[:docs, PREFIX:], 1)
-        prefix = near(block[:docs, :PREFIX])
-        found = select(block, other_cost)
+    prefix = near(lead)
+    found = call(
+        select_kernel, "select", [shape((groups, packed, half), BF16)] * subs, [lead, rest, inv, centre], cost=own_cost
+    )
+    members = [across(found)]
+    rests[0] = tied(rest, found)
+    send(rests, 0)
+    sums = call(
+        functools.partial(sums_kernel, subs),
+        "sums",
+        sum_shapes,
+        [lead, rest, prefix, cent_prefix, own_prefix],
+        cost=own_cost,
+    )
+    lead_sums, rest_sums = list(sums[:subs]), list(sums[subs:])
+
+    for group in groups_of_bits:
+        last = group == groups_of_bits[-1]
+        count = len(group)
+        before = members[:-1] if last else members
+        leads.update(zip(group, tied([leads[bits] for bits in group], found, lead_sums, rest_sums, before)))
+        for bits in group:
+            send(leads, bits)
+        prefixes = [near(leads[bits]) for bits in group]
+        row_shapes = [shape((count, groups, packed, PREFIX), BF16)] * subs
+        found = call(
+            functools.partial(select_lead_kernel, count, subs),
+            "select_lead",
+            [shape((subs * per * MOST, docs), BF16)] * count + row_shapes,
+            [inv, centre] + [leads[bits] for bits in group],
+            cost=other_cost,
+        )
+        picks, found = list(found[:count]), list(found[count:])
         members.append(across(found))
-        sums = add(block, prefix, sums, other_cost)
-
-    lead = tied(coming, found, sums, members)
-    prefix = near(lead[:docs])
-    half_rows = [shape((groups, packed, PREFIX), BF16)] * subs
-    pick, *lead_found = call(
-        select_lead_kernel,
-        "select_lead",
-        [shape((subs * per * MOST, docs), BF16)] + half_rows,
-        [lead, inv, centre],
-        cost=other_cost,
-    )
-    members.append(across(lead_found))
-    weights, *lead_sums = call(
-        functools.partial(sums_lead_kernel, subs),
-        "sums_lead",
-        [shape((subs * per, docs), BF16)] + [lead_sum] * subs,
-        [lead, prefix, cent_prefix, own_prefix] + sums[:subs],
-        {4 + i: 1 + i for i in range(subs)},
-        cost=other_cost,
-    )
-    lead_sums = across(lead_sums)
-    rest = tied(coming_rest, prefix)
-    half_rows = [shape((groups, packed, half - PREFIX), BF16)] * subs
-    found = call(select_rest_kernel, "select_rest", half_rows, [pick, rest, centre], cost=other_cost)
-    members.append(across(found))
-    rest_sums = call(
-        functools.partial(sums_rest_kernel, subs),
-        "sums_rest",
-        [rest_sum] * subs,
-        [weights, rest] + sums[subs:],
-        {2 + i: i for i in range(subs)},
-    )
+        weights = []
+        for bits, prefix in zip(group, prefixes):
+            weight, *lead_sums = call(
+                functools.partial(sums_lead_kernel, subs),
+                "sums_lead",
+                [shape((subs * per, docs), BF16)] + [lead_sum] * subs,
+                [leads[bits], prefix, cent_prefix, own_prefix] + lead_sums,
+                {4 + i: 1 + i for i in range(subs)},
+                cost=other_cost,
+            )
+            weights.append(weight)
+        if last:
+            lead_sums = across(lead_sums)
+            before = (prefixes, members[:-1])
+        else:
+            before = (found, weights, members)
+        rests.update(zip(group, tied([rests[bits] for bits in group], before)))
+        for bits in group:
+            send(rests, bits)
+        row_shapes = [shape((count, groups, packed, half - PREFIX), BF16)] * subs
+        found = call(
+            functools.partial(select_rest_kernel, count, subs),
+            "select_rest",
+            row_shapes,
+            [centre] + picks + [rests[bits] for bits in group],
+            cost=other_cost,
+        )
+        members.append(across(found))
+        rest_sums = call(
+            functools.partial(sums_rest_kernel, count, subs),
+            "sums_rest",
+            [rest_sum] * subs,
+            weights + [rests[bits] for bits in group] + list(rest_sums),
+            {2 * count + i: i for i in range(subs)},
+            cost=other_cost,
+        )
     rest_sums = across(rest_sums)
 
     (gram,) = call(
-        functools.partial(gram_kernel, order, subs),
+        functools.partial(gram_kernel, groups_of_bits, subs),
         "gram",
         [shape((groups, slots, slots * SUBLANES), F32)],
         [arrays[t] for t in range(subs) for arrays in members],

time: 66.2 us -> 64.6 us (0.976)
  waiting for transfers between devices: 31.6 us -> 28.3 us
  starting transfers between devices: 17.6 us -> 19 us
    ppermute x4 -> x6, waiting for transfers between devices: 16 us -> 12.6 us  [swap(): return lax.ppermute(value, 'rows', [(i, i ^ bit) for i in range(rows)])]
    ppermute x4 -> x6, starting transfers between devices: 7.75 us -> 9.6 us  [swap(): return lax.ppermute(value, 'rows', [(i, i ^ bit) for i in range(rows)])]
    ppermute x7, starting transfers between devices: 9.47 us -> 8.24 us  [across(): lax.ppermute(values[t], 'sub', [(i, (i + t) % subs) for i in range(subs)])]
    ppermute x5, starting transfers between devices: 0.36 us -> 1.17 us  [near(): return lax.ppermute(value, 'dim', [(0, 1), (1, 0)])]
    pallas_call x14 -> x15, Pallas kernels: 11.8 us -> 12.2 us  [call(): pl.pallas_call(kernel, out_shape=tuple(out_shape), in_specs=[place(at) fo...]
  transfers between devices with their start and end apart: 16 -> 18, of which waited for: 6 -> 7; matrix products, arithmetic and copies ran while one was open for 0% -> 0% of each run, Pallas kernels for 16% -> 17%
where the time goes in v7:
time: 64.6 us; the launch traced here: 64.3 us
  waiting for transfers between devices  28.3 us (44%)
  starting transfers between devices  19 us (29%)
  Pallas kernels  12.2 us (19%)
  local copies, waits for them, and re-layouts  3.99 us (6%)
  between operations  0.79 us (1%)
    ppermute x7, waiting for transfers between devices, across(): lax.ppermute(values[t], 'sub', [(i, (i + t) % subs) for i in range(subs)])  15.7 us
    ppermute x6, waiting for transfers between devices, swap(): return lax.ppermute(value, 'rows', [(i, i ^ bit) for i in range(rows)])  12.6 us
    pallas_call x15, Pallas kernels, call(): pl.pallas_call(kernel, out_shape=tuple(out_shape), in_specs=[place(at) fo...  12.2 us
    ppermute x6, starting transfers between devices, swap(): return lax.ppermute(value, 'rows', [(i, i ^ bit) for i in range(rows)])  9.6 us
    ppermute x7, starting transfers between devices, across(): lax.ppermute(values[t], 'sub', [(i, (i + t) % subs) for i in range(subs)])  8.24 us
    unnamed x8, local copies, waits for them, and re-layouts  3.99 us
  transfers between devices with their start and end apart: 18, of which 7 were waited for; matrix products, arithmetic and copies ran while one was open for 0% of the time, Pallas kernels for 17%

profile of v7, /device:TPU:0, one launch (start us, length us, event | category | flops | bytes accessed | tf_op | source)
XLA Modules:
  0.0 64.3 jit_solution(427527544066112160)
XLA Ops:
  0.6 1.0 %copy-done.1 = bf16[512,512]{1,0:T(8,128)(2,1)S(1)} copy-done((bf16[512,512]{1,0:T(8,128)(2,1)S(1)}, bf16[512,512]{1,0:T(8,128)(2,1)}, u32[]{:S(2)}) %copy-start.1) | copy-done | bytes 524312
  1.7 0.7 %copy-done.3 = s32[512,1]{0,1:T(1,128)S(1)} copy-done((s32[512,1]{0,1:T(1,128)S(1)}, s32[512,1]{0,1:T(1,128)}, u32[]{:S(2)}) %copy-start.3) | copy-done | bytes 2072
  2.4 0.5 collective-permute-start.2
  2.9 2.6 %collective-permute-start = (bf16[528,256]{1,0:T(8,128)(2,1)S(1)}, bf16[528,256]{1,0:T(8,128)(2,1)S(1)}, u32[]{:S(2)}, u32[]{:S(2)}) collective-permute-start(bf16[528,256]{1,0:T(8,128)(2,1)S(1)} %get-tuple-element.48.lead_ref), channel_id=1, source_target_pairs={{0,4},{4,0},{8,12},{12,8},{1,5},{5,1},{9,13},{13,9},{2,6},{6,2},{1... | collective-permute-start | bytes 811016 | tf_op jit(solution)/shard_map/ppermute | solution.py:333
  5.6 2.6 %collective-permute-start.1 = (bf16[528,256]{1,0:T(8,128)(2,1)S(1)}, bf16[528,256]{1,0:T(8,128)(2,1)S(1)}, u32[]{:S(2)}, u32[]{:S(2)}) collective-permute-start(bf16[528,256]{1,0:T(8,128)(2,1)S(1)} %get-tuple-element.48.lead_ref), channel_id=1, source_target_pairs={{0,8},{4,12},{8,0},{12,4},{1,9},{5,13},{9,1},{13,5},{2,10},{6,14},... | collective-permute-start | bytes 811016 | tf_op jit(solution)/shard_map/ppermute | solution.py:333
  8.2 1.6 %copy-done = bf16[1024,1024]{1,0:T(8,128)(2,1)S(1)} copy-done((bf16[1024,1024]{1,0:T(8,128)(2,1)S(1)}, bf16[1024,1024]{1,0:T(8,128)(2,1)}, u32[]{:S(2)}) %copy-start) | copy-done | bytes 2097176
  9.8 0.7 %copy-done.2 = s32[1024]{0:T(1024)S(1)} copy-done((s32[1024]{0:T(1024)S(1)}, s32[1024]{0:T(1024)}, u32[]{:S(2)}) %copy-start.2) | copy-done | bytes 4120
  10.4 0.8 %prep.1 = (f32[256,1]{1,0:T(8,128)S(1)}, bf16[256,512]{1,0:T(8,128)(2,1)S(1)}, bf16[256,256]{1,0:T(8,128)(2,1)S(1)}, bf16[128,512]{1,0:T(8,128)(2,1)S(1)}, bf16[1024,256]{1,0:T(8,128)(2,1)S(1)}) custom-call(s32[1,1024]{1,0:T(1,128)S(1)} %bitcast.3, bf16[1024,1024]{1,0:T(8,128)(2,1)S(1)} %copy-done), custom_call_target="tpu_custom_call" | custom-call | flops 209715200 | bytes 4194304 | tf_op jit(solution)/shard_map/prep/pallas_call | solution.py:32
  11.3 0.7 %select.1 = (bf16[16,16,512]{2,1,0:T(8,128)(2,1)S(1)}, bf16[16,16,512]{2,1,0:T(8,128)(2,1)S(1)}) custom-call(bf16[528,256]{1,0:T(8,128)(2,1)S(1)} %get-tuple-element.48.lead_ref, bf16[512,256]{1,0:T(8,128)(2,1)S(1)} %get-tuple-element.65.rest_ref, f32[256,1]{1,0:T(8,128)S(1)} %get-tuple-element.50.inv_ref, bf16[256,512]{1,0:T(8,128)(2,1)S(1)} %get-tuple-element.51.centre_ref), custom_call_target="tpu_custom_call" | custom-call | flops 104857600 | bytes 2097152 | tf_op jit(solution)/shard_map/select/pallas_call | solution.py:32
  12.0 1.6 %collective-permute-start.3 = (bf16[16,16,512]{2,1,0:T(8,128)(2,1)S(1)}, bf16[16,16,512]{2,1,0:T(8,128)(2,1)S(1)}, u32[]{:S(2)}, u32[]{:S(2)}) collective-permute-start(bf16[16,16,512]{2,1,0:T(8,128)(2,1)S(1)} %get-tuple-element.53), channel_id=1, source_target_pairs={{0,2},{2,0},{1,3},{3,1},{4,6},{6,4},{5,7},{7,5},{8,10},{10,8},{9,1... | collective-permute-start | bytes 786440 | tf_op jit(solution)/shard_map/ppermute | solution.py:326
  13.6 0.0 collective-permute-done.2.near_ref
  13.6 1.3 %sums.1 = (f32[136,256]{1,0:T(8,128)S(1)}, f32[136,256]{1,0:T(8,128)S(1)}, f32[128,256]{1,0:T(8,128)S(1)}, f32[128,256]{1,0:T(8,128)S(1)}) custom-call(bf16[528,256]{1,0:T(8,128)(2,1)S(1)} %get-tuple-element.48.lead_ref, bf16[512,256]{1,0:T(8,128)(2,1)S(1)} %get-tuple-element.65.rest_ref, bf16[528,256]{1,0:T(8,128)(2,1)S(1)} %collective-permute-done.2.near_ref, ...), custom_call_target="tpu_custom_call" | custom-call | flops 104857600 | bytes 2097152 | tf_op jit(solution)/shard_map/sums/pallas_call | solution.py:32
  14.9 5.3 %collective-permute-done.3.refs_5_ = bf16[16,16,512]{2,1,0:T(8,128)(2,1)S(1)} collective-permute-done((bf16[16,16,512]{2,1,0:T(8,128)(2,1)S(1)}, bf16[16,16,512]{2,1,0:T(8,128)(2,1)S(1)}, u32[]{:S(2)}, u32[]{:S(2)}) %collective-permute-start.3) | collective-permute-done | bytes 262176 | tf_op jit(solution)/shard_map/ppermute | solution.py:326
  20.2 0.0 collective-permute-done.refs_0_.lead_ref
  20.2 0.7 %collective-permute-done.1.refs_1_.lead_ref = bf16[528,256]{1,0:T(8,128)(2,1)S(1)} collective-permute-done((bf16[528,256]{1,0:T(8,128)(2,1)S(1)}, bf16[528,256]{1,0:T(8,128)(2,1)S(1)}, u32[]{:S(2)}, u32[]{:S(2)}) %collective-permute-start.1) | collective-permute-done | bytes 270368 | tf_op jit(solution)/shard_map/ppermute | solution.py:333
  20.9 0.5 collective-permute-start.7
  21.4 0.4 collective-permute-start.9
  21.8 1.6 %collective-permute-start.4 = (bf16[512,256]{1,0:T(8,128)(2,1)S(1)}, bf16[512,256]{1,0:T(8,128)(2,1)S(1)}, u32[]{:S(2)}, u32[]{:S(2)}) collective-permute-start(bf16[512,256]{1,0:T(8,128)(2,1)S(1)} %get-tuple-element.65.rest_ref), channel_id=1, source_target_pairs={{0,4},{4,0},{8,12},{12,8},{1,5},{5,1},{9,13},{13,9},{2,6},{6,2},{1... | collective-permute-start | bytes 786440 | tf_op jit(solution)/shard_map/ppermute | solution.py:333
  23.4 1.0 %collective-permute-start.5 = (bf16[512,256]{1,0:T(8,128)(2,1)S(1)}, bf16[512,256]{1,0:T(8,128)(2,1)S(1)}, u32[]{:S(2)}, u32[]{:S(2)}) collective-permute-start(bf16[512,256]{1,0:T(8,128)(2,1)S(1)} %get-tuple-element.65.rest_ref), channel_id=1, source_target_pairs={{0,8},{4,12},{8,0},{12,4},{1,9},{5,13},{9,1},{13,5},{2,10},{6,14},... | collective-permute-start | bytes 786440 | tf_op jit(solution)/shard_map/ppermute | solution.py:333
  24.4 1.1 %select_lead.2 = (bf16[512,512]{1,0:T(8,128)(2,1)S(1)}, bf16[512,512]{1,0:T(8,128)(2,1)S(1)}, bf16[2,16,16,256]{3,2,1,0:T(8,128)(2,1)S(1)}, bf16[2,16,16,256]{3,2,1,0:T(8,128)(2,1)S(1)}) custom-call(f32[256,1]{1,0:T(8,128)S(1)} %get-tuple-element.50.inv_ref, bf16[256,512]{1,0:T(8,128)(2,1)S(1)} %get-tuple-element.51.centre_ref, ...), custom_call_target="tpu_custom_call" | custom-call | flops 6553600 | bytes 131072 | tf_op jit(solution)/shard_map/select_lead/pallas_call | solution.py:32
  25.5 1.6 %collective-permute-start.8 = (bf16[2,16,16,256]{3,2,1,0:T(8,128)(2,1)S(1)}, bf16[2,16,16,256]{3,2,1,0:T(8,128)(2,1)S(1)}, u32[]{:S(2)}, u32[]{:S(2)}) collective-permute-start(bf16[2,16,16,256]{3,2,1,0:T(8,128)(2,1)S(1)} %get-tuple-element.66), channel_id=1, source_target_pairs={{0,2},{2,0},{1,3},{3,1},{4,6},{6,4},{5,7},{7,5},{8,10},{10,8},{9,1... | collective-permute-start | bytes 786440 | tf_op jit(solution)/shard_map/ppermute | solution.py:326
  27.1 1.4 %sums_lead.3 = (bf16[256,512]{1,0:T(8,128)(2,1)S(1)}, f32[136,256]{1,0:T(8,128)S(1)}, f32[136,256]{1,0:T(8,128)S(1)}) custom-call(bf16[528,256]{1,0:T(8,128)(2,1)S(1)} %collective-permute-done.refs_0_.lead_ref, bf16[528,256]{1,0:T(8,128)(2,1)S(1)} %collective-permute-done.6.near_ref, ...), custom_call_target="tpu_custom_call", output_to_operand_aliasing={{1}: (4, {}), {2}: (5, {})} | custom-call | flops 6553600 | bytes 131072 | tf_op jit(solution)/shard_map/sums_lead/pallas_call | solution.py:32
  28.5 0.0 collective-permute-done.7.near_ref
  28.5 1.4 %sums_lead.4 = (bf16[256,512]{1,0:T(8,128)(2,1)S(1)}, f32[136,256]{1,0:T(8,128)S(1)}, f32[136,256]{1,0:T(8,128)S(1)}) custom-call(bf16[528,256]{1,0:T(8,128)(2,1)S(1)} %collective-permute-done.1.refs_1_.lead_ref, bf16[528,256]{1,0:T(8,128)(2,1)S(1)} %collective-permute-done.7.near_ref, ...), custom_call_target="tpu_custom_call", output_to_operand_aliasing={{1}: (4, {}), {2}: (5, {})} | custom-call | flops 6553600 | bytes 131072 | tf_op jit(solution)/shard_map/sums_lead/pallas_call | solution.py:32
  29.9 11.1 %collective-permute-done.4.refs_2_ = bf16[512,256]{1,0:T(8,128)(2,1)S(1)} collective-permute-done((bf16[512,256]{1,0:T(8,128)(2,1)S(1)}, bf16[512,256]{1,0:T(8,128)(2,1)S(1)}, u32[]{:S(2)}, u32[]{:S(2)}) %collective-permute-start.4) | collective-permute-done | bytes 262176 | tf_op jit(solution)/shard_map/ppermute | solution.py:333
  41.0 0.3 sums_rest.2
  41.3 0.5 select_rest.2
  41.8 0.0 collective-permute-done.9.refs_0_.lead_ref
  41.8 0.1 collective-permute-start.11
  41.9 1.6 %collective-permute-start.12 = (bf16[2,16,16,256]{3,2,1,0:T(8,128)(2,1)S(1)}, bf16[2,16,16,256]{3,2,1,0:T(8,128)(2,1)S(1)}, u32[]{:S(2)}, u32[]{:S(2)}) collective-permute-start(bf16[2,16,16,256]{3,2,1,0:T(8,128)(2,1)S(1)} %get-tuple-element.74), channel_id=1, source_target_pairs={{0,2},{2,0},{1,3},{3,1},{4,6},{6,4},{5,7},{7,5},{8,10},{10,8},{9,1... | collective-permute-start | bytes 786440 | tf_op jit(solution)/shard_map/ppermute | solution.py:326
  43.4 1.3 %collective-permute-start.10 = (bf16[512,256]{1,0:T(8,128)(2,1)S(1)}, bf16[512,256]{1,0:T(8,128)(2,1)S(1)}, u32[]{:S(2)}, u32[]{:S(2)}) collective-permute-start(bf16[512,256]{1,0:T(8,128)(2,1)S(1)} %collective-permute-done.5.refs_3_), channel_id=1, source_target_pairs={{0,4},{4,0},{8,12},{12,8},{1,5},{5,1},{9,13},{13,9},{2,6},{6,2},{1... | collective-permute-start | bytes 786440 | tf_op jit(solution)/shard_map/ppermute | solution.py:333
  44.7 0.6 select_lead.3
  45.3 0.6 collective-permute-start.13
  45.9 5.1 %collective-permute-done.12.refs_7_ = bf16[2,16,16,256]{3,2,1,0:T(8,128)(2,1)S(1)} collective-permute-done((bf16[2,16,16,256]{3,2,1,0:T(8,128)(2,1)S(1)}, bf16[2,16,16,256]{3,2,1,0:T(8,128)(2,1)S(1)}, u32[]{:S(2)}, u32[]{:S(2)}) %collective-permute-start.12) | collective-permute-done | bytes 262176 | tf_op jit(solution)/shard_map/ppermute | solution.py:326
  51.0 0.8 %collective-permute-done.10.refs_1_ = bf16[512,256]{1,0:T(8,128)(2,1)S(1)} collective-permute-done((bf16[512,256]{1,0:T(8,128)(2,1)S(1)}, bf16[512,256]{1,0:T(8,128)(2,1)S(1)}, u32[]{:S(2)}, u32[]{:S(2)}) %collective-permute-start.10) | collective-permute-done | bytes 262176 | tf_op jit(solution)/shard_map/ppermute | solution.py:333
  51.8 0.0 collective-permute-done.11.near_ref
  51.8 0.3 select_rest.3
  52.1 0.8 %collective-permute-start.14 = (bf16[1,16,16,256]{3,2,1,0:T(8,128)(2,1)S(1)}, bf16[1,16,16,256]{3,2,1,0:T(8,128)(2,1)S(1)}, u32[]{:S(2)}, u32[]{:S(2)}) collective-permute-start(bf16[1,16,16,256]{3,2,1,0:T(8,128)(2,1)S(1)} %get-tuple-element.85), channel_id=1, source_target_pairs={{0,2},{2,0},{1,3},{3,1},{4,6},{6,4},{5,7},{7,5},{8,10},{10,8},{9,1... | collective-permute-start | bytes 393224 | tf_op jit(solution)/shard_map/ppermute | solution.py:326
  52.9 1.4 %sums_lead.5 = (bf16[256,512]{1,0:T(8,128)(2,1)S(1)}, f32[136,256]{1,0:T(8,128)S(1)}, f32[136,256]{1,0:T(8,128)S(1)}) custom-call(bf16[528,256]{1,0:T(8,128)(2,1)S(1)} %collective-permute-done.9.refs_0_.lead_ref, bf16[528,256]{1,0:T(8,128)(2,1)S(1)} %collective-permute-done.11.near_ref, ...), custom_call_target="tpu_custom_call", output_to_operand_aliasing={{1}: (4, {}), {2}: (5, {})} | custom-call | flops 6553600 | bytes 131072 | tf_op jit(solution)/shard_map/sums_lead/pallas_call | solution.py:32
  54.3 1.4 %collective-permute-start.16 = (f32[136,256]{1,0:T(8,128)S(1)}, f32[136,256]{1,0:T(8,128)S(1)}, u32[]{:S(2)}, u32[]{:S(2)}) collective-permute-start(f32[136,256]{1,0:T(8,128)S(1)} %get-tuple-element.87), channel_id=1, source_target_pairs={{0,2},{2,0},{1,3},{3,1},{4,6},{6,4},{5,7},{7,5},{8,10},{10,8},{9,1... | collective-permute-start | bytes 417800 | tf_op jit(solution)/shard_map/ppermute | solution.py:326
  55.7 0.2 sums_rest.3
  55.9 0.8 %collective-permute-start.17 = (f32[128,256]{1,0:T(8,128)S(1)}, f32[128,256]{1,0:T(8,128)S(1)}, u32[]{:S(2)}, u32[]{:S(2)}) collective-permute-start(f32[128,256]{1,0:T(8,128)S(1)} %get-tuple-element.90), channel_id=1, source_target_pairs={{0,2},{2,0},{1,3},{3,1},{4,6},{6,4},{5,7},{7,5},{8,10},{10,8},{9,1... | collective-permute-start | bytes 393224 | tf_op jit(solution)/shard_map/ppermute | solution.py:326
  56.7 1.7 %collective-permute-done.14.refs_9_ = bf16[1,16,16,256]{3,2,1,0:T(8,128)(2,1)S(1)} collective-permute-done((bf16[1,16,16,256]{3,2,1,0:T(8,128)(2,1)S(1)}, bf16[1,16,16,256]{3,2,1,0:T(8,128)(2,1)S(1)}, u32[]{:S(2)}, u32[]{:S(2)}) %collective-permute-start.14) | collective-permute-done | bytes 131104 | tf_op jit(solution)/shard_map/ppermute | solution.py:326
  58.4 0.9 %gram.1.mine_ref = f32[16,16,128]{2,1,0:T(8,128)S(1)} custom-call(bf16[16,16,512]{2,1,0:T(8,128)(2,1)S(1)} %get-tuple-element.52.refs_0_, bf16[2,16,16,256]{3,2,1,0:T(8,128)(2,1)S(1)} %get-tuple-element.62.refs_1_, bf16[2,16,16,256]{3,2,1,0:T(8,128)(2,1)S(1)} %get-tuple-element.73.refs_2_, bf16[1,16,16,256]{3,2,1,0:T(8,128)(2,1)S(1)} %get-tuple-element.80.refs_3_, ...), custom_call_target="tpu_custom_call" | custom-call | tf_op jit(solution)/shard_map/gram/pallas_call | solution.py:32
  59.3 0.1 collective-permute-start.15
  59.4 3.6 %collective-permute-done.17.refs_3_ = f32[128,256]{1,0:T(8,128)S(1)} collective-permute-done((f32[128,256]{1,0:T(8,128)S(1)}, f32[128,256]{1,0:T(8,128)S(1)}, u32[]{:S(2)}, u32[]{:S(2)}) %collective-permute-start.17) | collective-permute-done | bytes 131104 | tf_op jit(solution)/shard_map/ppermute | solution.py:326
  63.0 0.0 collective-permute-done.16.refs_1_
  63.0 1.4 %finish.1 = (f32[128,512]{1,0:T(8,128)}, bf16[8,16,128]{2,1,0:T(8,128)(2,1)}) custom-call(f32[16,16,128]{2,1,0:T(8,128)S(1)} %gram.1.mine_ref, f32[16,16,128]{2,1,0:T(8,128)S(1)} %collective-permute-done.15.other_ref, f32[136,256]{1,0:T(8,128)S(1)} %get-tuple-element.86.refs_0_, f32[136,256]{1,0:T(8,128)S(1)} %collective-permute-done.16.refs_1_, ...), custom_call_target="tpu_custom_call" | custom-call | tf_op jit(solution)/shard_map/finish/pallas_call | solution.py:32
  (11 shorter events, 0.1 us)
Async XLA Ops:
  0.6 1.0 %copy-start.1 = (bf16[512,512]{1,0:T(8,128)(2,1)S(1)}, bf16[512,512]{1,0:T(8,128)(2,1)}, u32[]{:S(2)}) copy-start(bf16[512,512]{1,0:T(8,128)(2,1)} %emb_ref.1) | copy-start | bytes 1572868
  1.7 0.7 %copy-start.3 = (s32[512,1]{0,1:T(1,128)S(1)}, s32[512,1]{0,1:T(1,128)}, u32[]{:S(2)}) copy-start(s32[512,1]{0,1:T(1,128)} %param.6) | copy-start | bytes 6148
  2.4 11.2 %collective-permute-start.2 = (bf16[528,256]{1,0:T(8,128)(2,1)S(1)}, bf16[528,256]{1,0:T(8,128)(2,1)S(1)}, u32[]{:S(2)}, u32[]{:S(2)}) collective-permute-start(bf16[528,256]{1,0:T(8,128)(2,1)S(1)} %get-tuple-element.48.lead_ref), channel_id=1, source_target_pairs={{0,1},{1,0},{2,3},{3,2},{4,5},{5,4},{6,7},{7,6},{8,9},{9,8},{10,11... | collective-permute-start | bytes 811016 | tf_op jit(solution)/shard_map/ppermute | solution.py:330
  2.9 17.3 %collective-permute-start = (bf16[528,256]{1,0:T(8,128)(2,1)S(1)}, bf16[528,256]{1,0:T(8,128)(2,1)S(1)}, u32[]{:S(2)}, u32[]{:S(2)}) collective-permute-start(bf16[528,256]{1,0:T(8,128)(2,1)S(1)} %get-tuple-element.48.lead_ref), channel_id=1, source_target_pairs={{0,4},{4,0},{8,12},{12,8},{1,5},{5,1},{9,13},{13,9},{2,6},{6,2},{1... | collective-permute-start | bytes 811016 | tf_op jit(solution)/shard_map/ppermute | solution.py:333
  5.6 15.3 %collective-permute-start.1 = (bf16[528,256]{1,0:T(8,128)(2,1)S(1)}, bf16[528,256]{1,0:T(8,128)(2,1)S(1)}, u32[]{:S(2)}, u32[]{:S(2)}) collective-permute-start(bf16[528,256]{1,0:T(8,128)(2,1)S(1)} %get-tuple-element.48.lead_ref), channel_id=1, source_target_pairs={{0,8},{4,12},{8,0},{12,4},{1,9},{5,13},{9,1},{13,5},{2,10},{6,14},... | collective-permute-start | bytes 811016 | tf_op jit(solution)/shard_map/ppermute | solution.py:333
  8.2 1.6 %copy-start = (bf16[1024,1024]{1,0:T(8,128)(2,1)S(1)}, bf16[1024,1024]{1,0:T(8,128)(2,1)}, u32[]{:S(2)}) copy-start(bf16[1024,1024]{1,0:T(8,128)(2,1)} %cent_ref.1) | copy-start | bytes 6291460
  9.8 0.7 %copy-start.2 = (s32[1024]{0:T(1024)S(1)}, s32[1024]{0:T(1024)}, u32[]{:S(2)}) copy-start(s32[1024]{0:T(1024)} %param.7) | copy-start | bytes 12292
  12.0 8.2 %collective-permute-start.3 = (bf16[16,16,512]{2,1,0:T(8,128)(2,1)S(1)}, bf16[16,16,512]{2,1,0:T(8,128)(2,1)S(1)}, u32[]{:S(2)}, u32[]{:S(2)}) collective-permute-start(bf16[16,16,512]{2,1,0:T(8,128)(2,1)S(1)} %get-tuple-element.53), channel_id=1, source_target_pairs={{0,2},{2,0},{1,3},{3,1},{4,6},{6,4},{5,7},{7,5},{8,10},{10,8},{9,1... | collective-permute-start | bytes 786440 | tf_op jit(solution)/shard_map/ppermute | solution.py:326
  20.9 4.7 %collective-permute-start.6 = (bf16[528,256]{1,0:T(8,128)(2,1)S(1)}, bf16[528,256]{1,0:T(8,128)(2,1)S(1)}, u32[]{:S(2)}, u32[]{:S(2)}) collective-permute-start(bf16[528,256]{1,0:T(8,128)(2,1)S(1)} %collective-permute-done.refs_0_.lead_ref), channel_id=1, source_target_pairs={{0,1},{1,0},{2,3},{3,2},{4,5},{5,4},{6,7},{7,6},{8,9},{9,8},{10,11... | collective-permute-start | bytes 811016 | tf_op jit(solution)/shard_map/ppermute | solution.py:330
  20.9 7.6 %collective-permute-start.7 = (bf16[528,256]{1,0:T(8,128)(2,1)S(1)}, bf16[528,256]{1,0:T(8,128)(2,1)S(1)}, u32[]{:S(2)}, u32[]{:S(2)}) collective-permute-start(bf16[528,256]{1,0:T(8,128)(2,1)S(1)} %collective-permute-done.1.refs_1_.lead_ref), channel_id=1, source_target_pairs={{0,1},{1,0},{2,3},{3,2},{4,5},{5,4},{6,7},{7,6},{8,9},{9,8},{10,11... | collective-permute-start | bytes 811016 | tf_op jit(solution)/shard_map/ppermute | solution.py:330
  21.4 20.4 %collective-permute-start.9 = (bf16[528,256]{1,0:T(8,128)(2,1)S(1)}, bf16[528,256]{1,0:T(8,128)(2,1)S(1)}, u32[]{:S(2)}, u32[]{:S(2)}) collective-permute-start(bf16[528,256]{1,0:T(8,128)(2,1)S(1)} %collective-permute-done.1.refs_1_.lead_ref), channel_id=1, source_target_pairs={{0,4},{4,0},{8,12},{12,8},{1,5},{5,1},{9,13},{13,9},{2,6},{6,2},{1... | collective-permute-start | bytes 811016 | tf_op jit(solution)/shard_map/ppermute | solution.py:333
  21.8 19.2 %collective-permute-start.4 = (bf16[512,256]{1,0:T(8,128)(2,1)S(1)}, bf16[512,256]{1,0:T(8,128)(2,1)S(1)}, u32[]{:S(2)}, u32[]{:S(2)}) collective-permute-start(bf16[512,256]{1,0:T(8,128)(2,1)S(1)} %get-tuple-element.65.rest_ref), channel_id=1, source_target_pairs={{0,4},{4,0},{8,12},{12,8},{1,5},{5,1},{9,13},{13,9},{2,6},{6,2},{1... | collective-permute-start | bytes 786440 | tf_op jit(solution)/shard_map/ppermute | solution.py:333
  23.4 17.6 %collective-permute-start.5 = (bf16[512,256]{1,0:T(8,128)(2,1)S(1)}, bf16[512,256]{1,0:T(8,128)(2,1)S(1)}, u32[]{:S(2)}, u32[]{:S(2)}) collective-permute-start(bf16[512,256]{1,0:T(8,128)(2,1)S(1)} %get-tuple-element.65.rest_ref), channel_id=1, source_target_pairs={{0,8},{4,12},{8,0},{12,4},{1,9},{5,13},{9,1},{13,5},{2,10},{6,14},... | collective-permute-start | bytes 786440 | tf_op jit(solution)/shard_map/ppermute | solution.py:333
  25.5 15.5 %collective-permute-start.8 = (bf16[2,16,16,256]{3,2,1,0:T(8,128)(2,1)S(1)}, bf16[2,16,16,256]{3,2,1,0:T(8,128)(2,1)S(1)}, u32[]{:S(2)}, u32[]{:S(2)}) collective-permute-start(bf16[2,16,16,256]{3,2,1,0:T(8,128)(2,1)S(1)} %get-tuple-element.66), channel_id=1, source_target_pairs={{0,2},{2,0},{1,3},{3,1},{4,6},{6,4},{5,7},{7,5},{8,10},{10,8},{9,1... | collective-permute-start | bytes 786440 | tf_op jit(solution)/shard_map/ppermute | solution.py:326
  41.8 10.0 %collective-permute-start.11 = (bf16[528,256]{1,0:T(8,128)(2,1)S(1)}, bf16[528,256]{1,0:T(8,128)(2,1)S(1)}, u32[]{:S(2)}, u32[]{:S(2)}) collective-permute-start(bf16[528,256]{1,0:T(8,128)(2,1)S(1)} %collective-permute-done.9.refs_0_.lead_ref), channel_id=1, source_target_pairs={{0,1},{1,0},{2,3},{3,2},{4,5},{5,4},{6,7},{7,6},{8,9},{9,8},{10,11... | collective-permute-start | bytes 811016 | tf_op jit(solution)/shard_map/ppermute | solution.py:330
  41.9 9.2 %collective-permute-start.12 = (bf16[2,16,16,256]{3,2,1,0:T(8,128)(2,1)S(1)}, bf16[2,16,16,256]{3,2,1,0:T(8,128)(2,1)S(1)}, u32[]{:S(2)}, u32[]{:S(2)}) collective-permute-start(bf16[2,16,16,256]{3,2,1,0:T(8,128)(2,1)S(1)} %get-tuple-element.74), channel_id=1, source_target_pairs={{0,2},{2,0},{1,3},{3,1},{4,6},{6,4},{5,7},{7,5},{8,10},{10,8},{9,1... | collective-permute-start | bytes 786440 | tf_op jit(solution)/shard_map/ppermute | solution.py:326
  43.4 8.4 %collective-permute-start.10 = (bf16[512,256]{1,0:T(8,128)(2,1)S(1)}, bf16[512,256]{1,0:T(8,128)(2,1)S(1)}, u32[]{:S(2)}, u32[]{:S(2)}) collective-permute-start(bf16[512,256]{1,0:T(8,128)(2,1)S(1)} %collective-permute-done.5.refs_3_), channel_id=1, source_target_pairs={{0,4},{4,0},{8,12},{12,8},{1,5},{5,1},{9,13},{13,9},{2,6},{6,2},{1... | collective-permute-start | bytes 786440 | tf_op jit(solution)/shard_map/ppermute | solution.py:333
  45.3 11.4 %collective-permute-start.13 = (bf16[1,16,16,256]{3,2,1,0:T(8,128)(2,1)S(1)}, bf16[1,16,16,256]{3,2,1,0:T(8,128)(2,1)S(1)}, u32[]{:S(2)}, u32[]{:S(2)}) collective-permute-start(bf16[1,16,16,256]{3,2,1,0:T(8,128)(2,1)S(1)} %get-tuple-element.84), channel_id=1, source_target_pairs={{0,2},{2,0},{1,3},{3,1},{4,6},{6,4},{5,7},{7,5},{8,10},{10,8},{9,1... | collective-permute-start | bytes 393224 | tf_op jit(solution)/shard_map/ppermute | solution.py:326
  52.1 6.3 %collective-permute-start.14 = (bf16[1,16,16,256]{3,2,1,0:T(8,128)(2,1)S(1)}, bf16[1,16,16,256]{3,2,1,0:T(8,128)(2,1)S(1)}, u32[]{:S(2)}, u32[]{:S(2)}) collective-permute-start(bf16[1,16,16,256]{3,2,1,0:T(8,128)(2,1)S(1)} %get-tuple-element.85), channel_id=1, source_target_pairs={{0,2},{2,0},{1,3},{3,1},{4,6},{6,4},{5,7},{7,5},{8,10},{10,8},{9,1... | collective-permute-start | bytes 393224 | tf_op jit(solution)/shard_map/ppermute | solution.py:326
  54.3 8.7 %collective-permute-start.16 = (f32[136,256]{1,0:T(8,128)S(1)}, f32[136,256]{1,0:T(8,128)S(1)}, u32[]{:S(2)}, u32[]{:S(2)}) collective-permute-start(f32[136,256]{1,0:T(8,128)S(1)} %get-tuple-element.87), channel_id=1, source_target_pairs={{0,2},{2,0},{1,3},{3,1},{4,6},{6,4},{5,7},{7,5},{8,10},{10,8},{9,1... | collective-permute-start | bytes 417800 | tf_op jit(solution)/shard_map/ppermute | solution.py:326
  55.9 7.1 %collective-permute-start.17 = (f32[128,256]{1,0:T(8,128)S(1)}, f32[128,256]{1,0:T(8,128)S(1)}, u32[]{:S(2)}, u32[]{:S(2)}) collective-permute-start(f32[128,256]{1,0:T(8,128)S(1)} %get-tuple-element.90), channel_id=1, source_target_pairs={{0,2},{2,0},{1,3},{3,1},{4,6},{6,4},{5,7},{7,5},{8,10},{10,8},{9,1... | collective-permute-start | bytes 393224 | tf_op jit(solution)/shard_map/ppermute | solution.py:326
  59.3 3.6 %collective-permute-start.15 = (f32[16,16,128]{2,1,0:T(8,128)S(1)}, f32[16,16,128]{2,1,0:T(8,128)S(1)}, u32[]{:S(2)}, u32[]{:S(2)}) collective-permute-start(f32[16,16,128]{2,1,0:T(8,128)S(1)} %gram.1.mine_ref), channel_id=1, source_target_pairs={{0,1},{1,0},{2,3},{3,2},{4,5},{5,4},{6,7},{7,6},{8,9},{9,8},{10,11... | collective-permute-start | bytes 393224 | tf_op jit(solution)/shard_map/ppermute | solution.py:330

commit v8 on v7

--- a/solution.py
+++ b/solution.py
@@ -63,7 +63,8 @@
 def pack_kernel(emb_ref, cid_ref, lead_ref, rest_ref):
     docs = emb_ref.shape[0]
     lead_ref[:docs, :] = emb_ref[:, :PREFIX]
-    rest_ref[...] = emb_ref[:, PREFIX:]
+    rest_ref[:docs, :] = emb_ref[:, PREFIX:]
+    rest_ref[docs:, :] = jnp.zeros((META, rest_ref.shape[1]), BF16)
     cid = cid_ref[...]
     high, low = (cid // DIGIT + 1).astype(F32), (cid % DIGIT).astype(F32)
     rows = []
@@ -123,10 +124,10 @@
 
 
 def select_kernel(lead_ref, rest_ref, inv_ref, centre_ref, *row_refs):
-    docs = rest_ref.shape[0]
+    docs = rest_ref.shape[0] - META
     pick = picked(lead_ref, inv_ref)
     groups, packed, _ = row_refs[0].shape
-    for columns, at in ((lead_ref[:docs, :], 0), (rest_ref[...], PREFIX)):
+    for columns, at in ((lead_ref[:docs, :], 0), (rest_ref[:docs, :], PREFIX)):
         width = columns.shape[1]
         rows = centred(pick, centre_ref[:, at : at + width], columns)
         rows = rows.reshape(len(row_refs), groups, packed, width)
@@ -149,7 +150,8 @@
 def select_rest_kernel(count, subs, centre_ref, *refs):
     pick_refs, rest_refs, row_refs = refs[:count], refs[count : 2 * count], refs[2 * count :]
     for i in range(count):
-        rows = centred(pick_refs[i][...], centre_ref[:, PREFIX:], rest_refs[i][...])
+        pick = pick_refs[i][...]
+        rows = centred(pick, centre_ref[:, PREFIX:], rest_refs[i][: pick.shape[1], :])
         rows = rows.reshape((subs,) + row_refs[0].shape[1:])
         for t in range(subs):
             row_refs[t][i] = rows[t]
@@ -196,7 +198,7 @@
 def sums_kernel(subs, lead_ref, rest_ref, near_ref, cent_ref, own_prefix_ref, *new):
     weights = soft_weights(lead_ref, near_ref, cent_ref, own_prefix_ref)
     add_lead(weights, lead_ref, (), new[:subs])
-    add_rest(weights.astype(BF16), rest_ref[...], (), new[subs:])
+    add_rest(weights.astype(BF16), rest_ref[: weights.shape[1], :], (), new[subs:])
 
 
 def sums_lead_kernel(subs, lead_ref, near_ref, cent_ref, own_prefix_ref, *refs):
@@ -208,7 +210,7 @@
 
 def sums_rest_kernel(count, subs, *refs):
     weights_refs, rest_refs, old, new = refs[:count], refs[count : 2 * count], refs[-2 * subs : -subs], refs[-subs:]
-    total = sum(dot(w[...], rest[...]) for w, rest in zip(weights_refs, rest_refs))
+    total = sum(dot(w[...], rest[: w.shape[1], :]) for w, rest in zip(weights_refs, rest_refs))
     per = new[0].shape[0]
     for t in range(subs):
         new[t][...] = old[t][...] + total[t * per : (t + 1) * per]
@@ -341,7 +343,7 @@
     lead, rest = call(
         pack_kernel,
         "pack",
-        [shape((docs + META, PREFIX), BF16), shape((docs, half - PREFIX), BF16)],
+        [shape((docs + META, PREFIX), BF16), shape((docs + META, half - PREFIX), BF16)],
         [embeddings, cluster_id.reshape(1, docs)],
     )
     leads, rests = {0: lead}, {0: rest}
@@ -363,7 +365,7 @@
 
     lead_sum, rest_sum = shape((per + SUBLANES, PREFIX), F32), shape((per, half - PREFIX), F32)
     sum_shapes = [lead_sum] * subs + [rest_sum] * subs
-    own_cost, other_cost = 2 * 1024 * 1024, 128 * 1024
+    own_cost, other_cost = 2 * 1024 * 1024, 0
 
     prefix = near(lead)
     found = call(
@@ -412,9 +414,9 @@
             weights.append(weight)
         if last:
             lead_sums = across(lead_sums)
-            before = (prefixes, members[:-1])
+            before = (found, members[:-1])
         else:
-            before = (found, weights, members)
+            before = (found, members)
         rests.update(zip(group, tied([rests[bits] for bits in group], before)))
         for bits in group:
             send(rests, bits)
@@ -426,6 +428,8 @@
             [centre] + picks + [rests[bits] for bits in group],
             cost=other_cost,
         )
+        if last:
+            found = tied(found, members)
         members.append(across(found))
         rest_sums = call(
             functools.partial(sums_rest_kernel, count, subs),

time: 64.6 us -> 59.7 us (0.924)
  waiting for transfers between devices: 28.3 us -> 22.7 us
  starting transfers between devices: 19 us -> 19.7 us
    ppermute x7, waiting for transfers between devices: 15.7 us -> 10.7 us  [across(): lax.ppermute(values[t], 'sub', [(i, (i + t) % subs) for i in range(subs)])]
    ppermute x7, starting transfers between devices: 8.24 us -> 10.6 us  [across(): lax.ppermute(values[t], 'sub', [(i, (i + t) % subs) for i in range(subs)])]
    ppermute x6, starting transfers between devices: 9.6 us -> 8.05 us  [swap(): return lax.ppermute(value, 'rows', [(i, i ^ bit) for i in range(rows)])]
    ppermute x6, waiting for transfers between devices: 12.6 us -> 11.9 us  [swap(): return lax.ppermute(value, 'rows', [(i, i ^ bit) for i in range(rows)])]
  transfers between devices with their start and end apart: 18 -> 18, of which waited for: 7 -> 8; matrix products, arithmetic and copies ran while one was open for 0% -> 0% of each run, Pallas kernels for 17% -> 18%
where the time goes in v8:
time: 59.7 us; the launch traced here: 59.4 us
  waiting for transfers between devices  22.7 us (38%)
  starting transfers between devices  19.7 us (33%)
  Pallas kernels  12.2 us (20%)
  local copies, waits for them, and re-layouts  3.99 us (7%)
  between operations  0.77 us (1%)
    pallas_call x15, Pallas kernels, call(): pl.pallas_call(kernel, out_shape=tuple(out_shape), in_specs=[place(at) fo...  12.2 us
    ppermute x6, waiting for transfers between devices, swap(): return lax.ppermute(value, 'rows', [(i, i ^ bit) for i in range(rows)])  11.9 us
    ppermute x7, waiting for transfers between devices, across(): lax.ppermute(values[t], 'sub', [(i, (i + t) % subs) for i in range(subs)])  10.7 us
    ppermute x7, starting transfers between devices, across(): lax.ppermute(values[t], 'sub', [(i, (i + t) % subs) for i in range(subs)])  10.6 us
    ppermute x6, starting transfers between devices, swap(): return lax.ppermute(value, 'rows', [(i, i ^ bit) for i in range(rows)])  8.05 us
    unnamed x8, local copies, waits for them, and re-layouts  3.99 us
  transfers between devices with their start and end apart: 18, of which 8 were waited for; matrix products, arithmetic and copies ran while one was open for 0% of the time, Pallas kernels for 18%

profile of v8, /device:TPU:0, one launch (start us, length us, event | category | flops | bytes accessed | tf_op | source)
XLA Modules:
  0.0 59.4 jit_solution(16894515948688922333)
XLA Ops:
  0.6 1.0 %copy-done.1 = bf16[512,512]{1,0:T(8,128)(2,1)S(1)} copy-done((bf16[512,512]{1,0:T(8,128)(2,1)S(1)}, bf16[512,512]{1,0:T(8,128)(2,1)}, u32[]{:S(2)}) %copy-start.1) | copy-done | bytes 524312
  1.7 0.7 %copy-done.3 = s32[512,1]{0,1:T(1,128)S(1)} copy-done((s32[512,1]{0,1:T(1,128)S(1)}, s32[512,1]{0,1:T(1,128)}, u32[]{:S(2)}) %copy-start.3) | copy-done | bytes 2072
  2.4 0.5 collective-permute-start.2
  2.9 3.7 %collective-permute-start.1 = (bf16[528,256]{1,0:T(8,128)(2,1)S(1)}, bf16[528,256]{1,0:T(8,128)(2,1)S(1)}, u32[]{:S(2)}, u32[]{:S(2)}) collective-permute-start(bf16[528,256]{1,0:T(8,128)(2,1)S(1)} %get-tuple-element.50.lead_ref), channel_id=1, source_target_pairs={{0,8},{4,12},{8,0},{12,4},{1,9},{5,13},{9,1},{13,5},{2,10},{6,14},... | collective-permute-start | bytes 811016 | tf_op jit(solution)/shard_map/ppermute | solution.py:335
  6.6 1.6 %collective-permute-start = (bf16[528,256]{1,0:T(8,128)(2,1)S(1)}, bf16[528,256]{1,0:T(8,128)(2,1)S(1)}, u32[]{:S(2)}, u32[]{:S(2)}) collective-permute-start(bf16[528,256]{1,0:T(8,128)(2,1)S(1)} %get-tuple-element.50.lead_ref), channel_id=1, source_target_pairs={{0,4},{4,0},{8,12},{12,8},{1,5},{5,1},{9,13},{13,9},{2,6},{6,2},{1... | collective-permute-start | bytes 811016 | tf_op jit(solution)/shard_map/ppermute | solution.py:335
  8.2 1.6 %copy-done = bf16[1024,1024]{1,0:T(8,128)(2,1)S(1)} copy-done((bf16[1024,1024]{1,0:T(8,128)(2,1)S(1)}, bf16[1024,1024]{1,0:T(8,128)(2,1)}, u32[]{:S(2)}) %copy-start) | copy-done | bytes 2097176
  9.8 0.7 %copy-done.2 = s32[1024]{0:T(1024)S(1)} copy-done((s32[1024]{0:T(1024)S(1)}, s32[1024]{0:T(1024)}, u32[]{:S(2)}) %copy-start.2) | copy-done | bytes 4120
  10.4 0.8 %prep.1 = (f32[256,1]{1,0:T(8,128)S(1)}, bf16[256,512]{1,0:T(8,128)(2,1)S(1)}, bf16[256,256]{1,0:T(8,128)(2,1)S(1)}, bf16[128,512]{1,0:T(8,128)(2,1)S(1)}, bf16[1024,256]{1,0:T(8,128)(2,1)S(1)}) custom-call(s32[1,1024]{1,0:T(1,128)S(1)} %bitcast.3, bf16[1024,1024]{1,0:T(8,128)(2,1)S(1)} %copy-done), custom_call_target="tpu_custom_call" | custom-call | flops 209715200 | bytes 4194304 | tf_op jit(solution)/shard_map/prep/pallas_call | solution.py:32
  11.3 0.7 %select.1 = (bf16[16,16,512]{2,1,0:T(8,128)(2,1)S(1)}, bf16[16,16,512]{2,1,0:T(8,128)(2,1)S(1)}) custom-call(bf16[528,256]{1,0:T(8,128)(2,1)S(1)} %get-tuple-element.50.lead_ref, bf16[528,256]{1,0:T(8,128)(2,1)S(1)} %get-tuple-element.67.rest_ref, f32[256,1]{1,0:T(8,128)S(1)} %get-tuple-element.52.inv_ref, bf16[256,512]{1,0:T(8,128)(2,1)S(1)} %get-tuple-element.53.centre_ref), custom_call_target="tpu_custom_call" | custom-call | flops 104857600 | bytes 2097152 | tf_op jit(solution)/shard_map/select/pallas_call | solution.py:32
  12.0 1.5 %collective-permute-start.3 = (bf16[16,16,512]{2,1,0:T(8,128)(2,1)S(1)}, bf16[16,16,512]{2,1,0:T(8,128)(2,1)S(1)}, u32[]{:S(2)}, u32[]{:S(2)}) collective-permute-start(bf16[16,16,512]{2,1,0:T(8,128)(2,1)S(1)} %get-tuple-element.55), channel_id=1, source_target_pairs={{0,2},{2,0},{1,3},{3,1},{4,6},{6,4},{5,7},{7,5},{8,10},{10,8},{9,1... | collective-permute-start | bytes 786440 | tf_op jit(solution)/shard_map/ppermute | solution.py:328
  13.6 0.3 collective-permute-start.5
  13.9 0.0 collective-permute-done.2.near_ref
  13.9 0.5 collective-permute-start.4
  14.4 1.3 %sums.1 = (f32[136,256]{1,0:T(8,128)S(1)}, f32[136,256]{1,0:T(8,128)S(1)}, f32[128,256]{1,0:T(8,128)S(1)}, f32[128,256]{1,0:T(8,128)S(1)}) custom-call(bf16[528,256]{1,0:T(8,128)(2,1)S(1)} %get-tuple-element.50.lead_ref, bf16[528,256]{1,0:T(8,128)(2,1)S(1)} %get-tuple-element.67.rest_ref, bf16[528,256]{1,0:T(8,128)(2,1)S(1)} %collective-permute-done.2.near_ref, ...), custom_call_target="tpu_custom_call" | custom-call | flops 104857600 | bytes 2097152 | tf_op jit(solution)/shard_map/sums/pallas_call | solution.py:32
  15.7 4.5 %collective-permute-done.3.refs_5_ = bf16[16,16,512]{2,1,0:T(8,128)(2,1)S(1)} collective-permute-done((bf16[16,16,512]{2,1,0:T(8,128)(2,1)S(1)}, bf16[16,16,512]{2,1,0:T(8,128)(2,1)S(1)}, u32[]{:S(2)}, u32[]{:S(2)}) %collective-permute-start.3) | collective-permute-done | bytes 262176 | tf_op jit(solution)/shard_map/ppermute | solution.py:328
  20.2 0.7 %collective-permute-done.refs_0_.lead_ref = bf16[528,256]{1,0:T(8,128)(2,1)S(1)} collective-permute-done((bf16[528,256]{1,0:T(8,128)(2,1)S(1)}, bf16[528,256]{1,0:T(8,128)(2,1)S(1)}, u32[]{:S(2)}, u32[]{:S(2)}) %collective-permute-start) | collective-permute-done | bytes 270368 | tf_op jit(solution)/shard_map/ppermute | solution.py:335
  20.9 1.1 %select_lead.2 = (bf16[512,512]{1,0:T(8,128)(2,1)S(1)}, bf16[512,512]{1,0:T(8,128)(2,1)S(1)}, bf16[2,16,16,256]{3,2,1,0:T(8,128)(2,1)S(1)}, bf16[2,16,16,256]{3,2,1,0:T(8,128)(2,1)S(1)}) custom-call(f32[256,1]{1,0:T(8,128)S(1)} %get-tuple-element.52.inv_ref, bf16[256,512]{1,0:T(8,128)(2,1)S(1)} %get-tuple-element.53.centre_ref, ...), custom_call_target="tpu_custom_call" | custom-call | tf_op jit(solution)/shard_map/select_lead/pallas_call | solution.py:32
  22.0 2.0 %collective-permute-start.6 = (bf16[2,16,16,256]{3,2,1,0:T(8,128)(2,1)S(1)}, bf16[2,16,16,256]{3,2,1,0:T(8,128)(2,1)S(1)}, u32[]{:S(2)}, u32[]{:S(2)}) collective-permute-start(bf16[2,16,16,256]{3,2,1,0:T(8,128)(2,1)S(1)} %get-tuple-element.68), channel_id=1, source_target_pairs={{0,2},{2,0},{1,3},{3,1},{4,6},{6,4},{5,7},{7,5},{8,10},{10,8},{9,1... | collective-permute-start | bytes 786440 | tf_op jit(solution)/shard_map/ppermute | solution.py:328
  24.0 0.5 collective-permute-start.8
  24.5 6.7 %collective-permute-done.5.refs_3_ = bf16[528,256]{1,0:T(8,128)(2,1)S(1)} collective-permute-done((bf16[528,256]{1,0:T(8,128)(2,1)S(1)}, bf16[528,256]{1,0:T(8,128)(2,1)S(1)}, u32[]{:S(2)}, u32[]{:S(2)}) %collective-permute-start.5) | collective-permute-done | bytes 270368 | tf_op jit(solution)/shard_map/ppermute | solution.py:335
  31.2 0.6 %collective-permute-start.7 = (bf16[528,256]{1,0:T(8,128)(2,1)S(1)}, bf16[528,256]{1,0:T(8,128)(2,1)S(1)}, u32[]{:S(2)}, u32[]{:S(2)}) collective-permute-start(bf16[528,256]{1,0:T(8,128)(2,1)S(1)} %collective-permute-done.1.refs_1_.lead_ref), channel_id=1, source_target_pairs={{0,4},{4,0},{8,12},{12,8},{1,5},{5,1},{9,13},{13,9},{2,6},{6,2},{1... | collective-permute-start | bytes 811016 | tf_op jit(solution)/shard_map/ppermute | solution.py:335
  31.8 0.0 collective-permute-done.4.refs_2_
  31.8 0.0 collective-permute-done.6.refs_6_
  31.8 1.4 %collective-permute-start.10 = (bf16[528,256]{1,0:T(8,128)(2,1)S(1)}, bf16[528,256]{1,0:T(8,128)(2,1)S(1)}, u32[]{:S(2)}, u32[]{:S(2)}) collective-permute-start(bf16[528,256]{1,0:T(8,128)(2,1)S(1)} %collective-permute-done.5.refs_3_), channel_id=1, source_target_pairs={{0,4},{4,0},{8,12},{12,8},{1,5},{5,1},{9,13},{13,9},{2,6},{6,2},{1... | collective-permute-start | bytes 811016 | tf_op jit(solution)/shard_map/ppermute | solution.py:335
  33.2 0.4 select_rest.2
  33.7 1.6 %collective-permute-start.11 = (bf16[2,16,16,256]{3,2,1,0:T(8,128)(2,1)S(1)}, bf16[2,16,16,256]{3,2,1,0:T(8,128)(2,1)S(1)}, u32[]{:S(2)}, u32[]{:S(2)}) collective-permute-start(bf16[2,16,16,256]{3,2,1,0:T(8,128)(2,1)S(1)} %get-tuple-element.72), channel_id=1, source_target_pairs={{0,2},{2,0},{1,3},{3,1},{4,6},{6,4},{5,7},{7,5},{8,10},{10,8},{9,1... | collective-permute-start | bytes 786440 | tf_op jit(solution)/shard_map/ppermute | solution.py:328
  35.3 1.4 %sums_lead.3 = (bf16[256,512]{1,0:T(8,128)(2,1)S(1)}, f32[136,256]{1,0:T(8,128)S(1)}, f32[136,256]{1,0:T(8,128)S(1)}) custom-call(bf16[528,256]{1,0:T(8,128)(2,1)S(1)} %collective-permute-done.refs_0_.lead_ref, bf16[528,256]{1,0:T(8,128)(2,1)S(1)} %collective-permute-done.9.near_ref, ...), custom_call_target="tpu_custom_call", output_to_operand_aliasing={{1}: (4, {}), {2}: (5, {})} | custom-call | tf_op jit(solution)/shard_map/sums_lead/pallas_call | solution.py:32
  36.7 1.4 %sums_lead.4 = (bf16[256,512]{1,0:T(8,128)(2,1)S(1)}, f32[136,256]{1,0:T(8,128)S(1)}, f32[136,256]{1,0:T(8,128)S(1)}) custom-call(bf16[528,256]{1,0:T(8,128)(2,1)S(1)} %collective-permute-done.1.refs_1_.lead_ref, bf16[528,256]{1,0:T(8,128)(2,1)S(1)} %collective-permute-done.8.near_ref, ...), custom_call_target="tpu_custom_call", output_to_operand_aliasing={{1}: (4, {}), {2}: (5, {})} | custom-call | tf_op jit(solution)/shard_map/sums_lead/pallas_call | solution.py:32
  38.1 0.3 sums_rest.2
  38.4 2.2 %collective-permute-done.7.refs_0_.lead_ref = bf16[528,256]{1,0:T(8,128)(2,1)S(1)} collective-permute-done((bf16[528,256]{1,0:T(8,128)(2,1)S(1)}, bf16[528,256]{1,0:T(8,128)(2,1)S(1)}, u32[]{:S(2)}, u32[]{:S(2)}) %collective-permute-start.7) | collective-permute-done | bytes 270368 | tf_op jit(solution)/shard_map/ppermute | solution.py:335
  40.6 0.6 select_lead.3
  41.2 1.7 %collective-permute-start.12 = (bf16[1,16,16,256]{3,2,1,0:T(8,128)(2,1)S(1)}, bf16[1,16,16,256]{3,2,1,0:T(8,128)(2,1)S(1)}, u32[]{:S(2)}, u32[]{:S(2)}) collective-permute-start(bf16[1,16,16,256]{3,2,1,0:T(8,128)(2,1)S(1)} %get-tuple-element.84), channel_id=1, source_target_pairs={{0,2},{2,0},{1,3},{3,1},{4,6},{6,4},{5,7},{7,5},{8,10},{10,8},{9,1... | collective-permute-start | bytes 393224 | tf_op jit(solution)/shard_map/ppermute | solution.py:328
  42.8 0.0 collective-permute-done.11.refs_7_
  42.8 2.3 %collective-permute-done.10.refs_1_ = bf16[528,256]{1,0:T(8,128)(2,1)S(1)} collective-permute-done((bf16[528,256]{1,0:T(8,128)(2,1)S(1)}, bf16[528,256]{1,0:T(8,128)(2,1)S(1)}, u32[]{:S(2)}, u32[]{:S(2)}) %collective-permute-start.10) | collective-permute-done | bytes 270368 | tf_op jit(solution)/shard_map/ppermute | solution.py:335
  45.2 0.3 select_rest.3
  45.5 1.7 %collective-permute-done.12.refs_8_ = bf16[1,16,16,256]{3,2,1,0:T(8,128)(2,1)S(1)} collective-permute-done((bf16[1,16,16,256]{3,2,1,0:T(8,128)(2,1)S(1)}, bf16[1,16,16,256]{3,2,1,0:T(8,128)(2,1)S(1)}, u32[]{:S(2)}, u32[]{:S(2)}) %collective-permute-start.12) | collective-permute-done | bytes 131104 | tf_op jit(solution)/shard_map/ppermute | solution.py:328
  47.1 1.6 %collective-permute-start.13 = (bf16[1,16,16,256]{3,2,1,0:T(8,128)(2,1)S(1)}, bf16[1,16,16,256]{3,2,1,0:T(8,128)(2,1)S(1)}, u32[]{:S(2)}, u32[]{:S(2)}) collective-permute-start(bf16[1,16,16,256]{3,2,1,0:T(8,128)(2,1)S(1)} %get-tuple-element.89), channel_id=1, source_target_pairs={{0,2},{2,0},{1,3},{3,1},{4,6},{6,4},{5,7},{7,5},{8,10},{10,8},{9,1... | collective-permute-start | bytes 393224 | tf_op jit(solution)/shard_map/ppermute | solution.py:328
  48.7 0.0 collective-permute-done.15.near_ref
  48.7 1.4 %sums_lead.5 = (bf16[256,512]{1,0:T(8,128)(2,1)S(1)}, f32[136,256]{1,0:T(8,128)S(1)}, f32[136,256]{1,0:T(8,128)S(1)}) custom-call(bf16[528,256]{1,0:T(8,128)(2,1)S(1)} %collective-permute-done.7.refs_0_.lead_ref, bf16[528,256]{1,0:T(8,128)(2,1)S(1)} %collective-permute-done.15.near_ref, ...), custom_call_target="tpu_custom_call", output_to_operand_aliasing={{1}: (4, {}), {2}: (5, {})} | custom-call | tf_op jit(solution)/shard_map/sums_lead/pallas_call | solution.py:32
  50.1 0.5 collective-permute-start.16
  50.6 0.2 sums_rest.3
  50.8 1.7 %collective-permute-start.17 = (f32[128,256]{1,0:T(8,128)S(1)}, f32[128,256]{1,0:T(8,128)S(1)}, u32[]{:S(2)}, u32[]{:S(2)}) collective-permute-start(f32[128,256]{1,0:T(8,128)S(1)} %get-tuple-element.94), channel_id=1, source_target_pairs={{0,2},{2,0},{1,3},{3,1},{4,6},{6,4},{5,7},{7,5},{8,10},{10,8},{9,1... | collective-permute-start | bytes 393224 | tf_op jit(solution)/shard_map/ppermute | solution.py:328
  52.5 0.1 collective-permute-done.13.refs_9_
  52.6 0.9 %gram.1.mine_ref = f32[16,16,128]{2,1,0:T(8,128)S(1)} custom-call(bf16[16,16,512]{2,1,0:T(8,128)(2,1)S(1)} %get-tuple-element.54.refs_0_, bf16[2,16,16,256]{3,2,1,0:T(8,128)(2,1)S(1)} %get-tuple-element.64.refs_1_, bf16[2,16,16,256]{3,2,1,0:T(8,128)(2,1)S(1)} %get-tuple-element.71.refs_2_, bf16[1,16,16,256]{3,2,1,0:T(8,128)(2,1)S(1)} %get-tuple-element.82.refs_3_, ...), custom_call_target="tpu_custom_call" | custom-call | tf_op jit(solution)/shard_map/gram/pallas_call | solution.py:32
  53.5 0.1 collective-permute-start.14
  53.6 4.5 %collective-permute-done.17.refs_3_ = f32[128,256]{1,0:T(8,128)S(1)} collective-permute-done((f32[128,256]{1,0:T(8,128)S(1)}, f32[128,256]{1,0:T(8,128)S(1)}, u32[]{:S(2)}, u32[]{:S(2)}) %collective-permute-start.17) | collective-permute-done | bytes 131104 | tf_op jit(solution)/shard_map/ppermute | solution.py:328
  58.1 0.0 collective-permute-done.16.refs_1_
  58.1 1.4 %finish.1 = (f32[128,512]{1,0:T(8,128)}, bf16[8,16,128]{2,1,0:T(8,128)(2,1)}) custom-call(f32[16,16,128]{2,1,0:T(8,128)S(1)} %gram.1.mine_ref, f32[16,16,128]{2,1,0:T(8,128)S(1)} %collective-permute-done.14.other_ref, f32[136,256]{1,0:T(8,128)S(1)} %get-tuple-element.90.refs_0_, f32[136,256]{1,0:T(8,128)S(1)} %collective-permute-done.16.refs_1_, ...), custom_call_target="tpu_custom_call" | custom-call | tf_op jit(solution)/shard_map/finish/pallas_call | solution.py:32
  (11 shorter events, 0.1 us)
Async XLA Ops:
  0.6 1.0 %copy-start.1 = (bf16[512,512]{1,0:T(8,128)(2,1)S(1)}, bf16[512,512]{1,0:T(8,128)(2,1)}, u32[]{:S(2)}) copy-start(bf16[512,512]{1,0:T(8,128)(2,1)} %emb_ref.1) | copy-start | bytes 1572868
  1.7 0.7 %copy-start.3 = (s32[512,1]{0,1:T(1,128)S(1)}, s32[512,1]{0,1:T(1,128)}, u32[]{:S(2)}) copy-start(s32[512,1]{0,1:T(1,128)} %param.6) | copy-start | bytes 6148
  2.4 11.5 %collective-permute-start.2 = (bf16[528,256]{1,0:T(8,128)(2,1)S(1)}, bf16[528,256]{1,0:T(8,128)(2,1)S(1)}, u32[]{:S(2)}, u32[]{:S(2)}) collective-permute-start(bf16[528,256]{1,0:T(8,128)(2,1)S(1)} %get-tuple-element.50.lead_ref), channel_id=1, source_target_pairs={{0,1},{1,0},{2,3},{3,2},{4,5},{5,4},{6,7},{7,6},{8,9},{9,8},{10,11... | collective-permute-start | bytes 811016 | tf_op jit(solution)/shard_map/ppermute | solution.py:332
  2.9 17.3 %collective-permute-start.1 = (bf16[528,256]{1,0:T(8,128)(2,1)S(1)}, bf16[528,256]{1,0:T(8,128)(2,1)S(1)}, u32[]{:S(2)}, u32[]{:S(2)}) collective-permute-start(bf16[528,256]{1,0:T(8,128)(2,1)S(1)} %get-tuple-element.50.lead_ref), channel_id=1, source_target_pairs={{0,8},{4,12},{8,0},{12,4},{1,9},{5,13},{9,1},{13,5},{2,10},{6,14},... | collective-permute-start | bytes 811016 | tf_op jit(solution)/shard_map/ppermute | solution.py:335
  6.6 14.3 %collective-permute-start = (bf16[528,256]{1,0:T(8,128)(2,1)S(1)}, bf16[528,256]{1,0:T(8,128)(2,1)S(1)}, u32[]{:S(2)}, u32[]{:S(2)}) collective-permute-start(bf16[528,256]{1,0:T(8,128)(2,1)S(1)} %get-tuple-element.50.lead_ref), channel_id=1, source_target_pairs={{0,4},{4,0},{8,12},{12,8},{1,5},{5,1},{9,13},{13,9},{2,6},{6,2},{1... | collective-permute-start | bytes 811016 | tf_op jit(solution)/shard_map/ppermute | solution.py:335
  8.2 1.6 %copy-start = (bf16[1024,1024]{1,0:T(8,128)(2,1)S(1)}, bf16[1024,1024]{1,0:T(8,128)(2,1)}, u32[]{:S(2)}) copy-start(bf16[1024,1024]{1,0:T(8,128)(2,1)} %cent_ref.1) | copy-start | bytes 6291460
  9.8 0.7 %copy-start.2 = (s32[1024]{0:T(1024)S(1)}, s32[1024]{0:T(1024)}, u32[]{:S(2)}) copy-start(s32[1024]{0:T(1024)} %param.7) | copy-start | bytes 12292
  12.0 8.1 %collective-permute-start.3 = (bf16[16,16,512]{2,1,0:T(8,128)(2,1)S(1)}, bf16[16,16,512]{2,1,0:T(8,128)(2,1)S(1)}, u32[]{:S(2)}, u32[]{:S(2)}) collective-permute-start(bf16[16,16,512]{2,1,0:T(8,128)(2,1)S(1)} %get-tuple-element.55), channel_id=1, source_target_pairs={{0,2},{2,0},{1,3},{3,1},{4,6},{6,4},{5,7},{7,5},{8,10},{10,8},{9,1... | collective-permute-start | bytes 786440 | tf_op jit(solution)/shard_map/ppermute | solution.py:328
  13.6 17.6 %collective-permute-start.5 = (bf16[528,256]{1,0:T(8,128)(2,1)S(1)}, bf16[528,256]{1,0:T(8,128)(2,1)S(1)}, u32[]{:S(2)}, u32[]{:S(2)}) collective-permute-start(bf16[528,256]{1,0:T(8,128)(2,1)S(1)} %get-tuple-element.67.rest_ref), channel_id=1, source_target_pairs={{0,8},{4,12},{8,0},{12,4},{1,9},{5,13},{9,1},{13,5},{2,10},{6,14},... | collective-permute-start | bytes 811016 | tf_op jit(solution)/shard_map/ppermute | solution.py:335
  13.9 17.9 %collective-permute-start.4 = (bf16[528,256]{1,0:T(8,128)(2,1)S(1)}, bf16[528,256]{1,0:T(8,128)(2,1)S(1)}, u32[]{:S(2)}, u32[]{:S(2)}) collective-permute-start(bf16[528,256]{1,0:T(8,128)(2,1)S(1)} %get-tuple-element.67.rest_ref), channel_id=1, source_target_pairs={{0,4},{4,0},{8,12},{12,8},{1,5},{5,1},{9,13},{13,9},{2,6},{6,2},{1... | collective-permute-start | bytes 811016 | tf_op jit(solution)/shard_map/ppermute | solution.py:335
  22.0 9.9 %collective-permute-start.6 = (bf16[2,16,16,256]{3,2,1,0:T(8,128)(2,1)S(1)}, bf16[2,16,16,256]{3,2,1,0:T(8,128)(2,1)S(1)}, u32[]{:S(2)}, u32[]{:S(2)}) collective-permute-start(bf16[2,16,16,256]{3,2,1,0:T(8,128)(2,1)S(1)} %get-tuple-element.68), channel_id=1, source_target_pairs={{0,2},{2,0},{1,3},{3,1},{4,6},{6,4},{5,7},{7,5},{8,10},{10,8},{9,1... | collective-permute-start | bytes 786440 | tf_op jit(solution)/shard_map/ppermute | solution.py:328
  24.0 11.3 %collective-permute-start.9 = (bf16[528,256]{1,0:T(8,128)(2,1)S(1)}, bf16[528,256]{1,0:T(8,128)(2,1)S(1)}, u32[]{:S(2)}, u32[]{:S(2)}) collective-permute-start(bf16[528,256]{1,0:T(8,128)(2,1)S(1)} %collective-permute-done.refs_0_.lead_ref), channel_id=1, source_target_pairs={{0,1},{1,0},{2,3},{3,2},{4,5},{5,4},{6,7},{7,6},{8,9},{9,8},{10,11... | collective-permute-start | bytes 811016 | tf_op jit(solution)/shard_map/ppermute | solution.py:332
  24.0 12.7 %collective-permute-start.8 = (bf16[528,256]{1,0:T(8,128)(2,1)S(1)}, bf16[528,256]{1,0:T(8,128)(2,1)S(1)}, u32[]{:S(2)}, u32[]{:S(2)}) collective-permute-start(bf16[528,256]{1,0:T(8,128)(2,1)S(1)} %collective-permute-done.1.refs_1_.lead_ref), channel_id=1, source_target_pairs={{0,1},{1,0},{2,3},{3,2},{4,5},{5,4},{6,7},{7,6},{8,9},{9,8},{10,11... | collective-permute-start | bytes 811016 | tf_op jit(solution)/shard_map/ppermute | solution.py:332
  31.2 9.4 %collective-permute-start.7 = (bf16[528,256]{1,0:T(8,128)(2,1)S(1)}, bf16[528,256]{1,0:T(8,128)(2,1)S(1)}, u32[]{:S(2)}, u32[]{:S(2)}) collective-permute-start(bf16[528,256]{1,0:T(8,128)(2,1)S(1)} %collective-permute-done.1.refs_1_.lead_ref), channel_id=1, source_target_pairs={{0,4},{4,0},{8,12},{12,8},{1,5},{5,1},{9,13},{13,9},{2,6},{6,2},{1... | collective-permute-start | bytes 811016 | tf_op jit(solution)/shard_map/ppermute | solution.py:335
  31.8 13.3 %collective-permute-start.10 = (bf16[528,256]{1,0:T(8,128)(2,1)S(1)}, bf16[528,256]{1,0:T(8,128)(2,1)S(1)}, u32[]{:S(2)}, u32[]{:S(2)}) collective-permute-start(bf16[528,256]{1,0:T(8,128)(2,1)S(1)} %collective-permute-done.5.refs_3_), channel_id=1, source_target_pairs={{0,4},{4,0},{8,12},{12,8},{1,5},{5,1},{9,13},{13,9},{2,6},{6,2},{1... | collective-permute-start | bytes 811016 | tf_op jit(solution)/shard_map/ppermute | solution.py:335
  33.7 9.2 %collective-permute-start.11 = (bf16[2,16,16,256]{3,2,1,0:T(8,128)(2,1)S(1)}, bf16[2,16,16,256]{3,2,1,0:T(8,128)(2,1)S(1)}, u32[]{:S(2)}, u32[]{:S(2)}) collective-permute-start(bf16[2,16,16,256]{3,2,1,0:T(8,128)(2,1)S(1)} %get-tuple-element.72), channel_id=1, source_target_pairs={{0,2},{2,0},{1,3},{3,1},{4,6},{6,4},{5,7},{7,5},{8,10},{10,8},{9,1... | collective-permute-start | bytes 786440 | tf_op jit(solution)/shard_map/ppermute | solution.py:328
  40.6 8.2 %collective-permute-start.15 = (bf16[528,256]{1,0:T(8,128)(2,1)S(1)}, bf16[528,256]{1,0:T(8,128)(2,1)S(1)}, u32[]{:S(2)}, u32[]{:S(2)}) collective-permute-start(bf16[528,256]{1,0:T(8,128)(2,1)S(1)} %collective-permute-done.7.refs_0_.lead_ref), channel_id=1, source_target_pairs={{0,1},{1,0},{2,3},{3,2},{4,5},{5,4},{6,7},{7,6},{8,9},{9,8},{10,11... | collective-permute-start | bytes 811016 | tf_op jit(solution)/shard_map/ppermute | solution.py:332
  41.2 6.0 %collective-permute-start.12 = (bf16[1,16,16,256]{3,2,1,0:T(8,128)(2,1)S(1)}, bf16[1,16,16,256]{3,2,1,0:T(8,128)(2,1)S(1)}, u32[]{:S(2)}, u32[]{:S(2)}) collective-permute-start(bf16[1,16,16,256]{3,2,1,0:T(8,128)(2,1)S(1)} %get-tuple-element.84), channel_id=1, source_target_pairs={{0,2},{2,0},{1,3},{3,1},{4,6},{6,4},{5,7},{7,5},{8,10},{10,8},{9,1... | collective-permute-start | bytes 393224 | tf_op jit(solution)/shard_map/ppermute | solution.py:328
  47.1 5.5 %collective-permute-start.13 = (bf16[1,16,16,256]{3,2,1,0:T(8,128)(2,1)S(1)}, bf16[1,16,16,256]{3,2,1,0:T(8,128)(2,1)S(1)}, u32[]{:S(2)}, u32[]{:S(2)}) collective-permute-start(bf16[1,16,16,256]{3,2,1,0:T(8,128)(2,1)S(1)} %get-tuple-element.89), channel_id=1, source_target_pairs={{0,2},{2,0},{1,3},{3,1},{4,6},{6,4},{5,7},{7,5},{8,10},{10,8},{9,1... | collective-permute-start | bytes 393224 | tf_op jit(solution)/shard_map/ppermute | solution.py:328
  50.1 7.9 %collective-permute-start.16 = (f32[136,256]{1,0:T(8,128)S(1)}, f32[136,256]{1,0:T(8,128)S(1)}, u32[]{:S(2)}, u32[]{:S(2)}) collective-permute-start(f32[136,256]{1,0:T(8,128)S(1)} %get-tuple-element.91), channel_id=1, source_target_pairs={{0,2},{2,0},{1,3},{3,1},{4,6},{6,4},{5,7},{7,5},{8,10},{10,8},{9,1... | collective-permute-start | bytes 417800 | tf_op jit(solution)/shard_map/ppermute | solution.py:328
  50.8 7.2 %collective-permute-start.17 = (f32[128,256]{1,0:T(8,128)S(1)}, f32[128,256]{1,0:T(8,128)S(1)}, u32[]{:S(2)}, u32[]{:S(2)}) collective-permute-start(f32[128,256]{1,0:T(8,128)S(1)} %get-tuple-element.94), channel_id=1, source_target_pairs={{0,2},{2,0},{1,3},{3,1},{4,6},{6,4},{5,7},{7,5},{8,10},{10,8},{9,1... | collective-permute-start | bytes 393224 | tf_op jit(solution)/shard_map/ppermute | solution.py:328
  53.5 4.6 %collective-permute-start.14 = (f32[16,16,128]{2,1,0:T(8,128)S(1)}, f32[16,16,128]{2,1,0:T(8,128)S(1)}, u32[]{:S(2)}, u32[]{:S(2)}) collective-permute-start(f32[16,16,128]{2,1,0:T(8,128)S(1)} %gram.1.mine_ref), channel_id=1, source_target_pairs={{0,1},{1,0},{2,3},{3,2},{4,5},{5,4},{6,7},{7,6},{8,9},{9,8},{10,11... | collective-permute-start | bytes 393224 | tf_op jit(solution)/shard_map/ppermute | solution.py:332

commit v9 on v8

--- a/solution.py
+++ b/solution.py
@@ -25,15 +25,15 @@
 NT = (((1,), (1,)), ((), ()))
 
 
-def call(kernel, name, out_shape, operands, aliases=None, scratch=(), far=0, cost=0):
-    def place(at):
-        return pl.BlockSpec(memory_space=pltpu.HBM if at < far else pltpu.VMEM)
+def call(kernel, name, out_shape, operands, aliases=None, scratch=(), cost=0):
+    def whole(_):
+        return pl.BlockSpec(memory_space=pltpu.VMEM)
 
     return pl.pallas_call(
         kernel,
         out_shape=tuple(out_shape),
-        in_specs=[place(at) for at in range(len(operands))],
-        out_specs=tuple(pl.BlockSpec(memory_space=pltpu.VMEM) for _ in out_shape),
+        in_specs=[whole(operand) for operand in operands],
+        out_specs=tuple(whole(out) for out in out_shape),
         input_output_aliases=aliases or {},
         scratch_shapes=list(scratch),
         compiler_params=pltpu.CompilerParams(vmem_limit_bytes=VMEM_LIMIT),
@@ -206,6 +206,18 @@
     weights = soft_weights(lead_ref, near_ref, cent_ref, own_prefix_ref)
     weights_ref[...] = weights.astype(BF16)
     add_lead(weights, lead_ref, old, new)
+
+
+def last_sums_kernel(subs, lead_ref, rest_ref, near_ref, cent_ref, own_prefix_ref, *refs):
+    old, new, totals = refs[: 2 * subs], refs[2 * subs : 3 * subs + 1], refs[3 * subs + 1 :]
+    weights = soft_weights(lead_ref, near_ref, cent_ref, own_prefix_ref)
+    add_lead(weights, lead_ref, old[:subs], new[:1] + totals[: subs - 1])
+    add_rest(weights.astype(BF16), rest_ref[: weights.shape[1], :], old[subs:], new[1:2] + totals[subs - 1 :])
+    for t in range(subs - 1):
+        lead, rest = totals[t][...], totals[subs - 1 + t][...]
+        mass = lead[-SUBLANES:]
+        high = mass.astype(BF16).astype(F32)
+        new[2 + t][...] = jnp.concatenate([lead[:-SUBLANES], rest, high, mass - high], axis=0).astype(BF16)
 
 
 def sums_rest_kernel(count, subs, *refs):
@@ -271,18 +283,24 @@
         scaled_ref[g] = own / width * row_scale * scale
 
 
-def finish_kernel(width, mine_ref, other_ref, *refs):
-    *part_refs, prior_ref, new_ref, tile_ref, scaled_ref = refs
-    subs = len(part_refs) // 2
-    lead = sum(ref[...] for ref in part_refs[1:subs]) + part_refs[0][...]
-    rest = sum(ref[...] for ref in part_refs[subs + 1 :]) + part_refs[subs][...]
-    per = rest.shape[0]
-    mass = jnp.transpose(lead[per:, :LANES])[:per, :1] + SMOOTH
+def centroid_kernel(lead_ref, rest_ref, *refs):
+    *sent_refs, prior_ref, new_ref = refs
+    per = prior_ref.shape[0]
+    lead, mass, rest = lead_ref[:per, :], lead_ref[per:, :], rest_ref[...]
+    for ref in sent_refs:
+        sent = ref[...].astype(F32)
+        lead = lead + sent[:per]
+        rest = rest + sent[per : 2 * per]
+        mass = mass + sent[2 * per : 2 * per + SUBLANES] + sent[2 * per + SUBLANES :]
+    mass = jnp.transpose(mass[:, :LANES])[:per, :1] + SMOOTH
     prior = SMOOTH * prior_ref[...].astype(F32)
-    new_ref[:, :PREFIX] = (lead[:per] + prior[:, :PREFIX]) / mass
+    new_ref[:, :PREFIX] = (lead + prior[:, :PREFIX]) / mass
     new_ref[:, PREFIX:] = (rest + prior[:, PREFIX:]) / mass
 
+
+def tile_kernel(width, mine_ref, other_ref, tile_ref, scaled_ref):
     scaled_tiles(width, mine_ref, other_ref, scaled_ref)
+    per = tile_ref.shape[2]
     groups, kept, size = scaled_ref.shape
     slots = size // SUBLANES
     at = lax.broadcasted_iota(jnp.int32, (groups * size, per), 0)
@@ -365,7 +383,7 @@
 
     lead_sum, rest_sum = shape((per + SUBLANES, PREFIX), F32), shape((per, half - PREFIX), F32)
     sum_shapes = [lead_sum] * subs + [rest_sum] * subs
-    own_cost, other_cost = 2 * 1024 * 1024, 0
+    own_cost = 2 * 1024 * 1024
 
     prefix = near(lead)
     found = call(
@@ -397,26 +415,23 @@
             "select_lead",
             [shape((subs * per * MOST, docs), BF16)] * count + row_shapes,
             [inv, centre] + [leads[bits] for bits in group],
-            cost=other_cost,
         )
         picks, found = list(found[:count]), list(found[count:])
         members.append(across(found))
-        weights = []
-        for bits, prefix in zip(group, prefixes):
-            weight, *lead_sums = call(
-                functools.partial(sums_lead_kernel, subs),
-                "sums_lead",
-                [shape((subs * per, docs), BF16)] + [lead_sum] * subs,
-                [leads[bits], prefix, cent_prefix, own_prefix] + lead_sums,
-                {4 + i: 1 + i for i in range(subs)},
-                cost=other_cost,
-            )
-            weights.append(weight)
         if last:
-            lead_sums = across(lead_sums)
             before = (found, members[:-1])
         else:
             before = (found, members)
+            weights = []
+            for bits, prefix in zip(group, prefixes):
+                weight, *lead_sums = call(
+                    functools.partial(sums_lead_kernel, subs),
+                    "sums_lead",
+                    [shape((subs * per, docs), BF16)] + [lead_sum] * subs,
+                    [leads[bits], prefix, cent_prefix, own_prefix] + lead_sums,
+                    {4 + i: 1 + i for i in range(subs)},
+                )
+                weights.append(weight)
         rests.update(zip(group, tied([rests[bits] for bits in group], before)))
         for bits in group:
             send(rests, bits)
@@ -426,20 +441,28 @@
             "select_rest",
             row_shapes,
             [centre] + picks + [rests[bits] for bits in group],
-            cost=other_cost,
         )
+        members.append(across(found))
         if last:
-            found = tied(found, members)
-        members.append(across(found))
+            break
         rest_sums = call(
             functools.partial(sums_rest_kernel, count, subs),
             "sums_rest",
             [rest_sum] * subs,
             weights + [rests[bits] for bits in group] + list(rest_sums),
             {2 * count + i: i for i in range(subs)},
-            cost=other_cost,
         )
-    rest_sums = across(rest_sums)
+
+    (bits,), (prefix,) = group, prefixes
+    lead, rest, *sent = call(
+        functools.partial(last_sums_kernel, subs),
+        "last_sums",
+        [lead_sum, rest_sum] + [shape((2 * per + 2 * SUBLANES, PREFIX), BF16)] * (subs - 1),
+        [leads[bits], rests[bits], prefix, cent_prefix, own_prefix] + list(lead_sums) + list(tied(rest_sums, members[:-1])),
+        {5: 0, 5 + subs: 1},
+        scratch=[pltpu.VMEM(total.shape, F32) for total in [lead_sum] * (subs - 1) + [rest_sum] * (subs - 1)],
+    )
+    _, *sent = across([None] + sent)
 
     (gram,) = call(
         functools.partial(gram_kernel, groups_of_bits, subs),
@@ -448,13 +471,14 @@
         [arrays[t] for t in range(subs) for arrays in members],
         scratch=[pltpu.VMEM((owners, groups, packed, half), BF16)],
     )
-    new_centroids, tiles = call(
-        functools.partial(finish_kernel, width),
-        "finish",
-        [shape((per, half), F32), shape((slots // 2, slots, per), BF16)],
-        [gram, near(gram)] + lead_sums + rest_sums + [prior],
+    (tiles,) = call(
+        functools.partial(tile_kernel, width),
+        "tiles",
+        [shape((slots // 2, slots, per), BF16)],
+        [gram, near(gram)],
         scratch=[pltpu.VMEM((groups, slots // 2, slots * SUBLANES), F32)],
     )
+    (new_centroids,) = call(centroid_kernel, "centroids", [shape((per, half), F32)], [lead, rest] + sent + [prior])
     return (new_centroids, jnp.transpose(tiles, (2, 0, 1)))
 
 

time: 59.7 us -> 56.3 us (0.943)
  waiting for transfers between devices: 22.7 us -> 19 us
  Pallas kernels: 12.2 us -> 12.8 us
    ppermute x7 -> x6, waiting for transfers between devices: 10.7 us -> 7.08 us  [across(): lax.ppermute(values[t], 'sub', [(i, (i + t) % subs) for i in range(subs)])]
    ppermute x7 -> x6, starting transfers between devices: 10.6 us -> 10.3 us  [across(): lax.ppermute(values[t], 'sub', [(i, (i + t) % subs) for i in range(subs)])]
  transfers between devices with their start and end apart: 18 -> 17, of which waited for: 8 -> 7; matrix products, arithmetic and copies ran while one was open for 0% -> 0% of each run, Pallas kernels for 18% -> 20%
where the time goes in v9:
time: 56.3 us; the launch traced here: 56 us
  starting transfers between devices  19.5 us (35%)
  waiting for transfers between devices  19 us (34%)
  Pallas kernels  12.8 us (23%)
  local copies, waits for them, and re-layouts  3.99 us (7%)
  between operations  0.76 us (1%)
    pallas_call x15, Pallas kernels, call(): pl.pallas_call(kernel, out_shape=tuple(out_shape), in_specs=[whole(operan...  12.8 us
    ppermute x6, waiting for transfers between devices, swap(): return lax.ppermute(value, 'rows', [(i, i ^ bit) for i in range(rows)])  11.9 us
    ppermute x6, starting transfers between devices, across(): lax.ppermute(values[t], 'sub', [(i, (i + t) % subs) for i in range(subs)])  10.3 us
    ppermute x6, starting transfers between devices, swap(): return lax.ppermute(value, 'rows', [(i, i ^ bit) for i in range(rows)])  8.05 us
    ppermute x6, waiting for transfers between devices, across(): lax.ppermute(values[t], 'sub', [(i, (i + t) % subs) for i in range(subs)])  7.08 us
    unnamed x8, local copies, waits for them, and re-layouts  3.99 us
  transfers between devices with their start and end apart: 17, of which 7 were waited for; matrix products, arithmetic and copies ran while one was open for 0% of the time, Pallas kernels for 20%

profile of v9, /device:TPU:0, one launch (start us, length us, event | category | flops | bytes accessed | tf_op | source)
XLA Modules:
  0.0 56.0 jit_solution(14020389881318323643)
XLA Ops:
  0.6 1.0 %copy-done.1 = bf16[512,512]{1,0:T(8,128)(2,1)S(1)} copy-done((bf16[512,512]{1,0:T(8,128)(2,1)S(1)}, bf16[512,512]{1,0:T(8,128)(2,1)}, u32[]{:S(2)}) %copy-start.1) | copy-done | bytes 524312
  1.7 0.7 %copy-done.3 = s32[512,1]{0,1:T(1,128)S(1)} copy-done((s32[512,1]{0,1:T(1,128)S(1)}, s32[512,1]{0,1:T(1,128)}, u32[]{:S(2)}) %copy-start.3) | copy-done | bytes 2072
  2.4 0.5 collective-permute-start.2
  2.9 3.7 %collective-permute-start.1 = (bf16[528,256]{1,0:T(8,128)(2,1)S(1)}, bf16[528,256]{1,0:T(8,128)(2,1)S(1)}, u32[]{:S(2)}, u32[]{:S(2)}) collective-permute-start(bf16[528,256]{1,0:T(8,128)(2,1)S(1)} %get-tuple-element.46.lead_ref), channel_id=1, source_target_pairs={{0,8},{4,12},{8,0},{12,4},{1,9},{5,13},{9,1},{13,5},{2,10},{6,14},... | collective-permute-start | bytes 811016 | tf_op jit(solution)/shard_map/ppermute | solution.py:353
  6.6 1.6 %collective-permute-start = (bf16[528,256]{1,0:T(8,128)(2,1)S(1)}, bf16[528,256]{1,0:T(8,128)(2,1)S(1)}, u32[]{:S(2)}, u32[]{:S(2)}) collective-permute-start(bf16[528,256]{1,0:T(8,128)(2,1)S(1)} %get-tuple-element.46.lead_ref), channel_id=1, source_target_pairs={{0,4},{4,0},{8,12},{12,8},{1,5},{5,1},{9,13},{13,9},{2,6},{6,2},{1... | collective-permute-start | bytes 811016 | tf_op jit(solution)/shard_map/ppermute | solution.py:353
  8.2 1.6 %copy-done = bf16[1024,1024]{1,0:T(8,128)(2,1)S(1)} copy-done((bf16[1024,1024]{1,0:T(8,128)(2,1)S(1)}, bf16[1024,1024]{1,0:T(8,128)(2,1)}, u32[]{:S(2)}) %copy-start) | copy-done | bytes 2097176
  9.8 0.7 %copy-done.2 = s32[1024]{0:T(1024)S(1)} copy-done((s32[1024]{0:T(1024)S(1)}, s32[1024]{0:T(1024)}, u32[]{:S(2)}) %copy-start.2) | copy-done | bytes 4120
  10.4 0.8 %prep.1 = (f32[256,1]{1,0:T(8,128)S(1)}, bf16[256,512]{1,0:T(8,128)(2,1)S(1)}, bf16[256,256]{1,0:T(8,128)(2,1)S(1)}, bf16[128,512]{1,0:T(8,128)(2,1)S(1)}, bf16[1024,256]{1,0:T(8,128)(2,1)S(1)}) custom-call(s32[1,1024]{1,0:T(1,128)S(1)} %bitcast.3, bf16[1024,1024]{1,0:T(8,128)(2,1)S(1)} %copy-done), custom_call_target="tpu_custom_call" | custom-call | flops 209715200 | bytes 4194304 | tf_op jit(solution)/shard_map/prep/pallas_call | solution.py:32
  11.3 0.7 %select.1 = (bf16[16,16,512]{2,1,0:T(8,128)(2,1)S(1)}, bf16[16,16,512]{2,1,0:T(8,128)(2,1)S(1)}) custom-call(bf16[528,256]{1,0:T(8,128)(2,1)S(1)} %get-tuple-element.46.lead_ref, bf16[528,256]{1,0:T(8,128)(2,1)S(1)} %get-tuple-element.62.rest_ref, f32[256,1]{1,0:T(8,128)S(1)} %get-tuple-element.48.inv_ref, bf16[256,512]{1,0:T(8,128)(2,1)S(1)} %get-tuple-element.49.centre_ref), custom_call_target="tpu_custom_call" | custom-call | flops 104857600 | bytes 2097152 | tf_op jit(solution)/shard_map/select/pallas_call | solution.py:32
  12.0 1.5 %collective-permute-start.3 = (bf16[16,16,512]{2,1,0:T(8,128)(2,1)S(1)}, bf16[16,16,512]{2,1,0:T(8,128)(2,1)S(1)}, u32[]{:S(2)}, u32[]{:S(2)}) collective-permute-start(bf16[16,16,512]{2,1,0:T(8,128)(2,1)S(1)} %get-tuple-element.51), channel_id=1, source_target_pairs={{0,2},{2,0},{1,3},{3,1},{4,6},{6,4},{5,7},{7,5},{8,10},{10,8},{9,1... | collective-permute-start | bytes 786440 | tf_op jit(solution)/shard_map/ppermute | solution.py:346
  13.6 0.3 collective-permute-start.6
  13.9 0.5 collective-permute-start.5
  14.4 1.3 %sums.1 = (f32[136,256]{1,0:T(8,128)S(1)}, f32[136,256]{1,0:T(8,128)S(1)}, f32[128,256]{1,0:T(8,128)S(1)}, f32[128,256]{1,0:T(8,128)S(1)}) custom-call(bf16[528,256]{1,0:T(8,128)(2,1)S(1)} %get-tuple-element.46.lead_ref, bf16[528,256]{1,0:T(8,128)(2,1)S(1)} %get-tuple-element.62.rest_ref, bf16[528,256]{1,0:T(8,128)(2,1)S(1)} %collective-permute-done.2.near_ref, ...), custom_call_target="tpu_custom_call" | custom-call | flops 104857600 | bytes 2097152 | tf_op jit(solution)/shard_map/sums/pallas_call | solution.py:32
  15.7 4.5 %collective-permute-done.3.refs_5_ = bf16[16,16,512]{2,1,0:T(8,128)(2,1)S(1)} collective-permute-done((bf16[16,16,512]{2,1,0:T(8,128)(2,1)S(1)}, bf16[16,16,512]{2,1,0:T(8,128)(2,1)S(1)}, u32[]{:S(2)}, u32[]{:S(2)}) %collective-permute-start.3) | collective-permute-done | bytes 262176 | tf_op jit(solution)/shard_map/ppermute | solution.py:346
  20.2 0.0 collective-permute-done.1.refs_1_.lead_ref
  20.2 0.7 %collective-permute-done.refs_0_.lead_ref = bf16[528,256]{1,0:T(8,128)(2,1)S(1)} collective-permute-done((bf16[528,256]{1,0:T(8,128)(2,1)S(1)}, bf16[528,256]{1,0:T(8,128)(2,1)S(1)}, u32[]{:S(2)}, u32[]{:S(2)}) %collective-permute-start) | collective-permute-done | bytes 270368 | tf_op jit(solution)/shard_map/ppermute | solution.py:353
  20.9 1.1 %select_lead.2 = (bf16[512,512]{1,0:T(8,128)(2,1)S(1)}, bf16[512,512]{1,0:T(8,128)(2,1)S(1)}, bf16[2,16,16,256]{3,2,1,0:T(8,128)(2,1)S(1)}, bf16[2,16,16,256]{3,2,1,0:T(8,128)(2,1)S(1)}) custom-call(f32[256,1]{1,0:T(8,128)S(1)} %get-tuple-element.48.inv_ref, bf16[256,512]{1,0:T(8,128)(2,1)S(1)} %get-tuple-element.49.centre_ref, ...), custom_call_target="tpu_custom_call" | custom-call | tf_op jit(solution)/shard_map/select_lead/pallas_call | solution.py:32
  22.0 2.0 %collective-permute-start.7 = (bf16[2,16,16,256]{3,2,1,0:T(8,128)(2,1)S(1)}, bf16[2,16,16,256]{3,2,1,0:T(8,128)(2,1)S(1)}, u32[]{:S(2)}, u32[]{:S(2)}) collective-permute-start(bf16[2,16,16,256]{3,2,1,0:T(8,128)(2,1)S(1)} %get-tuple-element.64), channel_id=1, source_target_pairs={{0,2},{2,0},{1,3},{3,1},{4,6},{6,4},{5,7},{7,5},{8,10},{10,8},{9,1... | collective-permute-start | bytes 786440 | tf_op jit(solution)/shard_map/ppermute | solution.py:346
  24.0 0.5 collective-permute-start.8
  24.5 6.7 %collective-permute-done.6.refs_3_ = bf16[528,256]{1,0:T(8,128)(2,1)S(1)} collective-permute-done((bf16[528,256]{1,0:T(8,128)(2,1)S(1)}, bf16[528,256]{1,0:T(8,128)(2,1)S(1)}, u32[]{:S(2)}, u32[]{:S(2)}) %collective-permute-start.6) | collective-permute-done | bytes 270368 | tf_op jit(solution)/shard_map/ppermute | solution.py:353
  31.2 0.6 %collective-permute-start.4 = (bf16[528,256]{1,0:T(8,128)(2,1)S(1)}, bf16[528,256]{1,0:T(8,128)(2,1)S(1)}, u32[]{:S(2)}, u32[]{:S(2)}) collective-permute-start(bf16[528,256]{1,0:T(8,128)(2,1)S(1)} %collective-permute-done.1.refs_1_.lead_ref), channel_id=1, source_target_pairs={{0,4},{4,0},{8,12},{12,8},{1,5},{5,1},{9,13},{13,9},{2,6},{6,2},{1... | collective-permute-start | bytes 811016 | tf_op jit(solution)/shard_map/ppermute | solution.py:353
  31.8 0.0 collective-permute-done.5.refs_2_
  31.8 0.0 collective-permute-done.7.refs_6_
  31.8 1.4 %collective-permute-start.10 = (bf16[528,256]{1,0:T(8,128)(2,1)S(1)}, bf16[528,256]{1,0:T(8,128)(2,1)S(1)}, u32[]{:S(2)}, u32[]{:S(2)}) collective-permute-start(bf16[528,256]{1,0:T(8,128)(2,1)S(1)} %collective-permute-done.6.refs_3_), channel_id=1, source_target_pairs={{0,4},{4,0},{8,12},{12,8},{1,5},{5,1},{9,13},{13,9},{2,6},{6,2},{1... | collective-permute-start | bytes 811016 | tf_op jit(solution)/shard_map/ppermute | solution.py:353
  33.2 0.4 select_rest.2
  33.7 1.6 %collective-permute-start.11 = (bf16[2,16,16,256]{3,2,1,0:T(8,128)(2,1)S(1)}, bf16[2,16,16,256]{3,2,1,0:T(8,128)(2,1)S(1)}, u32[]{:S(2)}, u32[]{:S(2)}) collective-permute-start(bf16[2,16,16,256]{3,2,1,0:T(8,128)(2,1)S(1)} %get-tuple-element.68), channel_id=1, source_target_pairs={{0,2},{2,0},{1,3},{3,1},{4,6},{6,4},{5,7},{7,5},{8,10},{10,8},{9,1... | collective-permute-start | bytes 786440 | tf_op jit(solution)/shard_map/ppermute | solution.py:346
  35.3 0.0 collective-permute-done.9.near_ref
  35.3 1.4 %sums_lead.2 = (bf16[256,512]{1,0:T(8,128)(2,1)S(1)}, f32[136,256]{1,0:T(8,128)S(1)}, f32[136,256]{1,0:T(8,128)S(1)}) custom-call(bf16[528,256]{1,0:T(8,128)(2,1)S(1)} %collective-permute-done.refs_0_.lead_ref, bf16[528,256]{1,0:T(8,128)(2,1)S(1)} %collective-permute-done.9.near_ref, ...), custom_call_target="tpu_custom_call", output_to_operand_aliasing={{1}: (4, {}), {2}: (5, {})} | custom-call | tf_op jit(solution)/shard_map/sums_lead/pallas_call | solution.py:32
  36.7 0.0 collective-permute-done.8.near_ref
  36.7 1.4 %sums_lead.3 = (bf16[256,512]{1,0:T(8,128)(2,1)S(1)}, f32[136,256]{1,0:T(8,128)S(1)}, f32[136,256]{1,0:T(8,128)S(1)}) custom-call(bf16[528,256]{1,0:T(8,128)(2,1)S(1)} %collective-permute-done.1.refs_1_.lead_ref, bf16[528,256]{1,0:T(8,128)(2,1)S(1)} %collective-permute-done.8.near_ref, ...), custom_call_target="tpu_custom_call", output_to_operand_aliasing={{1}: (4, {}), {2}: (5, {})} | custom-call | tf_op jit(solution)/shard_map/sums_lead/pallas_call | solution.py:32
  38.1 0.3 sums_rest.1
  38.4 2.2 %collective-permute-done.4.refs_0_.lead_ref = bf16[528,256]{1,0:T(8,128)(2,1)S(1)} collective-permute-done((bf16[528,256]{1,0:T(8,128)(2,1)S(1)}, bf16[528,256]{1,0:T(8,128)(2,1)S(1)}, u32[]{:S(2)}, u32[]{:S(2)}) %collective-permute-start.4) | collective-permute-done | bytes 270368 | tf_op jit(solution)/shard_map/ppermute | solution.py:353
  40.6 0.0 collective-permute-start.12
  40.6 0.6 %select_lead.3 = (bf16[512,512]{1,0:T(8,128)(2,1)S(1)}, bf16[1,16,16,256]{3,2,1,0:T(8,128)(2,1)S(1)}, bf16[1,16,16,256]{3,2,1,0:T(8,128)(2,1)S(1)}) custom-call(f32[256,1]{1,0:T(8,128)S(1)} %get-tuple-element.48.inv_ref, bf16[256,512]{1,0:T(8,128)(2,1)S(1)} %get-tuple-element.49.centre_ref, bf16[528,256]{1,0:T(8,128)(2,1)S(1)} %collective-permute-done.4.refs_0_.lead_ref), custom_call_target="tpu_custom_call" | custom-call | tf_op jit(solution)/shard_map/select_lead/pallas_call | solution.py:32
  41.2 1.7 %collective-permute-start.13 = (bf16[1,16,16,256]{3,2,1,0:T(8,128)(2,1)S(1)}, bf16[1,16,16,256]{3,2,1,0:T(8,128)(2,1)S(1)}, u32[]{:S(2)}, u32[]{:S(2)}) collective-permute-start(bf16[1,16,16,256]{3,2,1,0:T(8,128)(2,1)S(1)} %get-tuple-element.79), channel_id=1, source_target_pairs={{0,2},{2,0},{1,3},{3,1},{4,6},{6,4},{5,7},{7,5},{8,10},{10,8},{9,1... | collective-permute-start | bytes 393224 | tf_op jit(solution)/shard_map/ppermute | solution.py:346
  42.8 0.0 collective-permute-done.11.refs_7_
  42.8 2.3 %collective-permute-done.10.rest_ref.refs_1_ = bf16[528,256]{1,0:T(8,128)(2,1)S(1)} collective-permute-done((bf16[528,256]{1,0:T(8,128)(2,1)S(1)}, bf16[528,256]{1,0:T(8,128)(2,1)S(1)}, u32[]{:S(2)}, u32[]{:S(2)}) %collective-permute-start.10) | collective-permute-done | bytes 270368 | tf_op jit(solution)/shard_map/ppermute | solution.py:353
  45.2 0.3 select_rest.3
  45.5 1.4 %collective-permute-start.15 = (bf16[1,16,16,256]{3,2,1,0:T(8,128)(2,1)S(1)}, bf16[1,16,16,256]{3,2,1,0:T(8,128)(2,1)S(1)}, u32[]{:S(2)}, u32[]{:S(2)}) collective-permute-start(bf16[1,16,16,256]{3,2,1,0:T(8,128)(2,1)S(1)} %get-tuple-element.89), channel_id=1, source_target_pairs={{0,2},{2,0},{1,3},{3,1},{4,6},{6,4},{5,7},{7,5},{8,10},{10,8},{9,1... | collective-permute-start | bytes 393224 | tf_op jit(solution)/shard_map/ppermute | solution.py:346
  46.9 0.2 collective-permute-done.13.refs_8_
  47.1 1.3 %last_sums.1 = (f32[136,256]{1,0:T(8,128)S(1)}, f32[128,256]{1,0:T(8,128)S(1)}, bf16[272,256]{1,0:T(8,128)(2,1)S(1)}) custom-call(bf16[528,256]{1,0:T(8,128)(2,1)S(1)} %collective-permute-done.4.refs_0_.lead_ref, bf16[528,256]{1,0:T(8,128)(2,1)S(1)} %collective-permute-done.10.rest_ref.refs_1_, ...), custom_call_target="tpu_custom_call", output_to_operand_aliasing={{0}: (5, {}), {1}: (7, {})} | custom-call | tf_op jit(solution)/shard_map/last_sums/pallas_call | solution.py:32
  48.5 2.0 %collective-permute-start.14 = (bf16[272,256]{1,0:T(8,128)(2,1)S(1)}, bf16[272,256]{1,0:T(8,128)(2,1)S(1)}, u32[]{:S(2)}, u32[]{:S(2)}) collective-permute-start(bf16[272,256]{1,0:T(8,128)(2,1)S(1)} %get-tuple-element.85), channel_id=1, source_target_pairs={{0,2},{2,0},{1,3},{3,1},{4,6},{6,4},{5,7},{7,5},{8,10},{10,8},{9,1... | collective-permute-start | bytes 417800 | tf_op jit(solution)/shard_map/ppermute | solution.py:346
  50.5 0.0 collective-permute-done.15.refs_9_
  50.5 0.9 %gram.1.mine_ref = f32[16,16,128]{2,1,0:T(8,128)S(1)} custom-call(bf16[16,16,512]{2,1,0:T(8,128)(2,1)S(1)} %get-tuple-element.50.refs_0_, bf16[2,16,16,256]{3,2,1,0:T(8,128)(2,1)S(1)} %get-tuple-element.63.refs_1_, bf16[2,16,16,256]{3,2,1,0:T(8,128)(2,1)S(1)} %get-tuple-element.67.refs_2_, bf16[1,16,16,256]{3,2,1,0:T(8,128)(2,1)S(1)} %get-tuple-element.78.refs_3_, ...), custom_call_target="tpu_custom_call" | custom-call | tf_op jit(solution)/shard_map/gram/pallas_call | solution.py:32
  51.4 0.1 collective-permute-start.16
  51.5 2.3 %collective-permute-done.14.refs_0_ = bf16[272,256]{1,0:T(8,128)(2,1)S(1)} collective-permute-done((bf16[272,256]{1,0:T(8,128)(2,1)S(1)}, bf16[272,256]{1,0:T(8,128)(2,1)S(1)}, u32[]{:S(2)}, u32[]{:S(2)}) %collective-permute-start.14) | collective-permute-done | bytes 139296 | tf_op jit(solution)/shard_map/ppermute | solution.py:346
  53.8 0.9 %centroids.1 = f32[128,512]{1,0:T(8,128)} custom-call(f32[136,256]{1,0:T(8,128)S(1)} %get-tuple-element.83.lead_ref, f32[128,256]{1,0:T(8,128)S(1)} %get-tuple-element.84.rest_ref, bf16[272,256]{1,0:T(8,128)(2,1)S(1)} %collective-permute-done.14.refs_0_, bf16[128,512]{1,0:T(8,128)(2,1)S(1)} %get-tuple-element.86.refs_1_), custom_call_target="tpu_custom_call" | custom-call | tf_op jit(solution)/shard_map/centroids/pallas_call | solution.py:32
  54.7 1.3 %tiles.1 = bf16[8,16,128]{2,1,0:T(8,128)(2,1)} custom-call(f32[16,16,128]{2,1,0:T(8,128)S(1)} %gram.1.mine_ref, f32[16,16,128]{2,1,0:T(8,128)S(1)} %collective-permute-done.16.other_ref), custom_call_target="tpu_custom_call" | custom-call | tf_op jit(solution)/shard_map/tiles/pallas_call | solution.py:32
  (9 shorter events, 0.1 us)
Async XLA Ops:
  0.6 1.0 %copy-start.1 = (bf16[512,512]{1,0:T(8,128)(2,1)S(1)}, bf16[512,512]{1,0:T(8,128)(2,1)}, u32[]{:S(2)}) copy-start(bf16[512,512]{1,0:T(8,128)(2,1)} %emb_ref.1) | copy-start | bytes 1572868
  1.7 0.7 %copy-start.3 = (s32[512,1]{0,1:T(1,128)S(1)}, s32[512,1]{0,1:T(1,128)}, u32[]{:S(2)}) copy-start(s32[512,1]{0,1:T(1,128)} %param.6) | copy-start | bytes 6148
  2.4 11.5 %collective-permute-start.2 = (bf16[528,256]{1,0:T(8,128)(2,1)S(1)}, bf16[528,256]{1,0:T(8,128)(2,1)S(1)}, u32[]{:S(2)}, u32[]{:S(2)}) collective-permute-start(bf16[528,256]{1,0:T(8,128)(2,1)S(1)} %get-tuple-element.46.lead_ref), channel_id=1, source_target_pairs={{0,1},{1,0},{2,3},{3,2},{4,5},{5,4},{6,7},{7,6},{8,9},{9,8},{10,11... | collective-permute-start | bytes 811016 | tf_op jit(solution)/shard_map/ppermute | solution.py:350
  2.9 17.3 %collective-permute-start.1 = (bf16[528,256]{1,0:T(8,128)(2,1)S(1)}, bf16[528,256]{1,0:T(8,128)(2,1)S(1)}, u32[]{:S(2)}, u32[]{:S(2)}) collective-permute-start(bf16[528,256]{1,0:T(8,128)(2,1)S(1)} %get-tuple-element.46.lead_ref), channel_id=1, source_target_pairs={{0,8},{4,12},{8,0},{12,4},{1,9},{5,13},{9,1},{13,5},{2,10},{6,14},... | collective-permute-start | bytes 811016 | tf_op jit(solution)/shard_map/ppermute | solution.py:353
  6.6 14.3 %collective-permute-start = (bf16[528,256]{1,0:T(8,128)(2,1)S(1)}, bf16[528,256]{1,0:T(8,128)(2,1)S(1)}, u32[]{:S(2)}, u32[]{:S(2)}) collective-permute-start(bf16[528,256]{1,0:T(8,128)(2,1)S(1)} %get-tuple-element.46.lead_ref), channel_id=1, source_target_pairs={{0,4},{4,0},{8,12},{12,8},{1,5},{5,1},{9,13},{13,9},{2,6},{6,2},{1... | collective-permute-start | bytes 811016 | tf_op jit(solution)/shard_map/ppermute | solution.py:353
  8.2 1.6 %copy-start = (bf16[1024,1024]{1,0:T(8,128)(2,1)S(1)}, bf16[1024,1024]{1,0:T(8,128)(2,1)}, u32[]{:S(2)}) copy-start(bf16[1024,1024]{1,0:T(8,128)(2,1)} %cent_ref.1) | copy-start | bytes 6291460
  9.8 0.7 %copy-start.2 = (s32[1024]{0:T(1024)S(1)}, s32[1024]{0:T(1024)}, u32[]{:S(2)}) copy-start(s32[1024]{0:T(1024)} %param.7) | copy-start | bytes 12292
  12.0 8.1 %collective-permute-start.3 = (bf16[16,16,512]{2,1,0:T(8,128)(2,1)S(1)}, bf16[16,16,512]{2,1,0:T(8,128)(2,1)S(1)}, u32[]{:S(2)}, u32[]{:S(2)}) collective-permute-start(bf16[16,16,512]{2,1,0:T(8,128)(2,1)S(1)} %get-tuple-element.51), channel_id=1, source_target_pairs={{0,2},{2,0},{1,3},{3,1},{4,6},{6,4},{5,7},{7,5},{8,10},{10,8},{9,1... | collective-permute-start | bytes 786440 | tf_op jit(solution)/shard_map/ppermute | solution.py:346
  13.6 17.6 %collective-permute-start.6 = (bf16[528,256]{1,0:T(8,128)(2,1)S(1)}, bf16[528,256]{1,0:T(8,128)(2,1)S(1)}, u32[]{:S(2)}, u32[]{:S(2)}) collective-permute-start(bf16[528,256]{1,0:T(8,128)(2,1)S(1)} %get-tuple-element.62.rest_ref), channel_id=1, source_target_pairs={{0,8},{4,12},{8,0},{12,4},{1,9},{5,13},{9,1},{13,5},{2,10},{6,14},... | collective-permute-start | bytes 811016 | tf_op jit(solution)/shard_map/ppermute | solution.py:353
  13.9 17.9 %collective-permute-start.5 = (bf16[528,256]{1,0:T(8,128)(2,1)S(1)}, bf16[528,256]{1,0:T(8,128)(2,1)S(1)}, u32[]{:S(2)}, u32[]{:S(2)}) collective-permute-start(bf16[528,256]{1,0:T(8,128)(2,1)S(1)} %get-tuple-element.62.rest_ref), channel_id=1, source_target_pairs={{0,4},{4,0},{8,12},{12,8},{1,5},{5,1},{9,13},{13,9},{2,6},{6,2},{1... | collective-permute-start | bytes 811016 | tf_op jit(solution)/shard_map/ppermute | solution.py:353
  22.0 9.9 %collective-permute-start.7 = (bf16[2,16,16,256]{3,2,1,0:T(8,128)(2,1)S(1)}, bf16[2,16,16,256]{3,2,1,0:T(8,128)(2,1)S(1)}, u32[]{:S(2)}, u32[]{:S(2)}) collective-permute-start(bf16[2,16,16,256]{3,2,1,0:T(8,128)(2,1)S(1)} %get-tuple-element.64), channel_id=1, source_target_pairs={{0,2},{2,0},{1,3},{3,1},{4,6},{6,4},{5,7},{7,5},{8,10},{10,8},{9,1... | collective-permute-start | bytes 786440 | tf_op jit(solution)/shard_map/ppermute | solution.py:346
  24.0 11.3 %collective-permute-start.9 = (bf16[528,256]{1,0:T(8,128)(2,1)S(1)}, bf16[528,256]{1,0:T(8,128)(2,1)S(1)}, u32[]{:S(2)}, u32[]{:S(2)}) collective-permute-start(bf16[528,256]{1,0:T(8,128)(2,1)S(1)} %collective-permute-done.refs_0_.lead_ref), channel_id=1, source_target_pairs={{0,1},{1,0},{2,3},{3,2},{4,5},{5,4},{6,7},{7,6},{8,9},{9,8},{10,11... | collective-permute-start | bytes 811016 | tf_op jit(solution)/shard_map/ppermute | solution.py:350
  24.0 12.7 %collective-permute-start.8 = (bf16[528,256]{1,0:T(8,128)(2,1)S(1)}, bf16[528,256]{1,0:T(8,128)(2,1)S(1)}, u32[]{:S(2)}, u32[]{:S(2)}) collective-permute-start(bf16[528,256]{1,0:T(8,128)(2,1)S(1)} %collective-permute-done.1.refs_1_.lead_ref), channel_id=1, source_target_pairs={{0,1},{1,0},{2,3},{3,2},{4,5},{5,4},{6,7},{7,6},{8,9},{9,8},{10,11... | collective-permute-start | bytes 811016 | tf_op jit(solution)/shard_map/ppermute | solution.py:350
  31.2 9.4 %collective-permute-start.4 = (bf16[528,256]{1,0:T(8,128)(2,1)S(1)}, bf16[528,256]{1,0:T(8,128)(2,1)S(1)}, u32[]{:S(2)}, u32[]{:S(2)}) collective-permute-start(bf16[528,256]{1,0:T(8,128)(2,1)S(1)} %collective-permute-done.1.refs_1_.lead_ref), channel_id=1, source_target_pairs={{0,4},{4,0},{8,12},{12,8},{1,5},{5,1},{9,13},{13,9},{2,6},{6,2},{1... | collective-permute-start | bytes 811016 | tf_op jit(solution)/shard_map/ppermute | solution.py:353
  31.8 13.3 %collective-permute-start.10 = (bf16[528,256]{1,0:T(8,128)(2,1)S(1)}, bf16[528,256]{1,0:T(8,128)(2,1)S(1)}, u32[]{:S(2)}, u32[]{:S(2)}) collective-permute-start(bf16[528,256]{1,0:T(8,128)(2,1)S(1)} %collective-permute-done.6.refs_3_), channel_id=1, source_target_pairs={{0,4},{4,0},{8,12},{12,8},{1,5},{5,1},{9,13},{13,9},{2,6},{6,2},{1... | collective-permute-start | bytes 811016 | tf_op jit(solution)/shard_map/ppermute | solution.py:353
  33.7 9.2 %collective-permute-start.11 = (bf16[2,16,16,256]{3,2,1,0:T(8,128)(2,1)S(1)}, bf16[2,16,16,256]{3,2,1,0:T(8,128)(2,1)S(1)}, u32[]{:S(2)}, u32[]{:S(2)}) collective-permute-start(bf16[2,16,16,256]{3,2,1,0:T(8,128)(2,1)S(1)} %get-tuple-element.68), channel_id=1, source_target_pairs={{0,2},{2,0},{1,3},{3,1},{4,6},{6,4},{5,7},{7,5},{8,10},{10,8},{9,1... | collective-permute-start | bytes 786440 | tf_op jit(solution)/shard_map/ppermute | solution.py:346
  40.6 6.6 %collective-permute-start.12 = (bf16[528,256]{1,0:T(8,128)(2,1)S(1)}, bf16[528,256]{1,0:T(8,128)(2,1)S(1)}, u32[]{:S(2)}, u32[]{:S(2)}) collective-permute-start(bf16[528,256]{1,0:T(8,128)(2,1)S(1)} %collective-permute-done.4.refs_0_.lead_ref), channel_id=1, source_target_pairs={{0,1},{1,0},{2,3},{3,2},{4,5},{5,4},{6,7},{7,6},{8,9},{9,8},{10,11... | collective-permute-start | bytes 811016 | tf_op jit(solution)/shard_map/ppermute | solution.py:350
  41.2 6.0 %collective-permute-start.13 = (bf16[1,16,16,256]{3,2,1,0:T(8,128)(2,1)S(1)}, bf16[1,16,16,256]{3,2,1,0:T(8,128)(2,1)S(1)}, u32[]{:S(2)}, u32[]{:S(2)}) collective-permute-start(bf16[1,16,16,256]{3,2,1,0:T(8,128)(2,1)S(1)} %get-tuple-element.79), channel_id=1, source_target_pairs={{0,2},{2,0},{1,3},{3,1},{4,6},{6,4},{5,7},{7,5},{8,10},{10,8},{9,1... | collective-permute-start | bytes 393224 | tf_op jit(solution)/shard_map/ppermute | solution.py:346
  45.5 5.0 %collective-permute-start.15 = (bf16[1,16,16,256]{3,2,1,0:T(8,128)(2,1)S(1)}, bf16[1,16,16,256]{3,2,1,0:T(8,128)(2,1)S(1)}, u32[]{:S(2)}, u32[]{:S(2)}) collective-permute-start(bf16[1,16,16,256]{3,2,1,0:T(8,128)(2,1)S(1)} %get-tuple-element.89), channel_id=1, source_target_pairs={{0,2},{2,0},{1,3},{3,1},{4,6},{6,4},{5,7},{7,5},{8,10},{10,8},{9,1... | collective-permute-start | bytes 393224 | tf_op jit(solution)/shard_map/ppermute | solution.py:346
  48.5 5.4 %collective-permute-start.14 = (bf16[272,256]{1,0:T(8,128)(2,1)S(1)}, bf16[272,256]{1,0:T(8,128)(2,1)S(1)}, u32[]{:S(2)}, u32[]{:S(2)}) collective-permute-start(bf16[272,256]{1,0:T(8,128)(2,1)S(1)} %get-tuple-element.85), channel_id=1, source_target_pairs={{0,2},{2,0},{1,3},{3,1},{4,6},{6,4},{5,7},{7,5},{8,10},{10,8},{9,1... | collective-permute-start | bytes 417800 | tf_op jit(solution)/shard_map/ppermute | solution.py:346
  51.4 3.3 %collective-permute-start.16 = (f32[16,16,128]{2,1,0:T(8,128)S(1)}, f32[16,16,128]{2,1,0:T(8,128)S(1)}, u32[]{:S(2)}, u32[]{:S(2)}) collective-permute-start(f32[16,16,128]{2,1,0:T(8,128)S(1)} %gram.1.mine_ref), channel_id=1, source_target_pairs={{0,1},{1,0},{2,3},{3,2},{4,5},{5,4},{6,7},{7,6},{8,9},{9,8},{10,11... | collective-permute-start | bytes 393224 | tf_op jit(solution)/shard_map/ppermute | solution.py:350

commit v10 on v8

--- a/solution.py
+++ b/solution.py
@@ -25,15 +25,15 @@
 NT = (((1,), (1,)), ((), ()))
 
 
-def call(kernel, name, out_shape, operands, aliases=None, scratch=(), far=0, cost=0):
-    def place(at):
-        return pl.BlockSpec(memory_space=pltpu.HBM if at < far else pltpu.VMEM)
+def call(kernel, name, out_shape, operands, aliases=None, scratch=(), cost=0):
+    def whole(_):
+        return pl.BlockSpec(memory_space=pltpu.VMEM)
 
     return pl.pallas_call(
         kernel,
         out_shape=tuple(out_shape),
-        in_specs=[place(at) for at in range(len(operands))],
-        out_specs=tuple(pl.BlockSpec(memory_space=pltpu.VMEM) for _ in out_shape),
+        in_specs=[whole(operand) for operand in operands],
+        out_specs=tuple(whole(out) for out in out_shape),
         input_output_aliases=aliases or {},
         scratch_shapes=list(scratch),
         compiler_params=pltpu.CompilerParams(vmem_limit_bytes=VMEM_LIMIT),
@@ -157,10 +157,11 @@
             row_refs[t][i] = rows[t]
 
 
-def soft_weights(lead_ref, near_ref, cent_ref, own_prefix_ref):
+def soft_weights(lead_ref, near_refs, cent_ref, own_prefix_ref):
     docs = lead_ref.shape[0] - META
     h = lax.axis_index("dim")
-    prefix = jnp.where(h == 0, lead_ref[:docs, :], near_ref[:docs, :])
+    near = jnp.concatenate([ref[...] for ref in near_refs], axis=0)[:docs]
+    prefix = jnp.where(h == 0, lead_ref[:docs, :], near)
     scores = dot_nt(cent_ref[...], prefix) * TEMP
     top = jnp.max(scores, axis=0, keepdims=True)
     scale = 1.0 / jnp.sum(jnp.exp(scores - top), axis=0, keepdims=True)
@@ -196,28 +197,42 @@
 
 
 def sums_kernel(subs, lead_ref, rest_ref, near_ref, cent_ref, own_prefix_ref, *new):
-    weights = soft_weights(lead_ref, near_ref, cent_ref, own_prefix_ref)
+    weights = soft_weights(lead_ref, [near_ref], cent_ref, own_prefix_ref)
     add_lead(weights, lead_ref, (), new[:subs])
     add_rest(weights.astype(BF16), rest_ref[: weights.shape[1], :], (), new[subs:])
 
 
 def sums_lead_kernel(subs, lead_ref, near_ref, cent_ref, own_prefix_ref, *refs):
     old, weights_ref, new = refs[:subs], refs[subs], refs[subs + 1 :]
-    weights = soft_weights(lead_ref, near_ref, cent_ref, own_prefix_ref)
+    weights = soft_weights(lead_ref, [near_ref], cent_ref, own_prefix_ref)
     weights_ref[...] = weights.astype(BF16)
     add_lead(weights, lead_ref, old, new)
+
+
+def last_sums_lead_kernel(subs, lead_ref, low_ref, high_ref, cent_ref, own_prefix_ref, *refs):
+    old, weights_ref, new, totals = refs[:subs], refs[subs], refs[subs + 1 : 2 * subs + 1], refs[2 * subs + 1 :]
+    weights = soft_weights(lead_ref, [low_ref, high_ref], cent_ref, own_prefix_ref)
+    weights_ref[...] = weights.astype(BF16)
+    add_lead(weights, lead_ref, old, new[:1] + totals)
+    for sent, total in zip(new[1:], totals):
+        whole = total[...]
+        mass = whole[-SUBLANES:]
+        high = mass.astype(BF16).astype(F32)
+        sent[...] = jnp.concatenate([whole[:-SUBLANES], high, mass - high], axis=0).astype(BF16)
 
 
 def sums_rest_kernel(count, subs, *refs):
     weights_refs, rest_refs, old, new = refs[:count], refs[count : 2 * count], refs[-2 * subs : -subs], refs[-subs:]
     total = sum(dot(w[...], rest[: w.shape[1], :]) for w, rest in zip(weights_refs, rest_refs))
-    per = new[0].shape[0]
+    per = old[0].shape[0]
     for t in range(subs):
-        new[t][...] = old[t][...] + total[t * per : (t + 1) * per]
-
-
-def gram_kernel(groups_of_bits, subs, *refs):
-    *member_refs, gram_ref, held = refs
+        part = old[t][...] + total[t * per : (t + 1) * per]
+        padding = jnp.zeros((new[t].shape[0] - per, part.shape[1]), F32)
+        new[t][...] = jnp.concatenate([part, padding], axis=0).astype(new[t].dtype) if padding.shape[0] else part
+
+
+def gram_kernel(groups_of_bits, subs, parts, *refs):
+    member_refs, gram_refs, held = refs[: -parts - 1], refs[-parts - 1 : -1], refs[-1]
     z, x = lax.axis_index("rows"), lax.axis_index("sub")
     owners, groups, packed, half = held.shape
     each = len(member_refs) // subs
@@ -240,12 +255,14 @@
         for start in range(0, size, tile):
             part = dot_nt(mine[start : start + tile], mine)
             part = part.reshape(tile // SUBLANES, SUBLANES, size)
-            gram_ref[g, start // SUBLANES : (start + tile) // SUBLANES, :] = jnp.sum(part * same, axis=1)
-
-
-def scaled_tiles(width, mine_ref, other_ref, scaled_ref):
-    groups, slots, size = mine_ref.shape
-    kept = scaled_ref.shape[1]
+            at = slice(start // SUBLANES, (start + tile) // SUBLANES)
+            gram_refs[g * parts // groups][g % (groups // parts), at, :] = jnp.sum(part * same, axis=1)
+
+
+def scaled_tiles(width, mine_refs, other_refs, scaled_ref):
+    groups, kept, size = scaled_ref.shape
+    slots = mine_refs[0].shape[1]
+    each = groups // len(mine_refs)
     h = lax.axis_index("dim")
     start = pl.multiple_of(h * kept, kept)
     row = lax.broadcasted_iota(jnp.int32, (slots, size), 0)
@@ -255,34 +272,42 @@
     kept_lane = lax.broadcasted_iota(jnp.int32, (kept, size), 1)
     kept_diagonal = kept_row == kept_lane // SUBLANES
     for g in range(groups):
-        total = mine_ref[g] + other_ref[g]
+        mine_ref, other_ref, at = mine_refs[g // each], other_refs[g // each], g % each
+        total = mine_ref[at] + other_ref[at]
         norms = jnp.sum(jnp.where(diagonal, total, 0.0), axis=0, keepdims=True)
         scale = lax.rsqrt(norms / width + EPS)
         spread = jnp.where(kept_diagonal, jnp.broadcast_to(scale, (kept, size)), 0.0)
         folded = spread[:, :LANES]
-        for at in range(LANES, size, LANES):
-            folded = folded + spread[:, at : at + LANES]
+        for lanes in range(LANES, size, LANES):
+            folded = folded + spread[:, lanes : lanes + LANES]
         step = SUBLANES
         while step < LANES:
             folded = folded + pltpu.roll(folded, step, 1)
             step *= 2
         row_scale = jnp.concatenate([folded] * (size // LANES), axis=1)
-        own = mine_ref[g, pl.ds(start, kept), :] + other_ref[g, pl.ds(start, kept), :]
+        own = mine_ref[at, pl.ds(start, kept), :] + other_ref[at, pl.ds(start, kept), :]
         scaled_ref[g] = own / width * row_scale * scale
 
 
-def finish_kernel(width, mine_ref, other_ref, *refs):
-    *part_refs, prior_ref, new_ref, tile_ref, scaled_ref = refs
-    subs = len(part_refs) // 2
-    lead = sum(ref[...] for ref in part_refs[1:subs]) + part_refs[0][...]
-    rest = sum(ref[...] for ref in part_refs[subs + 1 :]) + part_refs[subs][...]
-    per = rest.shape[0]
-    mass = jnp.transpose(lead[per:, :LANES])[:per, :1] + SMOOTH
+def finish_kernel(width, subs, parts, *refs):
+    mine_refs, other_refs, refs = refs[:parts], refs[parts : 2 * parts], refs[2 * parts :]
+    lead_refs, rest_refs = refs[:subs], refs[subs : 2 * subs]
+    prior_ref, new_ref, tile_ref, scaled_ref = refs[2 * subs :]
+    per = prior_ref.shape[0]
+    lead, mass = lead_refs[0][:per, :], lead_refs[0][per:, :]
+    for ref in lead_refs[1:]:
+        sent = ref[...].astype(F32)
+        lead = lead + sent[:per]
+        mass = mass + sent[per : per + SUBLANES] + sent[per + SUBLANES :]
+    rest = rest_refs[0][...]
+    for ref in rest_refs[1:]:
+        rest = rest + ref[...].astype(F32)[:per]
+    mass = jnp.transpose(mass[:, :LANES])[:per, :1] + SMOOTH
     prior = SMOOTH * prior_ref[...].astype(F32)
-    new_ref[:, :PREFIX] = (lead[:per] + prior[:, :PREFIX]) / mass
+    new_ref[:, :PREFIX] = (lead + prior[:, :PREFIX]) / mass
     new_ref[:, PREFIX:] = (rest + prior[:, PREFIX:]) / mass
 
-    scaled_tiles(width, mine_ref, other_ref, scaled_ref)
+    scaled_tiles(width, mine_refs, other_refs, scaled_ref)
     groups, kept, size = scaled_ref.shape
     slots = size // SUBLANES
     at = lax.broadcasted_iota(jnp.int32, (groups * size, per), 0)
@@ -364,8 +389,9 @@
     )
 
     lead_sum, rest_sum = shape((per + SUBLANES, PREFIX), F32), shape((per, half - PREFIX), F32)
+    sent_lead, sent_rest = shape((per + 2 * SUBLANES, PREFIX), BF16), shape((per + 2 * SUBLANES, half - PREFIX), BF16)
     sum_shapes = [lead_sum] * subs + [rest_sum] * subs
-    own_cost, other_cost = 2 * 1024 * 1024, 0
+    own_cost = 2 * 1024 * 1024
 
     prefix = near(lead)
     found = call(
@@ -390,32 +416,34 @@
         leads.update(zip(group, tied([leads[bits] for bits in group], found, lead_sums, rest_sums, before)))
         for bits in group:
             send(leads, bits)
-        prefixes = [near(leads[bits]) for bits in group]
+        if last:
+            lead = leads[group[0]]
+            halves = [near(lead[: docs // 2]), near(lead[docs // 2 : docs])]
         row_shapes = [shape((count, groups, packed, PREFIX), BF16)] * subs
         found = call(
             functools.partial(select_lead_kernel, count, subs),
             "select_lead",
             [shape((subs * per * MOST, docs), BF16)] * count + row_shapes,
             [inv, centre] + [leads[bits] for bits in group],
-            cost=other_cost,
         )
         picks, found = list(found[:count]), list(found[count:])
-        members.append(across(found))
         weights = []
-        for bits, prefix in zip(group, prefixes):
+        if last:
+            found = tied(found, members)
             weight, *lead_sums = call(
-                functools.partial(sums_lead_kernel, subs),
+                functools.partial(last_sums_lead_kernel, subs),
                 "sums_lead",
-                [shape((subs * per, docs), BF16)] + [lead_sum] * subs,
-                [leads[bits], prefix, cent_prefix, own_prefix] + lead_sums,
-                {4 + i: 1 + i for i in range(subs)},
-                cost=other_cost,
+                [shape((subs * per, docs), BF16), lead_sum] + [sent_lead] * (subs - 1),
+                [lead] + halves + [cent_prefix, own_prefix] + lead_sums,
+                {5: 1},
+                scratch=[pltpu.VMEM(lead_sum.shape, F32)] * (subs - 1),
             )
             weights.append(weight)
-        if last:
+            members.append(across(found))
             lead_sums = across(lead_sums)
-            before = (found, members[:-1])
+            before = (found, weights)
         else:
+            members.append(across(found))
             before = (found, members)
         rests.update(zip(group, tied([rests[bits] for bits in group], before)))
         for bits in group:
@@ -426,33 +454,44 @@
             "select_rest",
             row_shapes,
             [centre] + picks + [rests[bits] for bits in group],
-            cost=other_cost,
         )
+        members.append(across(found))
         if last:
-            found = tied(found, members)
-        members.append(across(found))
+            rest_sums = tied(rest_sums, members[:-1])
+        else:
+            for bits in group:
+                prefix = near(tied(leads[bits], rests[bits]))
+                weight, *lead_sums = call(
+                    functools.partial(sums_lead_kernel, subs),
+                    "sums_lead",
+                    [shape((subs * per, docs), BF16)] + [lead_sum] * subs,
+                    [leads[bits], prefix, cent_prefix, own_prefix] + lead_sums,
+                    {4 + i: 1 + i for i in range(subs)},
+                )
+                weights.append(weight)
         rest_sums = call(
             functools.partial(sums_rest_kernel, count, subs),
             "sums_rest",
-            [rest_sum] * subs,
+            [rest_sum] + [sent_rest if last else rest_sum] * (subs - 1),
             weights + [rests[bits] for bits in group] + list(rest_sums),
-            {2 * count + i: i for i in range(subs)},
-            cost=other_cost,
+            {2 * count + i: i for i in range(1 if last else subs)},
         )
+    members = tied(members, rest_sums)
     rest_sums = across(rest_sums)
 
-    (gram,) = call(
-        functools.partial(gram_kernel, groups_of_bits, subs),
+    parts = 2 if groups % 2 == 0 else 1
+    grams = call(
+        functools.partial(gram_kernel, groups_of_bits, subs, parts),
         "gram",
-        [shape((groups, slots, slots * SUBLANES), F32)],
+        [shape((groups // parts, slots, slots * SUBLANES), F32)] * parts,
         [arrays[t] for t in range(subs) for arrays in members],
         scratch=[pltpu.VMEM((owners, groups, packed, half), BF16)],
     )
     new_centroids, tiles = call(
-        functools.partial(finish_kernel, width),
+        functools.partial(finish_kernel, width, subs, parts),
         "finish",
         [shape((per, half), F32), shape((slots // 2, slots, per), BF16)],
-        [gram, near(gram)] + lead_sums + rest_sums + [prior],
+        list(grams) + [near(gram) for gram in grams] + lead_sums + rest_sums + [prior],
         scratch=[pltpu.VMEM((groups, slots // 2, slots * SUBLANES), F32)],
     )
     return (new_centroids, jnp.transpose(tiles, (2, 0, 1)))

time: 59.7 us -> 58 us (0.972)
  waiting for transfers between devices: 22.7 us -> 20.6 us
    ppermute x7, waiting for transfers between devices: 10.7 us -> 7.35 us  [across(): lax.ppermute(values[t], 'sub', [(i, (i + t) % subs) for i in range(subs)])]
    ppermute x5 -> x7, starting transfers between devices: 1.1 us -> 2.16 us  [near(): return lax.ppermute(value, 'dim', [(0, 1), (1, 0)])]
    ppermute x6, waiting for transfers between devices: 11.9 us -> 12.7 us  [swap(): return lax.ppermute(value, 'rows', [(i, i ^ bit) for i in range(rows)])]
    ppermute x7, starting transfers between devices: 10.6 us -> 9.84 us  [across(): lax.ppermute(values[t], 'sub', [(i, (i + t) % subs) for i in range(subs)])]
  transfers between devices with their start and end apart: 18 -> 20, of which waited for: 8 -> 10; matrix products, arithmetic and copies ran while one was open for 0% -> 0% of each run, Pallas kernels for 18% -> 19%
where the time goes in v10:
time: 58 us; the launch traced here: 57.7 us
  waiting for transfers between devices  20.6 us (36%)
  starting transfers between devices  20.1 us (35%)
  Pallas kernels  12.2 us (21%)
  local copies, waits for them, and re-layouts  4.01 us (7%)
  between operations  0.79 us (1%)
    ppermute x6, waiting for transfers between devices, swap(): return lax.ppermute(value, 'rows', [(i, i ^ bit) for i in range(rows)])  12.7 us
    pallas_call x15, Pallas kernels, call(): pl.pallas_call(kernel, out_shape=tuple(out_shape), in_specs=[whole(operan...  12.2 us
    ppermute x7, starting transfers between devices, across(): lax.ppermute(values[t], 'sub', [(i, (i + t) % subs) for i in range(subs)])  9.84 us
    ppermute x6, starting transfers between devices, swap(): return lax.ppermute(value, 'rows', [(i, i ^ bit) for i in range(rows)])  8.05 us
    ppermute x7, waiting for transfers between devices, across(): lax.ppermute(values[t], 'sub', [(i, (i + t) % subs) for i in range(subs)])  7.35 us
    unnamed x8, local copies, waits for them, and re-layouts  3.99 us
    ppermute x7, starting transfers between devices, near(): return lax.ppermute(value, 'dim', [(0, 1), (1, 0)])  2.16 us
  transfers between devices with their start and end apart: 20, of which 10 were waited for; matrix products, arithmetic and copies ran while one was open for 0% of the time, Pallas kernels for 19%

profile of v10, /device:TPU:0, one launch (start us, length us, event | category | flops | bytes accessed | tf_op | source)
XLA Modules:
  0.0 57.7 jit_solution(2055607162525989750)
XLA Ops:
  0.6 1.0 %copy-done.1 = bf16[512,512]{1,0:T(8,128)(2,1)S(1)} copy-done((bf16[512,512]{1,0:T(8,128)(2,1)S(1)}, bf16[512,512]{1,0:T(8,128)(2,1)}, u32[]{:S(2)}) %copy-start.1) | copy-done | bytes 524312
  1.7 0.7 %copy-done.3 = s32[512,1]{0,1:T(1,128)S(1)} copy-done((s32[512,1]{0,1:T(1,128)S(1)}, s32[512,1]{0,1:T(1,128)}, u32[]{:S(2)}) %copy-start.3) | copy-done | bytes 2072
  2.4 0.5 collective-permute-start.3
  2.9 2.6 %collective-permute-start.1 = (bf16[528,256]{1,0:T(8,128)(2,1)S(1)}, bf16[528,256]{1,0:T(8,128)(2,1)S(1)}, u32[]{:S(2)}, u32[]{:S(2)}) collective-permute-start(bf16[528,256]{1,0:T(8,128)(2,1)S(1)} %get-tuple-element.66.lead_ref), channel_id=1, source_target_pairs={{0,4},{4,0},{8,12},{12,8},{1,5},{5,1},{9,13},{13,9},{2,6},{6,2},{1... | collective-permute-start | bytes 811016 | tf_op jit(solution)/shard_map/ppermute | solution.py:360
  5.6 2.6 %collective-permute-start.2 = (bf16[528,256]{1,0:T(8,128)(2,1)S(1)}, bf16[528,256]{1,0:T(8,128)(2,1)S(1)}, u32[]{:S(2)}, u32[]{:S(2)}) collective-permute-start(bf16[528,256]{1,0:T(8,128)(2,1)S(1)} %get-tuple-element.66.lead_ref), channel_id=1, source_target_pairs={{0,8},{4,12},{8,0},{12,4},{1,9},{5,13},{9,1},{13,5},{2,10},{6,14},... | collective-permute-start | bytes 811016 | tf_op jit(solution)/shard_map/ppermute | solution.py:360
  8.2 1.6 %copy-done = bf16[1024,1024]{1,0:T(8,128)(2,1)S(1)} copy-done((bf16[1024,1024]{1,0:T(8,128)(2,1)S(1)}, bf16[1024,1024]{1,0:T(8,128)(2,1)}, u32[]{:S(2)}) %copy-start) | copy-done | bytes 2097176
  9.8 0.7 %copy-done.2 = s32[1024]{0:T(1024)S(1)} copy-done((s32[1024]{0:T(1024)S(1)}, s32[1024]{0:T(1024)}, u32[]{:S(2)}) %copy-start.2) | copy-done | bytes 4120
  10.4 0.8 %prep.1 = (f32[256,1]{1,0:T(8,128)S(1)}, bf16[256,512]{1,0:T(8,128)(2,1)S(1)}, bf16[256,256]{1,0:T(8,128)(2,1)S(1)}, bf16[128,512]{1,0:T(8,128)(2,1)S(1)}, bf16[1024,256]{1,0:T(8,128)(2,1)S(1)}) custom-call(s32[1,1024]{1,0:T(1,128)S(1)} %bitcast.3, bf16[1024,1024]{1,0:T(8,128)(2,1)S(1)} %copy-done), custom_call_target="tpu_custom_call" | custom-call | flops 209715200 | bytes 4194304 | tf_op jit(solution)/shard_map/prep/pallas_call | solution.py:32
  11.3 0.8 %select.1 = (bf16[16,16,512]{2,1,0:T(8,128)(2,1)S(1)}, bf16[16,16,512]{2,1,0:T(8,128)(2,1)S(1)}) custom-call(bf16[528,256]{1,0:T(8,128)(2,1)S(1)} %get-tuple-element.66.lead_ref, bf16[528,256]{1,0:T(8,128)(2,1)S(1)} %get-tuple-element.84.rest_ref, f32[256,1]{1,0:T(8,128)S(1)} %get-tuple-element.68.inv_ref, bf16[256,512]{1,0:T(8,128)(2,1)S(1)} %get-tuple-element.69.centre_ref), custom_call_target="tpu_custom_call" | custom-call | flops 104857600 | bytes 2097152 | tf_op jit(solution)/shard_map/select/pallas_call | solution.py:32
  12.0 1.5 %collective-permute-start = (bf16[16,16,512]{2,1,0:T(8,128)(2,1)S(1)}, bf16[16,16,512]{2,1,0:T(8,128)(2,1)S(1)}, u32[]{:S(2)}, u32[]{:S(2)}) collective-permute-start(bf16[16,16,512]{2,1,0:T(8,128)(2,1)S(1)} %get-tuple-element.71), channel_id=1, source_target_pairs={{0,2},{2,0},{1,3},{3,1},{4,6},{6,4},{5,7},{7,5},{8,10},{10,8},{9,1... | collective-permute-start | bytes 786440 | tf_op jit(solution)/shard_map/ppermute | solution.py:353
  13.6 0.4 collective-permute-start.5
  14.0 0.3 collective-permute-start.6
  14.4 1.3 %sums.1 = (f32[136,256]{1,0:T(8,128)S(1)}, f32[136,256]{1,0:T(8,128)S(1)}, f32[128,256]{1,0:T(8,128)S(1)}, f32[128,256]{1,0:T(8,128)S(1)}) custom-call(bf16[528,256]{1,0:T(8,128)(2,1)S(1)} %get-tuple-element.66.lead_ref, bf16[528,256]{1,0:T(8,128)(2,1)S(1)} %get-tuple-element.84.rest_ref, bf16[528,256]{1,0:T(8,128)(2,1)S(1)} %collective-permute-done.3.near_ref, ...), custom_call_target="tpu_custom_call" | custom-call | flops 104857600 | bytes 2097152 | tf_op jit(solution)/shard_map/sums/pallas_call | solution.py:32
  15.7 4.5 %collective-permute-done.refs_5_ = bf16[16,16,512]{2,1,0:T(8,128)(2,1)S(1)} collective-permute-done((bf16[16,16,512]{2,1,0:T(8,128)(2,1)S(1)}, bf16[16,16,512]{2,1,0:T(8,128)(2,1)S(1)}, u32[]{:S(2)}, u32[]{:S(2)}) %collective-permute-start) | collective-permute-done | bytes 262176 | tf_op jit(solution)/shard_map/ppermute | solution.py:353
  20.2 0.5 collective-permute-done.2.refs_1_.lead_ref
  20.7 1.1 %select_lead.2 = (bf16[512,512]{1,0:T(8,128)(2,1)S(1)}, bf16[512,512]{1,0:T(8,128)(2,1)S(1)}, bf16[2,16,16,256]{3,2,1,0:T(8,128)(2,1)S(1)}, bf16[2,16,16,256]{3,2,1,0:T(8,128)(2,1)S(1)}) custom-call(f32[256,1]{1,0:T(8,128)S(1)} %get-tuple-element.68.inv_ref, bf16[256,512]{1,0:T(8,128)(2,1)S(1)} %get-tuple-element.69.centre_ref, ...), custom_call_target="tpu_custom_call" | custom-call | tf_op jit(solution)/shard_map/select_lead/pallas_call | solution.py:32
  21.8 1.6 %collective-permute-start.4 = (bf16[2,16,16,256]{3,2,1,0:T(8,128)(2,1)S(1)}, bf16[2,16,16,256]{3,2,1,0:T(8,128)(2,1)S(1)}, u32[]{:S(2)}, u32[]{:S(2)}) collective-permute-start(bf16[2,16,16,256]{3,2,1,0:T(8,128)(2,1)S(1)} %get-tuple-element.81), channel_id=1, source_target_pairs={{0,2},{2,0},{1,3},{3,1},{4,6},{6,4},{5,7},{7,5},{8,10},{10,8},{9,1... | collective-permute-start | bytes 786440 | tf_op jit(solution)/shard_map/ppermute | solution.py:353
  23.3 6.6 %collective-permute-done.5.refs_2_ = bf16[528,256]{1,0:T(8,128)(2,1)S(1)} collective-permute-done((bf16[528,256]{1,0:T(8,128)(2,1)S(1)}, bf16[528,256]{1,0:T(8,128)(2,1)S(1)}, u32[]{:S(2)}, u32[]{:S(2)}) %collective-permute-start.5) | collective-permute-done | bytes 270368 | tf_op jit(solution)/shard_map/ppermute | solution.py:360
  29.9 2.6 %collective-permute-done.6.refs_3_ = bf16[528,256]{1,0:T(8,128)(2,1)S(1)} collective-permute-done((bf16[528,256]{1,0:T(8,128)(2,1)S(1)}, bf16[528,256]{1,0:T(8,128)(2,1)S(1)}, u32[]{:S(2)}, u32[]{:S(2)}) %collective-permute-start.6) | collective-permute-done | bytes 270368 | tf_op jit(solution)/shard_map/ppermute | solution.py:360
  32.5 0.1 collective-permute-start.10
  32.6 0.4 collective-permute-start.9
  33.0 0.4 collective-permute-start.8
  33.5 1.6 %collective-permute-start.12 = (bf16[528,256]{1,0:T(8,128)(2,1)S(1)}, bf16[528,256]{1,0:T(8,128)(2,1)S(1)}, u32[]{:S(2)}, u32[]{:S(2)}) collective-permute-start(bf16[528,256]{1,0:T(8,128)(2,1)S(1)} %collective-permute-done.6.refs_3_), channel_id=1, source_target_pairs={{0,4},{4,0},{8,12},{12,8},{1,5},{5,1},{9,13},{13,9},{2,6},{6,2},{1... | collective-permute-start | bytes 811016 | tf_op jit(solution)/shard_map/ppermute | solution.py:360
  35.0 0.4 select_rest.2
  35.5 1.6 %collective-permute-start.7 = (bf16[2,16,16,256]{3,2,1,0:T(8,128)(2,1)S(1)}, bf16[2,16,16,256]{3,2,1,0:T(8,128)(2,1)S(1)}, u32[]{:S(2)}, u32[]{:S(2)}) collective-permute-start(bf16[2,16,16,256]{3,2,1,0:T(8,128)(2,1)S(1)} %get-tuple-element.88), channel_id=1, source_target_pairs={{0,2},{2,0},{1,3},{3,1},{4,6},{6,4},{5,7},{7,5},{8,10},{10,8},{9,1... | collective-permute-start | bytes 786440 | tf_op jit(solution)/shard_map/ppermute | solution.py:353
  37.0 1.4 %sums_lead.3 = (bf16[256,512]{1,0:T(8,128)(2,1)S(1)}, f32[136,256]{1,0:T(8,128)S(1)}, f32[136,256]{1,0:T(8,128)S(1)}) custom-call(bf16[528,256]{1,0:T(8,128)(2,1)S(1)} %collective-permute-done.1.refs_0_.lead_ref, bf16[528,256]{1,0:T(8,128)(2,1)S(1)} %collective-permute-done.10.near_ref, ...), custom_call_target="tpu_custom_call", output_to_operand_aliasing={{1}: (4, {}), {2}: (5, {})} | custom-call | tf_op jit(solution)/shard_map/sums_lead/pallas_call | solution.py:32
  38.4 1.4 %sums_lead.4 = (bf16[256,512]{1,0:T(8,128)(2,1)S(1)}, f32[136,256]{1,0:T(8,128)S(1)}, f32[136,256]{1,0:T(8,128)S(1)}) custom-call(bf16[528,256]{1,0:T(8,128)(2,1)S(1)} %collective-permute-done.2.refs_1_.lead_ref, bf16[528,256]{1,0:T(8,128)(2,1)S(1)} %collective-permute-done.9.near_ref, ...), custom_call_target="tpu_custom_call", output_to_operand_aliasing={{1}: (4, {}), {2}: (5, {})} | custom-call | tf_op jit(solution)/shard_map/sums_lead/pallas_call | solution.py:32
  39.8 0.3 sums_rest.2
  40.1 2.2 %collective-permute-done.8.refs_0_.lead_ref = bf16[528,256]{1,0:T(8,128)(2,1)S(1)} collective-permute-done((bf16[528,256]{1,0:T(8,128)(2,1)S(1)}, bf16[528,256]{1,0:T(8,128)(2,1)S(1)}, u32[]{:S(2)}, u32[]{:S(2)}) %collective-permute-start.8) | collective-permute-done | bytes 270368 | tf_op jit(solution)/shard_map/ppermute | solution.py:360
  42.4 0.1 collective-permute-start.13
  42.4 0.5 collective-permute-start.14
  42.9 0.6 %select_lead.3 = (bf16[512,512]{1,0:T(8,128)(2,1)S(1)}, bf16[1,16,16,256]{3,2,1,0:T(8,128)(2,1)S(1)}, bf16[1,16,16,256]{3,2,1,0:T(8,128)(2,1)S(1)}) custom-call(f32[256,1]{1,0:T(8,128)S(1)} %get-tuple-element.68.inv_ref, bf16[256,512]{1,0:T(8,128)(2,1)S(1)} %get-tuple-element.69.centre_ref, bf16[528,256]{1,0:T(8,128)(2,1)S(1)} %collective-permute-done.8.refs_0_.lead_ref), custom_call_target="tpu_custom_call" | custom-call | tf_op jit(solution)/shard_map/select_lead/pallas_call | solution.py:32
  43.5 1.6 %collective-permute-start.11 = (bf16[1,16,16,256]{3,2,1,0:T(8,128)(2,1)S(1)}, bf16[1,16,16,256]{3,2,1,0:T(8,128)(2,1)S(1)}, u32[]{:S(2)}, u32[]{:S(2)}) collective-permute-start(bf16[1,16,16,256]{3,2,1,0:T(8,128)(2,1)S(1)} %get-tuple-element.103), channel_id=1, source_target_pairs={{0,2},{2,0},{1,3},{3,1},{4,6},{6,4},{5,7},{7,5},{8,10},{10,8},{9,1... | collective-permute-start | bytes 393224 | tf_op jit(solution)/shard_map/ppermute | solution.py:353
  45.1 1.4 %sums_lead.5 = (bf16[256,512]{1,0:T(8,128)(2,1)S(1)}, f32[136,256]{1,0:T(8,128)S(1)}, bf16[144,256]{1,0:T(8,128)(2,1)S(1)}) custom-call(bf16[528,256]{1,0:T(8,128)(2,1)S(1)} %collective-permute-done.8.refs_0_.lead_ref, bf16[256,256]{1,0:T(8,128)(2,1)S(1)} %collective-permute-done.13.low_ref, ...), custom_call_target="tpu_custom_call", output_to_operand_aliasing={{1}: (5, {})} | custom-call | tf_op jit(solution)/shard_map/sums_lead/pallas_call | solution.py:32
  46.5 0.8 %collective-permute-done.12.refs_1_ = bf16[528,256]{1,0:T(8,128)(2,1)S(1)} collective-permute-done((bf16[528,256]{1,0:T(8,128)(2,1)S(1)}, bf16[528,256]{1,0:T(8,128)(2,1)S(1)}, u32[]{:S(2)}, u32[]{:S(2)}) %collective-permute-start.12) | collective-permute-done | bytes 270368 | tf_op jit(solution)/shard_map/ppermute | solution.py:360
  47.3 0.3 select_rest.3
  47.6 1.6 %collective-permute-start.15 = (bf16[1,16,16,256]{3,2,1,0:T(8,128)(2,1)S(1)}, bf16[1,16,16,256]{3,2,1,0:T(8,128)(2,1)S(1)}, u32[]{:S(2)}, u32[]{:S(2)}) collective-permute-start(bf16[1,16,16,256]{3,2,1,0:T(8,128)(2,1)S(1)} %get-tuple-element.108), channel_id=1, source_target_pairs={{0,2},{2,0},{1,3},{3,1},{4,6},{6,4},{5,7},{7,5},{8,10},{10,8},{9,1... | collective-permute-start | bytes 393224 | tf_op jit(solution)/shard_map/ppermute | solution.py:353
  49.1 0.2 sums_rest.3
  49.4 1.5 %collective-permute-start.19 = (bf16[144,256]{1,0:T(8,128)(2,1)S(1)}, bf16[144,256]{1,0:T(8,128)(2,1)S(1)}, u32[]{:S(2)}, u32[]{:S(2)}) collective-permute-start(bf16[144,256]{1,0:T(8,128)(2,1)S(1)} %get-tuple-element.112), channel_id=1, source_target_pairs={{0,2},{2,0},{1,3},{3,1},{4,6},{6,4},{5,7},{7,5},{8,10},{10,8},{9,1... | collective-permute-start | bytes 221192 | tf_op jit(solution)/shard_map/ppermute | solution.py:353
  50.9 0.6 collective-permute-start.18
  51.5 2.5 %collective-permute-done.15.refs_9_ = bf16[1,16,16,256]{3,2,1,0:T(8,128)(2,1)S(1)} collective-permute-done((bf16[1,16,16,256]{3,2,1,0:T(8,128)(2,1)S(1)}, bf16[1,16,16,256]{3,2,1,0:T(8,128)(2,1)S(1)}, u32[]{:S(2)}, u32[]{:S(2)}) %collective-permute-start.15) | collective-permute-done | bytes 131104 | tf_op jit(solution)/shard_map/ppermute | solution.py:353
  54.0 0.9 %gram.1 = (f32[8,16,128]{2,1,0:T(8,128)S(1)}, f32[8,16,128]{2,1,0:T(8,128)S(1)}) custom-call(bf16[16,16,512]{2,1,0:T(8,128)(2,1)S(1)} %get-tuple-element.113.refs_0_, bf16[2,16,16,256]{3,2,1,0:T(8,128)(2,1)S(1)} %get-tuple-element.114.refs_1_, bf16[2,16,16,256]{3,2,1,0:T(8,128)(2,1)S(1)} %get-tuple-element.115.refs_2_, ...), custom_call_target="tpu_custom_call" | custom-call | tf_op jit(solution)/shard_map/gram/pallas_call | solution.py:32
  54.9 0.1 collective-permute-start.16
  54.9 0.5 collective-permute-start.17
  55.4 0.3 collective-permute-done.18.refs_5_
  55.8 0.4 collective-permute-done.16.refs_2_
  56.2 0.2 collective-permute-done.17.refs_3_
  56.3 1.4 %finish.1 = (f32[128,512]{1,0:T(8,128)}, bf16[8,16,128]{2,1,0:T(8,128)(2,1)}) custom-call(f32[8,16,128]{2,1,0:T(8,128)S(1)} %get-tuple-element.123.refs_0_, f32[8,16,128]{2,1,0:T(8,128)S(1)} %get-tuple-element.124.refs_1_, f32[8,16,128]{2,1,0:T(8,128)S(1)} %collective-permute-done.16.refs_2_, f32[8,16,128]{2,1,0:T(8,128)S(1)} %collective-permute-done.17.refs_3_, ...), custom_call_target="tpu_custom_call" | custom-call | tf_op jit(solution)/shard_map/finish/pallas_call | solution.py:32
  (16 shorter events, 0.1 us)
Async XLA Ops:
  0.6 1.0 %copy-start.1 = (bf16[512,512]{1,0:T(8,128)(2,1)S(1)}, bf16[512,512]{1,0:T(8,128)(2,1)}, u32[]{:S(2)}) copy-start(bf16[512,512]{1,0:T(8,128)(2,1)} %emb_ref.1) | copy-start | bytes 1572868
  1.7 0.7 %copy-start.3 = (s32[512,1]{0,1:T(1,128)S(1)}, s32[512,1]{0,1:T(1,128)}, u32[]{:S(2)}) copy-start(s32[512,1]{0,1:T(1,128)} %param.6) | copy-start | bytes 6148
  2.4 11.6 %collective-permute-start.3 = (bf16[528,256]{1,0:T(8,128)(2,1)S(1)}, bf16[528,256]{1,0:T(8,128)(2,1)S(1)}, u32[]{:S(2)}, u32[]{:S(2)}) collective-permute-start(bf16[528,256]{1,0:T(8,128)(2,1)S(1)} %get-tuple-element.66.lead_ref), channel_id=1, source_target_pairs={{0,1},{1,0},{2,3},{3,2},{4,5},{5,4},{6,7},{7,6},{8,9},{9,8},{10,11... | collective-permute-start | bytes 811016 | tf_op jit(solution)/shard_map/ppermute | solution.py:357
  2.9 17.3 %collective-permute-start.1 = (bf16[528,256]{1,0:T(8,128)(2,1)S(1)}, bf16[528,256]{1,0:T(8,128)(2,1)S(1)}, u32[]{:S(2)}, u32[]{:S(2)}) collective-permute-start(bf16[528,256]{1,0:T(8,128)(2,1)S(1)} %get-tuple-element.66.lead_ref), channel_id=1, source_target_pairs={{0,4},{4,0},{8,12},{12,8},{1,5},{5,1},{9,13},{13,9},{2,6},{6,2},{1... | collective-permute-start | bytes 811016 | tf_op jit(solution)/shard_map/ppermute | solution.py:360
  5.6 15.1 %collective-permute-start.2 = (bf16[528,256]{1,0:T(8,128)(2,1)S(1)}, bf16[528,256]{1,0:T(8,128)(2,1)S(1)}, u32[]{:S(2)}, u32[]{:S(2)}) collective-permute-start(bf16[528,256]{1,0:T(8,128)(2,1)S(1)} %get-tuple-element.66.lead_ref), channel_id=1, source_target_pairs={{0,8},{4,12},{8,0},{12,4},{1,9},{5,13},{9,1},{13,5},{2,10},{6,14},... | collective-permute-start | bytes 811016 | tf_op jit(solution)/shard_map/ppermute | solution.py:360
  8.2 1.6 %copy-start = (bf16[1024,1024]{1,0:T(8,128)(2,1)S(1)}, bf16[1024,1024]{1,0:T(8,128)(2,1)}, u32[]{:S(2)}) copy-start(bf16[1024,1024]{1,0:T(8,128)(2,1)} %cent_ref.1) | copy-start | bytes 6291460
  9.8 0.7 %copy-start.2 = (s32[1024]{0:T(1024)S(1)}, s32[1024]{0:T(1024)}, u32[]{:S(2)}) copy-start(s32[1024]{0:T(1024)} %param.7) | copy-start | bytes 12292
  12.0 8.1 %collective-permute-start = (bf16[16,16,512]{2,1,0:T(8,128)(2,1)S(1)}, bf16[16,16,512]{2,1,0:T(8,128)(2,1)S(1)}, u32[]{:S(2)}, u32[]{:S(2)}) collective-permute-start(bf16[16,16,512]{2,1,0:T(8,128)(2,1)S(1)} %get-tuple-element.71), channel_id=1, source_target_pairs={{0,2},{2,0},{1,3},{3,1},{4,6},{6,4},{5,7},{7,5},{8,10},{10,8},{9,1... | collective-permute-start | bytes 786440 | tf_op jit(solution)/shard_map/ppermute | solution.py:353
  13.6 16.3 %collective-permute-start.5 = (bf16[528,256]{1,0:T(8,128)(2,1)S(1)}, bf16[528,256]{1,0:T(8,128)(2,1)S(1)}, u32[]{:S(2)}, u32[]{:S(2)}) collective-permute-start(bf16[528,256]{1,0:T(8,128)(2,1)S(1)} %get-tuple-element.84.rest_ref), channel_id=1, source_target_pairs={{0,4},{4,0},{8,12},{12,8},{1,5},{5,1},{9,13},{13,9},{2,6},{6,2},{1... | collective-permute-start | bytes 811016 | tf_op jit(solution)/shard_map/ppermute | solution.py:360
  14.0 18.5 %collective-permute-start.6 = (bf16[528,256]{1,0:T(8,128)(2,1)S(1)}, bf16[528,256]{1,0:T(8,128)(2,1)S(1)}, u32[]{:S(2)}, u32[]{:S(2)}) collective-permute-start(bf16[528,256]{1,0:T(8,128)(2,1)S(1)} %get-tuple-element.84.rest_ref), channel_id=1, source_target_pairs={{0,8},{4,12},{8,0},{12,4},{1,9},{5,13},{9,1},{13,5},{2,10},{6,14},... | collective-permute-start | bytes 811016 | tf_op jit(solution)/shard_map/ppermute | solution.py:360
  21.8 10.7 %collective-permute-start.4 = (bf16[2,16,16,256]{3,2,1,0:T(8,128)(2,1)S(1)}, bf16[2,16,16,256]{3,2,1,0:T(8,128)(2,1)S(1)}, u32[]{:S(2)}, u32[]{:S(2)}) collective-permute-start(bf16[2,16,16,256]{3,2,1,0:T(8,128)(2,1)S(1)} %get-tuple-element.81), channel_id=1, source_target_pairs={{0,2},{2,0},{1,3},{3,1},{4,6},{6,4},{5,7},{7,5},{8,10},{10,8},{9,1... | collective-permute-start | bytes 786440 | tf_op jit(solution)/shard_map/ppermute | solution.py:353
  32.5 4.6 %collective-permute-start.10 = (bf16[528,256]{1,0:T(8,128)(2,1)S(1)}, bf16[528,256]{1,0:T(8,128)(2,1)S(1)}, u32[]{:S(2)}, u32[]{:S(2)}) collective-permute-start(bf16[528,256]{1,0:T(8,128)(2,1)S(1)} %collective-permute-done.1.refs_0_.lead_ref), channel_id=1, source_target_pairs={{0,1},{1,0},{2,3},{3,2},{4,5},{5,4},{6,7},{7,6},{8,9},{9,8},{10,11... | collective-permute-start | bytes 811016 | tf_op jit(solution)/shard_map/ppermute | solution.py:357
  32.6 5.9 %collective-permute-start.9 = (bf16[528,256]{1,0:T(8,128)(2,1)S(1)}, bf16[528,256]{1,0:T(8,128)(2,1)S(1)}, u32[]{:S(2)}, u32[]{:S(2)}) collective-permute-start(bf16[528,256]{1,0:T(8,128)(2,1)S(1)} %collective-permute-done.2.refs_1_.lead_ref), channel_id=1, source_target_pairs={{0,1},{1,0},{2,3},{3,2},{4,5},{5,4},{6,7},{7,6},{8,9},{9,8},{10,11... | collective-permute-start | bytes 811016 | tf_op jit(solution)/shard_map/ppermute | solution.py:357
  33.0 9.3 %collective-permute-start.8 = (bf16[528,256]{1,0:T(8,128)(2,1)S(1)}, bf16[528,256]{1,0:T(8,128)(2,1)S(1)}, u32[]{:S(2)}, u32[]{:S(2)}) collective-permute-start(bf16[528,256]{1,0:T(8,128)(2,1)S(1)} %collective-permute-done.2.refs_1_.lead_ref), channel_id=1, source_target_pairs={{0,4},{4,0},{8,12},{12,8},{1,5},{5,1},{9,13},{13,9},{2,6},{6,2},{1... | collective-permute-start | bytes 811016 | tf_op jit(solution)/shard_map/ppermute | solution.py:360
  33.5 13.8 %collective-permute-start.12 = (bf16[528,256]{1,0:T(8,128)(2,1)S(1)}, bf16[528,256]{1,0:T(8,128)(2,1)S(1)}, u32[]{:S(2)}, u32[]{:S(2)}) collective-permute-start(bf16[528,256]{1,0:T(8,128)(2,1)S(1)} %collective-permute-done.6.refs_3_), channel_id=1, source_target_pairs={{0,4},{4,0},{8,12},{12,8},{1,5},{5,1},{9,13},{13,9},{2,6},{6,2},{1... | collective-permute-start | bytes 811016 | tf_op jit(solution)/shard_map/ppermute | solution.py:360
  35.5 8.0 %collective-permute-start.7 = (bf16[2,16,16,256]{3,2,1,0:T(8,128)(2,1)S(1)}, bf16[2,16,16,256]{3,2,1,0:T(8,128)(2,1)S(1)}, u32[]{:S(2)}, u32[]{:S(2)}) collective-permute-start(bf16[2,16,16,256]{3,2,1,0:T(8,128)(2,1)S(1)} %get-tuple-element.88), channel_id=1, source_target_pairs={{0,2},{2,0},{1,3},{3,1},{4,6},{6,4},{5,7},{7,5},{8,10},{10,8},{9,1... | collective-permute-start | bytes 786440 | tf_op jit(solution)/shard_map/ppermute | solution.py:353
  42.4 2.7 %collective-permute-start.13 = (bf16[256,256]{1,0:T(8,128)(2,1)S(1)}, bf16[256,256]{1,0:T(8,128)(2,1)S(1)}, u32[]{:S(2)}, u32[]{:S(2)}) collective-permute-start(bf16[256,256]{1,0:T(8,128)(2,1)S(1)} %get-tuple-element.131), channel_id=1, source_target_pairs={{0,1},{1,0},{2,3},{3,2},{4,5},{5,4},{6,7},{7,6},{8,9},{9,8},{10,11... | collective-permute-start | bytes 393224 | tf_op jit(solution)/shard_map/ppermute | solution.py:357
  42.4 2.7 %collective-permute-start.14 = (bf16[256,256]{1,0:T(8,128)(2,1)S(1)}, bf16[256,256]{1,0:T(8,128)(2,1)S(1)}, u32[]{:S(2)}, u32[]{:S(2)}) collective-permute-start(bf16[256,256]{1,0:T(8,128)(2,1)S(1)} %get-tuple-element.130), channel_id=1, source_target_pairs={{0,1},{1,0},{2,3},{3,2},{4,5},{5,4},{6,7},{7,6},{8,9},{9,8},{10,11... | collective-permute-start | bytes 393224 | tf_op jit(solution)/shard_map/ppermute | solution.py:357
  43.5 5.6 %collective-permute-start.11 = (bf16[1,16,16,256]{3,2,1,0:T(8,128)(2,1)S(1)}, bf16[1,16,16,256]{3,2,1,0:T(8,128)(2,1)S(1)}, u32[]{:S(2)}, u32[]{:S(2)}) collective-permute-start(bf16[1,16,16,256]{3,2,1,0:T(8,128)(2,1)S(1)} %get-tuple-element.103), channel_id=1, source_target_pairs={{0,2},{2,0},{1,3},{3,1},{4,6},{6,4},{5,7},{7,5},{8,10},{10,8},{9,1... | collective-permute-start | bytes 393224 | tf_op jit(solution)/shard_map/ppermute | solution.py:353
  47.6 6.4 %collective-permute-start.15 = (bf16[1,16,16,256]{3,2,1,0:T(8,128)(2,1)S(1)}, bf16[1,16,16,256]{3,2,1,0:T(8,128)(2,1)S(1)}, u32[]{:S(2)}, u32[]{:S(2)}) collective-permute-start(bf16[1,16,16,256]{3,2,1,0:T(8,128)(2,1)S(1)} %get-tuple-element.108), channel_id=1, source_target_pairs={{0,2},{2,0},{1,3},{3,1},{4,6},{6,4},{5,7},{7,5},{8,10},{10,8},{9,1... | collective-permute-start | bytes 393224 | tf_op jit(solution)/shard_map/ppermute | solution.py:353
  49.4 6.1 %collective-permute-start.19 = (bf16[144,256]{1,0:T(8,128)(2,1)S(1)}, bf16[144,256]{1,0:T(8,128)(2,1)S(1)}, u32[]{:S(2)}, u32[]{:S(2)}) collective-permute-start(bf16[144,256]{1,0:T(8,128)(2,1)S(1)} %get-tuple-element.112), channel_id=1, source_target_pairs={{0,2},{2,0},{1,3},{3,1},{4,6},{6,4},{5,7},{7,5},{8,10},{10,8},{9,1... | collective-permute-start | bytes 221192 | tf_op jit(solution)/shard_map/ppermute | solution.py:353
  50.9 4.9 %collective-permute-start.18 = (bf16[144,256]{1,0:T(8,128)(2,1)S(1)}, bf16[144,256]{1,0:T(8,128)(2,1)S(1)}, u32[]{:S(2)}, u32[]{:S(2)}) collective-permute-start(bf16[144,256]{1,0:T(8,128)(2,1)S(1)} %get-tuple-element.126), channel_id=1, source_target_pairs={{0,2},{2,0},{1,3},{3,1},{4,6},{6,4},{5,7},{7,5},{8,10},{10,8},{9,1... | collective-permute-start | bytes 221192 | tf_op jit(solution)/shard_map/ppermute | solution.py:353
  54.9 1.3 %collective-permute-start.16 = (f32[8,16,128]{2,1,0:T(8,128)S(1)}, f32[8,16,128]{2,1,0:T(8,128)S(1)}, u32[]{:S(2)}, u32[]{:S(2)}) collective-permute-start(f32[8,16,128]{2,1,0:T(8,128)S(1)} %get-tuple-element.123.refs_0_), channel_id=1, source_target_pairs={{0,1},{1,0},{2,3},{3,2},{4,5},{5,4},{6,7},{7,6},{8,9},{9,8},{10,11... | collective-permute-start | bytes 196616 | tf_op jit(solution)/shard_map/ppermute | solution.py:357
  54.9 1.4 %collective-permute-start.17 = (f32[8,16,128]{2,1,0:T(8,128)S(1)}, f32[8,16,128]{2,1,0:T(8,128)S(1)}, u32[]{:S(2)}, u32[]{:S(2)}) collective-permute-start(f32[8,16,128]{2,1,0:T(8,128)S(1)} %get-tuple-element.124.refs_1_), channel_id=1, source_target_pairs={{0,1},{1,0},{2,3},{3,2},{4,5},{5,4},{6,7},{7,6},{8,9},{9,8},{10,11... | collective-permute-start | bytes 196616 | tf_op jit(solution)/shard_map/ppermute | solution.py:357

commit v11 on v10

--- a/solution.py
+++ b/solution.py
@@ -359,10 +359,10 @@
     def swap(value, bit):
         return lax.ppermute(value, "rows", [(i, i ^ bit) for i in range(rows)])
 
-    def send(blocks, bits):
+    def send(blocks, bits, value):
         bit = (bits & -bits or rows) // 2
         while bit:
-            blocks[bits | bit] = swap(blocks[bits], bit)
+            blocks[bits | bit] = swap(value, bit)
             bit //= 2
 
     lead, rest = call(
@@ -372,7 +372,7 @@
         [embeddings, cluster_id.reshape(1, docs)],
     )
     leads, rests = {0: lead}, {0: rest}
-    send(leads, 0)
+    send(leads, 0, lead)
 
     inv, centre, own_prefix, prior, cent_prefix = call(
         functools.partial(prep_kernel, subs, per),
@@ -399,7 +399,7 @@
     )
     members = [across(found)]
     rests[0] = tied(rest, found)
-    send(rests, 0)
+    send(rests, 0, rests[0])
     sums = call(
         functools.partial(sums_kernel, subs),
         "sums",
@@ -414,8 +414,6 @@
         count = len(group)
         before = members[:-1] if last else members
         leads.update(zip(group, tied([leads[bits] for bits in group], found, lead_sums, rest_sums, before)))
-        for bits in group:
-            send(leads, bits)
         if last:
             lead = leads[group[0]]
             halves = [near(lead[: docs // 2]), near(lead[docs // 2 : docs])]
@@ -445,9 +443,19 @@
         else:
             members.append(across(found))
             before = (found, members)
+            for bits in group:
+                prefix = near(leads[bits])
+                weight, *lead_sums = call(
+                    functools.partial(sums_lead_kernel, subs),
+                    "sums_lead",
+                    [shape((subs * per, docs), BF16)] + [lead_sum] * subs,
+                    [leads[bits], prefix, cent_prefix, own_prefix] + lead_sums,
+                    {4 + i: 1 + i for i in range(subs)},
+                )
+                weights.append(weight)
         rests.update(zip(group, tied([rests[bits] for bits in group], before)))
         for bits in group:
-            send(rests, bits)
+            send(leads, bits, tied(leads[bits], rests[bits]))
         row_shapes = [shape((count, groups, packed, half - PREFIX), BF16)] * subs
         found = call(
             functools.partial(select_rest_kernel, count, subs),
@@ -456,19 +464,11 @@
             [centre] + picks + [rests[bits] for bits in group],
         )
         members.append(across(found))
+        for bits in group:
+            rests[bits] = tied(rests[bits], found)
+            send(rests, bits, rests[bits])
         if last:
             rest_sums = tied(rest_sums, members[:-1])
-        else:
-            for bits in group:
-                prefix = near(tied(leads[bits], rests[bits]))
-                weight, *lead_sums = call(
-                    functools.partial(sums_lead_kernel, subs),
-                    "sums_lead",
-                    [shape((subs * per, docs), BF16)] + [lead_sum] * subs,
-                    [leads[bits], prefix, cent_prefix, own_prefix] + lead_sums,
-                    {4 + i: 1 + i for i in range(subs)},
-                )
-                weights.append(weight)
         rest_sums = call(
             functools.partial(sums_rest_kernel, count, subs),
             "sums_rest",

time: 58 us -> 57.4 us (0.990)
  no operation moved by 1% of the time
where the time goes in v11:
time: 57.4 us; the launch traced here: 57.2 us
  starting transfers between devices  20.1 us (35%)
  waiting for transfers between devices  20.1 us (35%)
  Pallas kernels  12.3 us (21%)
  local copies, waits for them, and re-layouts  4.01 us (7%)
  between operations  0.79 us (1%)
    pallas_call x15, Pallas kernels, call(): pl.pallas_call(kernel, out_shape=tuple(out_shape), in_specs=[whole(operan...  12.3 us
    ppermute x6, waiting for transfers between devices, swap(): return lax.ppermute(value, 'rows', [(i, i ^ bit) for i in range(rows)])  12.1 us
    ppermute x7, starting transfers between devices, across(): lax.ppermute(values[t], 'sub', [(i, (i + t) % subs) for i in range(subs)])  9.84 us
    ppermute x6, starting transfers between devices, swap(): return lax.ppermute(value, 'rows', [(i, i ^ bit) for i in range(rows)])  8.05 us
    ppermute x7, waiting for transfers between devices, across(): lax.ppermute(values[t], 'sub', [(i, (i + t) % subs) for i in range(subs)])  7.35 us
    unnamed x8, local copies, waits for them, and re-layouts  3.99 us
    ppermute x7, starting transfers between devices, near(): return lax.ppermute(value, 'dim', [(0, 1), (1, 0)])  2.16 us
  transfers between devices with their start and end apart: 20, of which 10 were waited for; matrix products, arithmetic and copies ran while one was open for 0% of the time, Pallas kernels for 19%

profile of v11, /device:TPU:0, one launch (start us, length us, event | category | flops | bytes accessed | tf_op | source)
XLA Modules:
  0.0 57.2 jit_solution(10015631100073967684)
XLA Ops:
  0.6 1.0 %copy-done.1 = bf16[512,512]{1,0:T(8,128)(2,1)S(1)} copy-done((bf16[512,512]{1,0:T(8,128)(2,1)S(1)}, bf16[512,512]{1,0:T(8,128)(2,1)}, u32[]{:S(2)}) %copy-start.1) | copy-done | bytes 524312
  1.7 0.7 %copy-done.3 = s32[512,1]{0,1:T(1,128)S(1)} copy-done((s32[512,1]{0,1:T(1,128)S(1)}, s32[512,1]{0,1:T(1,128)}, u32[]{:S(2)}) %copy-start.3) | copy-done | bytes 2072
  2.4 0.5 collective-permute-start.3
  2.9 2.6 %collective-permute-start.1 = (bf16[528,256]{1,0:T(8,128)(2,1)S(1)}, bf16[528,256]{1,0:T(8,128)(2,1)S(1)}, u32[]{:S(2)}, u32[]{:S(2)}) collective-permute-start(bf16[528,256]{1,0:T(8,128)(2,1)S(1)} %get-tuple-element.68.lead_ref), channel_id=1, source_target_pairs={{0,4},{4,0},{8,12},{12,8},{1,5},{5,1},{9,13},{13,9},{2,6},{6,2},{1... | collective-permute-start | bytes 811016 | tf_op jit(solution)/shard_map/ppermute | solution.py:360
  5.6 2.6 %collective-permute-start.2 = (bf16[528,256]{1,0:T(8,128)(2,1)S(1)}, bf16[528,256]{1,0:T(8,128)(2,1)S(1)}, u32[]{:S(2)}, u32[]{:S(2)}) collective-permute-start(bf16[528,256]{1,0:T(8,128)(2,1)S(1)} %get-tuple-element.68.lead_ref), channel_id=1, source_target_pairs={{0,8},{4,12},{8,0},{12,4},{1,9},{5,13},{9,1},{13,5},{2,10},{6,14},... | collective-permute-start | bytes 811016 | tf_op jit(solution)/shard_map/ppermute | solution.py:360
  8.2 1.6 %copy-done = bf16[1024,1024]{1,0:T(8,128)(2,1)S(1)} copy-done((bf16[1024,1024]{1,0:T(8,128)(2,1)S(1)}, bf16[1024,1024]{1,0:T(8,128)(2,1)}, u32[]{:S(2)}) %copy-start) | copy-done | bytes 2097176
  9.8 0.7 %copy-done.2 = s32[1024]{0:T(1024)S(1)} copy-done((s32[1024]{0:T(1024)S(1)}, s32[1024]{0:T(1024)}, u32[]{:S(2)}) %copy-start.2) | copy-done | bytes 4120
  10.4 0.8 %prep.1 = (f32[256,1]{1,0:T(8,128)S(1)}, bf16[256,512]{1,0:T(8,128)(2,1)S(1)}, bf16[256,256]{1,0:T(8,128)(2,1)S(1)}, bf16[128,512]{1,0:T(8,128)(2,1)S(1)}, bf16[1024,256]{1,0:T(8,128)(2,1)S(1)}) custom-call(s32[1,1024]{1,0:T(1,128)S(1)} %bitcast.3, bf16[1024,1024]{1,0:T(8,128)(2,1)S(1)} %copy-done), custom_call_target="tpu_custom_call" | custom-call | flops 209715200 | bytes 4194304 | tf_op jit(solution)/shard_map/prep/pallas_call | solution.py:32
  11.3 0.8 %select.1 = (bf16[16,16,512]{2,1,0:T(8,128)(2,1)S(1)}, bf16[16,16,512]{2,1,0:T(8,128)(2,1)S(1)}) custom-call(bf16[528,256]{1,0:T(8,128)(2,1)S(1)} %get-tuple-element.68.lead_ref, bf16[528,256]{1,0:T(8,128)(2,1)S(1)} %get-tuple-element.86.rest_ref, f32[256,1]{1,0:T(8,128)S(1)} %get-tuple-element.70.inv_ref, bf16[256,512]{1,0:T(8,128)(2,1)S(1)} %get-tuple-element.71.centre_ref), custom_call_target="tpu_custom_call" | custom-call | flops 104857600 | bytes 2097152 | tf_op jit(solution)/shard_map/select/pallas_call | solution.py:32
  12.0 1.5 %collective-permute-start = (bf16[16,16,512]{2,1,0:T(8,128)(2,1)S(1)}, bf16[16,16,512]{2,1,0:T(8,128)(2,1)S(1)}, u32[]{:S(2)}, u32[]{:S(2)}) collective-permute-start(bf16[16,16,512]{2,1,0:T(8,128)(2,1)S(1)} %get-tuple-element.73), channel_id=1, source_target_pairs={{0,2},{2,0},{1,3},{3,1},{4,6},{6,4},{5,7},{7,5},{8,10},{10,8},{9,1... | collective-permute-start | bytes 786440 | tf_op jit(solution)/shard_map/ppermute | solution.py:353
  13.6 0.4 collective-permute-start.5
  14.0 0.3 collective-permute-start.6
  14.4 1.3 %sums.1 = (f32[136,256]{1,0:T(8,128)S(1)}, f32[136,256]{1,0:T(8,128)S(1)}, f32[128,256]{1,0:T(8,128)S(1)}, f32[128,256]{1,0:T(8,128)S(1)}) custom-call(bf16[528,256]{1,0:T(8,128)(2,1)S(1)} %get-tuple-element.68.lead_ref, bf16[528,256]{1,0:T(8,128)(2,1)S(1)} %get-tuple-element.86.rest_ref, bf16[528,256]{1,0:T(8,128)(2,1)S(1)} %collective-permute-done.3.near_ref, ...), custom_call_target="tpu_custom_call" | custom-call | flops 104857600 | bytes 2097152 | tf_op jit(solution)/shard_map/sums/pallas_call | solution.py:32
  15.7 4.5 %collective-permute-done.refs_5_ = bf16[16,16,512]{2,1,0:T(8,128)(2,1)S(1)} collective-permute-done((bf16[16,16,512]{2,1,0:T(8,128)(2,1)S(1)}, bf16[16,16,512]{2,1,0:T(8,128)(2,1)S(1)}, u32[]{:S(2)}, u32[]{:S(2)}) %collective-permute-start) | collective-permute-done | bytes 262176 | tf_op jit(solution)/shard_map/ppermute | solution.py:353
  20.2 0.5 collective-permute-done.2.refs_1_.lead_ref
  20.7 1.1 %select_lead.2 = (bf16[512,512]{1,0:T(8,128)(2,1)S(1)}, bf16[512,512]{1,0:T(8,128)(2,1)S(1)}, bf16[2,16,16,256]{3,2,1,0:T(8,128)(2,1)S(1)}, bf16[2,16,16,256]{3,2,1,0:T(8,128)(2,1)S(1)}) custom-call(f32[256,1]{1,0:T(8,128)S(1)} %get-tuple-element.70.inv_ref, bf16[256,512]{1,0:T(8,128)(2,1)S(1)} %get-tuple-element.71.centre_ref, ...), custom_call_target="tpu_custom_call" | custom-call | tf_op jit(solution)/shard_map/select_lead/pallas_call | solution.py:32
  21.8 1.6 %collective-permute-start.4 = (bf16[2,16,16,256]{3,2,1,0:T(8,128)(2,1)S(1)}, bf16[2,16,16,256]{3,2,1,0:T(8,128)(2,1)S(1)}, u32[]{:S(2)}, u32[]{:S(2)}) collective-permute-start(bf16[2,16,16,256]{3,2,1,0:T(8,128)(2,1)S(1)} %get-tuple-element.83), channel_id=1, source_target_pairs={{0,2},{2,0},{1,3},{3,1},{4,6},{6,4},{5,7},{7,5},{8,10},{10,8},{9,1... | collective-permute-start | bytes 786440 | tf_op jit(solution)/shard_map/ppermute | solution.py:353
  23.3 0.0 collective-permute-start.10
  23.3 0.5 collective-permute-start.9
  23.8 6.1 %collective-permute-done.5.refs_2_ = bf16[528,256]{1,0:T(8,128)(2,1)S(1)} collective-permute-done((bf16[528,256]{1,0:T(8,128)(2,1)S(1)}, bf16[528,256]{1,0:T(8,128)(2,1)S(1)}, u32[]{:S(2)}, u32[]{:S(2)}) %collective-permute-start.5) | collective-permute-done | bytes 270368 | tf_op jit(solution)/shard_map/ppermute | solution.py:360
  29.9 2.6 %collective-permute-done.6.refs_3_ = bf16[528,256]{1,0:T(8,128)(2,1)S(1)} collective-permute-done((bf16[528,256]{1,0:T(8,128)(2,1)S(1)}, bf16[528,256]{1,0:T(8,128)(2,1)S(1)}, u32[]{:S(2)}, u32[]{:S(2)}) %collective-permute-start.6) | collective-permute-done | bytes 270368 | tf_op jit(solution)/shard_map/ppermute | solution.py:360
  32.5 0.4 collective-permute-start.8
  32.9 0.4 select_rest.2
  33.4 1.6 %collective-permute-start.7 = (bf16[2,16,16,256]{3,2,1,0:T(8,128)(2,1)S(1)}, bf16[2,16,16,256]{3,2,1,0:T(8,128)(2,1)S(1)}, u32[]{:S(2)}, u32[]{:S(2)}) collective-permute-start(bf16[2,16,16,256]{3,2,1,0:T(8,128)(2,1)S(1)} %get-tuple-element.90), channel_id=1, source_target_pairs={{0,2},{2,0},{1,3},{3,1},{4,6},{6,4},{5,7},{7,5},{8,10},{10,8},{9,1... | collective-permute-start | bytes 786440 | tf_op jit(solution)/shard_map/ppermute | solution.py:353
  35.0 1.6 %collective-permute-start.12 = (bf16[528,256]{1,0:T(8,128)(2,1)S(1)}, bf16[528,256]{1,0:T(8,128)(2,1)S(1)}, u32[]{:S(2)}, u32[]{:S(2)}) collective-permute-start(bf16[528,256]{1,0:T(8,128)(2,1)S(1)} %collective-permute-done.6.refs_3_), channel_id=1, source_target_pairs={{0,4},{4,0},{8,12},{12,8},{1,5},{5,1},{9,13},{13,9},{2,6},{6,2},{1... | collective-permute-start | bytes 811016 | tf_op jit(solution)/shard_map/ppermute | solution.py:360
  36.5 1.4 %sums_lead.3 = (bf16[256,512]{1,0:T(8,128)(2,1)S(1)}, f32[136,256]{1,0:T(8,128)S(1)}, f32[136,256]{1,0:T(8,128)S(1)}) custom-call(bf16[528,256]{1,0:T(8,128)(2,1)S(1)} %collective-permute-done.1.refs_0_.lead_ref, bf16[528,256]{1,0:T(8,128)(2,1)S(1)} %collective-permute-done.10.near_ref, ...), custom_call_target="tpu_custom_call", output_to_operand_aliasing={{1}: (4, {}), {2}: (5, {})} | custom-call | tf_op jit(solution)/shard_map/sums_lead/pallas_call | solution.py:32
  37.9 1.4 %sums_lead.4 = (bf16[256,512]{1,0:T(8,128)(2,1)S(1)}, f32[136,256]{1,0:T(8,128)S(1)}, f32[136,256]{1,0:T(8,128)S(1)}) custom-call(bf16[528,256]{1,0:T(8,128)(2,1)S(1)} %collective-permute-done.2.refs_1_.lead_ref, bf16[528,256]{1,0:T(8,128)(2,1)S(1)} %collective-permute-done.9.near_ref, ...), custom_call_target="tpu_custom_call", output_to_operand_aliasing={{1}: (4, {}), {2}: (5, {})} | custom-call | tf_op jit(solution)/shard_map/sums_lead/pallas_call | solution.py:32
  39.3 0.3 sums_rest.2
  39.6 2.2 %collective-permute-done.8.refs_0_.lead_ref = bf16[528,256]{1,0:T(8,128)(2,1)S(1)} collective-permute-done((bf16[528,256]{1,0:T(8,128)(2,1)S(1)}, bf16[528,256]{1,0:T(8,128)(2,1)S(1)}, u32[]{:S(2)}, u32[]{:S(2)}) %collective-permute-start.8) | collective-permute-done | bytes 270368 | tf_op jit(solution)/shard_map/ppermute | solution.py:360
  41.9 0.1 collective-permute-start.13
  41.9 0.5 collective-permute-start.14
  42.4 0.6 %select_lead.3 = (bf16[512,512]{1,0:T(8,128)(2,1)S(1)}, bf16[1,16,16,256]{3,2,1,0:T(8,128)(2,1)S(1)}, bf16[1,16,16,256]{3,2,1,0:T(8,128)(2,1)S(1)}) custom-call(f32[256,1]{1,0:T(8,128)S(1)} %get-tuple-element.70.inv_ref, bf16[256,512]{1,0:T(8,128)(2,1)S(1)} %get-tuple-element.71.centre_ref, bf16[528,256]{1,0:T(8,128)(2,1)S(1)} %collective-permute-done.8.refs_0_.lead_ref), custom_call_target="tpu_custom_call" | custom-call | tf_op jit(solution)/shard_map/select_lead/pallas_call | solution.py:32
  43.0 1.6 %collective-permute-start.11 = (bf16[1,16,16,256]{3,2,1,0:T(8,128)(2,1)S(1)}, bf16[1,16,16,256]{3,2,1,0:T(8,128)(2,1)S(1)}, u32[]{:S(2)}, u32[]{:S(2)}) collective-permute-start(bf16[1,16,16,256]{3,2,1,0:T(8,128)(2,1)S(1)} %get-tuple-element.106), channel_id=1, source_target_pairs={{0,2},{2,0},{1,3},{3,1},{4,6},{6,4},{5,7},{7,5},{8,10},{10,8},{9,1... | collective-permute-start | bytes 393224 | tf_op jit(solution)/shard_map/ppermute | solution.py:353
  44.6 1.4 %sums_lead.5 = (bf16[256,512]{1,0:T(8,128)(2,1)S(1)}, f32[136,256]{1,0:T(8,128)S(1)}, bf16[144,256]{1,0:T(8,128)(2,1)S(1)}) custom-call(bf16[528,256]{1,0:T(8,128)(2,1)S(1)} %collective-permute-done.8.refs_0_.lead_ref, bf16[256,256]{1,0:T(8,128)(2,1)S(1)} %collective-permute-done.13.low_ref, ...), custom_call_target="tpu_custom_call", output_to_operand_aliasing={{1}: (5, {})} | custom-call | tf_op jit(solution)/shard_map/sums_lead/pallas_call | solution.py:32
  46.0 0.8 %collective-permute-done.12.refs_1_ = bf16[528,256]{1,0:T(8,128)(2,1)S(1)} collective-permute-done((bf16[528,256]{1,0:T(8,128)(2,1)S(1)}, bf16[528,256]{1,0:T(8,128)(2,1)S(1)}, u32[]{:S(2)}, u32[]{:S(2)}) %collective-permute-start.12) | collective-permute-done | bytes 270368 | tf_op jit(solution)/shard_map/ppermute | solution.py:360
  46.7 0.3 select_rest.3
  47.1 1.6 %collective-permute-start.15 = (bf16[1,16,16,256]{3,2,1,0:T(8,128)(2,1)S(1)}, bf16[1,16,16,256]{3,2,1,0:T(8,128)(2,1)S(1)}, u32[]{:S(2)}, u32[]{:S(2)}) collective-permute-start(bf16[1,16,16,256]{3,2,1,0:T(8,128)(2,1)S(1)} %get-tuple-element.111), channel_id=1, source_target_pairs={{0,2},{2,0},{1,3},{3,1},{4,6},{6,4},{5,7},{7,5},{8,10},{10,8},{9,1... | collective-permute-start | bytes 393224 | tf_op jit(solution)/shard_map/ppermute | solution.py:353
  48.6 0.2 sums_rest.3
  48.9 1.5 %collective-permute-start.19 = (bf16[144,256]{1,0:T(8,128)(2,1)S(1)}, bf16[144,256]{1,0:T(8,128)(2,1)S(1)}, u32[]{:S(2)}, u32[]{:S(2)}) collective-permute-start(bf16[144,256]{1,0:T(8,128)(2,1)S(1)} %get-tuple-element.116), channel_id=1, source_target_pairs={{0,2},{2,0},{1,3},{3,1},{4,6},{6,4},{5,7},{7,5},{8,10},{10,8},{9,1... | collective-permute-start | bytes 221192 | tf_op jit(solution)/shard_map/ppermute | solution.py:353
  50.4 0.6 collective-permute-start.18
  50.9 2.5 %collective-permute-done.15.refs_9_ = bf16[1,16,16,256]{3,2,1,0:T(8,128)(2,1)S(1)} collective-permute-done((bf16[1,16,16,256]{3,2,1,0:T(8,128)(2,1)S(1)}, bf16[1,16,16,256]{3,2,1,0:T(8,128)(2,1)S(1)}, u32[]{:S(2)}, u32[]{:S(2)}) %collective-permute-start.15) | collective-permute-done | bytes 131104 | tf_op jit(solution)/shard_map/ppermute | solution.py:353
  53.5 0.9 %gram.1 = (f32[8,16,128]{2,1,0:T(8,128)S(1)}, f32[8,16,128]{2,1,0:T(8,128)S(1)}) custom-call(bf16[16,16,512]{2,1,0:T(8,128)(2,1)S(1)} %get-tuple-element.117.refs_0_, bf16[2,16,16,256]{3,2,1,0:T(8,128)(2,1)S(1)} %get-tuple-element.118.refs_1_, bf16[2,16,16,256]{3,2,1,0:T(8,128)(2,1)S(1)} %get-tuple-element.119.refs_2_, ...), custom_call_target="tpu_custom_call" | custom-call | tf_op jit(solution)/shard_map/gram/pallas_call | solution.py:32
  54.4 0.1 collective-permute-start.16
  54.4 0.5 collective-permute-start.17
  54.9 0.3 collective-permute-done.18.refs_5_
  55.3 0.4 collective-permute-done.16.refs_2_
  55.7 0.2 collective-permute-done.17.refs_3_
  55.8 1.4 %finish.1 = (f32[128,512]{1,0:T(8,128)}, bf16[8,16,128]{2,1,0:T(8,128)(2,1)}) custom-call(f32[8,16,128]{2,1,0:T(8,128)S(1)} %get-tuple-element.127.refs_0_, f32[8,16,128]{2,1,0:T(8,128)S(1)} %get-tuple-element.128.refs_1_, f32[8,16,128]{2,1,0:T(8,128)S(1)} %collective-permute-done.16.refs_2_, f32[8,16,128]{2,1,0:T(8,128)S(1)} %collective-permute-done.17.refs_3_, ...), custom_call_target="tpu_custom_call" | custom-call | tf_op jit(solution)/shard_map/finish/pallas_call | solution.py:32
  (16 shorter events, 0.1 us)
Async XLA Ops:
  0.6 1.0 %copy-start.1 = (bf16[512,512]{1,0:T(8,128)(2,1)S(1)}, bf16[512,512]{1,0:T(8,128)(2,1)}, u32[]{:S(2)}) copy-start(bf16[512,512]{1,0:T(8,128)(2,1)} %emb_ref.1) | copy-start | bytes 1572868
  1.7 0.7 %copy-start.3 = (s32[512,1]{0,1:T(1,128)S(1)}, s32[512,1]{0,1:T(1,128)}, u32[]{:S(2)}) copy-start(s32[512,1]{0,1:T(1,128)} %param.6) | copy-start | bytes 6148
  2.4 11.6 %collective-permute-start.3 = (bf16[528,256]{1,0:T(8,128)(2,1)S(1)}, bf16[528,256]{1,0:T(8,128)(2,1)S(1)}, u32[]{:S(2)}, u32[]{:S(2)}) collective-permute-start(bf16[528,256]{1,0:T(8,128)(2,1)S(1)} %get-tuple-element.68.lead_ref), channel_id=1, source_target_pairs={{0,1},{1,0},{2,3},{3,2},{4,5},{5,4},{6,7},{7,6},{8,9},{9,8},{10,11... | collective-permute-start | bytes 811016 | tf_op jit(solution)/shard_map/ppermute | solution.py:357
  2.9 17.3 %collective-permute-start.1 = (bf16[528,256]{1,0:T(8,128)(2,1)S(1)}, bf16[528,256]{1,0:T(8,128)(2,1)S(1)}, u32[]{:S(2)}, u32[]{:S(2)}) collective-permute-start(bf16[528,256]{1,0:T(8,128)(2,1)S(1)} %get-tuple-element.68.lead_ref), channel_id=1, source_target_pairs={{0,4},{4,0},{8,12},{12,8},{1,5},{5,1},{9,13},{13,9},{2,6},{6,2},{1... | collective-permute-start | bytes 811016 | tf_op jit(solution)/shard_map/ppermute | solution.py:360
  5.6 15.1 %collective-permute-start.2 = (bf16[528,256]{1,0:T(8,128)(2,1)S(1)}, bf16[528,256]{1,0:T(8,128)(2,1)S(1)}, u32[]{:S(2)}, u32[]{:S(2)}) collective-permute-start(bf16[528,256]{1,0:T(8,128)(2,1)S(1)} %get-tuple-element.68.lead_ref), channel_id=1, source_target_pairs={{0,8},{4,12},{8,0},{12,4},{1,9},{5,13},{9,1},{13,5},{2,10},{6,14},... | collective-permute-start | bytes 811016 | tf_op jit(solution)/shard_map/ppermute | solution.py:360
  8.2 1.6 %copy-start = (bf16[1024,1024]{1,0:T(8,128)(2,1)S(1)}, bf16[1024,1024]{1,0:T(8,128)(2,1)}, u32[]{:S(2)}) copy-start(bf16[1024,1024]{1,0:T(8,128)(2,1)} %cent_ref.1) | copy-start | bytes 6291460
  9.8 0.7 %copy-start.2 = (s32[1024]{0:T(1024)S(1)}, s32[1024]{0:T(1024)}, u32[]{:S(2)}) copy-start(s32[1024]{0:T(1024)} %param.7) | copy-start | bytes 12292
  12.0 8.1 %collective-permute-start = (bf16[16,16,512]{2,1,0:T(8,128)(2,1)S(1)}, bf16[16,16,512]{2,1,0:T(8,128)(2,1)S(1)}, u32[]{:S(2)}, u32[]{:S(2)}) collective-permute-start(bf16[16,16,512]{2,1,0:T(8,128)(2,1)S(1)} %get-tuple-element.73), channel_id=1, source_target_pairs={{0,2},{2,0},{1,3},{3,1},{4,6},{6,4},{5,7},{7,5},{8,10},{10,8},{9,1... | collective-permute-start | bytes 786440 | tf_op jit(solution)/shard_map/ppermute | solution.py:353
  13.6 16.3 %collective-permute-start.5 = (bf16[528,256]{1,0:T(8,128)(2,1)S(1)}, bf16[528,256]{1,0:T(8,128)(2,1)S(1)}, u32[]{:S(2)}, u32[]{:S(2)}) collective-permute-start(bf16[528,256]{1,0:T(8,128)(2,1)S(1)} %get-tuple-element.86.rest_ref), channel_id=1, source_target_pairs={{0,4},{4,0},{8,12},{12,8},{1,5},{5,1},{9,13},{13,9},{2,6},{6,2},{1... | collective-permute-start | bytes 811016 | tf_op jit(solution)/shard_map/ppermute | solution.py:360
  14.0 18.5 %collective-permute-start.6 = (bf16[528,256]{1,0:T(8,128)(2,1)S(1)}, bf16[528,256]{1,0:T(8,128)(2,1)S(1)}, u32[]{:S(2)}, u32[]{:S(2)}) collective-permute-start(bf16[528,256]{1,0:T(8,128)(2,1)S(1)} %get-tuple-element.86.rest_ref), channel_id=1, source_target_pairs={{0,8},{4,12},{8,0},{12,4},{1,9},{5,13},{9,1},{13,5},{2,10},{6,14},... | collective-permute-start | bytes 811016 | tf_op jit(solution)/shard_map/ppermute | solution.py:360
  21.8 10.7 %collective-permute-start.4 = (bf16[2,16,16,256]{3,2,1,0:T(8,128)(2,1)S(1)}, bf16[2,16,16,256]{3,2,1,0:T(8,128)(2,1)S(1)}, u32[]{:S(2)}, u32[]{:S(2)}) collective-permute-start(bf16[2,16,16,256]{3,2,1,0:T(8,128)(2,1)S(1)} %get-tuple-element.83), channel_id=1, source_target_pairs={{0,2},{2,0},{1,3},{3,1},{4,6},{6,4},{5,7},{7,5},{8,10},{10,8},{9,1... | collective-permute-start | bytes 786440 | tf_op jit(solution)/shard_map/ppermute | solution.py:353
  23.3 13.2 %collective-permute-start.10 = (bf16[528,256]{1,0:T(8,128)(2,1)S(1)}, bf16[528,256]{1,0:T(8,128)(2,1)S(1)}, u32[]{:S(2)}, u32[]{:S(2)}) collective-permute-start(bf16[528,256]{1,0:T(8,128)(2,1)S(1)} %collective-permute-done.1.refs_0_.lead_ref), channel_id=1, source_target_pairs={{0,1},{1,0},{2,3},{3,2},{4,5},{5,4},{6,7},{7,6},{8,9},{9,8},{10,11... | collective-permute-start | bytes 811016 | tf_op jit(solution)/shard_map/ppermute | solution.py:357
  23.3 14.6 %collective-permute-start.9 = (bf16[528,256]{1,0:T(8,128)(2,1)S(1)}, bf16[528,256]{1,0:T(8,128)(2,1)S(1)}, u32[]{:S(2)}, u32[]{:S(2)}) collective-permute-start(bf16[528,256]{1,0:T(8,128)(2,1)S(1)} %collective-permute-done.2.refs_1_.lead_ref), channel_id=1, source_target_pairs={{0,1},{1,0},{2,3},{3,2},{4,5},{5,4},{6,7},{7,6},{8,9},{9,8},{10,11... | collective-permute-start | bytes 811016 | tf_op jit(solution)/shard_map/ppermute | solution.py:357
  32.5 9.3 %collective-permute-start.8 = (bf16[528,256]{1,0:T(8,128)(2,1)S(1)}, bf16[528,256]{1,0:T(8,128)(2,1)S(1)}, u32[]{:S(2)}, u32[]{:S(2)}) collective-permute-start(bf16[528,256]{1,0:T(8,128)(2,1)S(1)} %collective-permute-done.2.refs_1_.lead_ref), channel_id=1, source_target_pairs={{0,4},{4,0},{8,12},{12,8},{1,5},{5,1},{9,13},{13,9},{2,6},{6,2},{1... | collective-permute-start | bytes 811016 | tf_op jit(solution)/shard_map/ppermute | solution.py:360
  33.4 9.6 %collective-permute-start.7 = (bf16[2,16,16,256]{3,2,1,0:T(8,128)(2,1)S(1)}, bf16[2,16,16,256]{3,2,1,0:T(8,128)(2,1)S(1)}, u32[]{:S(2)}, u32[]{:S(2)}) collective-permute-start(bf16[2,16,16,256]{3,2,1,0:T(8,128)(2,1)S(1)} %get-tuple-element.90), channel_id=1, source_target_pairs={{0,2},{2,0},{1,3},{3,1},{4,6},{6,4},{5,7},{7,5},{8,10},{10,8},{9,1... | collective-permute-start | bytes 786440 | tf_op jit(solution)/shard_map/ppermute | solution.py:353
  35.0 11.8 %collective-permute-start.12 = (bf16[528,256]{1,0:T(8,128)(2,1)S(1)}, bf16[528,256]{1,0:T(8,128)(2,1)S(1)}, u32[]{:S(2)}, u32[]{:S(2)}) collective-permute-start(bf16[528,256]{1,0:T(8,128)(2,1)S(1)} %collective-permute-done.6.refs_3_), channel_id=1, source_target_pairs={{0,4},{4,0},{8,12},{12,8},{1,5},{5,1},{9,13},{13,9},{2,6},{6,2},{1... | collective-permute-start | bytes 811016 | tf_op jit(solution)/shard_map/ppermute | solution.py:360
  41.9 2.7 %collective-permute-start.13 = (bf16[256,256]{1,0:T(8,128)(2,1)S(1)}, bf16[256,256]{1,0:T(8,128)(2,1)S(1)}, u32[]{:S(2)}, u32[]{:S(2)}) collective-permute-start(bf16[256,256]{1,0:T(8,128)(2,1)S(1)} %get-tuple-element.135), channel_id=1, source_target_pairs={{0,1},{1,0},{2,3},{3,2},{4,5},{5,4},{6,7},{7,6},{8,9},{9,8},{10,11... | collective-permute-start | bytes 393224 | tf_op jit(solution)/shard_map/ppermute | solution.py:357
  41.9 2.7 %collective-permute-start.14 = (bf16[256,256]{1,0:T(8,128)(2,1)S(1)}, bf16[256,256]{1,0:T(8,128)(2,1)S(1)}, u32[]{:S(2)}, u32[]{:S(2)}) collective-permute-start(bf16[256,256]{1,0:T(8,128)(2,1)S(1)} %get-tuple-element.134), channel_id=1, source_target_pairs={{0,1},{1,0},{2,3},{3,2},{4,5},{5,4},{6,7},{7,6},{8,9},{9,8},{10,11... | collective-permute-start | bytes 393224 | tf_op jit(solution)/shard_map/ppermute | solution.py:357
  43.0 5.6 %collective-permute-start.11 = (bf16[1,16,16,256]{3,2,1,0:T(8,128)(2,1)S(1)}, bf16[1,16,16,256]{3,2,1,0:T(8,128)(2,1)S(1)}, u32[]{:S(2)}, u32[]{:S(2)}) collective-permute-start(bf16[1,16,16,256]{3,2,1,0:T(8,128)(2,1)S(1)} %get-tuple-element.106), channel_id=1, source_target_pairs={{0,2},{2,0},{1,3},{3,1},{4,6},{6,4},{5,7},{7,5},{8,10},{10,8},{9,1... | collective-permute-start | bytes 393224 | tf_op jit(solution)/shard_map/ppermute | solution.py:353
  47.1 6.4 %collective-permute-start.15 = (bf16[1,16,16,256]{3,2,1,0:T(8,128)(2,1)S(1)}, bf16[1,16,16,256]{3,2,1,0:T(8,128)(2,1)S(1)}, u32[]{:S(2)}, u32[]{:S(2)}) collective-permute-start(bf16[1,16,16,256]{3,2,1,0:T(8,128)(2,1)S(1)} %get-tuple-element.111), channel_id=1, source_target_pairs={{0,2},{2,0},{1,3},{3,1},{4,6},{6,4},{5,7},{7,5},{8,10},{10,8},{9,1... | collective-permute-start | bytes 393224 | tf_op jit(solution)/shard_map/ppermute | solution.py:353
  48.9 6.1 %collective-permute-start.19 = (bf16[144,256]{1,0:T(8,128)(2,1)S(1)}, bf16[144,256]{1,0:T(8,128)(2,1)S(1)}, u32[]{:S(2)}, u32[]{:S(2)}) collective-permute-start(bf16[144,256]{1,0:T(8,128)(2,1)S(1)} %get-tuple-element.116), channel_id=1, source_target_pairs={{0,2},{2,0},{1,3},{3,1},{4,6},{6,4},{5,7},{7,5},{8,10},{10,8},{9,1... | collective-permute-start | bytes 221192 | tf_op jit(solution)/shard_map/ppermute | solution.py:353
  50.4 4.9 %collective-permute-start.18 = (bf16[144,256]{1,0:T(8,128)(2,1)S(1)}, bf16[144,256]{1,0:T(8,128)(2,1)S(1)}, u32[]{:S(2)}, u32[]{:S(2)}) collective-permute-start(bf16[144,256]{1,0:T(8,128)(2,1)S(1)} %get-tuple-element.130), channel_id=1, source_target_pairs={{0,2},{2,0},{1,3},{3,1},{4,6},{6,4},{5,7},{7,5},{8,10},{10,8},{9,1... | collective-permute-start | bytes 221192 | tf_op jit(solution)/shard_map/ppermute | solution.py:353
  54.4 1.3 %collective-permute-start.16 = (f32[8,16,128]{2,1,0:T(8,128)S(1)}, f32[8,16,128]{2,1,0:T(8,128)S(1)}, u32[]{:S(2)}, u32[]{:S(2)}) collective-permute-start(f32[8,16,128]{2,1,0:T(8,128)S(1)} %get-tuple-element.127.refs_0_), channel_id=1, source_target_pairs={{0,1},{1,0},{2,3},{3,2},{4,5},{5,4},{6,7},{7,6},{8,9},{9,8},{10,11... | collective-permute-start | bytes 196616 | tf_op jit(solution)/shard_map/ppermute | solution.py:357
  54.4 1.4 %collective-permute-start.17 = (f32[8,16,128]{2,1,0:T(8,128)S(1)}, f32[8,16,128]{2,1,0:T(8,128)S(1)}, u32[]{:S(2)}, u32[]{:S(2)}) collective-permute-start(f32[8,16,128]{2,1,0:T(8,128)S(1)} %get-tuple-element.128.refs_1_), channel_id=1, source_target_pairs={{0,1},{1,0},{2,3},{3,2},{4,5},{5,4},{6,7},{7,6},{8,9},{9,8},{10,11... | collective-permute-start | bytes 196616 | tf_op jit(solution)/shard_map/ppermute | solution.py:357

commit v12 on v11

--- a/solution.py
+++ b/solution.py
@@ -64,7 +64,7 @@
     docs = emb_ref.shape[0]
     lead_ref[:docs, :] = emb_ref[:, :PREFIX]
     rest_ref[:docs, :] = emb_ref[:, PREFIX:]
-    rest_ref[docs:, :] = jnp.zeros((META, rest_ref.shape[1]), BF16)
+    rest_ref[docs:, :] = jnp.zeros((rest_ref.shape[0] - docs, rest_ref.shape[1]), BF16)
     cid = cid_ref[...]
     high, low = (cid // DIGIT + 1).astype(F32), (cid % DIGIT).astype(F32)
     rows = []
@@ -124,7 +124,7 @@
 
 
 def select_kernel(lead_ref, rest_ref, inv_ref, centre_ref, *row_refs):
-    docs = rest_ref.shape[0] - META
+    docs = lead_ref.shape[0] - META
     pick = picked(lead_ref, inv_ref)
     groups, packed, _ = row_refs[0].shape
     for columns, at in ((lead_ref[:docs, :], 0), (rest_ref[:docs, :], PREFIX)):
@@ -363,12 +363,13 @@
         bit = (bits & -bits or rows) // 2
         while bit:
             blocks[bits | bit] = swap(value, bit)
+            value = value[: docs + META]
             bit //= 2
 
     lead, rest = call(
         pack_kernel,
         "pack",
-        [shape((docs + META, PREFIX), BF16), shape((docs + META, half - PREFIX), BF16)],
+        [shape((docs + META, PREFIX), BF16), shape((docs + 2 * META, half - PREFIX), BF16)],
         [embeddings, cluster_id.reshape(1, docs)],
     )
     leads, rests = {0: lead}, {0: rest}
@@ -437,7 +438,7 @@
                 scratch=[pltpu.VMEM(lead_sum.shape, F32)] * (subs - 1),
             )
             weights.append(weight)
-            members.append(across(found))
+            members.append(across(tied(found, weights)))
             lead_sums = across(lead_sums)
             before = (found, weights)
         else:
@@ -463,10 +464,9 @@
             row_shapes,
             [centre] + picks + [rests[bits] for bits in group],
         )
+        if last:
+            found = tied(found, lead_sums)
         members.append(across(found))
-        for bits in group:
-            rests[bits] = tied(rests[bits], found)
-            send(rests, bits, rests[bits])
         if last:
             rest_sums = tied(rest_sums, members[:-1])
         rest_sums = call(
@@ -476,6 +476,9 @@
             weights + [rests[bits] for bits in group] + list(rest_sums),
             {2 * count + i: i for i in range(1 if last else subs)},
         )
+        for bits in group:
+            rests[bits] = tied(rests[bits], weights[:1])
+            send(rests, bits, rests[bits])
     members = tied(members, rest_sums)
     rest_sums = across(rest_sums)
 

time: 57.4 us -> 58.2 us (1.014)
  starting transfers between devices: 20.1 us -> 20.9 us
    ppermute x6, waiting for transfers between devices: 12.1 us -> 9.14 us  [swap(): return lax.ppermute(value, 'rows', [(i, i ^ bit) for i in range(rows)])]
    ppermute x7, waiting for transfers between devices: 7.35 us -> 9.57 us  [across(): lax.ppermute(values[t], 'sub', [(i, (i + t) % subs) for i in range(subs)])]
    ppermute x7, waiting for transfers between devices: 0.6 us -> 1.29 us  [near(): return lax.ppermute(value, 'dim', [(0, 1), (1, 0)])]
    ppermute x7, starting transfers between devices: 9.84 us -> 10.5 us  [across(): lax.ppermute(values[t], 'sub', [(i, (i + t) % subs) for i in range(subs)])]
  transfers between devices with their start and end apart: 20 -> 20, of which waited for: 10 -> 14; matrix products, arithmetic and copies ran while one was open for 0% -> 0% of each run, Pallas kernels for 19% -> 19%
where the time goes in v12:
time: 58.2 us; the launch traced here: 58 us
  starting transfers between devices  20.9 us (36%)
  waiting for transfers between devices  20 us (34%)
  Pallas kernels  12.3 us (21%)
  local copies, waits for them, and re-layouts  4.03 us (7%)
  between operations  0.8 us (1%)
    pallas_call x15, Pallas kernels, call(): pl.pallas_call(kernel, out_shape=tuple(out_shape), in_specs=[whole(operan...  12.3 us
    ppermute x7, starting transfers between devices, across(): lax.ppermute(values[t], 'sub', [(i, (i + t) % subs) for i in range(subs)])  10.5 us
    ppermute x7, waiting for transfers between devices, across(): lax.ppermute(values[t], 'sub', [(i, (i + t) % subs) for i in range(subs)])  9.57 us
    ppermute x6, waiting for transfers between devices, swap(): return lax.ppermute(value, 'rows', [(i, i ^ bit) for i in range(rows)])  9.14 us
    ppermute x6, starting transfers between devices, swap(): return lax.ppermute(value, 'rows', [(i, i ^ bit) for i in range(rows)])  8.25 us
    unnamed x8, local copies, waits for them, and re-layouts  3.99 us
    ppermute x7, starting transfers between devices, near(): return lax.ppermute(value, 'dim', [(0, 1), (1, 0)])  2.16 us
    ppermute x7, waiting for transfers between devices, near(): return lax.ppermute(value, 'dim', [(0, 1), (1, 0)])  1.29 us
  transfers between devices with their start and end apart: 20, of which 14 were waited for; matrix products, arithmetic and copies ran while one was open for 0% of the time, Pallas kernels for 19%

profile of v12, /device:TPU:0, one launch (start us, length us, event | category | flops | bytes accessed | tf_op | source)
XLA Modules:
  0.0 58.0 jit_solution(5907298795772802470)
XLA Ops:
  0.6 1.0 %copy-done.1 = bf16[512,512]{1,0:T(8,128)(2,1)S(1)} copy-done((bf16[512,512]{1,0:T(8,128)(2,1)S(1)}, bf16[512,512]{1,0:T(8,128)(2,1)}, u32[]{:S(2)}) %copy-start.1) | copy-done | bytes 524312
  1.7 0.7 %copy-done.3 = s32[512,1]{0,1:T(1,128)S(1)} copy-done((s32[512,1]{0,1:T(1,128)S(1)}, s32[512,1]{0,1:T(1,128)}, u32[]{:S(2)}) %copy-start.3) | copy-done | bytes 2072
  2.4 0.5 collective-permute-start.3
  2.9 3.7 %collective-permute-start.2 = (bf16[528,256]{1,0:T(8,128)(2,1)S(1)}, bf16[528,256]{1,0:T(8,128)(2,1)S(1)}, u32[]{:S(2)}, u32[]{:S(2)}) collective-permute-start(bf16[528,256]{1,0:T(8,128)(2,1)S(1)} %get-tuple-element.70.lead_ref), channel_id=1, source_target_pairs={{0,8},{4,12},{8,0},{12,4},{1,9},{5,13},{9,1},{13,5},{2,10},{6,14},... | collective-permute-start | bytes 811016 | tf_op jit(solution)/shard_map/ppermute | solution.py:360
  6.6 1.6 %collective-permute-start.1 = (bf16[528,256]{1,0:T(8,128)(2,1)S(1)}, bf16[528,256]{1,0:T(8,128)(2,1)S(1)}, u32[]{:S(2)}, u32[]{:S(2)}) collective-permute-start(bf16[528,256]{1,0:T(8,128)(2,1)S(1)} %get-tuple-element.70.lead_ref), channel_id=1, source_target_pairs={{0,4},{4,0},{8,12},{12,8},{1,5},{5,1},{9,13},{13,9},{2,6},{6,2},{1... | collective-permute-start | bytes 811016 | tf_op jit(solution)/shard_map/ppermute | solution.py:360
  8.2 1.6 %copy-done = bf16[1024,1024]{1,0:T(8,128)(2,1)S(1)} copy-done((bf16[1024,1024]{1,0:T(8,128)(2,1)S(1)}, bf16[1024,1024]{1,0:T(8,128)(2,1)}, u32[]{:S(2)}) %copy-start) | copy-done | bytes 2097176
  9.8 0.7 %copy-done.2 = s32[1024]{0:T(1024)S(1)} copy-done((s32[1024]{0:T(1024)S(1)}, s32[1024]{0:T(1024)}, u32[]{:S(2)}) %copy-start.2) | copy-done | bytes 4120
  10.4 0.8 %prep.1 = (f32[256,1]{1,0:T(8,128)S(1)}, bf16[256,512]{1,0:T(8,128)(2,1)S(1)}, bf16[256,256]{1,0:T(8,128)(2,1)S(1)}, bf16[128,512]{1,0:T(8,128)(2,1)S(1)}, bf16[1024,256]{1,0:T(8,128)(2,1)S(1)}) custom-call(s32[1,1024]{1,0:T(1,128)S(1)} %bitcast.3, bf16[1024,1024]{1,0:T(8,128)(2,1)S(1)} %copy-done), custom_call_target="tpu_custom_call" | custom-call | flops 209715200 | bytes 4194304 | tf_op jit(solution)/shard_map/prep/pallas_call | solution.py:32
  11.3 0.8 %select.1 = (bf16[16,16,512]{2,1,0:T(8,128)(2,1)S(1)}, bf16[16,16,512]{2,1,0:T(8,128)(2,1)S(1)}) custom-call(bf16[528,256]{1,0:T(8,128)(2,1)S(1)} %get-tuple-element.70.lead_ref, bf16[544,256]{1,0:T(8,128)(2,1)S(1)} %get-tuple-element.88.rest_ref, f32[256,1]{1,0:T(8,128)S(1)} %get-tuple-element.72.inv_ref, bf16[256,512]{1,0:T(8,128)(2,1)S(1)} %get-tuple-element.73.centre_ref), custom_call_target="tpu_custom_call" | custom-call | flops 104857600 | bytes 2097152 | tf_op jit(solution)/shard_map/select/pallas_call | solution.py:32
  12.0 1.5 %collective-permute-start = (bf16[16,16,512]{2,1,0:T(8,128)(2,1)S(1)}, bf16[16,16,512]{2,1,0:T(8,128)(2,1)S(1)}, u32[]{:S(2)}, u32[]{:S(2)}) collective-permute-start(bf16[16,16,512]{2,1,0:T(8,128)(2,1)S(1)} %get-tuple-element.75), channel_id=1, source_target_pairs={{0,2},{2,0},{1,3},{3,1},{4,6},{6,4},{5,7},{7,5},{8,10},{10,8},{9,1... | collective-permute-start | bytes 786440 | tf_op jit(solution)/shard_map/ppermute | solution.py:353
  13.6 0.3 collective-permute-start.6
  13.9 0.5 collective-permute-start.5
  14.4 1.3 %sums.1 = (f32[136,256]{1,0:T(8,128)S(1)}, f32[136,256]{1,0:T(8,128)S(1)}, f32[128,256]{1,0:T(8,128)S(1)}, f32[128,256]{1,0:T(8,128)S(1)}) custom-call(bf16[528,256]{1,0:T(8,128)(2,1)S(1)} %get-tuple-element.70.lead_ref, bf16[544,256]{1,0:T(8,128)(2,1)S(1)} %get-tuple-element.88.rest_ref, bf16[528,256]{1,0:T(8,128)(2,1)S(1)} %collective-permute-done.3.near_ref, ...), custom_call_target="tpu_custom_call" | custom-call | flops 104857600 | bytes 2097152 | tf_op jit(solution)/shard_map/sums/pallas_call | solution.py:32
  15.8 4.4 %collective-permute-done.refs_5_ = bf16[16,16,512]{2,1,0:T(8,128)(2,1)S(1)} collective-permute-done((bf16[16,16,512]{2,1,0:T(8,128)(2,1)S(1)}, bf16[16,16,512]{2,1,0:T(8,128)(2,1)S(1)}, u32[]{:S(2)}, u32[]{:S(2)}) %collective-permute-start) | collective-permute-done | bytes 262176 | tf_op jit(solution)/shard_map/ppermute | solution.py:353
  20.2 0.7 %collective-permute-done.1.refs_0_.lead_ref = bf16[528,256]{1,0:T(8,128)(2,1)S(1)} collective-permute-done((bf16[528,256]{1,0:T(8,128)(2,1)S(1)}, bf16[528,256]{1,0:T(8,128)(2,1)S(1)}, u32[]{:S(2)}, u32[]{:S(2)}) %collective-permute-start.1) | collective-permute-done | bytes 270368 | tf_op jit(solution)/shard_map/ppermute | solution.py:360
  20.9 1.1 %select_lead.2 = (bf16[512,512]{1,0:T(8,128)(2,1)S(1)}, bf16[512,512]{1,0:T(8,128)(2,1)S(1)}, bf16[2,16,16,256]{3,2,1,0:T(8,128)(2,1)S(1)}, bf16[2,16,16,256]{3,2,1,0:T(8,128)(2,1)S(1)}) custom-call(f32[256,1]{1,0:T(8,128)S(1)} %get-tuple-element.72.inv_ref, bf16[256,512]{1,0:T(8,128)(2,1)S(1)} %get-tuple-element.73.centre_ref, ...), custom_call_target="tpu_custom_call" | custom-call | tf_op jit(solution)/shard_map/select_lead/pallas_call | solution.py:32
  22.0 2.0 %collective-permute-start.4 = (bf16[2,16,16,256]{3,2,1,0:T(8,128)(2,1)S(1)}, bf16[2,16,16,256]{3,2,1,0:T(8,128)(2,1)S(1)}, u32[]{:S(2)}, u32[]{:S(2)}) collective-permute-start(bf16[2,16,16,256]{3,2,1,0:T(8,128)(2,1)S(1)} %get-tuple-element.85), channel_id=1, source_target_pairs={{0,2},{2,0},{1,3},{3,1},{4,6},{6,4},{5,7},{7,5},{8,10},{10,8},{9,1... | collective-permute-start | bytes 786440 | tf_op jit(solution)/shard_map/ppermute | solution.py:353
  23.9 0.5 collective-permute-start.9
  24.5 6.1 %collective-permute-done.5.refs_2_ = bf16[528,256]{1,0:T(8,128)(2,1)S(1)} collective-permute-done((bf16[528,256]{1,0:T(8,128)(2,1)S(1)}, bf16[528,256]{1,0:T(8,128)(2,1)S(1)}, u32[]{:S(2)}, u32[]{:S(2)}) %collective-permute-start.5) | collective-permute-done | bytes 270368 | tf_op jit(solution)/shard_map/ppermute | solution.py:360
  30.6 0.9 %collective-permute-done.6.refs_3_ = bf16[544,256]{1,0:T(8,128)(2,1)S(1)} collective-permute-done((bf16[544,256]{1,0:T(8,128)(2,1)S(1)}, bf16[544,256]{1,0:T(8,128)(2,1)S(1)}, u32[]{:S(2)}, u32[]{:S(2)}) %collective-permute-start.6) | collective-permute-done | bytes 278560 | tf_op jit(solution)/shard_map/ppermute | solution.py:360
  31.5 1.6 %collective-permute-start.8 = (bf16[528,256]{1,0:T(8,128)(2,1)S(1)}, bf16[528,256]{1,0:T(8,128)(2,1)S(1)}, u32[]{:S(2)}, u32[]{:S(2)}) collective-permute-start(bf16[528,256]{1,0:T(8,128)(2,1)S(1)} %collective-permute-done.2.refs_1_.lead_ref), channel_id=1, source_target_pairs={{0,4},{4,0},{8,12},{12,8},{1,5},{5,1},{9,13},{13,9},{2,6},{6,2},{1... | collective-permute-start | bytes 811016 | tf_op jit(solution)/shard_map/ppermute | solution.py:360
  33.1 0.4 select_rest.2
  33.5 1.6 %collective-permute-start.7 = (bf16[2,16,16,256]{3,2,1,0:T(8,128)(2,1)S(1)}, bf16[2,16,16,256]{3,2,1,0:T(8,128)(2,1)S(1)}, u32[]{:S(2)}, u32[]{:S(2)}) collective-permute-start(bf16[2,16,16,256]{3,2,1,0:T(8,128)(2,1)S(1)} %get-tuple-element.92), channel_id=1, source_target_pairs={{0,2},{2,0},{1,3},{3,1},{4,6},{6,4},{5,7},{7,5},{8,10},{10,8},{9,1... | collective-permute-start | bytes 786440 | tf_op jit(solution)/shard_map/ppermute | solution.py:353
  35.1 1.4 %sums_lead.3 = (bf16[256,512]{1,0:T(8,128)(2,1)S(1)}, f32[136,256]{1,0:T(8,128)S(1)}, f32[136,256]{1,0:T(8,128)S(1)}) custom-call(bf16[528,256]{1,0:T(8,128)(2,1)S(1)} %collective-permute-done.1.refs_0_.lead_ref, bf16[528,256]{1,0:T(8,128)(2,1)S(1)} %collective-permute-done.10.near_ref, ...), custom_call_target="tpu_custom_call", output_to_operand_aliasing={{1}: (4, {}), {2}: (5, {})} | custom-call | tf_op jit(solution)/shard_map/sums_lead/pallas_call | solution.py:32
  36.5 1.4 %sums_lead.4 = (bf16[256,512]{1,0:T(8,128)(2,1)S(1)}, f32[136,256]{1,0:T(8,128)S(1)}, f32[136,256]{1,0:T(8,128)S(1)}) custom-call(bf16[528,256]{1,0:T(8,128)(2,1)S(1)} %collective-permute-done.2.refs_1_.lead_ref, bf16[528,256]{1,0:T(8,128)(2,1)S(1)} %collective-permute-done.9.near_ref, ...), custom_call_target="tpu_custom_call", output_to_operand_aliasing={{1}: (4, {}), {2}: (5, {})} | custom-call | tf_op jit(solution)/shard_map/sums_lead/pallas_call | solution.py:32
  37.9 0.3 sums_rest.2
  38.2 0.6 %collective-permute-start.14 = (bf16[544,256]{1,0:T(8,128)(2,1)S(1)}, bf16[544,256]{1,0:T(8,128)(2,1)S(1)}, u32[]{:S(2)}, u32[]{:S(2)}) collective-permute-start(bf16[544,256]{1,0:T(8,128)(2,1)S(1)} %collective-permute-done.6.refs_3_), channel_id=1, source_target_pairs={{0,4},{4,0},{8,12},{12,8},{1,5},{5,1},{9,13},{13,9},{2,6},{6,2},{1... | collective-permute-start | bytes 835592 | tf_op jit(solution)/shard_map/ppermute | solution.py:360
  38.8 0.9 %collective-permute-done.8.refs_0_.lead_ref = bf16[528,256]{1,0:T(8,128)(2,1)S(1)} collective-permute-done((bf16[528,256]{1,0:T(8,128)(2,1)S(1)}, bf16[528,256]{1,0:T(8,128)(2,1)S(1)}, u32[]{:S(2)}, u32[]{:S(2)}) %collective-permute-start.8) | collective-permute-done | bytes 270368 | tf_op jit(solution)/shard_map/ppermute | solution.py:360
  39.8 0.5 collective-permute-start.11
  40.3 0.8 %collective-permute-done.12.high_ref = bf16[256,256]{1,0:T(8,128)(2,1)S(1)} collective-permute-done((bf16[256,256]{1,0:T(8,128)(2,1)S(1)}, bf16[256,256]{1,0:T(8,128)(2,1)S(1)}, u32[]{:S(2)}, u32[]{:S(2)}) %collective-permute-start.12) | collective-permute-done | bytes 131104 | tf_op jit(solution)/shard_map/ppermute | solution.py:357
  41.1 0.2 collective-permute-done.11.low_ref
  41.3 1.4 %sums_lead.5 = (bf16[256,512]{1,0:T(8,128)(2,1)S(1)}, f32[136,256]{1,0:T(8,128)S(1)}, bf16[144,256]{1,0:T(8,128)(2,1)S(1)}) custom-call(bf16[528,256]{1,0:T(8,128)(2,1)S(1)} %collective-permute-done.8.refs_0_.lead_ref, bf16[256,256]{1,0:T(8,128)(2,1)S(1)} %collective-permute-done.11.low_ref, ...), custom_call_target="tpu_custom_call", output_to_operand_aliasing={{1}: (5, {})} | custom-call | tf_op jit(solution)/shard_map/sums_lead/pallas_call | solution.py:32
  42.7 2.0 %collective-permute-start.15 = (bf16[144,256]{1,0:T(8,128)(2,1)S(1)}, bf16[144,256]{1,0:T(8,128)(2,1)S(1)}, u32[]{:S(2)}, u32[]{:S(2)}) collective-permute-start(bf16[144,256]{1,0:T(8,128)(2,1)S(1)} %get-tuple-element.116), channel_id=1, source_target_pairs={{0,2},{2,0},{1,3},{3,1},{4,6},{6,4},{5,7},{7,5},{8,10},{10,8},{9,1... | collective-permute-start | bytes 221192 | tf_op jit(solution)/shard_map/ppermute | solution.py:353
  44.7 0.6 %select_lead.3 = (bf16[512,512]{1,0:T(8,128)(2,1)S(1)}, bf16[1,16,16,256]{3,2,1,0:T(8,128)(2,1)S(1)}, bf16[1,16,16,256]{3,2,1,0:T(8,128)(2,1)S(1)}) custom-call(f32[256,1]{1,0:T(8,128)S(1)} %get-tuple-element.72.inv_ref, bf16[256,512]{1,0:T(8,128)(2,1)S(1)} %get-tuple-element.73.centre_ref, bf16[528,256]{1,0:T(8,128)(2,1)S(1)} %collective-permute-done.8.refs_0_.lead_ref), custom_call_target="tpu_custom_call" | custom-call | tf_op jit(solution)/shard_map/select_lead/pallas_call | solution.py:32
  45.3 0.2 collective-permute-start.13
  45.5 0.4 collective-permute-done.14.refs_1_
  45.9 0.3 select_rest.3
  46.2 1.2 %collective-permute-done.15.refs_5_ = bf16[144,256]{1,0:T(8,128)(2,1)S(1)} collective-permute-done((bf16[144,256]{1,0:T(8,128)(2,1)S(1)}, bf16[144,256]{1,0:T(8,128)(2,1)S(1)}, u32[]{:S(2)}, u32[]{:S(2)}) %collective-permute-start.15) | collective-permute-done | bytes 73760 | tf_op jit(solution)/shard_map/ppermute | solution.py:353
  47.4 2.3 %collective-permute-start.16 = (bf16[1,16,16,256]{3,2,1,0:T(8,128)(2,1)S(1)}, bf16[1,16,16,256]{3,2,1,0:T(8,128)(2,1)S(1)}, u32[]{:S(2)}, u32[]{:S(2)}) collective-permute-start(bf16[1,16,16,256]{3,2,1,0:T(8,128)(2,1)S(1)} %get-tuple-element.118), channel_id=1, source_target_pairs={{0,2},{2,0},{1,3},{3,1},{4,6},{6,4},{5,7},{7,5},{8,10},{10,8},{9,1... | collective-permute-start | bytes 393224 | tf_op jit(solution)/shard_map/ppermute | solution.py:353
  49.7 1.9 %collective-permute-done.13.refs_8_ = bf16[1,16,16,256]{3,2,1,0:T(8,128)(2,1)S(1)} collective-permute-done((bf16[1,16,16,256]{3,2,1,0:T(8,128)(2,1)S(1)}, bf16[1,16,16,256]{3,2,1,0:T(8,128)(2,1)S(1)}, u32[]{:S(2)}, u32[]{:S(2)}) %collective-permute-start.13) | collective-permute-done | bytes 131104 | tf_op jit(solution)/shard_map/ppermute | solution.py:353
  51.7 0.2 sums_rest.3
  51.9 0.9 %collective-permute-start.19 = (bf16[144,256]{1,0:T(8,128)(2,1)S(1)}, bf16[144,256]{1,0:T(8,128)(2,1)S(1)}, u32[]{:S(2)}, u32[]{:S(2)}) collective-permute-start(bf16[144,256]{1,0:T(8,128)(2,1)S(1)} %get-tuple-element.122), channel_id=1, source_target_pairs={{0,2},{2,0},{1,3},{3,1},{4,6},{6,4},{5,7},{7,5},{8,10},{10,8},{9,1... | collective-permute-start | bytes 221192 | tf_op jit(solution)/shard_map/ppermute | solution.py:353
  52.9 1.4 %collective-permute-done.16.refs_9_ = bf16[1,16,16,256]{3,2,1,0:T(8,128)(2,1)S(1)} collective-permute-done((bf16[1,16,16,256]{3,2,1,0:T(8,128)(2,1)S(1)}, bf16[1,16,16,256]{3,2,1,0:T(8,128)(2,1)S(1)}, u32[]{:S(2)}, u32[]{:S(2)}) %collective-permute-start.16) | collective-permute-done | bytes 131104 | tf_op jit(solution)/shard_map/ppermute | solution.py:353
  54.2 0.9 %gram.1 = (f32[8,16,128]{2,1,0:T(8,128)S(1)}, f32[8,16,128]{2,1,0:T(8,128)S(1)}) custom-call(bf16[16,16,512]{2,1,0:T(8,128)(2,1)S(1)} %get-tuple-element.123.refs_0_, bf16[2,16,16,256]{3,2,1,0:T(8,128)(2,1)S(1)} %get-tuple-element.124.refs_1_, bf16[2,16,16,256]{3,2,1,0:T(8,128)(2,1)S(1)} %get-tuple-element.125.refs_2_, ...), custom_call_target="tpu_custom_call" | custom-call | tf_op jit(solution)/shard_map/gram/pallas_call | solution.py:32
  55.2 0.5 collective-permute-start.18
  55.7 0.6 %collective-permute-done.19.refs_7_ = bf16[144,256]{1,0:T(8,128)(2,1)S(1)} collective-permute-done((bf16[144,256]{1,0:T(8,128)(2,1)S(1)}, bf16[144,256]{1,0:T(8,128)(2,1)S(1)}, u32[]{:S(2)}, u32[]{:S(2)}) %collective-permute-start.19) | collective-permute-done | bytes 73760 | tf_op jit(solution)/shard_map/ppermute | solution.py:353
  56.4 0.2 collective-permute-done.18.refs_3_
  56.6 1.4 %finish.1 = (f32[128,512]{1,0:T(8,128)}, bf16[8,16,128]{2,1,0:T(8,128)(2,1)}) custom-call(f32[8,16,128]{2,1,0:T(8,128)S(1)} %get-tuple-element.133.refs_0_, f32[8,16,128]{2,1,0:T(8,128)S(1)} %get-tuple-element.134.refs_1_, f32[8,16,128]{2,1,0:T(8,128)S(1)} %collective-permute-done.17.refs_2_, f32[8,16,128]{2,1,0:T(8,128)S(1)} %collective-permute-done.18.refs_3_, ...), custom_call_target="tpu_custom_call" | custom-call | tf_op jit(solution)/shard_map/finish/pallas_call | solution.py:32
  (17 shorter events, 0.4 us)
Async XLA Ops:
  0.6 1.0 %copy-start.1 = (bf16[512,512]{1,0:T(8,128)(2,1)S(1)}, bf16[512,512]{1,0:T(8,128)(2,1)}, u32[]{:S(2)}) copy-start(bf16[512,512]{1,0:T(8,128)(2,1)} %emb_ref.1) | copy-start | bytes 1572868
  1.7 0.7 %copy-start.3 = (s32[512,1]{0,1:T(1,128)S(1)}, s32[512,1]{0,1:T(1,128)}, u32[]{:S(2)}) copy-start(s32[512,1]{0,1:T(1,128)} %param.6) | copy-start | bytes 6148
  2.4 11.5 %collective-permute-start.3 = (bf16[528,256]{1,0:T(8,128)(2,1)S(1)}, bf16[528,256]{1,0:T(8,128)(2,1)S(1)}, u32[]{:S(2)}, u32[]{:S(2)}) collective-permute-start(bf16[528,256]{1,0:T(8,128)(2,1)S(1)} %get-tuple-element.70.lead_ref), channel_id=1, source_target_pairs={{0,1},{1,0},{2,3},{3,2},{4,5},{5,4},{6,7},{7,6},{8,9},{9,8},{10,11... | collective-permute-start | bytes 811016 | tf_op jit(solution)/shard_map/ppermute | solution.py:357
  2.9 17.3 %collective-permute-start.2 = (bf16[528,256]{1,0:T(8,128)(2,1)S(1)}, bf16[528,256]{1,0:T(8,128)(2,1)S(1)}, u32[]{:S(2)}, u32[]{:S(2)}) collective-permute-start(bf16[528,256]{1,0:T(8,128)(2,1)S(1)} %get-tuple-element.70.lead_ref), channel_id=1, source_target_pairs={{0,8},{4,12},{8,0},{12,4},{1,9},{5,13},{9,1},{13,5},{2,10},{6,14},... | collective-permute-start | bytes 811016 | tf_op jit(solution)/shard_map/ppermute | solution.py:360
  6.6 14.3 %collective-permute-start.1 = (bf16[528,256]{1,0:T(8,128)(2,1)S(1)}, bf16[528,256]{1,0:T(8,128)(2,1)S(1)}, u32[]{:S(2)}, u32[]{:S(2)}) collective-permute-start(bf16[528,256]{1,0:T(8,128)(2,1)S(1)} %get-tuple-element.70.lead_ref), channel_id=1, source_target_pairs={{0,4},{4,0},{8,12},{12,8},{1,5},{5,1},{9,13},{13,9},{2,6},{6,2},{1... | collective-permute-start | bytes 811016 | tf_op jit(solution)/shard_map/ppermute | solution.py:360
  8.2 1.6 %copy-start = (bf16[1024,1024]{1,0:T(8,128)(2,1)S(1)}, bf16[1024,1024]{1,0:T(8,128)(2,1)}, u32[]{:S(2)}) copy-start(bf16[1024,1024]{1,0:T(8,128)(2,1)} %cent_ref.1) | copy-start | bytes 6291460
  9.8 0.7 %copy-start.2 = (s32[1024]{0:T(1024)S(1)}, s32[1024]{0:T(1024)}, u32[]{:S(2)}) copy-start(s32[1024]{0:T(1024)} %param.7) | copy-start | bytes 12292
  12.0 8.1 %collective-permute-start = (bf16[16,16,512]{2,1,0:T(8,128)(2,1)S(1)}, bf16[16,16,512]{2,1,0:T(8,128)(2,1)S(1)}, u32[]{:S(2)}, u32[]{:S(2)}) collective-permute-start(bf16[16,16,512]{2,1,0:T(8,128)(2,1)S(1)} %get-tuple-element.75), channel_id=1, source_target_pairs={{0,2},{2,0},{1,3},{3,1},{4,6},{6,4},{5,7},{7,5},{8,10},{10,8},{9,1... | collective-permute-start | bytes 786440 | tf_op jit(solution)/shard_map/ppermute | solution.py:353
  13.6 17.9 %collective-permute-start.6 = (bf16[544,256]{1,0:T(8,128)(2,1)S(1)}, bf16[544,256]{1,0:T(8,128)(2,1)S(1)}, u32[]{:S(2)}, u32[]{:S(2)}) collective-permute-start(bf16[544,256]{1,0:T(8,128)(2,1)S(1)} %get-tuple-element.88.rest_ref), channel_id=1, source_target_pairs={{0,8},{4,12},{8,0},{12,4},{1,9},{5,13},{9,1},{13,5},{2,10},{6,14},... | collective-permute-start | bytes 835592 | tf_op jit(solution)/shard_map/ppermute | solution.py:360
  13.9 16.6 %collective-permute-start.5 = (bf16[528,256]{1,0:T(8,128)(2,1)S(1)}, bf16[528,256]{1,0:T(8,128)(2,1)S(1)}, u32[]{:S(2)}, u32[]{:S(2)}) collective-permute-start(bf16[528,256]{1,0:T(8,128)(2,1)S(1)} %slice.9), channel_id=1, source_target_pairs={{0,4},{4,0},{8,12},{12,8},{1,5},{5,1},{9,13},{13,9},{2,6},{6,2},{1... | collective-permute-start | bytes 811016 | tf_op jit(solution)/shard_map/ppermute | solution.py:360
  22.0 9.5 %collective-permute-start.4 = (bf16[2,16,16,256]{3,2,1,0:T(8,128)(2,1)S(1)}, bf16[2,16,16,256]{3,2,1,0:T(8,128)(2,1)S(1)}, u32[]{:S(2)}, u32[]{:S(2)}) collective-permute-start(bf16[2,16,16,256]{3,2,1,0:T(8,128)(2,1)S(1)} %get-tuple-element.85), channel_id=1, source_target_pairs={{0,2},{2,0},{1,3},{3,1},{4,6},{6,4},{5,7},{7,5},{8,10},{10,8},{9,1... | collective-permute-start | bytes 786440 | tf_op jit(solution)/shard_map/ppermute | solution.py:353
  23.9 11.1 %collective-permute-start.10 = (bf16[528,256]{1,0:T(8,128)(2,1)S(1)}, bf16[528,256]{1,0:T(8,128)(2,1)S(1)}, u32[]{:S(2)}, u32[]{:S(2)}) collective-permute-start(bf16[528,256]{1,0:T(8,128)(2,1)S(1)} %collective-permute-done.1.refs_0_.lead_ref), channel_id=1, source_target_pairs={{0,1},{1,0},{2,3},{3,2},{4,5},{5,4},{6,7},{7,6},{8,9},{9,8},{10,11... | collective-permute-start | bytes 811016 | tf_op jit(solution)/shard_map/ppermute | solution.py:357
  23.9 12.5 %collective-permute-start.9 = (bf16[528,256]{1,0:T(8,128)(2,1)S(1)}, bf16[528,256]{1,0:T(8,128)(2,1)S(1)}, u32[]{:S(2)}, u32[]{:S(2)}) collective-permute-start(bf16[528,256]{1,0:T(8,128)(2,1)S(1)} %collective-permute-done.2.refs_1_.lead_ref), channel_id=1, source_target_pairs={{0,1},{1,0},{2,3},{3,2},{4,5},{5,4},{6,7},{7,6},{8,9},{9,8},{10,11... | collective-permute-start | bytes 811016 | tf_op jit(solution)/shard_map/ppermute | solution.py:357
  31.5 8.2 %collective-permute-start.8 = (bf16[528,256]{1,0:T(8,128)(2,1)S(1)}, bf16[528,256]{1,0:T(8,128)(2,1)S(1)}, u32[]{:S(2)}, u32[]{:S(2)}) collective-permute-start(bf16[528,256]{1,0:T(8,128)(2,1)S(1)} %collective-permute-done.2.refs_1_.lead_ref), channel_id=1, source_target_pairs={{0,4},{4,0},{8,12},{12,8},{1,5},{5,1},{9,13},{13,9},{2,6},{6,2},{1... | collective-permute-start | bytes 811016 | tf_op jit(solution)/shard_map/ppermute | solution.py:360
  33.5 11.7 %collective-permute-start.7 = (bf16[2,16,16,256]{3,2,1,0:T(8,128)(2,1)S(1)}, bf16[2,16,16,256]{3,2,1,0:T(8,128)(2,1)S(1)}, u32[]{:S(2)}, u32[]{:S(2)}) collective-permute-start(bf16[2,16,16,256]{3,2,1,0:T(8,128)(2,1)S(1)} %get-tuple-element.92), channel_id=1, source_target_pairs={{0,2},{2,0},{1,3},{3,1},{4,6},{6,4},{5,7},{7,5},{8,10},{10,8},{9,1... | collective-permute-start | bytes 786440 | tf_op jit(solution)/shard_map/ppermute | solution.py:353
  38.2 7.7 %collective-permute-start.14 = (bf16[544,256]{1,0:T(8,128)(2,1)S(1)}, bf16[544,256]{1,0:T(8,128)(2,1)S(1)}, u32[]{:S(2)}, u32[]{:S(2)}) collective-permute-start(bf16[544,256]{1,0:T(8,128)(2,1)S(1)} %collective-permute-done.6.refs_3_), channel_id=1, source_target_pairs={{0,4},{4,0},{8,12},{12,8},{1,5},{5,1},{9,13},{13,9},{2,6},{6,2},{1... | collective-permute-start | bytes 835592 | tf_op jit(solution)/shard_map/ppermute | solution.py:360
  39.7 1.4 %collective-permute-start.12 = (bf16[256,256]{1,0:T(8,128)(2,1)S(1)}, bf16[256,256]{1,0:T(8,128)(2,1)S(1)}, u32[]{:S(2)}, u32[]{:S(2)}) collective-permute-start(bf16[256,256]{1,0:T(8,128)(2,1)S(1)} %get-tuple-element.138), channel_id=1, source_target_pairs={{0,1},{1,0},{2,3},{3,2},{4,5},{5,4},{6,7},{7,6},{8,9},{9,8},{10,11... | collective-permute-start | bytes 393224 | tf_op jit(solution)/shard_map/ppermute | solution.py:357
  39.8 1.5 %collective-permute-start.11 = (bf16[256,256]{1,0:T(8,128)(2,1)S(1)}, bf16[256,256]{1,0:T(8,128)(2,1)S(1)}, u32[]{:S(2)}, u32[]{:S(2)}) collective-permute-start(bf16[256,256]{1,0:T(8,128)(2,1)S(1)} %get-tuple-element.139), channel_id=1, source_target_pairs={{0,1},{1,0},{2,3},{3,2},{4,5},{5,4},{6,7},{7,6},{8,9},{9,8},{10,11... | collective-permute-start | bytes 393224 | tf_op jit(solution)/shard_map/ppermute | solution.py:357
  42.7 4.7 %collective-permute-start.15 = (bf16[144,256]{1,0:T(8,128)(2,1)S(1)}, bf16[144,256]{1,0:T(8,128)(2,1)S(1)}, u32[]{:S(2)}, u32[]{:S(2)}) collective-permute-start(bf16[144,256]{1,0:T(8,128)(2,1)S(1)} %get-tuple-element.116), channel_id=1, source_target_pairs={{0,2},{2,0},{1,3},{3,1},{4,6},{6,4},{5,7},{7,5},{8,10},{10,8},{9,1... | collective-permute-start | bytes 221192 | tf_op jit(solution)/shard_map/ppermute | solution.py:353
  45.3 6.4 %collective-permute-start.13 = (bf16[1,16,16,256]{3,2,1,0:T(8,128)(2,1)S(1)}, bf16[1,16,16,256]{3,2,1,0:T(8,128)(2,1)S(1)}, u32[]{:S(2)}, u32[]{:S(2)}) collective-permute-start(bf16[1,16,16,256]{3,2,1,0:T(8,128)(2,1)S(1)} %get-tuple-element.109), channel_id=1, source_target_pairs={{0,2},{2,0},{1,3},{3,1},{4,6},{6,4},{5,7},{7,5},{8,10},{10,8},{9,1... | collective-permute-start | bytes 393224 | tf_op jit(solution)/shard_map/ppermute | solution.py:353
  47.4 6.8 %collective-permute-start.16 = (bf16[1,16,16,256]{3,2,1,0:T(8,128)(2,1)S(1)}, bf16[1,16,16,256]{3,2,1,0:T(8,128)(2,1)S(1)}, u32[]{:S(2)}, u32[]{:S(2)}) collective-permute-start(bf16[1,16,16,256]{3,2,1,0:T(8,128)(2,1)S(1)} %get-tuple-element.118), channel_id=1, source_target_pairs={{0,2},{2,0},{1,3},{3,1},{4,6},{6,4},{5,7},{7,5},{8,10},{10,8},{9,1... | collective-permute-start | bytes 393224 | tf_op jit(solution)/shard_map/ppermute | solution.py:353
  51.9 4.4 %collective-permute-start.19 = (bf16[144,256]{1,0:T(8,128)(2,1)S(1)}, bf16[144,256]{1,0:T(8,128)(2,1)S(1)}, u32[]{:S(2)}, u32[]{:S(2)}) collective-permute-start(bf16[144,256]{1,0:T(8,128)(2,1)S(1)} %get-tuple-element.122), channel_id=1, source_target_pairs={{0,2},{2,0},{1,3},{3,1},{4,6},{6,4},{5,7},{7,5},{8,10},{10,8},{9,1... | collective-permute-start | bytes 221192 | tf_op jit(solution)/shard_map/ppermute | solution.py:353
  55.1 1.3 %collective-permute-start.17 = (f32[8,16,128]{2,1,0:T(8,128)S(1)}, f32[8,16,128]{2,1,0:T(8,128)S(1)}, u32[]{:S(2)}, u32[]{:S(2)}) collective-permute-start(f32[8,16,128]{2,1,0:T(8,128)S(1)} %get-tuple-element.133.refs_0_), channel_id=1, source_target_pairs={{0,1},{1,0},{2,3},{3,2},{4,5},{5,4},{6,7},{7,6},{8,9},{9,8},{10,11... | collective-permute-start | bytes 196616 | tf_op jit(solution)/shard_map/ppermute | solution.py:357
  55.2 1.4 %collective-permute-start.18 = (f32[8,16,128]{2,1,0:T(8,128)S(1)}, f32[8,16,128]{2,1,0:T(8,128)S(1)}, u32[]{:S(2)}, u32[]{:S(2)}) collective-permute-start(f32[8,16,128]{2,1,0:T(8,128)S(1)} %get-tuple-element.134.refs_1_), channel_id=1, source_target_pairs={{0,1},{1,0},{2,3},{3,2},{4,5},{5,4},{6,7},{7,6},{8,9},{9,8},{10,11... | collective-permute-start | bytes 196616 | tf_op jit(solution)/shard_map/ppermute | solution.py:357

commit v13 on v12

--- a/solution.py
+++ b/solution.py
@@ -433,12 +433,12 @@
                 functools.partial(last_sums_lead_kernel, subs),
                 "sums_lead",
                 [shape((subs * per, docs), BF16), lead_sum] + [sent_lead] * (subs - 1),
-                [lead] + halves + [cent_prefix, own_prefix] + lead_sums,
+                [tied(lead, picks)] + halves + [cent_prefix, own_prefix] + lead_sums,
                 {5: 1},
                 scratch=[pltpu.VMEM(lead_sum.shape, F32)] * (subs - 1),
             )
             weights.append(weight)
-            members.append(across(tied(found, weights)))
+            members.append(across(found))
             lead_sums = across(lead_sums)
             before = (found, weights)
         else:
@@ -465,7 +465,7 @@
             [centre] + picks + [rests[bits] for bits in group],
         )
         if last:
-            found = tied(found, lead_sums)
+            found = tied(found, lead_sums, members)
         members.append(across(found))
         if last:
             rest_sums = tied(rest_sums, members[:-1])

time: 58.2 us -> 58.1 us (level)
  starting transfers between devices: 20.9 us -> 19.6 us
  waiting for transfers between devices: 20 us -> 21.1 us
    ppermute x7, starting transfers between devices: 10.5 us -> 9.23 us  [across(): lax.ppermute(values[t], 'sub', [(i, (i + t) % subs) for i in range(subs)])]
    ppermute x6, waiting for transfers between devices: 9.14 us -> 9.95 us  [swap(): return lax.ppermute(value, 'rows', [(i, i ^ bit) for i in range(rows)])]
    ppermute x7, waiting for transfers between devices: 9.57 us -> 10.2 us  [across(): lax.ppermute(values[t], 'sub', [(i, (i + t) % subs) for i in range(subs)])]
  transfers between devices with their start and end apart: 20 -> 20, of which waited for: 14 -> 12; matrix products, arithmetic and copies ran while one was open for 0% -> 0% of each run, Pallas kernels for 19% -> 19%
where the time goes in v13:
time: 58.1 us; the launch traced here: 57.8 us
  waiting for transfers between devices  21.1 us (36%)
  starting transfers between devices  19.6 us (34%)
  Pallas kernels  12.3 us (21%)
  local copies, waits for them, and re-layouts  4.03 us (7%)
  between operations  0.79 us (1%)
    pallas_call x15, Pallas kernels, call(): pl.pallas_call(kernel, out_shape=tuple(out_shape), in_specs=[whole(operan...  12.3 us
    ppermute x7, waiting for transfers between devices, across(): lax.ppermute(values[t], 'sub', [(i, (i + t) % subs) for i in range(subs)])  10.2 us
    ppermute x6, waiting for transfers between devices, swap(): return lax.ppermute(value, 'rows', [(i, i ^ bit) for i in range(rows)])  9.95 us
    ppermute x7, starting transfers between devices, across(): lax.ppermute(values[t], 'sub', [(i, (i + t) % subs) for i in range(subs)])  9.23 us
    ppermute x6, starting transfers between devices, swap(): return lax.ppermute(value, 'rows', [(i, i ^ bit) for i in range(rows)])  8.25 us
    unnamed x8, local copies, waits for them, and re-layouts  3.99 us
    ppermute x7, starting transfers between devices, near(): return lax.ppermute(value, 'dim', [(0, 1), (1, 0)])  2.16 us
  transfers between devices with their start and end apart: 20, of which 12 were waited for; matrix products, arithmetic and copies ran while one was open for 0% of the time, Pallas kernels for 19%

profile of v13, /device:TPU:0, one launch (start us, length us, event | category | flops | bytes accessed | tf_op | source)
XLA Modules:
  0.0 57.8 jit_solution(5008656823764504508)
XLA Ops:
  0.6 1.0 %copy-done.1 = bf16[512,512]{1,0:T(8,128)(2,1)S(1)} copy-done((bf16[512,512]{1,0:T(8,128)(2,1)S(1)}, bf16[512,512]{1,0:T(8,128)(2,1)}, u32[]{:S(2)}) %copy-start.1) | copy-done | bytes 524312
  1.7 0.7 %copy-done.3 = s32[512,1]{0,1:T(1,128)S(1)} copy-done((s32[512,1]{0,1:T(1,128)S(1)}, s32[512,1]{0,1:T(1,128)}, u32[]{:S(2)}) %copy-start.3) | copy-done | bytes 2072
  2.4 0.5 collective-permute-start.3
  2.9 3.7 %collective-permute-start.2 = (bf16[528,256]{1,0:T(8,128)(2,1)S(1)}, bf16[528,256]{1,0:T(8,128)(2,1)S(1)}, u32[]{:S(2)}, u32[]{:S(2)}) collective-permute-start(bf16[528,256]{1,0:T(8,128)(2,1)S(1)} %get-tuple-element.69.lead_ref), channel_id=1, source_target_pairs={{0,8},{4,12},{8,0},{12,4},{1,9},{5,13},{9,1},{13,5},{2,10},{6,14},... | collective-permute-start | bytes 811016 | tf_op jit(solution)/shard_map/ppermute | solution.py:360
  6.6 1.6 %collective-permute-start.1 = (bf16[528,256]{1,0:T(8,128)(2,1)S(1)}, bf16[528,256]{1,0:T(8,128)(2,1)S(1)}, u32[]{:S(2)}, u32[]{:S(2)}) collective-permute-start(bf16[528,256]{1,0:T(8,128)(2,1)S(1)} %get-tuple-element.69.lead_ref), channel_id=1, source_target_pairs={{0,4},{4,0},{8,12},{12,8},{1,5},{5,1},{9,13},{13,9},{2,6},{6,2},{1... | collective-permute-start | bytes 811016 | tf_op jit(solution)/shard_map/ppermute | solution.py:360
  8.2 1.6 %copy-done = bf16[1024,1024]{1,0:T(8,128)(2,1)S(1)} copy-done((bf16[1024,1024]{1,0:T(8,128)(2,1)S(1)}, bf16[1024,1024]{1,0:T(8,128)(2,1)}, u32[]{:S(2)}) %copy-start) | copy-done | bytes 2097176
  9.8 0.7 %copy-done.2 = s32[1024]{0:T(1024)S(1)} copy-done((s32[1024]{0:T(1024)S(1)}, s32[1024]{0:T(1024)}, u32[]{:S(2)}) %copy-start.2) | copy-done | bytes 4120
  10.4 0.8 %prep.1 = (f32[256,1]{1,0:T(8,128)S(1)}, bf16[256,512]{1,0:T(8,128)(2,1)S(1)}, bf16[256,256]{1,0:T(8,128)(2,1)S(1)}, bf16[128,512]{1,0:T(8,128)(2,1)S(1)}, bf16[1024,256]{1,0:T(8,128)(2,1)S(1)}) custom-call(s32[1,1024]{1,0:T(1,128)S(1)} %bitcast.3, bf16[1024,1024]{1,0:T(8,128)(2,1)S(1)} %copy-done), custom_call_target="tpu_custom_call" | custom-call | flops 209715200 | bytes 4194304 | tf_op jit(solution)/shard_map/prep/pallas_call | solution.py:32
  11.3 0.8 %select.1 = (bf16[16,16,512]{2,1,0:T(8,128)(2,1)S(1)}, bf16[16,16,512]{2,1,0:T(8,128)(2,1)S(1)}) custom-call(bf16[528,256]{1,0:T(8,128)(2,1)S(1)} %get-tuple-element.69.lead_ref, bf16[544,256]{1,0:T(8,128)(2,1)S(1)} %get-tuple-element.87.rest_ref, f32[256,1]{1,0:T(8,128)S(1)} %get-tuple-element.71.inv_ref, bf16[256,512]{1,0:T(8,128)(2,1)S(1)} %get-tuple-element.72.centre_ref), custom_call_target="tpu_custom_call" | custom-call | flops 104857600 | bytes 2097152 | tf_op jit(solution)/shard_map/select/pallas_call | solution.py:32
  12.0 1.5 %collective-permute-start = (bf16[16,16,512]{2,1,0:T(8,128)(2,1)S(1)}, bf16[16,16,512]{2,1,0:T(8,128)(2,1)S(1)}, u32[]{:S(2)}, u32[]{:S(2)}) collective-permute-start(bf16[16,16,512]{2,1,0:T(8,128)(2,1)S(1)} %get-tuple-element.74), channel_id=1, source_target_pairs={{0,2},{2,0},{1,3},{3,1},{4,6},{6,4},{5,7},{7,5},{8,10},{10,8},{9,1... | collective-permute-start | bytes 786440 | tf_op jit(solution)/shard_map/ppermute | solution.py:353
  13.6 0.3 collective-permute-start.6
  13.9 0.5 collective-permute-start.5
  14.4 1.3 %sums.1 = (f32[136,256]{1,0:T(8,128)S(1)}, f32[136,256]{1,0:T(8,128)S(1)}, f32[128,256]{1,0:T(8,128)S(1)}, f32[128,256]{1,0:T(8,128)S(1)}) custom-call(bf16[528,256]{1,0:T(8,128)(2,1)S(1)} %get-tuple-element.69.lead_ref, bf16[544,256]{1,0:T(8,128)(2,1)S(1)} %get-tuple-element.87.rest_ref, bf16[528,256]{1,0:T(8,128)(2,1)S(1)} %collective-permute-done.3.near_ref, ...), custom_call_target="tpu_custom_call" | custom-call | flops 104857600 | bytes 2097152 | tf_op jit(solution)/shard_map/sums/pallas_call | solution.py:32
  15.8 4.4 %collective-permute-done.refs_5_ = bf16[16,16,512]{2,1,0:T(8,128)(2,1)S(1)} collective-permute-done((bf16[16,16,512]{2,1,0:T(8,128)(2,1)S(1)}, bf16[16,16,512]{2,1,0:T(8,128)(2,1)S(1)}, u32[]{:S(2)}, u32[]{:S(2)}) %collective-permute-start) | collective-permute-done | bytes 262176 | tf_op jit(solution)/shard_map/ppermute | solution.py:353
  20.2 0.7 %collective-permute-done.1.refs_0_.lead_ref = bf16[528,256]{1,0:T(8,128)(2,1)S(1)} collective-permute-done((bf16[528,256]{1,0:T(8,128)(2,1)S(1)}, bf16[528,256]{1,0:T(8,128)(2,1)S(1)}, u32[]{:S(2)}, u32[]{:S(2)}) %collective-permute-start.1) | collective-permute-done | bytes 270368 | tf_op jit(solution)/shard_map/ppermute | solution.py:360
  20.9 1.1 %select_lead.2 = (bf16[512,512]{1,0:T(8,128)(2,1)S(1)}, bf16[512,512]{1,0:T(8,128)(2,1)S(1)}, bf16[2,16,16,256]{3,2,1,0:T(8,128)(2,1)S(1)}, bf16[2,16,16,256]{3,2,1,0:T(8,128)(2,1)S(1)}) custom-call(f32[256,1]{1,0:T(8,128)S(1)} %get-tuple-element.71.inv_ref, bf16[256,512]{1,0:T(8,128)(2,1)S(1)} %get-tuple-element.72.centre_ref, ...), custom_call_target="tpu_custom_call" | custom-call | tf_op jit(solution)/shard_map/select_lead/pallas_call | solution.py:32
  22.0 2.0 %collective-permute-start.4 = (bf16[2,16,16,256]{3,2,1,0:T(8,128)(2,1)S(1)}, bf16[2,16,16,256]{3,2,1,0:T(8,128)(2,1)S(1)}, u32[]{:S(2)}, u32[]{:S(2)}) collective-permute-start(bf16[2,16,16,256]{3,2,1,0:T(8,128)(2,1)S(1)} %get-tuple-element.84), channel_id=1, source_target_pairs={{0,2},{2,0},{1,3},{3,1},{4,6},{6,4},{5,7},{7,5},{8,10},{10,8},{9,1... | collective-permute-start | bytes 786440 | tf_op jit(solution)/shard_map/ppermute | solution.py:353
  23.9 0.5 collective-permute-start.9
  24.5 6.1 %collective-permute-done.5.refs_2_ = bf16[528,256]{1,0:T(8,128)(2,1)S(1)} collective-permute-done((bf16[528,256]{1,0:T(8,128)(2,1)S(1)}, bf16[528,256]{1,0:T(8,128)(2,1)S(1)}, u32[]{:S(2)}, u32[]{:S(2)}) %collective-permute-start.5) | collective-permute-done | bytes 270368 | tf_op jit(solution)/shard_map/ppermute | solution.py:360
  30.6 0.9 %collective-permute-done.6.refs_3_ = bf16[544,256]{1,0:T(8,128)(2,1)S(1)} collective-permute-done((bf16[544,256]{1,0:T(8,128)(2,1)S(1)}, bf16[544,256]{1,0:T(8,128)(2,1)S(1)}, u32[]{:S(2)}, u32[]{:S(2)}) %collective-permute-start.6) | collective-permute-done | bytes 278560 | tf_op jit(solution)/shard_map/ppermute | solution.py:360
  31.5 1.6 %collective-permute-start.8 = (bf16[528,256]{1,0:T(8,128)(2,1)S(1)}, bf16[528,256]{1,0:T(8,128)(2,1)S(1)}, u32[]{:S(2)}, u32[]{:S(2)}) collective-permute-start(bf16[528,256]{1,0:T(8,128)(2,1)S(1)} %collective-permute-done.2.refs_1_.lead_ref), channel_id=1, source_target_pairs={{0,4},{4,0},{8,12},{12,8},{1,5},{5,1},{9,13},{13,9},{2,6},{6,2},{1... | collective-permute-start | bytes 811016 | tf_op jit(solution)/shard_map/ppermute | solution.py:360
  33.1 0.4 select_rest.2
  33.5 1.6 %collective-permute-start.7 = (bf16[2,16,16,256]{3,2,1,0:T(8,128)(2,1)S(1)}, bf16[2,16,16,256]{3,2,1,0:T(8,128)(2,1)S(1)}, u32[]{:S(2)}, u32[]{:S(2)}) collective-permute-start(bf16[2,16,16,256]{3,2,1,0:T(8,128)(2,1)S(1)} %get-tuple-element.91), channel_id=1, source_target_pairs={{0,2},{2,0},{1,3},{3,1},{4,6},{6,4},{5,7},{7,5},{8,10},{10,8},{9,1... | collective-permute-start | bytes 786440 | tf_op jit(solution)/shard_map/ppermute | solution.py:353
  35.1 1.4 %sums_lead.3 = (bf16[256,512]{1,0:T(8,128)(2,1)S(1)}, f32[136,256]{1,0:T(8,128)S(1)}, f32[136,256]{1,0:T(8,128)S(1)}) custom-call(bf16[528,256]{1,0:T(8,128)(2,1)S(1)} %collective-permute-done.1.refs_0_.lead_ref, bf16[528,256]{1,0:T(8,128)(2,1)S(1)} %collective-permute-done.10.near_ref, ...), custom_call_target="tpu_custom_call", output_to_operand_aliasing={{1}: (4, {}), {2}: (5, {})} | custom-call | tf_op jit(solution)/shard_map/sums_lead/pallas_call | solution.py:32
  36.5 1.4 %sums_lead.4 = (bf16[256,512]{1,0:T(8,128)(2,1)S(1)}, f32[136,256]{1,0:T(8,128)S(1)}, f32[136,256]{1,0:T(8,128)S(1)}) custom-call(bf16[528,256]{1,0:T(8,128)(2,1)S(1)} %collective-permute-done.2.refs_1_.lead_ref, bf16[528,256]{1,0:T(8,128)(2,1)S(1)} %collective-permute-done.9.near_ref, ...), custom_call_target="tpu_custom_call", output_to_operand_aliasing={{1}: (4, {}), {2}: (5, {})} | custom-call | tf_op jit(solution)/shard_map/sums_lead/pallas_call | solution.py:32
  37.9 0.3 sums_rest.2
  38.2 0.6 %collective-permute-start.12 = (bf16[544,256]{1,0:T(8,128)(2,1)S(1)}, bf16[544,256]{1,0:T(8,128)(2,1)S(1)}, u32[]{:S(2)}, u32[]{:S(2)}) collective-permute-start(bf16[544,256]{1,0:T(8,128)(2,1)S(1)} %collective-permute-done.6.refs_3_), channel_id=1, source_target_pairs={{0,4},{4,0},{8,12},{12,8},{1,5},{5,1},{9,13},{13,9},{2,6},{6,2},{1... | collective-permute-start | bytes 835592 | tf_op jit(solution)/shard_map/ppermute | solution.py:360
  38.8 0.9 %collective-permute-done.8.refs_0_.lead_ref = bf16[528,256]{1,0:T(8,128)(2,1)S(1)} collective-permute-done((bf16[528,256]{1,0:T(8,128)(2,1)S(1)}, bf16[528,256]{1,0:T(8,128)(2,1)S(1)}, u32[]{:S(2)}, u32[]{:S(2)}) %collective-permute-start.8) | collective-permute-done | bytes 270368 | tf_op jit(solution)/shard_map/ppermute | solution.py:360
  39.7 0.1 collective-permute-start.14
  39.8 0.5 collective-permute-start.13
  40.3 0.6 %select_lead.3 = (bf16[512,512]{1,0:T(8,128)(2,1)S(1)}, bf16[1,16,16,256]{3,2,1,0:T(8,128)(2,1)S(1)}, bf16[1,16,16,256]{3,2,1,0:T(8,128)(2,1)S(1)}) custom-call(f32[256,1]{1,0:T(8,128)S(1)} %get-tuple-element.71.inv_ref, bf16[256,512]{1,0:T(8,128)(2,1)S(1)} %get-tuple-element.72.centre_ref, bf16[528,256]{1,0:T(8,128)(2,1)S(1)} %collective-permute-done.8.refs_0_.lead_ref), custom_call_target="tpu_custom_call" | custom-call | tf_op jit(solution)/shard_map/select_lead/pallas_call | solution.py:32
  40.9 0.3 collective-permute-done.7.refs_7_
  41.2 1.7 %collective-permute-start.11 = (bf16[1,16,16,256]{3,2,1,0:T(8,128)(2,1)S(1)}, bf16[1,16,16,256]{3,2,1,0:T(8,128)(2,1)S(1)}, u32[]{:S(2)}, u32[]{:S(2)}) collective-permute-start(bf16[1,16,16,256]{3,2,1,0:T(8,128)(2,1)S(1)} %get-tuple-element.105), channel_id=1, source_target_pairs={{0,2},{2,0},{1,3},{3,1},{4,6},{6,4},{5,7},{7,5},{8,10},{10,8},{9,1... | collective-permute-start | bytes 393224 | tf_op jit(solution)/shard_map/ppermute | solution.py:353
  42.9 1.4 %sums_lead.5 = (bf16[256,512]{1,0:T(8,128)(2,1)S(1)}, f32[136,256]{1,0:T(8,128)S(1)}, bf16[144,256]{1,0:T(8,128)(2,1)S(1)}) custom-call(bf16[528,256]{1,0:T(8,128)(2,1)S(1)} %collective-permute-done.8.refs_0_.lead_ref, bf16[256,256]{1,0:T(8,128)(2,1)S(1)} %collective-permute-done.13.low_ref, ...), custom_call_target="tpu_custom_call", output_to_operand_aliasing={{1}: (5, {})} | custom-call | tf_op jit(solution)/shard_map/sums_lead/pallas_call | solution.py:32
  44.2 0.4 collective-permute-start.15
  44.7 1.3 %collective-permute-done.12.refs_1_ = bf16[544,256]{1,0:T(8,128)(2,1)S(1)} collective-permute-done((bf16[544,256]{1,0:T(8,128)(2,1)S(1)}, bf16[544,256]{1,0:T(8,128)(2,1)S(1)}, u32[]{:S(2)}, u32[]{:S(2)}) %collective-permute-start.12) | collective-permute-done | bytes 278560 | tf_op jit(solution)/shard_map/ppermute | solution.py:360
  45.9 0.3 select_rest.3
  46.2 0.4 collective-permute-done.11.refs_8_
  46.6 2.1 %collective-permute-done.15.refs_5_ = bf16[144,256]{1,0:T(8,128)(2,1)S(1)} collective-permute-done((bf16[144,256]{1,0:T(8,128)(2,1)S(1)}, bf16[144,256]{1,0:T(8,128)(2,1)S(1)}, u32[]{:S(2)}, u32[]{:S(2)}) %collective-permute-start.15) | collective-permute-done | bytes 73760 | tf_op jit(solution)/shard_map/ppermute | solution.py:353
  48.7 1.3 %collective-permute-start.16 = (bf16[1,16,16,256]{3,2,1,0:T(8,128)(2,1)S(1)}, bf16[1,16,16,256]{3,2,1,0:T(8,128)(2,1)S(1)}, u32[]{:S(2)}, u32[]{:S(2)}) collective-permute-start(bf16[1,16,16,256]{3,2,1,0:T(8,128)(2,1)S(1)} %get-tuple-element.116), channel_id=1, source_target_pairs={{0,2},{2,0},{1,3},{3,1},{4,6},{6,4},{5,7},{7,5},{8,10},{10,8},{9,1... | collective-permute-start | bytes 393224 | tf_op jit(solution)/shard_map/ppermute | solution.py:353
  49.9 0.2 sums_rest.3
  50.2 0.8 %collective-permute-start.19 = (bf16[144,256]{1,0:T(8,128)(2,1)S(1)}, bf16[144,256]{1,0:T(8,128)(2,1)S(1)}, u32[]{:S(2)}, u32[]{:S(2)}) collective-permute-start(bf16[144,256]{1,0:T(8,128)(2,1)S(1)} %get-tuple-element.120), channel_id=1, source_target_pairs={{0,2},{2,0},{1,3},{3,1},{4,6},{6,4},{5,7},{7,5},{8,10},{10,8},{9,1... | collective-permute-start | bytes 221192 | tf_op jit(solution)/shard_map/ppermute | solution.py:353
  51.0 3.1 %collective-permute-done.16.refs_9_ = bf16[1,16,16,256]{3,2,1,0:T(8,128)(2,1)S(1)} collective-permute-done((bf16[1,16,16,256]{3,2,1,0:T(8,128)(2,1)S(1)}, bf16[1,16,16,256]{3,2,1,0:T(8,128)(2,1)S(1)}, u32[]{:S(2)}, u32[]{:S(2)}) %collective-permute-start.16) | collective-permute-done | bytes 131104 | tf_op jit(solution)/shard_map/ppermute | solution.py:353
  54.1 0.9 %gram.1 = (f32[8,16,128]{2,1,0:T(8,128)S(1)}, f32[8,16,128]{2,1,0:T(8,128)S(1)}) custom-call(bf16[16,16,512]{2,1,0:T(8,128)(2,1)S(1)} %get-tuple-element.121.refs_0_, bf16[2,16,16,256]{3,2,1,0:T(8,128)(2,1)S(1)} %get-tuple-element.122.refs_1_, bf16[2,16,16,256]{3,2,1,0:T(8,128)(2,1)S(1)} %get-tuple-element.123.refs_2_, ...), custom_call_target="tpu_custom_call" | custom-call | tf_op jit(solution)/shard_map/gram/pallas_call | solution.py:32
  55.1 0.5 collective-permute-start.18
  55.6 0.7 %collective-permute-done.17.refs_2_ = f32[8,16,128]{2,1,0:T(8,128)S(1)} collective-permute-done((f32[8,16,128]{2,1,0:T(8,128)S(1)}, f32[8,16,128]{2,1,0:T(8,128)S(1)}, u32[]{:S(2)}, u32[]{:S(2)}) %collective-permute-start.17) | collective-permute-done | bytes 65568 | tf_op jit(solution)/shard_map/ppermute | solution.py:357
  56.3 0.2 collective-permute-done.18.refs_3_
  56.5 1.4 %finish.1 = (f32[128,512]{1,0:T(8,128)}, bf16[8,16,128]{2,1,0:T(8,128)(2,1)}) custom-call(f32[8,16,128]{2,1,0:T(8,128)S(1)} %get-tuple-element.131.refs_0_, f32[8,16,128]{2,1,0:T(8,128)S(1)} %get-tuple-element.132.refs_1_, f32[8,16,128]{2,1,0:T(8,128)S(1)} %collective-permute-done.17.refs_2_, f32[8,16,128]{2,1,0:T(8,128)S(1)} %collective-permute-done.18.refs_3_, ...), custom_call_target="tpu_custom_call" | custom-call | tf_op jit(solution)/shard_map/finish/pallas_call | solution.py:32
  (17 shorter events, 0.2 us)
Async XLA Ops:
  0.6 1.0 %copy-start.1 = (bf16[512,512]{1,0:T(8,128)(2,1)S(1)}, bf16[512,512]{1,0:T(8,128)(2,1)}, u32[]{:S(2)}) copy-start(bf16[512,512]{1,0:T(8,128)(2,1)} %emb_ref.1) | copy-start | bytes 1572868
  1.7 0.7 %copy-start.3 = (s32[512,1]{0,1:T(1,128)S(1)}, s32[512,1]{0,1:T(1,128)}, u32[]{:S(2)}) copy-start(s32[512,1]{0,1:T(1,128)} %param.6) | copy-start | bytes 6148
  2.4 11.5 %collective-permute-start.3 = (bf16[528,256]{1,0:T(8,128)(2,1)S(1)}, bf16[528,256]{1,0:T(8,128)(2,1)S(1)}, u32[]{:S(2)}, u32[]{:S(2)}) collective-permute-start(bf16[528,256]{1,0:T(8,128)(2,1)S(1)} %get-tuple-element.69.lead_ref), channel_id=1, source_target_pairs={{0,1},{1,0},{2,3},{3,2},{4,5},{5,4},{6,7},{7,6},{8,9},{9,8},{10,11... | collective-permute-start | bytes 811016 | tf_op jit(solution)/shard_map/ppermute | solution.py:357
  2.9 17.3 %collective-permute-start.2 = (bf16[528,256]{1,0:T(8,128)(2,1)S(1)}, bf16[528,256]{1,0:T(8,128)(2,1)S(1)}, u32[]{:S(2)}, u32[]{:S(2)}) collective-permute-start(bf16[528,256]{1,0:T(8,128)(2,1)S(1)} %get-tuple-element.69.lead_ref), channel_id=1, source_target_pairs={{0,8},{4,12},{8,0},{12,4},{1,9},{5,13},{9,1},{13,5},{2,10},{6,14},... | collective-permute-start | bytes 811016 | tf_op jit(solution)/shard_map/ppermute | solution.py:360
  6.6 14.3 %collective-permute-start.1 = (bf16[528,256]{1,0:T(8,128)(2,1)S(1)}, bf16[528,256]{1,0:T(8,128)(2,1)S(1)}, u32[]{:S(2)}, u32[]{:S(2)}) collective-permute-start(bf16[528,256]{1,0:T(8,128)(2,1)S(1)} %get-tuple-element.69.lead_ref), channel_id=1, source_target_pairs={{0,4},{4,0},{8,12},{12,8},{1,5},{5,1},{9,13},{13,9},{2,6},{6,2},{1... | collective-permute-start | bytes 811016 | tf_op jit(solution)/shard_map/ppermute | solution.py:360
  8.2 1.6 %copy-start = (bf16[1024,1024]{1,0:T(8,128)(2,1)S(1)}, bf16[1024,1024]{1,0:T(8,128)(2,1)}, u32[]{:S(2)}) copy-start(bf16[1024,1024]{1,0:T(8,128)(2,1)} %cent_ref.1) | copy-start | bytes 6291460
  9.8 0.7 %copy-start.2 = (s32[1024]{0:T(1024)S(1)}, s32[1024]{0:T(1024)}, u32[]{:S(2)}) copy-start(s32[1024]{0:T(1024)} %param.7) | copy-start | bytes 12292
  12.0 8.1 %collective-permute-start = (bf16[16,16,512]{2,1,0:T(8,128)(2,1)S(1)}, bf16[16,16,512]{2,1,0:T(8,128)(2,1)S(1)}, u32[]{:S(2)}, u32[]{:S(2)}) collective-permute-start(bf16[16,16,512]{2,1,0:T(8,128)(2,1)S(1)} %get-tuple-element.74), channel_id=1, source_target_pairs={{0,2},{2,0},{1,3},{3,1},{4,6},{6,4},{5,7},{7,5},{8,10},{10,8},{9,1... | collective-permute-start | bytes 786440 | tf_op jit(solution)/shard_map/ppermute | solution.py:353
  13.6 17.9 %collective-permute-start.6 = (bf16[544,256]{1,0:T(8,128)(2,1)S(1)}, bf16[544,256]{1,0:T(8,128)(2,1)S(1)}, u32[]{:S(2)}, u32[]{:S(2)}) collective-permute-start(bf16[544,256]{1,0:T(8,128)(2,1)S(1)} %get-tuple-element.87.rest_ref), channel_id=1, source_target_pairs={{0,8},{4,12},{8,0},{12,4},{1,9},{5,13},{9,1},{13,5},{2,10},{6,14},... | collective-permute-start | bytes 835592 | tf_op jit(solution)/shard_map/ppermute | solution.py:360
  13.9 16.6 %collective-permute-start.5 = (bf16[528,256]{1,0:T(8,128)(2,1)S(1)}, bf16[528,256]{1,0:T(8,128)(2,1)S(1)}, u32[]{:S(2)}, u32[]{:S(2)}) collective-permute-start(bf16[528,256]{1,0:T(8,128)(2,1)S(1)} %slice.9), channel_id=1, source_target_pairs={{0,4},{4,0},{8,12},{12,8},{1,5},{5,1},{9,13},{13,9},{2,6},{6,2},{1... | collective-permute-start | bytes 811016 | tf_op jit(solution)/shard_map/ppermute | solution.py:360
  22.0 9.5 %collective-permute-start.4 = (bf16[2,16,16,256]{3,2,1,0:T(8,128)(2,1)S(1)}, bf16[2,16,16,256]{3,2,1,0:T(8,128)(2,1)S(1)}, u32[]{:S(2)}, u32[]{:S(2)}) collective-permute-start(bf16[2,16,16,256]{3,2,1,0:T(8,128)(2,1)S(1)} %get-tuple-element.84), channel_id=1, source_target_pairs={{0,2},{2,0},{1,3},{3,1},{4,6},{6,4},{5,7},{7,5},{8,10},{10,8},{9,1... | collective-permute-start | bytes 786440 | tf_op jit(solution)/shard_map/ppermute | solution.py:353
  23.9 11.1 %collective-permute-start.10 = (bf16[528,256]{1,0:T(8,128)(2,1)S(1)}, bf16[528,256]{1,0:T(8,128)(2,1)S(1)}, u32[]{:S(2)}, u32[]{:S(2)}) collective-permute-start(bf16[528,256]{1,0:T(8,128)(2,1)S(1)} %collective-permute-done.1.refs_0_.lead_ref), channel_id=1, source_target_pairs={{0,1},{1,0},{2,3},{3,2},{4,5},{5,4},{6,7},{7,6},{8,9},{9,8},{10,11... | collective-permute-start | bytes 811016 | tf_op jit(solution)/shard_map/ppermute | solution.py:357
  23.9 12.5 %collective-permute-start.9 = (bf16[528,256]{1,0:T(8,128)(2,1)S(1)}, bf16[528,256]{1,0:T(8,128)(2,1)S(1)}, u32[]{:S(2)}, u32[]{:S(2)}) collective-permute-start(bf16[528,256]{1,0:T(8,128)(2,1)S(1)} %collective-permute-done.2.refs_1_.lead_ref), channel_id=1, source_target_pairs={{0,1},{1,0},{2,3},{3,2},{4,5},{5,4},{6,7},{7,6},{8,9},{9,8},{10,11... | collective-permute-start | bytes 811016 | tf_op jit(solution)/shard_map/ppermute | solution.py:357
  31.5 8.2 %collective-permute-start.8 = (bf16[528,256]{1,0:T(8,128)(2,1)S(1)}, bf16[528,256]{1,0:T(8,128)(2,1)S(1)}, u32[]{:S(2)}, u32[]{:S(2)}) collective-permute-start(bf16[528,256]{1,0:T(8,128)(2,1)S(1)} %collective-permute-done.2.refs_1_.lead_ref), channel_id=1, source_target_pairs={{0,4},{4,0},{8,12},{12,8},{1,5},{5,1},{9,13},{13,9},{2,6},{6,2},{1... | collective-permute-start | bytes 811016 | tf_op jit(solution)/shard_map/ppermute | solution.py:360
  33.5 7.7 %collective-permute-start.7 = (bf16[2,16,16,256]{3,2,1,0:T(8,128)(2,1)S(1)}, bf16[2,16,16,256]{3,2,1,0:T(8,128)(2,1)S(1)}, u32[]{:S(2)}, u32[]{:S(2)}) collective-permute-start(bf16[2,16,16,256]{3,2,1,0:T(8,128)(2,1)S(1)} %get-tuple-element.91), channel_id=1, source_target_pairs={{0,2},{2,0},{1,3},{3,1},{4,6},{6,4},{5,7},{7,5},{8,10},{10,8},{9,1... | collective-permute-start | bytes 786440 | tf_op jit(solution)/shard_map/ppermute | solution.py:353
  38.2 7.7 %collective-permute-start.12 = (bf16[544,256]{1,0:T(8,128)(2,1)S(1)}, bf16[544,256]{1,0:T(8,128)(2,1)S(1)}, u32[]{:S(2)}, u32[]{:S(2)}) collective-permute-start(bf16[544,256]{1,0:T(8,128)(2,1)S(1)} %collective-permute-done.6.refs_3_), channel_id=1, source_target_pairs={{0,4},{4,0},{8,12},{12,8},{1,5},{5,1},{9,13},{13,9},{2,6},{6,2},{1... | collective-permute-start | bytes 835592 | tf_op jit(solution)/shard_map/ppermute | solution.py:360
  39.7 3.1 %collective-permute-start.14 = (bf16[256,256]{1,0:T(8,128)(2,1)S(1)}, bf16[256,256]{1,0:T(8,128)(2,1)S(1)}, u32[]{:S(2)}, u32[]{:S(2)}) collective-permute-start(bf16[256,256]{1,0:T(8,128)(2,1)S(1)} %get-tuple-element.136), channel_id=1, source_target_pairs={{0,1},{1,0},{2,3},{3,2},{4,5},{5,4},{6,7},{7,6},{8,9},{9,8},{10,11... | collective-permute-start | bytes 393224 | tf_op jit(solution)/shard_map/ppermute | solution.py:357
  39.8 3.1 %collective-permute-start.13 = (bf16[256,256]{1,0:T(8,128)(2,1)S(1)}, bf16[256,256]{1,0:T(8,128)(2,1)S(1)}, u32[]{:S(2)}, u32[]{:S(2)}) collective-permute-start(bf16[256,256]{1,0:T(8,128)(2,1)S(1)} %get-tuple-element.137), channel_id=1, source_target_pairs={{0,1},{1,0},{2,3},{3,2},{4,5},{5,4},{6,7},{7,6},{8,9},{9,8},{10,11... | collective-permute-start | bytes 393224 | tf_op jit(solution)/shard_map/ppermute | solution.py:357
  41.2 5.4 %collective-permute-start.11 = (bf16[1,16,16,256]{3,2,1,0:T(8,128)(2,1)S(1)}, bf16[1,16,16,256]{3,2,1,0:T(8,128)(2,1)S(1)}, u32[]{:S(2)}, u32[]{:S(2)}) collective-permute-start(bf16[1,16,16,256]{3,2,1,0:T(8,128)(2,1)S(1)} %get-tuple-element.105), channel_id=1, source_target_pairs={{0,2},{2,0},{1,3},{3,1},{4,6},{6,4},{5,7},{7,5},{8,10},{10,8},{9,1... | collective-permute-start | bytes 393224 | tf_op jit(solution)/shard_map/ppermute | solution.py:353
  44.2 4.4 %collective-permute-start.15 = (bf16[144,256]{1,0:T(8,128)(2,1)S(1)}, bf16[144,256]{1,0:T(8,128)(2,1)S(1)}, u32[]{:S(2)}, u32[]{:S(2)}) collective-permute-start(bf16[144,256]{1,0:T(8,128)(2,1)S(1)} %get-tuple-element.114), channel_id=1, source_target_pairs={{0,2},{2,0},{1,3},{3,1},{4,6},{6,4},{5,7},{7,5},{8,10},{10,8},{9,1... | collective-permute-start | bytes 221192 | tf_op jit(solution)/shard_map/ppermute | solution.py:353
  48.7 5.5 %collective-permute-start.16 = (bf16[1,16,16,256]{3,2,1,0:T(8,128)(2,1)S(1)}, bf16[1,16,16,256]{3,2,1,0:T(8,128)(2,1)S(1)}, u32[]{:S(2)}, u32[]{:S(2)}) collective-permute-start(bf16[1,16,16,256]{3,2,1,0:T(8,128)(2,1)S(1)} %get-tuple-element.116), channel_id=1, source_target_pairs={{0,2},{2,0},{1,3},{3,1},{4,6},{6,4},{5,7},{7,5},{8,10},{10,8},{9,1... | collective-permute-start | bytes 393224 | tf_op jit(solution)/shard_map/ppermute | solution.py:353
  50.2 5.4 %collective-permute-start.19 = (bf16[144,256]{1,0:T(8,128)(2,1)S(1)}, bf16[144,256]{1,0:T(8,128)(2,1)S(1)}, u32[]{:S(2)}, u32[]{:S(2)}) collective-permute-start(bf16[144,256]{1,0:T(8,128)(2,1)S(1)} %get-tuple-element.120), channel_id=1, source_target_pairs={{0,2},{2,0},{1,3},{3,1},{4,6},{6,4},{5,7},{7,5},{8,10},{10,8},{9,1... | collective-permute-start | bytes 221192 | tf_op jit(solution)/shard_map/ppermute | solution.py:353
  55.0 1.3 %collective-permute-start.17 = (f32[8,16,128]{2,1,0:T(8,128)S(1)}, f32[8,16,128]{2,1,0:T(8,128)S(1)}, u32[]{:S(2)}, u32[]{:S(2)}) collective-permute-start(f32[8,16,128]{2,1,0:T(8,128)S(1)} %get-tuple-element.131.refs_0_), channel_id=1, source_target_pairs={{0,1},{1,0},{2,3},{3,2},{4,5},{5,4},{6,7},{7,6},{8,9},{9,8},{10,11... | collective-permute-start | bytes 196616 | tf_op jit(solution)/shard_map/ppermute | solution.py:357
  55.1 1.4 %collective-permute-start.18 = (f32[8,16,128]{2,1,0:T(8,128)S(1)}, f32[8,16,128]{2,1,0:T(8,128)S(1)}, u32[]{:S(2)}, u32[]{:S(2)}) collective-permute-start(f32[8,16,128]{2,1,0:T(8,128)S(1)} %get-tuple-element.132.refs_1_), channel_id=1, source_target_pairs={{0,1},{1,0},{2,3},{3,2},{4,5},{5,4},{6,7},{7,6},{8,9},{9,8},{10,11... | collective-permute-start | bytes 196616 | tf_op jit(solution)/shard_map/ppermute | solution.py:357

commit v14 on v13

--- a/solution.py
+++ b/solution.py
@@ -209,16 +209,24 @@
     add_lead(weights, lead_ref, old, new)
 
 
-def last_sums_lead_kernel(subs, lead_ref, low_ref, high_ref, cent_ref, own_prefix_ref, *refs):
-    old, weights_ref, new, totals = refs[:subs], refs[subs], refs[subs + 1 : 2 * subs + 1], refs[2 * subs + 1 :]
+def last_lead_kernel(subs, lead_ref, low_ref, high_ref, cent_ref, own_prefix_ref, inv_ref, centre_ref, *refs):
+    old, new, totals = refs[:subs], refs[subs : 2 * subs + 3], refs[2 * subs + 3 :]
+    weights_ref, pick_ref, sums_ref, rows_ref, *sent_refs = new
+    docs = lead_ref.shape[0] - META
+    pick = picked(lead_ref, inv_ref)
+    pick_ref[...] = pick
+    rows = centred(pick, centre_ref[:, :PREFIX], lead_ref[:docs, :])
+    slots = rows.shape[0] // subs
+    rows_ref[0] = rows[:slots].reshape(rows_ref.shape[1:])
     weights = soft_weights(lead_ref, [low_ref, high_ref], cent_ref, own_prefix_ref)
     weights_ref[...] = weights.astype(BF16)
-    add_lead(weights, lead_ref, old, new[:1] + totals)
-    for sent, total in zip(new[1:], totals):
+    add_lead(weights, lead_ref, old, (sums_ref,) + tuple(totals))
+    for t, (sent, total) in enumerate(zip(sent_refs, totals), 1):
         whole = total[...]
         mass = whole[-SUBLANES:]
         high = mass.astype(BF16).astype(F32)
-        sent[...] = jnp.concatenate([whole[:-SUBLANES], high, mass - high], axis=0).astype(BF16)
+        sent[:slots, :] = rows[t * slots : (t + 1) * slots]
+        sent[slots:, :] = jnp.concatenate([whole[:-SUBLANES], high, mass - high], axis=0).astype(BF16)
 
 
 def sums_rest_kernel(count, subs, *refs):
@@ -243,7 +251,10 @@
         for k, group in enumerate(groups_of_bits):
             for i, bits in enumerate(group):
                 row = (z ^ bits) * subs + column
-                held[row, :, :, :PREFIX] = chunks[2 * k][i]
+                lead = chunks[2 * k]
+                held[row, :, :, :PREFIX] = lead[i] if len(lead.shape) == 4 else lead[: groups * packed, :].reshape(
+                    groups, packed, PREFIX
+                )
                 held[row, :, :, PREFIX:] = chunks[2 * k + 1][i]
 
     size = owners * packed
@@ -296,7 +307,7 @@
     per = prior_ref.shape[0]
     lead, mass = lead_refs[0][:per, :], lead_refs[0][per:, :]
     for ref in lead_refs[1:]:
-        sent = ref[...].astype(F32)
+        sent = ref[...].astype(F32)[-per - 2 * SUBLANES :]
         lead = lead + sent[:per]
         mass = mass + sent[per : per + SUBLANES] + sent[per + SUBLANES :]
     rest = rest_refs[0][...]
@@ -390,7 +401,7 @@
     )
 
     lead_sum, rest_sum = shape((per + SUBLANES, PREFIX), F32), shape((per, half - PREFIX), F32)
-    sent_lead, sent_rest = shape((per + 2 * SUBLANES, PREFIX), BF16), shape((per + 2 * SUBLANES, half - PREFIX), BF16)
+    sent_rest = shape((per + 2 * SUBLANES, half - PREFIX), BF16)
     sum_shapes = [lead_sum] * subs + [rest_sum] * subs
     own_cost = 2 * 1024 * 1024
 
@@ -418,38 +429,40 @@
         if last:
             lead = leads[group[0]]
             halves = [near(lead[: docs // 2]), near(lead[docs // 2 : docs])]
-        row_shapes = [shape((count, groups, packed, PREFIX), BF16)] * subs
-        found = call(
-            functools.partial(select_lead_kernel, count, subs),
-            "select_lead",
-            [shape((subs * per * MOST, docs), BF16)] * count + row_shapes,
-            [inv, centre] + [leads[bits] for bits in group],
-        )
-        picks, found = list(found[:count]), list(found[count:])
-        weights = []
+        row_shape = shape((count, groups, packed, PREFIX), BF16)
+        pick_shapes = [shape((subs * per * MOST, docs), BF16)] * count
+        weight_shape = shape((subs * per, docs), BF16)
         if last:
-            found = tied(found, members)
-            weight, *lead_sums = call(
-                functools.partial(last_sums_lead_kernel, subs),
-                "sums_lead",
-                [shape((subs * per, docs), BF16), lead_sum] + [sent_lead] * (subs - 1),
-                [tied(lead, picks)] + halves + [cent_prefix, own_prefix] + lead_sums,
-                {5: 1},
+            sent_lead = shape((groups * packed + per + 2 * SUBLANES, PREFIX), BF16)
+            weight, pick, own_sums, *found = call(
+                functools.partial(last_lead_kernel, subs),
+                "last_lead",
+                [weight_shape] + pick_shapes + [lead_sum, row_shape] + [sent_lead] * (subs - 1),
+                [lead] + halves + [cent_prefix, own_prefix, inv, centre] + lead_sums,
+                {7: 2},
                 scratch=[pltpu.VMEM(lead_sum.shape, F32)] * (subs - 1),
             )
-            weights.append(weight)
-            members.append(across(found))
-            lead_sums = across(lead_sums)
+            weights, picks = [weight], [pick]
+            members.append(across(tied(found, members)))
+            lead_sums = [own_sums] + members[-1][1:]
             before = (found, weights)
         else:
+            found = call(
+                functools.partial(select_lead_kernel, count, subs),
+                "select_lead",
+                pick_shapes + [row_shape] * subs,
+                [inv, centre] + [leads[bits] for bits in group],
+            )
+            picks, found = list(found[:count]), list(found[count:])
             members.append(across(found))
             before = (found, members)
+            weights = []
             for bits in group:
                 prefix = near(leads[bits])
                 weight, *lead_sums = call(
                     functools.partial(sums_lead_kernel, subs),
                     "sums_lead",
-                    [shape((subs * per, docs), BF16)] + [lead_sum] * subs,
+                    [weight_shape] + [lead_sum] * subs,
                     [leads[bits], prefix, cent_prefix, own_prefix] + lead_sums,
                     {4 + i: 1 + i for i in range(subs)},
                 )
@@ -464,8 +477,6 @@
             row_shapes,
             [centre] + picks + [rests[bits] for bits in group],
         )
-        if last:
-            found = tied(found, lead_sums, members)
         members.append(across(found))
         if last:
             rest_sums = tied(rest_sums, members[:-1])

time: 58.1 us -> 57.7 us (level)
  waiting for transfers between devices: 21.1 us -> 19.8 us
  starting transfers between devices: 19.6 us -> 20.6 us
    ppermute x7 -> x6, waiting for transfers between devices: 10.2 us -> 8.15 us  [across(): lax.ppermute(values[t], 'sub', [(i, (i + t) % subs) for i in range(subs)])]
    ppermute x7, waiting for transfers between devices: 0.91 us -> 1.93 us  [near(): return lax.ppermute(value, 'dim', [(0, 1), (1, 0)])]
    ppermute x7 -> x6, starting transfers between devices: 9.23 us -> 10.2 us  [across(): lax.ppermute(values[t], 'sub', [(i, (i + t) % subs) for i in range(subs)])]
    pallas_call x15 -> x14, Pallas kernels: 12.3 us -> 11.9 us  [call(): pl.pallas_call(kernel, out_shape=tuple(out_shape), in_specs=[whole(operan...]
  transfers between devices with their start and end apart: 20 -> 19, of which waited for: 12 -> 12; matrix products, arithmetic and copies ran while one was open for 0% -> 0% of each run, Pallas kernels for 19% -> 18%
where the time goes in v14:
time: 57.7 us; the launch traced here: 57.1 us
  starting transfers between devices  20.6 us (36%)
  waiting for transfers between devices  19.8 us (34%)
  Pallas kernels  11.9 us (21%)
  local copies, waits for them, and re-layouts  4.03 us (7%)
  between operations  0.78 us (1%)
    pallas_call x14, Pallas kernels, call(): pl.pallas_call(kernel, out_shape=tuple(out_shape), in_specs=[whole(operan...  11.9 us
    ppermute x6, starting transfers between devices, across(): lax.ppermute(values[t], 'sub', [(i, (i + t) % subs) for i in range(subs)])  10.2 us
    ppermute x6, waiting for transfers between devices, swap(): return lax.ppermute(value, 'rows', [(i, i ^ bit) for i in range(rows)])  9.74 us
    ppermute x6, starting transfers between devices, swap(): return lax.ppermute(value, 'rows', [(i, i ^ bit) for i in range(rows)])  8.23 us
    ppermute x6, waiting for transfers between devices, across(): lax.ppermute(values[t], 'sub', [(i, (i + t) % subs) for i in range(subs)])  8.15 us
    unnamed x8, local copies, waits for them, and re-layouts  3.99 us
    ppermute x7, starting transfers between devices, near(): return lax.ppermute(value, 'dim', [(0, 1), (1, 0)])  2.16 us
    ppermute x7, waiting for transfers between devices, near(): return lax.ppermute(value, 'dim', [(0, 1), (1, 0)])  1.93 us
  transfers between devices with their start and end apart: 19, of which 12 were waited for; matrix products, arithmetic and copies ran while one was open for 0% of the time, Pallas kernels for 18%

profile of v14, /device:TPU:0, one launch (start us, length us, event | category | flops | bytes accessed | tf_op | source)
XLA Modules:
  0.0 57.1 jit_solution(14485936813145448231)
XLA Ops:
  0.6 1.0 %copy-done.1 = bf16[512,512]{1,0:T(8,128)(2,1)S(1)} copy-done((bf16[512,512]{1,0:T(8,128)(2,1)S(1)}, bf16[512,512]{1,0:T(8,128)(2,1)}, u32[]{:S(2)}) %copy-start.1) | copy-done | bytes 524312
  1.7 0.7 %copy-done.3 = s32[512,1]{0,1:T(1,128)S(1)} copy-done((s32[512,1]{0,1:T(1,128)S(1)}, s32[512,1]{0,1:T(1,128)}, u32[]{:S(2)}) %copy-start.3) | copy-done | bytes 2072
  2.4 0.5 collective-permute-start.3
  2.9 3.7 %collective-permute-start.2 = (bf16[528,256]{1,0:T(8,128)(2,1)S(1)}, bf16[528,256]{1,0:T(8,128)(2,1)S(1)}, u32[]{:S(2)}, u32[]{:S(2)}) collective-permute-start(bf16[528,256]{1,0:T(8,128)(2,1)S(1)} %get-tuple-element.65.lead_ref), channel_id=1, source_target_pairs={{0,8},{4,12},{8,0},{12,4},{1,9},{5,13},{9,1},{13,5},{2,10},{6,14},... | collective-permute-start | bytes 811016 | tf_op jit(solution)/shard_map/ppermute | solution.py:371
  6.6 1.6 %collective-permute-start.1 = (bf16[528,256]{1,0:T(8,128)(2,1)S(1)}, bf16[528,256]{1,0:T(8,128)(2,1)S(1)}, u32[]{:S(2)}, u32[]{:S(2)}) collective-permute-start(bf16[528,256]{1,0:T(8,128)(2,1)S(1)} %get-tuple-element.65.lead_ref), channel_id=1, source_target_pairs={{0,4},{4,0},{8,12},{12,8},{1,5},{5,1},{9,13},{13,9},{2,6},{6,2},{1... | collective-permute-start | bytes 811016 | tf_op jit(solution)/shard_map/ppermute | solution.py:371
  8.2 1.6 %copy-done = bf16[1024,1024]{1,0:T(8,128)(2,1)S(1)} copy-done((bf16[1024,1024]{1,0:T(8,128)(2,1)S(1)}, bf16[1024,1024]{1,0:T(8,128)(2,1)}, u32[]{:S(2)}) %copy-start) | copy-done | bytes 2097176
  9.8 0.7 %copy-done.2 = s32[1024]{0:T(1024)S(1)} copy-done((s32[1024]{0:T(1024)S(1)}, s32[1024]{0:T(1024)}, u32[]{:S(2)}) %copy-start.2) | copy-done | bytes 4120
  10.4 0.8 %prep.1 = (f32[256,1]{1,0:T(8,128)S(1)}, bf16[256,512]{1,0:T(8,128)(2,1)S(1)}, bf16[256,256]{1,0:T(8,128)(2,1)S(1)}, bf16[128,512]{1,0:T(8,128)(2,1)S(1)}, bf16[1024,256]{1,0:T(8,128)(2,1)S(1)}) custom-call(s32[1,1024]{1,0:T(1,128)S(1)} %bitcast.3, bf16[1024,1024]{1,0:T(8,128)(2,1)S(1)} %copy-done), custom_call_target="tpu_custom_call" | custom-call | flops 209715200 | bytes 4194304 | tf_op jit(solution)/shard_map/prep/pallas_call | solution.py:32
  11.3 0.7 %select.1 = (bf16[16,16,512]{2,1,0:T(8,128)(2,1)S(1)}, bf16[16,16,512]{2,1,0:T(8,128)(2,1)S(1)}) custom-call(bf16[528,256]{1,0:T(8,128)(2,1)S(1)} %get-tuple-element.65.lead_ref, bf16[544,256]{1,0:T(8,128)(2,1)S(1)} %get-tuple-element.83.rest_ref, f32[256,1]{1,0:T(8,128)S(1)} %get-tuple-element.67.inv_ref, bf16[256,512]{1,0:T(8,128)(2,1)S(1)} %get-tuple-element.68.centre_ref), custom_call_target="tpu_custom_call" | custom-call | flops 104857600 | bytes 2097152 | tf_op jit(solution)/shard_map/select/pallas_call | solution.py:32
  12.0 1.5 %collective-permute-start = (bf16[16,16,512]{2,1,0:T(8,128)(2,1)S(1)}, bf16[16,16,512]{2,1,0:T(8,128)(2,1)S(1)}, u32[]{:S(2)}, u32[]{:S(2)}) collective-permute-start(bf16[16,16,512]{2,1,0:T(8,128)(2,1)S(1)} %get-tuple-element.70), channel_id=1, source_target_pairs={{0,2},{2,0},{1,3},{3,1},{4,6},{6,4},{5,7},{7,5},{8,10},{10,8},{9,1... | collective-permute-start | bytes 786440 | tf_op jit(solution)/shard_map/ppermute | solution.py:364
  13.6 0.3 collective-permute-start.6
  13.9 0.5 collective-permute-start.5
  14.4 1.3 %sums.1 = (f32[136,256]{1,0:T(8,128)S(1)}, f32[136,256]{1,0:T(8,128)S(1)}, f32[128,256]{1,0:T(8,128)S(1)}, f32[128,256]{1,0:T(8,128)S(1)}) custom-call(bf16[528,256]{1,0:T(8,128)(2,1)S(1)} %get-tuple-element.65.lead_ref, bf16[544,256]{1,0:T(8,128)(2,1)S(1)} %get-tuple-element.83.rest_ref, bf16[528,256]{1,0:T(8,128)(2,1)S(1)} %collective-permute-done.3.near_ref, ...), custom_call_target="tpu_custom_call" | custom-call | flops 104857600 | bytes 2097152 | tf_op jit(solution)/shard_map/sums/pallas_call | solution.py:32
  15.8 4.4 %collective-permute-done.refs_5_ = bf16[16,16,512]{2,1,0:T(8,128)(2,1)S(1)} collective-permute-done((bf16[16,16,512]{2,1,0:T(8,128)(2,1)S(1)}, bf16[16,16,512]{2,1,0:T(8,128)(2,1)S(1)}, u32[]{:S(2)}, u32[]{:S(2)}) %collective-permute-start) | collective-permute-done | bytes 262176 | tf_op jit(solution)/shard_map/ppermute | solution.py:364
  20.2 0.0 collective-permute-done.2.refs_1_.lead_ref
  20.2 0.7 %collective-permute-done.1.refs_0_.lead_ref = bf16[528,256]{1,0:T(8,128)(2,1)S(1)} collective-permute-done((bf16[528,256]{1,0:T(8,128)(2,1)S(1)}, bf16[528,256]{1,0:T(8,128)(2,1)S(1)}, u32[]{:S(2)}, u32[]{:S(2)}) %collective-permute-start.1) | collective-permute-done | bytes 270368 | tf_op jit(solution)/shard_map/ppermute | solution.py:371
  20.9 1.1 %select_lead.1 = (bf16[512,512]{1,0:T(8,128)(2,1)S(1)}, bf16[512,512]{1,0:T(8,128)(2,1)S(1)}, bf16[2,16,16,256]{3,2,1,0:T(8,128)(2,1)S(1)}, bf16[2,16,16,256]{3,2,1,0:T(8,128)(2,1)S(1)}) custom-call(f32[256,1]{1,0:T(8,128)S(1)} %get-tuple-element.67.inv_ref, bf16[256,512]{1,0:T(8,128)(2,1)S(1)} %get-tuple-element.68.centre_ref, ...), custom_call_target="tpu_custom_call" | custom-call | tf_op jit(solution)/shard_map/select_lead/pallas_call | solution.py:32
  22.0 2.0 %collective-permute-start.4 = (bf16[2,16,16,256]{3,2,1,0:T(8,128)(2,1)S(1)}, bf16[2,16,16,256]{3,2,1,0:T(8,128)(2,1)S(1)}, u32[]{:S(2)}, u32[]{:S(2)}) collective-permute-start(bf16[2,16,16,256]{3,2,1,0:T(8,128)(2,1)S(1)} %get-tuple-element.80), channel_id=1, source_target_pairs={{0,2},{2,0},{1,3},{3,1},{4,6},{6,4},{5,7},{7,5},{8,10},{10,8},{9,1... | collective-permute-start | bytes 786440 | tf_op jit(solution)/shard_map/ppermute | solution.py:364
  23.9 0.5 collective-permute-start.9
  24.5 6.1 %collective-permute-done.5.refs_2_ = bf16[528,256]{1,0:T(8,128)(2,1)S(1)} collective-permute-done((bf16[528,256]{1,0:T(8,128)(2,1)S(1)}, bf16[528,256]{1,0:T(8,128)(2,1)S(1)}, u32[]{:S(2)}, u32[]{:S(2)}) %collective-permute-start.5) | collective-permute-done | bytes 270368 | tf_op jit(solution)/shard_map/ppermute | solution.py:371
  30.6 0.9 %collective-permute-done.6.refs_3_ = bf16[544,256]{1,0:T(8,128)(2,1)S(1)} collective-permute-done((bf16[544,256]{1,0:T(8,128)(2,1)S(1)}, bf16[544,256]{1,0:T(8,128)(2,1)S(1)}, u32[]{:S(2)}, u32[]{:S(2)}) %collective-permute-start.6) | collective-permute-done | bytes 278560 | tf_op jit(solution)/shard_map/ppermute | solution.py:371
  31.5 1.6 %collective-permute-start.8 = (bf16[528,256]{1,0:T(8,128)(2,1)S(1)}, bf16[528,256]{1,0:T(8,128)(2,1)S(1)}, u32[]{:S(2)}, u32[]{:S(2)}) collective-permute-start(bf16[528,256]{1,0:T(8,128)(2,1)S(1)} %collective-permute-done.2.refs_1_.lead_ref), channel_id=1, source_target_pairs={{0,4},{4,0},{8,12},{12,8},{1,5},{5,1},{9,13},{13,9},{2,6},{6,2},{1... | collective-permute-start | bytes 811016 | tf_op jit(solution)/shard_map/ppermute | solution.py:371
  33.1 0.4 select_rest.2
  33.5 1.6 %collective-permute-start.7 = (bf16[2,16,16,256]{3,2,1,0:T(8,128)(2,1)S(1)}, bf16[2,16,16,256]{3,2,1,0:T(8,128)(2,1)S(1)}, u32[]{:S(2)}, u32[]{:S(2)}) collective-permute-start(bf16[2,16,16,256]{3,2,1,0:T(8,128)(2,1)S(1)} %get-tuple-element.87), channel_id=1, source_target_pairs={{0,2},{2,0},{1,3},{3,1},{4,6},{6,4},{5,7},{7,5},{8,10},{10,8},{9,1... | collective-permute-start | bytes 786440 | tf_op jit(solution)/shard_map/ppermute | solution.py:364
  35.1 1.4 %sums_lead.2 = (bf16[256,512]{1,0:T(8,128)(2,1)S(1)}, f32[136,256]{1,0:T(8,128)S(1)}, f32[136,256]{1,0:T(8,128)S(1)}) custom-call(bf16[528,256]{1,0:T(8,128)(2,1)S(1)} %collective-permute-done.1.refs_0_.lead_ref, bf16[528,256]{1,0:T(8,128)(2,1)S(1)} %collective-permute-done.10.near_ref, ...), custom_call_target="tpu_custom_call", output_to_operand_aliasing={{1}: (4, {}), {2}: (5, {})} | custom-call | tf_op jit(solution)/shard_map/sums_lead/pallas_call | solution.py:32
  36.5 1.4 %sums_lead.3 = (bf16[256,512]{1,0:T(8,128)(2,1)S(1)}, f32[136,256]{1,0:T(8,128)S(1)}, f32[136,256]{1,0:T(8,128)S(1)}) custom-call(bf16[528,256]{1,0:T(8,128)(2,1)S(1)} %collective-permute-done.2.refs_1_.lead_ref, bf16[528,256]{1,0:T(8,128)(2,1)S(1)} %collective-permute-done.9.near_ref, ...), custom_call_target="tpu_custom_call", output_to_operand_aliasing={{1}: (4, {}), {2}: (5, {})} | custom-call | tf_op jit(solution)/shard_map/sums_lead/pallas_call | solution.py:32
  37.9 0.3 sums_rest.2
  38.2 0.6 %collective-permute-start.14 = (bf16[544,256]{1,0:T(8,128)(2,1)S(1)}, bf16[544,256]{1,0:T(8,128)(2,1)S(1)}, u32[]{:S(2)}, u32[]{:S(2)}) collective-permute-start(bf16[544,256]{1,0:T(8,128)(2,1)S(1)} %collective-permute-done.6.refs_3_), channel_id=1, source_target_pairs={{0,4},{4,0},{8,12},{12,8},{1,5},{5,1},{9,13},{13,9},{2,6},{6,2},{1... | collective-permute-start | bytes 835592 | tf_op jit(solution)/shard_map/ppermute | solution.py:371
  38.8 0.9 %collective-permute-done.8.lead_ref = bf16[528,256]{1,0:T(8,128)(2,1)S(1)} collective-permute-done((bf16[528,256]{1,0:T(8,128)(2,1)S(1)}, bf16[528,256]{1,0:T(8,128)(2,1)S(1)}, u32[]{:S(2)}, u32[]{:S(2)}) %collective-permute-start.8) | collective-permute-done | bytes 270368 | tf_op jit(solution)/shard_map/ppermute | solution.py:371
  39.7 0.1 collective-permute-start.12
  39.8 0.5 collective-permute-start.11
  40.3 0.8 %collective-permute-done.12.high_ref = bf16[256,256]{1,0:T(8,128)(2,1)S(1)} collective-permute-done((bf16[256,256]{1,0:T(8,128)(2,1)S(1)}, bf16[256,256]{1,0:T(8,128)(2,1)S(1)}, u32[]{:S(2)}, u32[]{:S(2)}) %collective-permute-start.12) | collective-permute-done | bytes 131104 | tf_op jit(solution)/shard_map/ppermute | solution.py:368
  41.1 0.2 collective-permute-done.11.low_ref
  41.3 1.6 %last_lead.1 = (bf16[256,512]{1,0:T(8,128)(2,1)S(1)}, bf16[512,512]{1,0:T(8,128)(2,1)S(1)}, f32[136,256]{1,0:T(8,128)S(1)}, bf16[1,16,16,256]{3,2,1,0:T(8,128)(2,1)S(1)}, bf16[400,256]{1,0:T(8,128)(2,1)S(1)}) custom-call(bf16[528,256]{1,0:T(8,128)(2,1)S(1)} %collective-permute-done.8.lead_ref, ...), custom_call_target="tpu_custom_call", output_to_operand_aliasing={{2}: (7, {})} | custom-call | tf_op jit(solution)/shard_map/last_lead/pallas_call | solution.py:32
  42.9 2.0 %collective-permute-start.13 = (bf16[400,256]{1,0:T(8,128)(2,1)S(1)}, bf16[400,256]{1,0:T(8,128)(2,1)S(1)}, u32[]{:S(2)}, u32[]{:S(2)}) collective-permute-start(bf16[400,256]{1,0:T(8,128)(2,1)S(1)} %get-tuple-element.101), channel_id=1, source_target_pairs={{0,2},{2,0},{1,3},{3,1},{4,6},{6,4},{5,7},{7,5},{8,10},{10,8},{9,1... | collective-permute-start | bytes 614408 | tf_op jit(solution)/shard_map/ppermute | solution.py:364
  44.9 1.0 %collective-permute-done.14.refs_1_ = bf16[544,256]{1,0:T(8,128)(2,1)S(1)} collective-permute-done((bf16[544,256]{1,0:T(8,128)(2,1)S(1)}, bf16[544,256]{1,0:T(8,128)(2,1)S(1)}, u32[]{:S(2)}, u32[]{:S(2)}) %collective-permute-start.14) | collective-permute-done | bytes 278560 | tf_op jit(solution)/shard_map/ppermute | solution.py:371
  45.9 0.3 select_rest.3
  46.2 1.2 %collective-permute-start.15 = (bf16[1,16,16,256]{3,2,1,0:T(8,128)(2,1)S(1)}, bf16[1,16,16,256]{3,2,1,0:T(8,128)(2,1)S(1)}, u32[]{:S(2)}, u32[]{:S(2)}) collective-permute-start(bf16[1,16,16,256]{3,2,1,0:T(8,128)(2,1)S(1)} %get-tuple-element.107), channel_id=1, source_target_pairs={{0,2},{2,0},{1,3},{3,1},{4,6},{6,4},{5,7},{7,5},{8,10},{10,8},{9,1... | collective-permute-start | bytes 393224 | tf_op jit(solution)/shard_map/ppermute | solution.py:364
  47.4 3.4 %collective-permute-done.13.refs_8_.refs_5_ = bf16[400,256]{1,0:T(8,128)(2,1)S(1)} collective-permute-done((bf16[400,256]{1,0:T(8,128)(2,1)S(1)}, bf16[400,256]{1,0:T(8,128)(2,1)S(1)}, u32[]{:S(2)}, u32[]{:S(2)}) %collective-permute-start.13) | collective-permute-done | bytes 204832 | tf_op jit(solution)/shard_map/ppermute | solution.py:364
  50.8 0.2 sums_rest.3
  51.1 2.0 %collective-permute-start.18 = (bf16[144,256]{1,0:T(8,128)(2,1)S(1)}, bf16[144,256]{1,0:T(8,128)(2,1)S(1)}, u32[]{:S(2)}, u32[]{:S(2)}) collective-permute-start(bf16[144,256]{1,0:T(8,128)(2,1)S(1)} %get-tuple-element.111), channel_id=1, source_target_pairs={{0,2},{2,0},{1,3},{3,1},{4,6},{6,4},{5,7},{7,5},{8,10},{10,8},{9,1... | collective-permute-start | bytes 221192 | tf_op jit(solution)/shard_map/ppermute | solution.py:364
  53.1 0.3 collective-permute-done.15.refs_9_
  53.4 0.9 %gram.1 = (f32[8,16,128]{2,1,0:T(8,128)S(1)}, f32[8,16,128]{2,1,0:T(8,128)S(1)}) custom-call(bf16[16,16,512]{2,1,0:T(8,128)(2,1)S(1)} %get-tuple-element.112.refs_0_, bf16[2,16,16,256]{3,2,1,0:T(8,128)(2,1)S(1)} %get-tuple-element.113.refs_1_, bf16[2,16,16,256]{3,2,1,0:T(8,128)(2,1)S(1)} %get-tuple-element.114.refs_2_, ...), custom_call_target="tpu_custom_call" | custom-call | tf_op jit(solution)/shard_map/gram/pallas_call | solution.py:32
  54.3 0.1 collective-permute-start.16
  54.4 0.5 collective-permute-start.17
  54.8 0.7 %collective-permute-done.16.refs_2_ = f32[8,16,128]{2,1,0:T(8,128)S(1)} collective-permute-done((f32[8,16,128]{2,1,0:T(8,128)S(1)}, f32[8,16,128]{2,1,0:T(8,128)S(1)}, u32[]{:S(2)}, u32[]{:S(2)}) %collective-permute-start.16) | collective-permute-done | bytes 65568 | tf_op jit(solution)/shard_map/ppermute | solution.py:368
  55.6 0.2 collective-permute-done.17.refs_3_
  55.8 1.4 %finish.1 = (f32[128,512]{1,0:T(8,128)}, bf16[8,16,128]{2,1,0:T(8,128)(2,1)}) custom-call(f32[8,16,128]{2,1,0:T(8,128)S(1)} %get-tuple-element.122.refs_0_, f32[8,16,128]{2,1,0:T(8,128)S(1)} %get-tuple-element.123.refs_1_, f32[8,16,128]{2,1,0:T(8,128)S(1)} %collective-permute-done.16.refs_2_, f32[8,16,128]{2,1,0:T(8,128)S(1)} %collective-permute-done.17.refs_3_, ...), custom_call_target="tpu_custom_call" | custom-call | tf_op jit(solution)/shard_map/finish/pallas_call | solution.py:32
  (14 shorter events, 0.1 us)
Async XLA Ops:
  0.6 1.0 %copy-start.1 = (bf16[512,512]{1,0:T(8,128)(2,1)S(1)}, bf16[512,512]{1,0:T(8,128)(2,1)}, u32[]{:S(2)}) copy-start(bf16[512,512]{1,0:T(8,128)(2,1)} %emb_ref.1) | copy-start | bytes 1572868
  1.7 0.7 %copy-start.3 = (s32[512,1]{0,1:T(1,128)S(1)}, s32[512,1]{0,1:T(1,128)}, u32[]{:S(2)}) copy-start(s32[512,1]{0,1:T(1,128)} %param.6) | copy-start | bytes 6148
  2.4 11.5 %collective-permute-start.3 = (bf16[528,256]{1,0:T(8,128)(2,1)S(1)}, bf16[528,256]{1,0:T(8,128)(2,1)S(1)}, u32[]{:S(2)}, u32[]{:S(2)}) collective-permute-start(bf16[528,256]{1,0:T(8,128)(2,1)S(1)} %get-tuple-element.65.lead_ref), channel_id=1, source_target_pairs={{0,1},{1,0},{2,3},{3,2},{4,5},{5,4},{6,7},{7,6},{8,9},{9,8},{10,11... | collective-permute-start | bytes 811016 | tf_op jit(solution)/shard_map/ppermute | solution.py:368
  2.9 17.3 %collective-permute-start.2 = (bf16[528,256]{1,0:T(8,128)(2,1)S(1)}, bf16[528,256]{1,0:T(8,128)(2,1)S(1)}, u32[]{:S(2)}, u32[]{:S(2)}) collective-permute-start(bf16[528,256]{1,0:T(8,128)(2,1)S(1)} %get-tuple-element.65.lead_ref), channel_id=1, source_target_pairs={{0,8},{4,12},{8,0},{12,4},{1,9},{5,13},{9,1},{13,5},{2,10},{6,14},... | collective-permute-start | bytes 811016 | tf_op jit(solution)/shard_map/ppermute | solution.py:371
  6.6 14.3 %collective-permute-start.1 = (bf16[528,256]{1,0:T(8,128)(2,1)S(1)}, bf16[528,256]{1,0:T(8,128)(2,1)S(1)}, u32[]{:S(2)}, u32[]{:S(2)}) collective-permute-start(bf16[528,256]{1,0:T(8,128)(2,1)S(1)} %get-tuple-element.65.lead_ref), channel_id=1, source_target_pairs={{0,4},{4,0},{8,12},{12,8},{1,5},{5,1},{9,13},{13,9},{2,6},{6,2},{1... | collective-permute-start | bytes 811016 | tf_op jit(solution)/shard_map/ppermute | solution.py:371
  8.2 1.6 %copy-start = (bf16[1024,1024]{1,0:T(8,128)(2,1)S(1)}, bf16[1024,1024]{1,0:T(8,128)(2,1)}, u32[]{:S(2)}) copy-start(bf16[1024,1024]{1,0:T(8,128)(2,1)} %cent_ref.1) | copy-start | bytes 6291460
  9.8 0.7 %copy-start.2 = (s32[1024]{0:T(1024)S(1)}, s32[1024]{0:T(1024)}, u32[]{:S(2)}) copy-start(s32[1024]{0:T(1024)} %param.7) | copy-start | bytes 12292
  12.0 8.1 %collective-permute-start = (bf16[16,16,512]{2,1,0:T(8,128)(2,1)S(1)}, bf16[16,16,512]{2,1,0:T(8,128)(2,1)S(1)}, u32[]{:S(2)}, u32[]{:S(2)}) collective-permute-start(bf16[16,16,512]{2,1,0:T(8,128)(2,1)S(1)} %get-tuple-element.70), channel_id=1, source_target_pairs={{0,2},{2,0},{1,3},{3,1},{4,6},{6,4},{5,7},{7,5},{8,10},{10,8},{9,1... | collective-permute-start | bytes 786440 | tf_op jit(solution)/shard_map/ppermute | solution.py:364
  13.6 17.9 %collective-permute-start.6 = (bf16[544,256]{1,0:T(8,128)(2,1)S(1)}, bf16[544,256]{1,0:T(8,128)(2,1)S(1)}, u32[]{:S(2)}, u32[]{:S(2)}) collective-permute-start(bf16[544,256]{1,0:T(8,128)(2,1)S(1)} %get-tuple-element.83.rest_ref), channel_id=1, source_target_pairs={{0,8},{4,12},{8,0},{12,4},{1,9},{5,13},{9,1},{13,5},{2,10},{6,14},... | collective-permute-start | bytes 835592 | tf_op jit(solution)/shard_map/ppermute | solution.py:371
  13.9 16.6 %collective-permute-start.5 = (bf16[528,256]{1,0:T(8,128)(2,1)S(1)}, bf16[528,256]{1,0:T(8,128)(2,1)S(1)}, u32[]{:S(2)}, u32[]{:S(2)}) collective-permute-start(bf16[528,256]{1,0:T(8,128)(2,1)S(1)} %slice.9), channel_id=1, source_target_pairs={{0,4},{4,0},{8,12},{12,8},{1,5},{5,1},{9,13},{13,9},{2,6},{6,2},{1... | collective-permute-start | bytes 811016 | tf_op jit(solution)/shard_map/ppermute | solution.py:371
  22.0 9.5 %collective-permute-start.4 = (bf16[2,16,16,256]{3,2,1,0:T(8,128)(2,1)S(1)}, bf16[2,16,16,256]{3,2,1,0:T(8,128)(2,1)S(1)}, u32[]{:S(2)}, u32[]{:S(2)}) collective-permute-start(bf16[2,16,16,256]{3,2,1,0:T(8,128)(2,1)S(1)} %get-tuple-element.80), channel_id=1, source_target_pairs={{0,2},{2,0},{1,3},{3,1},{4,6},{6,4},{5,7},{7,5},{8,10},{10,8},{9,1... | collective-permute-start | bytes 786440 | tf_op jit(solution)/shard_map/ppermute | solution.py:364
  23.9 11.1 %collective-permute-start.10 = (bf16[528,256]{1,0:T(8,128)(2,1)S(1)}, bf16[528,256]{1,0:T(8,128)(2,1)S(1)}, u32[]{:S(2)}, u32[]{:S(2)}) collective-permute-start(bf16[528,256]{1,0:T(8,128)(2,1)S(1)} %collective-permute-done.1.refs_0_.lead_ref), channel_id=1, source_target_pairs={{0,1},{1,0},{2,3},{3,2},{4,5},{5,4},{6,7},{7,6},{8,9},{9,8},{10,11... | collective-permute-start | bytes 811016 | tf_op jit(solution)/shard_map/ppermute | solution.py:368
  23.9 12.5 %collective-permute-start.9 = (bf16[528,256]{1,0:T(8,128)(2,1)S(1)}, bf16[528,256]{1,0:T(8,128)(2,1)S(1)}, u32[]{:S(2)}, u32[]{:S(2)}) collective-permute-start(bf16[528,256]{1,0:T(8,128)(2,1)S(1)} %collective-permute-done.2.refs_1_.lead_ref), channel_id=1, source_target_pairs={{0,1},{1,0},{2,3},{3,2},{4,5},{5,4},{6,7},{7,6},{8,9},{9,8},{10,11... | collective-permute-start | bytes 811016 | tf_op jit(solution)/shard_map/ppermute | solution.py:368
  31.5 8.2 %collective-permute-start.8 = (bf16[528,256]{1,0:T(8,128)(2,1)S(1)}, bf16[528,256]{1,0:T(8,128)(2,1)S(1)}, u32[]{:S(2)}, u32[]{:S(2)}) collective-permute-start(bf16[528,256]{1,0:T(8,128)(2,1)S(1)} %collective-permute-done.2.refs_1_.lead_ref), channel_id=1, source_target_pairs={{0,4},{4,0},{8,12},{12,8},{1,5},{5,1},{9,13},{13,9},{2,6},{6,2},{1... | collective-permute-start | bytes 811016 | tf_op jit(solution)/shard_map/ppermute | solution.py:371
  33.5 9.4 %collective-permute-start.7 = (bf16[2,16,16,256]{3,2,1,0:T(8,128)(2,1)S(1)}, bf16[2,16,16,256]{3,2,1,0:T(8,128)(2,1)S(1)}, u32[]{:S(2)}, u32[]{:S(2)}) collective-permute-start(bf16[2,16,16,256]{3,2,1,0:T(8,128)(2,1)S(1)} %get-tuple-element.87), channel_id=1, source_target_pairs={{0,2},{2,0},{1,3},{3,1},{4,6},{6,4},{5,7},{7,5},{8,10},{10,8},{9,1... | collective-permute-start | bytes 786440 | tf_op jit(solution)/shard_map/ppermute | solution.py:364
  38.2 7.7 %collective-permute-start.14 = (bf16[544,256]{1,0:T(8,128)(2,1)S(1)}, bf16[544,256]{1,0:T(8,128)(2,1)S(1)}, u32[]{:S(2)}, u32[]{:S(2)}) collective-permute-start(bf16[544,256]{1,0:T(8,128)(2,1)S(1)} %collective-permute-done.6.refs_3_), channel_id=1, source_target_pairs={{0,4},{4,0},{8,12},{12,8},{1,5},{5,1},{9,13},{13,9},{2,6},{6,2},{1... | collective-permute-start | bytes 835592 | tf_op jit(solution)/shard_map/ppermute | solution.py:371
  39.7 1.4 %collective-permute-start.12 = (bf16[256,256]{1,0:T(8,128)(2,1)S(1)}, bf16[256,256]{1,0:T(8,128)(2,1)S(1)}, u32[]{:S(2)}, u32[]{:S(2)}) collective-permute-start(bf16[256,256]{1,0:T(8,128)(2,1)S(1)} %get-tuple-element.128), channel_id=1, source_target_pairs={{0,1},{1,0},{2,3},{3,2},{4,5},{5,4},{6,7},{7,6},{8,9},{9,8},{10,11... | collective-permute-start | bytes 393224 | tf_op jit(solution)/shard_map/ppermute | solution.py:368
  39.8 1.5 %collective-permute-start.11 = (bf16[256,256]{1,0:T(8,128)(2,1)S(1)}, bf16[256,256]{1,0:T(8,128)(2,1)S(1)}, u32[]{:S(2)}, u32[]{:S(2)}) collective-permute-start(bf16[256,256]{1,0:T(8,128)(2,1)S(1)} %get-tuple-element.129), channel_id=1, source_target_pairs={{0,1},{1,0},{2,3},{3,2},{4,5},{5,4},{6,7},{7,6},{8,9},{9,8},{10,11... | collective-permute-start | bytes 393224 | tf_op jit(solution)/shard_map/ppermute | solution.py:368
  42.9 7.9 %collective-permute-start.13 = (bf16[400,256]{1,0:T(8,128)(2,1)S(1)}, bf16[400,256]{1,0:T(8,128)(2,1)S(1)}, u32[]{:S(2)}, u32[]{:S(2)}) collective-permute-start(bf16[400,256]{1,0:T(8,128)(2,1)S(1)} %get-tuple-element.101), channel_id=1, source_target_pairs={{0,2},{2,0},{1,3},{3,1},{4,6},{6,4},{5,7},{7,5},{8,10},{10,8},{9,1... | collective-permute-start | bytes 614408 | tf_op jit(solution)/shard_map/ppermute | solution.py:364
  46.2 7.2 %collective-permute-start.15 = (bf16[1,16,16,256]{3,2,1,0:T(8,128)(2,1)S(1)}, bf16[1,16,16,256]{3,2,1,0:T(8,128)(2,1)S(1)}, u32[]{:S(2)}, u32[]{:S(2)}) collective-permute-start(bf16[1,16,16,256]{3,2,1,0:T(8,128)(2,1)S(1)} %get-tuple-element.107), channel_id=1, source_target_pairs={{0,2},{2,0},{1,3},{3,1},{4,6},{6,4},{5,7},{7,5},{8,10},{10,8},{9,1... | collective-permute-start | bytes 393224 | tf_op jit(solution)/shard_map/ppermute | solution.py:364
  51.1 4.7 %collective-permute-start.18 = (bf16[144,256]{1,0:T(8,128)(2,1)S(1)}, bf16[144,256]{1,0:T(8,128)(2,1)S(1)}, u32[]{:S(2)}, u32[]{:S(2)}) collective-permute-start(bf16[144,256]{1,0:T(8,128)(2,1)S(1)} %get-tuple-element.111), channel_id=1, source_target_pairs={{0,2},{2,0},{1,3},{3,1},{4,6},{6,4},{5,7},{7,5},{8,10},{10,8},{9,1... | collective-permute-start | bytes 221192 | tf_op jit(solution)/shard_map/ppermute | solution.py:364
  54.3 1.3 %collective-permute-start.16 = (f32[8,16,128]{2,1,0:T(8,128)S(1)}, f32[8,16,128]{2,1,0:T(8,128)S(1)}, u32[]{:S(2)}, u32[]{:S(2)}) collective-permute-start(f32[8,16,128]{2,1,0:T(8,128)S(1)} %get-tuple-element.122.refs_0_), channel_id=1, source_target_pairs={{0,1},{1,0},{2,3},{3,2},{4,5},{5,4},{6,7},{7,6},{8,9},{9,8},{10,11... | collective-permute-start | bytes 196616 | tf_op jit(solution)/shard_map/ppermute | solution.py:368
  54.4 1.4 %collective-permute-start.17 = (f32[8,16,128]{2,1,0:T(8,128)S(1)}, f32[8,16,128]{2,1,0:T(8,128)S(1)}, u32[]{:S(2)}, u32[]{:S(2)}) collective-permute-start(f32[8,16,128]{2,1,0:T(8,128)S(1)} %get-tuple-element.123.refs_1_), channel_id=1, source_target_pairs={{0,1},{1,0},{2,3},{3,2},{4,5},{5,4},{6,7},{7,6},{8,9},{9,8},{10,11... | collective-permute-start | bytes 196616 | tf_op jit(solution)/shard_map/ppermute | solution.py:368

commit v15 on v9

--- a/solution.py
+++ b/solution.py
@@ -478,7 +478,7 @@
         [gram, near(gram)],
         scratch=[pltpu.VMEM((groups, slots // 2, slots * SUBLANES), F32)],
     )
-    (new_centroids,) = call(centroid_kernel, "centroids", [shape((per, half), F32)], [lead, rest] + sent + [prior])
+    (new_centroids,) = call(centroid_kernel, "centroids", [shape((per, half), F32)], [lead, rest] + tied(sent, tiles) + [prior])
     return (new_centroids, jnp.transpose(tiles, (2, 0, 1)))
 
 

time: 56.3 us -> 55.3 us (0.982)
  waiting for transfers between devices: 19 us -> 18 us
    ppermute x6, waiting for transfers between devices: 7.08 us -> 4.74 us  [across(): lax.ppermute(values[t], 'sub', [(i, (i + t) % subs) for i in range(subs)])]
    ppermute x5, waiting for transfers between devices: 0.01 us -> 1.35 us  [near(): return lax.ppermute(value, 'dim', [(0, 1), (1, 0)])]
  transfers between devices with their start and end apart: 17 -> 17, of which waited for: 7 -> 7; matrix products, arithmetic and copies ran while one was open for 0% -> 0% of each run, Pallas kernels for 20% -> 22%
where the time goes in v15:
time: 55.3 us; the launch traced here: 55 us
  starting transfers between devices  19.5 us (35%)
  waiting for transfers between devices  18 us (33%)
  Pallas kernels  12.8 us (23%)
  local copies, waits for them, and re-layouts  3.99 us (7%)
  between operations  0.76 us (1%)
    pallas_call x15, Pallas kernels, call(): pl.pallas_call(kernel, out_shape=tuple(out_shape), in_specs=[whole(operan...  12.8 us
    ppermute x6, waiting for transfers between devices, swap(): return lax.ppermute(value, 'rows', [(i, i ^ bit) for i in range(rows)])  11.9 us
    ppermute x6, starting transfers between devices, across(): lax.ppermute(values[t], 'sub', [(i, (i + t) % subs) for i in range(subs)])  10.3 us
    ppermute x6, starting transfers between devices, swap(): return lax.ppermute(value, 'rows', [(i, i ^ bit) for i in range(rows)])  8.05 us
    ppermute x6, waiting for transfers between devices, across(): lax.ppermute(values[t], 'sub', [(i, (i + t) % subs) for i in range(subs)])  4.74 us
    unnamed x8, local copies, waits for them, and re-layouts  3.99 us
    ppermute x5, waiting for transfers between devices, near(): return lax.ppermute(value, 'dim', [(0, 1), (1, 0)])  1.35 us
  transfers between devices with their start and end apart: 17, of which 7 were waited for; matrix products, arithmetic and copies ran while one was open for 0% of the time, Pallas kernels for 22%

profile of v15, /device:TPU:0, one launch (start us, length us, event | category | flops | bytes accessed | tf_op | source)
XLA Modules:
  0.0 55.0 jit_solution(7925316683777363806)
XLA Ops:
  0.6 1.0 %copy-done.1 = bf16[512,512]{1,0:T(8,128)(2,1)S(1)} copy-done((bf16[512,512]{1,0:T(8,128)(2,1)S(1)}, bf16[512,512]{1,0:T(8,128)(2,1)}, u32[]{:S(2)}) %copy-start.1) | copy-done | bytes 524312
  1.7 0.7 %copy-done.3 = s32[512,1]{0,1:T(1,128)S(1)} copy-done((s32[512,1]{0,1:T(1,128)S(1)}, s32[512,1]{0,1:T(1,128)}, u32[]{:S(2)}) %copy-start.3) | copy-done | bytes 2072
  2.4 0.5 collective-permute-start.2
  2.9 3.7 %collective-permute-start.1 = (bf16[528,256]{1,0:T(8,128)(2,1)S(1)}, bf16[528,256]{1,0:T(8,128)(2,1)S(1)}, u32[]{:S(2)}, u32[]{:S(2)}) collective-permute-start(bf16[528,256]{1,0:T(8,128)(2,1)S(1)} %get-tuple-element.47.lead_ref), channel_id=1, source_target_pairs={{0,8},{4,12},{8,0},{12,4},{1,9},{5,13},{9,1},{13,5},{2,10},{6,14},... | collective-permute-start | bytes 811016 | tf_op jit(solution)/shard_map/ppermute | solution.py:353
  6.6 1.6 %collective-permute-start = (bf16[528,256]{1,0:T(8,128)(2,1)S(1)}, bf16[528,256]{1,0:T(8,128)(2,1)S(1)}, u32[]{:S(2)}, u32[]{:S(2)}) collective-permute-start(bf16[528,256]{1,0:T(8,128)(2,1)S(1)} %get-tuple-element.47.lead_ref), channel_id=1, source_target_pairs={{0,4},{4,0},{8,12},{12,8},{1,5},{5,1},{9,13},{13,9},{2,6},{6,2},{1... | collective-permute-start | bytes 811016 | tf_op jit(solution)/shard_map/ppermute | solution.py:353
  8.2 1.6 %copy-done = bf16[1024,1024]{1,0:T(8,128)(2,1)S(1)} copy-done((bf16[1024,1024]{1,0:T(8,128)(2,1)S(1)}, bf16[1024,1024]{1,0:T(8,128)(2,1)}, u32[]{:S(2)}) %copy-start) | copy-done | bytes 2097176
  9.8 0.7 %copy-done.2 = s32[1024]{0:T(1024)S(1)} copy-done((s32[1024]{0:T(1024)S(1)}, s32[1024]{0:T(1024)}, u32[]{:S(2)}) %copy-start.2) | copy-done | bytes 4120
  10.4 0.8 %prep.1 = (f32[256,1]{1,0:T(8,128)S(1)}, bf16[256,512]{1,0:T(8,128)(2,1)S(1)}, bf16[256,256]{1,0:T(8,128)(2,1)S(1)}, bf16[128,512]{1,0:T(8,128)(2,1)S(1)}, bf16[1024,256]{1,0:T(8,128)(2,1)S(1)}) custom-call(s32[1,1024]{1,0:T(1,128)S(1)} %bitcast.3, bf16[1024,1024]{1,0:T(8,128)(2,1)S(1)} %copy-done), custom_call_target="tpu_custom_call" | custom-call | flops 209715200 | bytes 4194304 | tf_op jit(solution)/shard_map/prep/pallas_call | solution.py:32
  11.3 0.7 %select.1 = (bf16[16,16,512]{2,1,0:T(8,128)(2,1)S(1)}, bf16[16,16,512]{2,1,0:T(8,128)(2,1)S(1)}) custom-call(bf16[528,256]{1,0:T(8,128)(2,1)S(1)} %get-tuple-element.47.lead_ref, bf16[528,256]{1,0:T(8,128)(2,1)S(1)} %get-tuple-element.63.rest_ref, f32[256,1]{1,0:T(8,128)S(1)} %get-tuple-element.49.inv_ref, bf16[256,512]{1,0:T(8,128)(2,1)S(1)} %get-tuple-element.50.centre_ref), custom_call_target="tpu_custom_call" | custom-call | flops 104857600 | bytes 2097152 | tf_op jit(solution)/shard_map/select/pallas_call | solution.py:32
  12.0 1.5 %collective-permute-start.3 = (bf16[16,16,512]{2,1,0:T(8,128)(2,1)S(1)}, bf16[16,16,512]{2,1,0:T(8,128)(2,1)S(1)}, u32[]{:S(2)}, u32[]{:S(2)}) collective-permute-start(bf16[16,16,512]{2,1,0:T(8,128)(2,1)S(1)} %get-tuple-element.52), channel_id=1, source_target_pairs={{0,2},{2,0},{1,3},{3,1},{4,6},{6,4},{5,7},{7,5},{8,10},{10,8},{9,1... | collective-permute-start | bytes 786440 | tf_op jit(solution)/shard_map/ppermute | solution.py:346
  13.6 0.3 collective-permute-start.6
  13.9 0.5 collective-permute-start.5
  14.4 1.3 %sums.1 = (f32[136,256]{1,0:T(8,128)S(1)}, f32[136,256]{1,0:T(8,128)S(1)}, f32[128,256]{1,0:T(8,128)S(1)}, f32[128,256]{1,0:T(8,128)S(1)}) custom-call(bf16[528,256]{1,0:T(8,128)(2,1)S(1)} %get-tuple-element.47.lead_ref, bf16[528,256]{1,0:T(8,128)(2,1)S(1)} %get-tuple-element.63.rest_ref, bf16[528,256]{1,0:T(8,128)(2,1)S(1)} %collective-permute-done.2.near_ref, ...), custom_call_target="tpu_custom_call" | custom-call | flops 104857600 | bytes 2097152 | tf_op jit(solution)/shard_map/sums/pallas_call | solution.py:32
  15.7 4.5 %collective-permute-done.3.refs_5_ = bf16[16,16,512]{2,1,0:T(8,128)(2,1)S(1)} collective-permute-done((bf16[16,16,512]{2,1,0:T(8,128)(2,1)S(1)}, bf16[16,16,512]{2,1,0:T(8,128)(2,1)S(1)}, u32[]{:S(2)}, u32[]{:S(2)}) %collective-permute-start.3) | collective-permute-done | bytes 262176 | tf_op jit(solution)/shard_map/ppermute | solution.py:346
  20.2 0.0 collective-permute-done.1.refs_1_.lead_ref
  20.2 0.7 %collective-permute-done.refs_0_.lead_ref = bf16[528,256]{1,0:T(8,128)(2,1)S(1)} collective-permute-done((bf16[528,256]{1,0:T(8,128)(2,1)S(1)}, bf16[528,256]{1,0:T(8,128)(2,1)S(1)}, u32[]{:S(2)}, u32[]{:S(2)}) %collective-permute-start) | collective-permute-done | bytes 270368 | tf_op jit(solution)/shard_map/ppermute | solution.py:353
  20.9 1.1 %select_lead.2 = (bf16[512,512]{1,0:T(8,128)(2,1)S(1)}, bf16[512,512]{1,0:T(8,128)(2,1)S(1)}, bf16[2,16,16,256]{3,2,1,0:T(8,128)(2,1)S(1)}, bf16[2,16,16,256]{3,2,1,0:T(8,128)(2,1)S(1)}) custom-call(f32[256,1]{1,0:T(8,128)S(1)} %get-tuple-element.49.inv_ref, bf16[256,512]{1,0:T(8,128)(2,1)S(1)} %get-tuple-element.50.centre_ref, ...), custom_call_target="tpu_custom_call" | custom-call | tf_op jit(solution)/shard_map/select_lead/pallas_call | solution.py:32
  22.0 2.0 %collective-permute-start.7 = (bf16[2,16,16,256]{3,2,1,0:T(8,128)(2,1)S(1)}, bf16[2,16,16,256]{3,2,1,0:T(8,128)(2,1)S(1)}, u32[]{:S(2)}, u32[]{:S(2)}) collective-permute-start(bf16[2,16,16,256]{3,2,1,0:T(8,128)(2,1)S(1)} %get-tuple-element.65), channel_id=1, source_target_pairs={{0,2},{2,0},{1,3},{3,1},{4,6},{6,4},{5,7},{7,5},{8,10},{10,8},{9,1... | collective-permute-start | bytes 786440 | tf_op jit(solution)/shard_map/ppermute | solution.py:346
  24.0 0.5 collective-permute-start.8
  24.5 6.7 %collective-permute-done.6.refs_3_ = bf16[528,256]{1,0:T(8,128)(2,1)S(1)} collective-permute-done((bf16[528,256]{1,0:T(8,128)(2,1)S(1)}, bf16[528,256]{1,0:T(8,128)(2,1)S(1)}, u32[]{:S(2)}, u32[]{:S(2)}) %collective-permute-start.6) | collective-permute-done | bytes 270368 | tf_op jit(solution)/shard_map/ppermute | solution.py:353
  31.2 0.6 %collective-permute-start.4 = (bf16[528,256]{1,0:T(8,128)(2,1)S(1)}, bf16[528,256]{1,0:T(8,128)(2,1)S(1)}, u32[]{:S(2)}, u32[]{:S(2)}) collective-permute-start(bf16[528,256]{1,0:T(8,128)(2,1)S(1)} %collective-permute-done.1.refs_1_.lead_ref), channel_id=1, source_target_pairs={{0,4},{4,0},{8,12},{12,8},{1,5},{5,1},{9,13},{13,9},{2,6},{6,2},{1... | collective-permute-start | bytes 811016 | tf_op jit(solution)/shard_map/ppermute | solution.py:353
  31.8 0.0 collective-permute-done.5.refs_2_
  31.8 0.0 collective-permute-done.7.refs_6_
  31.8 1.4 %collective-permute-start.10 = (bf16[528,256]{1,0:T(8,128)(2,1)S(1)}, bf16[528,256]{1,0:T(8,128)(2,1)S(1)}, u32[]{:S(2)}, u32[]{:S(2)}) collective-permute-start(bf16[528,256]{1,0:T(8,128)(2,1)S(1)} %collective-permute-done.6.refs_3_), channel_id=1, source_target_pairs={{0,4},{4,0},{8,12},{12,8},{1,5},{5,1},{9,13},{13,9},{2,6},{6,2},{1... | collective-permute-start | bytes 811016 | tf_op jit(solution)/shard_map/ppermute | solution.py:353
  33.2 0.4 select_rest.2
  33.7 1.6 %collective-permute-start.11 = (bf16[2,16,16,256]{3,2,1,0:T(8,128)(2,1)S(1)}, bf16[2,16,16,256]{3,2,1,0:T(8,128)(2,1)S(1)}, u32[]{:S(2)}, u32[]{:S(2)}) collective-permute-start(bf16[2,16,16,256]{3,2,1,0:T(8,128)(2,1)S(1)} %get-tuple-element.69), channel_id=1, source_target_pairs={{0,2},{2,0},{1,3},{3,1},{4,6},{6,4},{5,7},{7,5},{8,10},{10,8},{9,1... | collective-permute-start | bytes 786440 | tf_op jit(solution)/shard_map/ppermute | solution.py:346
  35.3 0.0 collective-permute-done.9.near_ref
  35.3 1.4 %sums_lead.2 = (bf16[256,512]{1,0:T(8,128)(2,1)S(1)}, f32[136,256]{1,0:T(8,128)S(1)}, f32[136,256]{1,0:T(8,128)S(1)}) custom-call(bf16[528,256]{1,0:T(8,128)(2,1)S(1)} %collective-permute-done.refs_0_.lead_ref, bf16[528,256]{1,0:T(8,128)(2,1)S(1)} %collective-permute-done.9.near_ref, ...), custom_call_target="tpu_custom_call", output_to_operand_aliasing={{1}: (4, {}), {2}: (5, {})} | custom-call | tf_op jit(solution)/shard_map/sums_lead/pallas_call | solution.py:32
  36.7 0.0 collective-permute-done.8.near_ref
  36.7 1.4 %sums_lead.3 = (bf16[256,512]{1,0:T(8,128)(2,1)S(1)}, f32[136,256]{1,0:T(8,128)S(1)}, f32[136,256]{1,0:T(8,128)S(1)}) custom-call(bf16[528,256]{1,0:T(8,128)(2,1)S(1)} %collective-permute-done.1.refs_1_.lead_ref, bf16[528,256]{1,0:T(8,128)(2,1)S(1)} %collective-permute-done.8.near_ref, ...), custom_call_target="tpu_custom_call", output_to_operand_aliasing={{1}: (4, {}), {2}: (5, {})} | custom-call | tf_op jit(solution)/shard_map/sums_lead/pallas_call | solution.py:32
  38.1 0.3 sums_rest.1
  38.4 2.2 %collective-permute-done.4.refs_0_.lead_ref = bf16[528,256]{1,0:T(8,128)(2,1)S(1)} collective-permute-done((bf16[528,256]{1,0:T(8,128)(2,1)S(1)}, bf16[528,256]{1,0:T(8,128)(2,1)S(1)}, u32[]{:S(2)}, u32[]{:S(2)}) %collective-permute-start.4) | collective-permute-done | bytes 270368 | tf_op jit(solution)/shard_map/ppermute | solution.py:353
  40.6 0.0 collective-permute-start.12
  40.6 0.6 %select_lead.3 = (bf16[512,512]{1,0:T(8,128)(2,1)S(1)}, bf16[1,16,16,256]{3,2,1,0:T(8,128)(2,1)S(1)}, bf16[1,16,16,256]{3,2,1,0:T(8,128)(2,1)S(1)}) custom-call(f32[256,1]{1,0:T(8,128)S(1)} %get-tuple-element.49.inv_ref, bf16[256,512]{1,0:T(8,128)(2,1)S(1)} %get-tuple-element.50.centre_ref, bf16[528,256]{1,0:T(8,128)(2,1)S(1)} %collective-permute-done.4.refs_0_.lead_ref), custom_call_target="tpu_custom_call" | custom-call | tf_op jit(solution)/shard_map/select_lead/pallas_call | solution.py:32
  41.2 1.7 %collective-permute-start.13 = (bf16[1,16,16,256]{3,2,1,0:T(8,128)(2,1)S(1)}, bf16[1,16,16,256]{3,2,1,0:T(8,128)(2,1)S(1)}, u32[]{:S(2)}, u32[]{:S(2)}) collective-permute-start(bf16[1,16,16,256]{3,2,1,0:T(8,128)(2,1)S(1)} %get-tuple-element.80), channel_id=1, source_target_pairs={{0,2},{2,0},{1,3},{3,1},{4,6},{6,4},{5,7},{7,5},{8,10},{10,8},{9,1... | collective-permute-start | bytes 393224 | tf_op jit(solution)/shard_map/ppermute | solution.py:346
  42.8 0.0 collective-permute-done.11.refs_7_
  42.8 2.3 %collective-permute-done.10.rest_ref.refs_1_ = bf16[528,256]{1,0:T(8,128)(2,1)S(1)} collective-permute-done((bf16[528,256]{1,0:T(8,128)(2,1)S(1)}, bf16[528,256]{1,0:T(8,128)(2,1)S(1)}, u32[]{:S(2)}, u32[]{:S(2)}) %collective-permute-start.10) | collective-permute-done | bytes 270368 | tf_op jit(solution)/shard_map/ppermute | solution.py:353
  45.2 0.3 select_rest.3
  45.5 1.4 %collective-permute-start.15 = (bf16[1,16,16,256]{3,2,1,0:T(8,128)(2,1)S(1)}, bf16[1,16,16,256]{3,2,1,0:T(8,128)(2,1)S(1)}, u32[]{:S(2)}, u32[]{:S(2)}) collective-permute-start(bf16[1,16,16,256]{3,2,1,0:T(8,128)(2,1)S(1)} %get-tuple-element.89), channel_id=1, source_target_pairs={{0,2},{2,0},{1,3},{3,1},{4,6},{6,4},{5,7},{7,5},{8,10},{10,8},{9,1... | collective-permute-start | bytes 393224 | tf_op jit(solution)/shard_map/ppermute | solution.py:346
  46.9 0.2 collective-permute-done.13.refs_8_
  47.1 1.3 %last_sums.1 = (f32[136,256]{1,0:T(8,128)S(1)}, f32[128,256]{1,0:T(8,128)S(1)}, bf16[272,256]{1,0:T(8,128)(2,1)S(1)}) custom-call(bf16[528,256]{1,0:T(8,128)(2,1)S(1)} %collective-permute-done.4.refs_0_.lead_ref, bf16[528,256]{1,0:T(8,128)(2,1)S(1)} %collective-permute-done.10.rest_ref.refs_1_, ...), custom_call_target="tpu_custom_call", output_to_operand_aliasing={{0}: (5, {}), {1}: (7, {})} | custom-call | tf_op jit(solution)/shard_map/last_sums/pallas_call | solution.py:32
  48.5 2.0 %collective-permute-start.14 = (bf16[272,256]{1,0:T(8,128)(2,1)S(1)}, bf16[272,256]{1,0:T(8,128)(2,1)S(1)}, u32[]{:S(2)}, u32[]{:S(2)}) collective-permute-start(bf16[272,256]{1,0:T(8,128)(2,1)S(1)} %get-tuple-element.86), channel_id=1, source_target_pairs={{0,2},{2,0},{1,3},{3,1},{4,6},{6,4},{5,7},{7,5},{8,10},{10,8},{9,1... | collective-permute-start | bytes 417800 | tf_op jit(solution)/shard_map/ppermute | solution.py:346
  50.5 0.0 collective-permute-done.15.refs_9_
  50.5 0.9 %gram.1.mine_ref = f32[16,16,128]{2,1,0:T(8,128)S(1)} custom-call(bf16[16,16,512]{2,1,0:T(8,128)(2,1)S(1)} %get-tuple-element.51.refs_0_, bf16[2,16,16,256]{3,2,1,0:T(8,128)(2,1)S(1)} %get-tuple-element.64.refs_1_, bf16[2,16,16,256]{3,2,1,0:T(8,128)(2,1)S(1)} %get-tuple-element.68.refs_2_, bf16[1,16,16,256]{3,2,1,0:T(8,128)(2,1)S(1)} %get-tuple-element.79.refs_3_, ...), custom_call_target="tpu_custom_call" | custom-call | tf_op jit(solution)/shard_map/gram/pallas_call | solution.py:32
  51.4 0.1 collective-permute-start.16
  51.5 1.3 %collective-permute-done.16.other_ref = f32[16,16,128]{2,1,0:T(8,128)S(1)} collective-permute-done((f32[16,16,128]{2,1,0:T(8,128)S(1)}, f32[16,16,128]{2,1,0:T(8,128)S(1)}, u32[]{:S(2)}, u32[]{:S(2)}) %collective-permute-start.16) | collective-permute-done | bytes 131104 | tf_op jit(solution)/shard_map/ppermute | solution.py:350
  52.8 1.3 %tiles.1 = bf16[8,16,128]{2,1,0:T(8,128)(2,1)} custom-call(f32[16,16,128]{2,1,0:T(8,128)S(1)} %gram.1.mine_ref, f32[16,16,128]{2,1,0:T(8,128)S(1)} %collective-permute-done.16.other_ref), custom_call_target="tpu_custom_call" | custom-call | tf_op jit(solution)/shard_map/tiles/pallas_call | solution.py:32
  54.1 0.9 %centroids.1 = f32[128,512]{1,0:T(8,128)} custom-call(f32[136,256]{1,0:T(8,128)S(1)} %get-tuple-element.84.lead_ref, f32[128,256]{1,0:T(8,128)S(1)} %get-tuple-element.85.rest_ref, bf16[272,256]{1,0:T(8,128)(2,1)S(1)} %collective-permute-done.14.refs_0_, bf16[128,512]{1,0:T(8,128)(2,1)S(1)} %get-tuple-element.91.refs_1_), custom_call_target="tpu_custom_call" | custom-call | tf_op jit(solution)/shard_map/centroids/pallas_call | solution.py:32
  (9 shorter events, 0.1 us)
Async XLA Ops:
  0.6 1.0 %copy-start.1 = (bf16[512,512]{1,0:T(8,128)(2,1)S(1)}, bf16[512,512]{1,0:T(8,128)(2,1)}, u32[]{:S(2)}) copy-start(bf16[512,512]{1,0:T(8,128)(2,1)} %emb_ref.1) | copy-start | bytes 1572868
  1.7 0.7 %copy-start.3 = (s32[512,1]{0,1:T(1,128)S(1)}, s32[512,1]{0,1:T(1,128)}, u32[]{:S(2)}) copy-start(s32[512,1]{0,1:T(1,128)} %param.6) | copy-start | bytes 6148
  2.4 11.5 %collective-permute-start.2 = (bf16[528,256]{1,0:T(8,128)(2,1)S(1)}, bf16[528,256]{1,0:T(8,128)(2,1)S(1)}, u32[]{:S(2)}, u32[]{:S(2)}) collective-permute-start(bf16[528,256]{1,0:T(8,128)(2,1)S(1)} %get-tuple-element.47.lead_ref), channel_id=1, source_target_pairs={{0,1},{1,0},{2,3},{3,2},{4,5},{5,4},{6,7},{7,6},{8,9},{9,8},{10,11... | collective-permute-start | bytes 811016 | tf_op jit(solution)/shard_map/ppermute | solution.py:350
  2.9 17.3 %collective-permute-start.1 = (bf16[528,256]{1,0:T(8,128)(2,1)S(1)}, bf16[528,256]{1,0:T(8,128)(2,1)S(1)}, u32[]{:S(2)}, u32[]{:S(2)}) collective-permute-start(bf16[528,256]{1,0:T(8,128)(2,1)S(1)} %get-tuple-element.47.lead_ref), channel_id=1, source_target_pairs={{0,8},{4,12},{8,0},{12,4},{1,9},{5,13},{9,1},{13,5},{2,10},{6,14},... | collective-permute-start | bytes 811016 | tf_op jit(solution)/shard_map/ppermute | solution.py:353
  6.6 14.3 %collective-permute-start = (bf16[528,256]{1,0:T(8,128)(2,1)S(1)}, bf16[528,256]{1,0:T(8,128)(2,1)S(1)}, u32[]{:S(2)}, u32[]{:S(2)}) collective-permute-start(bf16[528,256]{1,0:T(8,128)(2,1)S(1)} %get-tuple-element.47.lead_ref), channel_id=1, source_target_pairs={{0,4},{4,0},{8,12},{12,8},{1,5},{5,1},{9,13},{13,9},{2,6},{6,2},{1... | collective-permute-start | bytes 811016 | tf_op jit(solution)/shard_map/ppermute | solution.py:353
  8.2 1.6 %copy-start = (bf16[1024,1024]{1,0:T(8,128)(2,1)S(1)}, bf16[1024,1024]{1,0:T(8,128)(2,1)}, u32[]{:S(2)}) copy-start(bf16[1024,1024]{1,0:T(8,128)(2,1)} %cent_ref.1) | copy-start | bytes 6291460
  9.8 0.7 %copy-start.2 = (s32[1024]{0:T(1024)S(1)}, s32[1024]{0:T(1024)}, u32[]{:S(2)}) copy-start(s32[1024]{0:T(1024)} %param.7) | copy-start | bytes 12292
  12.0 8.1 %collective-permute-start.3 = (bf16[16,16,512]{2,1,0:T(8,128)(2,1)S(1)}, bf16[16,16,512]{2,1,0:T(8,128)(2,1)S(1)}, u32[]{:S(2)}, u32[]{:S(2)}) collective-permute-start(bf16[16,16,512]{2,1,0:T(8,128)(2,1)S(1)} %get-tuple-element.52), channel_id=1, source_target_pairs={{0,2},{2,0},{1,3},{3,1},{4,6},{6,4},{5,7},{7,5},{8,10},{10,8},{9,1... | collective-permute-start | bytes 786440 | tf_op jit(solution)/shard_map/ppermute | solution.py:346
  13.6 17.6 %collective-permute-start.6 = (bf16[528,256]{1,0:T(8,128)(2,1)S(1)}, bf16[528,256]{1,0:T(8,128)(2,1)S(1)}, u32[]{:S(2)}, u32[]{:S(2)}) collective-permute-start(bf16[528,256]{1,0:T(8,128)(2,1)S(1)} %get-tuple-element.63.rest_ref), channel_id=1, source_target_pairs={{0,8},{4,12},{8,0},{12,4},{1,9},{5,13},{9,1},{13,5},{2,10},{6,14},... | collective-permute-start | bytes 811016 | tf_op jit(solution)/shard_map/ppermute | solution.py:353
  13.9 17.9 %collective-permute-start.5 = (bf16[528,256]{1,0:T(8,128)(2,1)S(1)}, bf16[528,256]{1,0:T(8,128)(2,1)S(1)}, u32[]{:S(2)}, u32[]{:S(2)}) collective-permute-start(bf16[528,256]{1,0:T(8,128)(2,1)S(1)} %get-tuple-element.63.rest_ref), channel_id=1, source_target_pairs={{0,4},{4,0},{8,12},{12,8},{1,5},{5,1},{9,13},{13,9},{2,6},{6,2},{1... | collective-permute-start | bytes 811016 | tf_op jit(solution)/shard_map/ppermute | solution.py:353
  22.0 9.9 %collective-permute-start.7 = (bf16[2,16,16,256]{3,2,1,0:T(8,128)(2,1)S(1)}, bf16[2,16,16,256]{3,2,1,0:T(8,128)(2,1)S(1)}, u32[]{:S(2)}, u32[]{:S(2)}) collective-permute-start(bf16[2,16,16,256]{3,2,1,0:T(8,128)(2,1)S(1)} %get-tuple-element.65), channel_id=1, source_target_pairs={{0,2},{2,0},{1,3},{3,1},{4,6},{6,4},{5,7},{7,5},{8,10},{10,8},{9,1... | collective-permute-start | bytes 786440 | tf_op jit(solution)/shard_map/ppermute | solution.py:346
  24.0 11.3 %collective-permute-start.9 = (bf16[528,256]{1,0:T(8,128)(2,1)S(1)}, bf16[528,256]{1,0:T(8,128)(2,1)S(1)}, u32[]{:S(2)}, u32[]{:S(2)}) collective-permute-start(bf16[528,256]{1,0:T(8,128)(2,1)S(1)} %collective-permute-done.refs_0_.lead_ref), channel_id=1, source_target_pairs={{0,1},{1,0},{2,3},{3,2},{4,5},{5,4},{6,7},{7,6},{8,9},{9,8},{10,11... | collective-permute-start | bytes 811016 | tf_op jit(solution)/shard_map/ppermute | solution.py:350
  24.0 12.7 %collective-permute-start.8 = (bf16[528,256]{1,0:T(8,128)(2,1)S(1)}, bf16[528,256]{1,0:T(8,128)(2,1)S(1)}, u32[]{:S(2)}, u32[]{:S(2)}) collective-permute-start(bf16[528,256]{1,0:T(8,128)(2,1)S(1)} %collective-permute-done.1.refs_1_.lead_ref), channel_id=1, source_target_pairs={{0,1},{1,0},{2,3},{3,2},{4,5},{5,4},{6,7},{7,6},{8,9},{9,8},{10,11... | collective-permute-start | bytes 811016 | tf_op jit(solution)/shard_map/ppermute | solution.py:350
  31.2 9.4 %collective-permute-start.4 = (bf16[528,256]{1,0:T(8,128)(2,1)S(1)}, bf16[528,256]{1,0:T(8,128)(2,1)S(1)}, u32[]{:S(2)}, u32[]{:S(2)}) collective-permute-start(bf16[528,256]{1,0:T(8,128)(2,1)S(1)} %collective-permute-done.1.refs_1_.lead_ref), channel_id=1, source_target_pairs={{0,4},{4,0},{8,12},{12,8},{1,5},{5,1},{9,13},{13,9},{2,6},{6,2},{1... | collective-permute-start | bytes 811016 | tf_op jit(solution)/shard_map/ppermute | solution.py:353
  31.8 13.3 %collective-permute-start.10 = (bf16[528,256]{1,0:T(8,128)(2,1)S(1)}, bf16[528,256]{1,0:T(8,128)(2,1)S(1)}, u32[]{:S(2)}, u32[]{:S(2)}) collective-permute-start(bf16[528,256]{1,0:T(8,128)(2,1)S(1)} %collective-permute-done.6.refs_3_), channel_id=1, source_target_pairs={{0,4},{4,0},{8,12},{12,8},{1,5},{5,1},{9,13},{13,9},{2,6},{6,2},{1... | collective-permute-start | bytes 811016 | tf_op jit(solution)/shard_map/ppermute | solution.py:353
  33.7 9.2 %collective-permute-start.11 = (bf16[2,16,16,256]{3,2,1,0:T(8,128)(2,1)S(1)}, bf16[2,16,16,256]{3,2,1,0:T(8,128)(2,1)S(1)}, u32[]{:S(2)}, u32[]{:S(2)}) collective-permute-start(bf16[2,16,16,256]{3,2,1,0:T(8,128)(2,1)S(1)} %get-tuple-element.69), channel_id=1, source_target_pairs={{0,2},{2,0},{1,3},{3,1},{4,6},{6,4},{5,7},{7,5},{8,10},{10,8},{9,1... | collective-permute-start | bytes 786440 | tf_op jit(solution)/shard_map/ppermute | solution.py:346
  40.6 6.6 %collective-permute-start.12 = (bf16[528,256]{1,0:T(8,128)(2,1)S(1)}, bf16[528,256]{1,0:T(8,128)(2,1)S(1)}, u32[]{:S(2)}, u32[]{:S(2)}) collective-permute-start(bf16[528,256]{1,0:T(8,128)(2,1)S(1)} %collective-permute-done.4.refs_0_.lead_ref), channel_id=1, source_target_pairs={{0,1},{1,0},{2,3},{3,2},{4,5},{5,4},{6,7},{7,6},{8,9},{9,8},{10,11... | collective-permute-start | bytes 811016 | tf_op jit(solution)/shard_map/ppermute | solution.py:350
  41.2 6.0 %collective-permute-start.13 = (bf16[1,16,16,256]{3,2,1,0:T(8,128)(2,1)S(1)}, bf16[1,16,16,256]{3,2,1,0:T(8,128)(2,1)S(1)}, u32[]{:S(2)}, u32[]{:S(2)}) collective-permute-start(bf16[1,16,16,256]{3,2,1,0:T(8,128)(2,1)S(1)} %get-tuple-element.80), channel_id=1, source_target_pairs={{0,2},{2,0},{1,3},{3,1},{4,6},{6,4},{5,7},{7,5},{8,10},{10,8},{9,1... | collective-permute-start | bytes 393224 | tf_op jit(solution)/shard_map/ppermute | solution.py:346
  45.5 5.0 %collective-permute-start.15 = (bf16[1,16,16,256]{3,2,1,0:T(8,128)(2,1)S(1)}, bf16[1,16,16,256]{3,2,1,0:T(8,128)(2,1)S(1)}, u32[]{:S(2)}, u32[]{:S(2)}) collective-permute-start(bf16[1,16,16,256]{3,2,1,0:T(8,128)(2,1)S(1)} %get-tuple-element.89), channel_id=1, source_target_pairs={{0,2},{2,0},{1,3},{3,1},{4,6},{6,4},{5,7},{7,5},{8,10},{10,8},{9,1... | collective-permute-start | bytes 393224 | tf_op jit(solution)/shard_map/ppermute | solution.py:346
  48.5 5.7 %collective-permute-start.14 = (bf16[272,256]{1,0:T(8,128)(2,1)S(1)}, bf16[272,256]{1,0:T(8,128)(2,1)S(1)}, u32[]{:S(2)}, u32[]{:S(2)}) collective-permute-start(bf16[272,256]{1,0:T(8,128)(2,1)S(1)} %get-tuple-element.86), channel_id=1, source_target_pairs={{0,2},{2,0},{1,3},{3,1},{4,6},{6,4},{5,7},{7,5},{8,10},{10,8},{9,1... | collective-permute-start | bytes 417800 | tf_op jit(solution)/shard_map/ppermute | solution.py:346
  51.4 1.4 %collective-permute-start.16 = (f32[16,16,128]{2,1,0:T(8,128)S(1)}, f32[16,16,128]{2,1,0:T(8,128)S(1)}, u32[]{:S(2)}, u32[]{:S(2)}) collective-permute-start(f32[16,16,128]{2,1,0:T(8,128)S(1)} %gram.1.mine_ref), channel_id=1, source_target_pairs={{0,1},{1,0},{2,3},{3,2},{4,5},{5,4},{6,7},{7,6},{8,9},{9,8},{10,11... | collective-permute-start | bytes 393224 | tf_op jit(solution)/shard_map/ppermute | solution.py:350

commit v16 on v15

--- a/solution.py
+++ b/solution.py
@@ -458,7 +458,7 @@
         functools.partial(last_sums_kernel, subs),
         "last_sums",
         [lead_sum, rest_sum] + [shape((2 * per + 2 * SUBLANES, PREFIX), BF16)] * (subs - 1),
-        [leads[bits], rests[bits], prefix, cent_prefix, own_prefix] + list(lead_sums) + list(tied(rest_sums, members[:-1])),
+        [leads[bits], rests[bits], prefix, cent_prefix, own_prefix] + list(lead_sums) + list(tied(rest_sums, members[:-2])),
         {5: 0, 5 + subs: 1},
         scratch=[pltpu.VMEM(total.shape, F32) for total in [lead_sum] * (subs - 1) + [rest_sum] * (subs - 1)],
     )

time: 55.3 us -> 56.5 us (1.022)
  waiting for transfers between devices: 18 us -> 20.5 us
  starting transfers between devices: 19.5 us -> 18.1 us
    ppermute x6, waiting for transfers between devices: 4.74 us -> 7.25 us  [across(): lax.ppermute(values[t], 'sub', [(i, (i + t) % subs) for i in range(subs)])]
    ppermute x6, starting transfers between devices: 10.3 us -> 9 us  [across(): lax.ppermute(values[t], 'sub', [(i, (i + t) % subs) for i in range(subs)])]
  transfers between devices with their start and end apart: 17 -> 17, of which waited for: 7 -> 7; matrix products, arithmetic and copies ran while one was open for 0% -> 0% of each run, Pallas kernels for 22% -> 21%
where the time goes in v16:
time: 56.5 us; the launch traced here: 56.2 us
  waiting for transfers between devices  20.5 us (36%)
  starting transfers between devices  18.1 us (32%)
  Pallas kernels  12.8 us (23%)
  local copies, waits for them, and re-layouts  3.99 us (7%)
  between operations  0.76 us (1%)
    pallas_call x15, Pallas kernels, call(): pl.pallas_call(kernel, out_shape=tuple(out_shape), in_specs=[whole(operan...  12.8 us
    ppermute x6, waiting for transfers between devices, swap(): return lax.ppermute(value, 'rows', [(i, i ^ bit) for i in range(rows)])  11.9 us
    ppermute x6, starting transfers between devices, across(): lax.ppermute(values[t], 'sub', [(i, (i + t) % subs) for i in range(subs)])  9 us
    ppermute x6, starting transfers between devices, swap(): return lax.ppermute(value, 'rows', [(i, i ^ bit) for i in range(rows)])  8.05 us
    ppermute x6, waiting for transfers between devices, across(): lax.ppermute(values[t], 'sub', [(i, (i + t) % subs) for i in range(subs)])  7.25 us
    unnamed x8, local copies, waits for them, and re-layouts  3.99 us
    ppermute x5, waiting for transfers between devices, near(): return lax.ppermute(value, 'dim', [(0, 1), (1, 0)])  1.35 us
  transfers between devices with their start and end apart: 17, of which 7 were waited for; matrix products, arithmetic and copies ran while one was open for 0% of the time, Pallas kernels for 21%

profile of v16, /device:TPU:0, one launch (start us, length us, event | category | flops | bytes accessed | tf_op | source)
XLA Modules:
  0.0 56.2 jit_solution(2082813892017475698)
XLA Ops:
  0.6 1.0 %copy-done.1 = bf16[512,512]{1,0:T(8,128)(2,1)S(1)} copy-done((bf16[512,512]{1,0:T(8,128)(2,1)S(1)}, bf16[512,512]{1,0:T(8,128)(2,1)}, u32[]{:S(2)}) %copy-start.1) | copy-done | bytes 524312
  1.7 0.7 %copy-done.3 = s32[512,1]{0,1:T(1,128)S(1)} copy-done((s32[512,1]{0,1:T(1,128)S(1)}, s32[512,1]{0,1:T(1,128)}, u32[]{:S(2)}) %copy-start.3) | copy-done | bytes 2072
  2.4 0.5 collective-permute-start.2
  2.9 3.7 %collective-permute-start.1 = (bf16[528,256]{1,0:T(8,128)(2,1)S(1)}, bf16[528,256]{1,0:T(8,128)(2,1)S(1)}, u32[]{:S(2)}, u32[]{:S(2)}) collective-permute-start(bf16[528,256]{1,0:T(8,128)(2,1)S(1)} %get-tuple-element.47.lead_ref), channel_id=1, source_target_pairs={{0,8},{4,12},{8,0},{12,4},{1,9},{5,13},{9,1},{13,5},{2,10},{6,14},... | collective-permute-start | bytes 811016 | tf_op jit(solution)/shard_map/ppermute | solution.py:353
  6.6 1.6 %collective-permute-start = (bf16[528,256]{1,0:T(8,128)(2,1)S(1)}, bf16[528,256]{1,0:T(8,128)(2,1)S(1)}, u32[]{:S(2)}, u32[]{:S(2)}) collective-permute-start(bf16[528,256]{1,0:T(8,128)(2,1)S(1)} %get-tuple-element.47.lead_ref), channel_id=1, source_target_pairs={{0,4},{4,0},{8,12},{12,8},{1,5},{5,1},{9,13},{13,9},{2,6},{6,2},{1... | collective-permute-start | bytes 811016 | tf_op jit(solution)/shard_map/ppermute | solution.py:353
  8.2 1.6 %copy-done = bf16[1024,1024]{1,0:T(8,128)(2,1)S(1)} copy-done((bf16[1024,1024]{1,0:T(8,128)(2,1)S(1)}, bf16[1024,1024]{1,0:T(8,128)(2,1)}, u32[]{:S(2)}) %copy-start) | copy-done | bytes 2097176
  9.8 0.7 %copy-done.2 = s32[1024]{0:T(1024)S(1)} copy-done((s32[1024]{0:T(1024)S(1)}, s32[1024]{0:T(1024)}, u32[]{:S(2)}) %copy-start.2) | copy-done | bytes 4120
  10.4 0.8 %prep.1 = (f32[256,1]{1,0:T(8,128)S(1)}, bf16[256,512]{1,0:T(8,128)(2,1)S(1)}, bf16[256,256]{1,0:T(8,128)(2,1)S(1)}, bf16[128,512]{1,0:T(8,128)(2,1)S(1)}, bf16[1024,256]{1,0:T(8,128)(2,1)S(1)}) custom-call(s32[1,1024]{1,0:T(1,128)S(1)} %bitcast.3, bf16[1024,1024]{1,0:T(8,128)(2,1)S(1)} %copy-done), custom_call_target="tpu_custom_call" | custom-call | flops 209715200 | bytes 4194304 | tf_op jit(solution)/shard_map/prep/pallas_call | solution.py:32
  11.3 0.7 %select.1 = (bf16[16,16,512]{2,1,0:T(8,128)(2,1)S(1)}, bf16[16,16,512]{2,1,0:T(8,128)(2,1)S(1)}) custom-call(bf16[528,256]{1,0:T(8,128)(2,1)S(1)} %get-tuple-element.47.lead_ref, bf16[528,256]{1,0:T(8,128)(2,1)S(1)} %get-tuple-element.63.rest_ref, f32[256,1]{1,0:T(8,128)S(1)} %get-tuple-element.49.inv_ref, bf16[256,512]{1,0:T(8,128)(2,1)S(1)} %get-tuple-element.50.centre_ref), custom_call_target="tpu_custom_call" | custom-call | flops 104857600 | bytes 2097152 | tf_op jit(solution)/shard_map/select/pallas_call | solution.py:32
  12.0 1.5 %collective-permute-start.3 = (bf16[16,16,512]{2,1,0:T(8,128)(2,1)S(1)}, bf16[16,16,512]{2,1,0:T(8,128)(2,1)S(1)}, u32[]{:S(2)}, u32[]{:S(2)}) collective-permute-start(bf16[16,16,512]{2,1,0:T(8,128)(2,1)S(1)} %get-tuple-element.52), channel_id=1, source_target_pairs={{0,2},{2,0},{1,3},{3,1},{4,6},{6,4},{5,7},{7,5},{8,10},{10,8},{9,1... | collective-permute-start | bytes 786440 | tf_op jit(solution)/shard_map/ppermute | solution.py:346
  13.6 0.3 collective-permute-start.6
  13.9 0.5 collective-permute-start.5
  14.4 1.3 %sums.1 = (f32[136,256]{1,0:T(8,128)S(1)}, f32[136,256]{1,0:T(8,128)S(1)}, f32[128,256]{1,0:T(8,128)S(1)}, f32[128,256]{1,0:T(8,128)S(1)}) custom-call(bf16[528,256]{1,0:T(8,128)(2,1)S(1)} %get-tuple-element.47.lead_ref, bf16[528,256]{1,0:T(8,128)(2,1)S(1)} %get-tuple-element.63.rest_ref, bf16[528,256]{1,0:T(8,128)(2,1)S(1)} %collective-permute-done.2.near_ref, ...), custom_call_target="tpu_custom_call" | custom-call | flops 104857600 | bytes 2097152 | tf_op jit(solution)/shard_map/sums/pallas_call | solution.py:32
  15.7 4.5 %collective-permute-done.3.refs_5_ = bf16[16,16,512]{2,1,0:T(8,128)(2,1)S(1)} collective-permute-done((bf16[16,16,512]{2,1,0:T(8,128)(2,1)S(1)}, bf16[16,16,512]{2,1,0:T(8,128)(2,1)S(1)}, u32[]{:S(2)}, u32[]{:S(2)}) %collective-permute-start.3) | collective-permute-done | bytes 262176 | tf_op jit(solution)/shard_map/ppermute | solution.py:346
  20.2 0.0 collective-permute-done.1.refs_1_.lead_ref
  20.2 0.7 %collective-permute-done.refs_0_.lead_ref = bf16[528,256]{1,0:T(8,128)(2,1)S(1)} collective-permute-done((bf16[528,256]{1,0:T(8,128)(2,1)S(1)}, bf16[528,256]{1,0:T(8,128)(2,1)S(1)}, u32[]{:S(2)}, u32[]{:S(2)}) %collective-permute-start) | collective-permute-done | bytes 270368 | tf_op jit(solution)/shard_map/ppermute | solution.py:353
  20.9 1.1 %select_lead.2 = (bf16[512,512]{1,0:T(8,128)(2,1)S(1)}, bf16[512,512]{1,0:T(8,128)(2,1)S(1)}, bf16[2,16,16,256]{3,2,1,0:T(8,128)(2,1)S(1)}, bf16[2,16,16,256]{3,2,1,0:T(8,128)(2,1)S(1)}) custom-call(f32[256,1]{1,0:T(8,128)S(1)} %get-tuple-element.49.inv_ref, bf16[256,512]{1,0:T(8,128)(2,1)S(1)} %get-tuple-element.50.centre_ref, ...), custom_call_target="tpu_custom_call" | custom-call | tf_op jit(solution)/shard_map/select_lead/pallas_call | solution.py:32
  22.0 2.0 %collective-permute-start.7 = (bf16[2,16,16,256]{3,2,1,0:T(8,128)(2,1)S(1)}, bf16[2,16,16,256]{3,2,1,0:T(8,128)(2,1)S(1)}, u32[]{:S(2)}, u32[]{:S(2)}) collective-permute-start(bf16[2,16,16,256]{3,2,1,0:T(8,128)(2,1)S(1)} %get-tuple-element.65), channel_id=1, source_target_pairs={{0,2},{2,0},{1,3},{3,1},{4,6},{6,4},{5,7},{7,5},{8,10},{10,8},{9,1... | collective-permute-start | bytes 786440 | tf_op jit(solution)/shard_map/ppermute | solution.py:346
  24.0 0.0 collective-permute-start.9
  24.0 0.5 collective-permute-start.8
  24.5 6.7 %collective-permute-done.6.refs_3_ = bf16[528,256]{1,0:T(8,128)(2,1)S(1)} collective-permute-done((bf16[528,256]{1,0:T(8,128)(2,1)S(1)}, bf16[528,256]{1,0:T(8,128)(2,1)S(1)}, u32[]{:S(2)}, u32[]{:S(2)}) %collective-permute-start.6) | collective-permute-done | bytes 270368 | tf_op jit(solution)/shard_map/ppermute | solution.py:353
  31.2 0.6 %collective-permute-start.4 = (bf16[528,256]{1,0:T(8,128)(2,1)S(1)}, bf16[528,256]{1,0:T(8,128)(2,1)S(1)}, u32[]{:S(2)}, u32[]{:S(2)}) collective-permute-start(bf16[528,256]{1,0:T(8,128)(2,1)S(1)} %collective-permute-done.1.refs_1_.lead_ref), channel_id=1, source_target_pairs={{0,4},{4,0},{8,12},{12,8},{1,5},{5,1},{9,13},{13,9},{2,6},{6,2},{1... | collective-permute-start | bytes 811016 | tf_op jit(solution)/shard_map/ppermute | solution.py:353
  31.8 0.0 collective-permute-done.5.refs_2_
  31.8 1.4 %collective-permute-start.10 = (bf16[528,256]{1,0:T(8,128)(2,1)S(1)}, bf16[528,256]{1,0:T(8,128)(2,1)S(1)}, u32[]{:S(2)}, u32[]{:S(2)}) collective-permute-start(bf16[528,256]{1,0:T(8,128)(2,1)S(1)} %collective-permute-done.6.refs_3_), channel_id=1, source_target_pairs={{0,4},{4,0},{8,12},{12,8},{1,5},{5,1},{9,13},{13,9},{2,6},{6,2},{1... | collective-permute-start | bytes 811016 | tf_op jit(solution)/shard_map/ppermute | solution.py:353
  33.2 0.4 select_rest.2
  33.7 1.6 %collective-permute-start.11 = (bf16[2,16,16,256]{3,2,1,0:T(8,128)(2,1)S(1)}, bf16[2,16,16,256]{3,2,1,0:T(8,128)(2,1)S(1)}, u32[]{:S(2)}, u32[]{:S(2)}) collective-permute-start(bf16[2,16,16,256]{3,2,1,0:T(8,128)(2,1)S(1)} %get-tuple-element.69), channel_id=1, source_target_pairs={{0,2},{2,0},{1,3},{3,1},{4,6},{6,4},{5,7},{7,5},{8,10},{10,8},{9,1... | collective-permute-start | bytes 786440 | tf_op jit(solution)/shard_map/ppermute | solution.py:346
  35.3 0.0 collective-permute-done.9.near_ref
  35.3 1.4 %sums_lead.2 = (bf16[256,512]{1,0:T(8,128)(2,1)S(1)}, f32[136,256]{1,0:T(8,128)S(1)}, f32[136,256]{1,0:T(8,128)S(1)}) custom-call(bf16[528,256]{1,0:T(8,128)(2,1)S(1)} %collective-permute-done.refs_0_.lead_ref, bf16[528,256]{1,0:T(8,128)(2,1)S(1)} %collective-permute-done.9.near_ref, ...), custom_call_target="tpu_custom_call", output_to_operand_aliasing={{1}: (4, {}), {2}: (5, {})} | custom-call | tf_op jit(solution)/shard_map/sums_lead/pallas_call | solution.py:32
  36.7 0.0 collective-permute-done.8.near_ref
  36.7 1.4 %sums_lead.3 = (bf16[256,512]{1,0:T(8,128)(2,1)S(1)}, f32[136,256]{1,0:T(8,128)S(1)}, f32[136,256]{1,0:T(8,128)S(1)}) custom-call(bf16[528,256]{1,0:T(8,128)(2,1)S(1)} %collective-permute-done.1.refs_1_.lead_ref, bf16[528,256]{1,0:T(8,128)(2,1)S(1)} %collective-permute-done.8.near_ref, ...), custom_call_target="tpu_custom_call", output_to_operand_aliasing={{1}: (4, {}), {2}: (5, {})} | custom-call | tf_op jit(solution)/shard_map/sums_lead/pallas_call | solution.py:32
  38.1 0.3 sums_rest.1
  38.4 2.2 %collective-permute-done.4.refs_0_.lead_ref = bf16[528,256]{1,0:T(8,128)(2,1)S(1)} collective-permute-done((bf16[528,256]{1,0:T(8,128)(2,1)S(1)}, bf16[528,256]{1,0:T(8,128)(2,1)S(1)}, u32[]{:S(2)}, u32[]{:S(2)}) %collective-permute-start.4) | collective-permute-done | bytes 270368 | tf_op jit(solution)/shard_map/ppermute | solution.py:353
  40.6 0.0 collective-permute-start.12
  40.6 0.6 %select_lead.3 = (bf16[512,512]{1,0:T(8,128)(2,1)S(1)}, bf16[1,16,16,256]{3,2,1,0:T(8,128)(2,1)S(1)}, bf16[1,16,16,256]{3,2,1,0:T(8,128)(2,1)S(1)}) custom-call(f32[256,1]{1,0:T(8,128)S(1)} %get-tuple-element.49.inv_ref, bf16[256,512]{1,0:T(8,128)(2,1)S(1)} %get-tuple-element.50.centre_ref, bf16[528,256]{1,0:T(8,128)(2,1)S(1)} %collective-permute-done.4.refs_0_.lead_ref), custom_call_target="tpu_custom_call" | custom-call | tf_op jit(solution)/shard_map/select_lead/pallas_call | solution.py:32
  41.2 1.7 %collective-permute-start.14 = (bf16[1,16,16,256]{3,2,1,0:T(8,128)(2,1)S(1)}, bf16[1,16,16,256]{3,2,1,0:T(8,128)(2,1)S(1)}, u32[]{:S(2)}, u32[]{:S(2)}) collective-permute-start(bf16[1,16,16,256]{3,2,1,0:T(8,128)(2,1)S(1)} %get-tuple-element.80), channel_id=1, source_target_pairs={{0,2},{2,0},{1,3},{3,1},{4,6},{6,4},{5,7},{7,5},{8,10},{10,8},{9,1... | collective-permute-start | bytes 393224 | tf_op jit(solution)/shard_map/ppermute | solution.py:346
  42.8 2.3 %collective-permute-done.10.rest_ref.refs_1_ = bf16[528,256]{1,0:T(8,128)(2,1)S(1)} collective-permute-done((bf16[528,256]{1,0:T(8,128)(2,1)S(1)}, bf16[528,256]{1,0:T(8,128)(2,1)S(1)}, u32[]{:S(2)}, u32[]{:S(2)}) %collective-permute-start.10) | collective-permute-done | bytes 270368 | tf_op jit(solution)/shard_map/ppermute | solution.py:353
  45.2 0.3 select_rest.3
  45.5 1.4 %collective-permute-start.15 = (bf16[1,16,16,256]{3,2,1,0:T(8,128)(2,1)S(1)}, bf16[1,16,16,256]{3,2,1,0:T(8,128)(2,1)S(1)}, u32[]{:S(2)}, u32[]{:S(2)}) collective-permute-start(bf16[1,16,16,256]{3,2,1,0:T(8,128)(2,1)S(1)} %get-tuple-element.89), channel_id=1, source_target_pairs={{0,2},{2,0},{1,3},{3,1},{4,6},{6,4},{5,7},{7,5},{8,10},{10,8},{9,1... | collective-permute-start | bytes 393224 | tf_op jit(solution)/shard_map/ppermute | solution.py:346
  46.9 1.3 %last_sums.1 = (f32[136,256]{1,0:T(8,128)S(1)}, f32[128,256]{1,0:T(8,128)S(1)}, bf16[272,256]{1,0:T(8,128)(2,1)S(1)}) custom-call(bf16[528,256]{1,0:T(8,128)(2,1)S(1)} %collective-permute-done.4.refs_0_.lead_ref, bf16[528,256]{1,0:T(8,128)(2,1)S(1)} %collective-permute-done.10.rest_ref.refs_1_, ...), custom_call_target="tpu_custom_call", output_to_operand_aliasing={{0}: (5, {}), {1}: (7, {})} | custom-call | tf_op jit(solution)/shard_map/last_sums/pallas_call | solution.py:32
  48.2 0.7 %collective-permute-start.13 = (bf16[272,256]{1,0:T(8,128)(2,1)S(1)}, bf16[272,256]{1,0:T(8,128)(2,1)S(1)}, u32[]{:S(2)}, u32[]{:S(2)}) collective-permute-start(bf16[272,256]{1,0:T(8,128)(2,1)S(1)} %get-tuple-element.86), channel_id=1, source_target_pairs={{0,2},{2,0},{1,3},{3,1},{4,6},{6,4},{5,7},{7,5},{8,10},{10,8},{9,1... | collective-permute-start | bytes 417800 | tf_op jit(solution)/shard_map/ppermute | solution.py:346
  49.0 0.0 collective-permute-done.14.refs_8_
  49.0 2.7 %collective-permute-done.15.refs_9_ = bf16[1,16,16,256]{3,2,1,0:T(8,128)(2,1)S(1)} collective-permute-done((bf16[1,16,16,256]{3,2,1,0:T(8,128)(2,1)S(1)}, bf16[1,16,16,256]{3,2,1,0:T(8,128)(2,1)S(1)}, u32[]{:S(2)}, u32[]{:S(2)}) %collective-permute-start.15) | collective-permute-done | bytes 131104 | tf_op jit(solution)/shard_map/ppermute | solution.py:346
  51.7 0.9 %gram.1.mine_ref = f32[16,16,128]{2,1,0:T(8,128)S(1)} custom-call(bf16[16,16,512]{2,1,0:T(8,128)(2,1)S(1)} %get-tuple-element.51.refs_0_, bf16[2,16,16,256]{3,2,1,0:T(8,128)(2,1)S(1)} %get-tuple-element.64.refs_1_, bf16[2,16,16,256]{3,2,1,0:T(8,128)(2,1)S(1)} %get-tuple-element.68.refs_2_, bf16[1,16,16,256]{3,2,1,0:T(8,128)(2,1)S(1)} %get-tuple-element.79.refs_3_, ...), custom_call_target="tpu_custom_call" | custom-call | tf_op jit(solution)/shard_map/gram/pallas_call | solution.py:32
  52.6 0.1 collective-permute-start.16
  52.7 1.3 %collective-permute-done.16.other_ref = f32[16,16,128]{2,1,0:T(8,128)S(1)} collective-permute-done((f32[16,16,128]{2,1,0:T(8,128)S(1)}, f32[16,16,128]{2,1,0:T(8,128)S(1)}, u32[]{:S(2)}, u32[]{:S(2)}) %collective-permute-start.16) | collective-permute-done | bytes 131104 | tf_op jit(solution)/shard_map/ppermute | solution.py:350
  54.0 1.3 %tiles.1 = bf16[8,16,128]{2,1,0:T(8,128)(2,1)} custom-call(f32[16,16,128]{2,1,0:T(8,128)S(1)} %gram.1.mine_ref, f32[16,16,128]{2,1,0:T(8,128)S(1)} %collective-permute-done.16.other_ref), custom_call_target="tpu_custom_call" | custom-call | tf_op jit(solution)/shard_map/tiles/pallas_call | solution.py:32
  55.3 0.0 collective-permute-done.13.refs_0_
  55.3 0.9 %centroids.1 = f32[128,512]{1,0:T(8,128)} custom-call(f32[136,256]{1,0:T(8,128)S(1)} %get-tuple-element.84.lead_ref, f32[128,256]{1,0:T(8,128)S(1)} %get-tuple-element.85.rest_ref, bf16[272,256]{1,0:T(8,128)(2,1)S(1)} %collective-permute-done.13.refs_0_, bf16[128,512]{1,0:T(8,128)(2,1)S(1)} %get-tuple-element.91.refs_1_), custom_call_target="tpu_custom_call" | custom-call | tf_op jit(solution)/shard_map/centroids/pallas_call | solution.py:32
  (9 shorter events, 0.1 us)
Async XLA Ops:
  0.6 1.0 %copy-start.1 = (bf16[512,512]{1,0:T(8,128)(2,1)S(1)}, bf16[512,512]{1,0:T(8,128)(2,1)}, u32[]{:S(2)}) copy-start(bf16[512,512]{1,0:T(8,128)(2,1)} %emb_ref.1) | copy-start | bytes 1572868
  1.7 0.7 %copy-start.3 = (s32[512,1]{0,1:T(1,128)S(1)}, s32[512,1]{0,1:T(1,128)}, u32[]{:S(2)}) copy-start(s32[512,1]{0,1:T(1,128)} %param.6) | copy-start | bytes 6148
  2.4 11.5 %collective-permute-start.2 = (bf16[528,256]{1,0:T(8,128)(2,1)S(1)}, bf16[528,256]{1,0:T(8,128)(2,1)S(1)}, u32[]{:S(2)}, u32[]{:S(2)}) collective-permute-start(bf16[528,256]{1,0:T(8,128)(2,1)S(1)} %get-tuple-element.47.lead_ref), channel_id=1, source_target_pairs={{0,1},{1,0},{2,3},{3,2},{4,5},{5,4},{6,7},{7,6},{8,9},{9,8},{10,11... | collective-permute-start | bytes 811016 | tf_op jit(solution)/shard_map/ppermute | solution.py:350
  2.9 17.3 %collective-permute-start.1 = (bf16[528,256]{1,0:T(8,128)(2,1)S(1)}, bf16[528,256]{1,0:T(8,128)(2,1)S(1)}, u32[]{:S(2)}, u32[]{:S(2)}) collective-permute-start(bf16[528,256]{1,0:T(8,128)(2,1)S(1)} %get-tuple-element.47.lead_ref), channel_id=1, source_target_pairs={{0,8},{4,12},{8,0},{12,4},{1,9},{5,13},{9,1},{13,5},{2,10},{6,14},... | collective-permute-start | bytes 811016 | tf_op jit(solution)/shard_map/ppermute | solution.py:353
  6.6 14.3 %collective-permute-start = (bf16[528,256]{1,0:T(8,128)(2,1)S(1)}, bf16[528,256]{1,0:T(8,128)(2,1)S(1)}, u32[]{:S(2)}, u32[]{:S(2)}) collective-permute-start(bf16[528,256]{1,0:T(8,128)(2,1)S(1)} %get-tuple-element.47.lead_ref), channel_id=1, source_target_pairs={{0,4},{4,0},{8,12},{12,8},{1,5},{5,1},{9,13},{13,9},{2,6},{6,2},{1... | collective-permute-start | bytes 811016 | tf_op jit(solution)/shard_map/ppermute | solution.py:353
  8.2 1.6 %copy-start = (bf16[1024,1024]{1,0:T(8,128)(2,1)S(1)}, bf16[1024,1024]{1,0:T(8,128)(2,1)}, u32[]{:S(2)}) copy-start(bf16[1024,1024]{1,0:T(8,128)(2,1)} %cent_ref.1) | copy-start | bytes 6291460
  9.8 0.7 %copy-start.2 = (s32[1024]{0:T(1024)S(1)}, s32[1024]{0:T(1024)}, u32[]{:S(2)}) copy-start(s32[1024]{0:T(1024)} %param.7) | copy-start | bytes 12292
  12.0 8.1 %collective-permute-start.3 = (bf16[16,16,512]{2,1,0:T(8,128)(2,1)S(1)}, bf16[16,16,512]{2,1,0:T(8,128)(2,1)S(1)}, u32[]{:S(2)}, u32[]{:S(2)}) collective-permute-start(bf16[16,16,512]{2,1,0:T(8,128)(2,1)S(1)} %get-tuple-element.52), channel_id=1, source_target_pairs={{0,2},{2,0},{1,3},{3,1},{4,6},{6,4},{5,7},{7,5},{8,10},{10,8},{9,1... | collective-permute-start | bytes 786440 | tf_op jit(solution)/shard_map/ppermute | solution.py:346
  13.6 17.6 %collective-permute-start.6 = (bf16[528,256]{1,0:T(8,128)(2,1)S(1)}, bf16[528,256]{1,0:T(8,128)(2,1)S(1)}, u32[]{:S(2)}, u32[]{:S(2)}) collective-permute-start(bf16[528,256]{1,0:T(8,128)(2,1)S(1)} %get-tuple-element.63.rest_ref), channel_id=1, source_target_pairs={{0,8},{4,12},{8,0},{12,4},{1,9},{5,13},{9,1},{13,5},{2,10},{6,14},... | collective-permute-start | bytes 811016 | tf_op jit(solution)/shard_map/ppermute | solution.py:353
  13.9 17.9 %collective-permute-start.5 = (bf16[528,256]{1,0:T(8,128)(2,1)S(1)}, bf16[528,256]{1,0:T(8,128)(2,1)S(1)}, u32[]{:S(2)}, u32[]{:S(2)}) collective-permute-start(bf16[528,256]{1,0:T(8,128)(2,1)S(1)} %get-tuple-element.63.rest_ref), channel_id=1, source_target_pairs={{0,4},{4,0},{8,12},{12,8},{1,5},{5,1},{9,13},{13,9},{2,6},{6,2},{1... | collective-permute-start | bytes 811016 | tf_op jit(solution)/shard_map/ppermute | solution.py:353
  22.0 9.9 %collective-permute-start.7 = (bf16[2,16,16,256]{3,2,1,0:T(8,128)(2,1)S(1)}, bf16[2,16,16,256]{3,2,1,0:T(8,128)(2,1)S(1)}, u32[]{:S(2)}, u32[]{:S(2)}) collective-permute-start(bf16[2,16,16,256]{3,2,1,0:T(8,128)(2,1)S(1)} %get-tuple-element.65), channel_id=1, source_target_pairs={{0,2},{2,0},{1,3},{3,1},{4,6},{6,4},{5,7},{7,5},{8,10},{10,8},{9,1... | collective-permute-start | bytes 786440 | tf_op jit(solution)/shard_map/ppermute | solution.py:346
  24.0 11.3 %collective-permute-start.9 = (bf16[528,256]{1,0:T(8,128)(2,1)S(1)}, bf16[528,256]{1,0:T(8,128)(2,1)S(1)}, u32[]{:S(2)}, u32[]{:S(2)}) collective-permute-start(bf16[528,256]{1,0:T(8,128)(2,1)S(1)} %collective-permute-done.refs_0_.lead_ref), channel_id=1, source_target_pairs={{0,1},{1,0},{2,3},{3,2},{4,5},{5,4},{6,7},{7,6},{8,9},{9,8},{10,11... | collective-permute-start | bytes 811016 | tf_op jit(solution)/shard_map/ppermute | solution.py:350
  24.0 12.7 %collective-permute-start.8 = (bf16[528,256]{1,0:T(8,128)(2,1)S(1)}, bf16[528,256]{1,0:T(8,128)(2,1)S(1)}, u32[]{:S(2)}, u32[]{:S(2)}) collective-permute-start(bf16[528,256]{1,0:T(8,128)(2,1)S(1)} %collective-permute-done.1.refs_1_.lead_ref), channel_id=1, source_target_pairs={{0,1},{1,0},{2,3},{3,2},{4,5},{5,4},{6,7},{7,6},{8,9},{9,8},{10,11... | collective-permute-start | bytes 811016 | tf_op jit(solution)/shard_map/ppermute | solution.py:350
  31.2 9.4 %collective-permute-start.4 = (bf16[528,256]{1,0:T(8,128)(2,1)S(1)}, bf16[528,256]{1,0:T(8,128)(2,1)S(1)}, u32[]{:S(2)}, u32[]{:S(2)}) collective-permute-start(bf16[528,256]{1,0:T(8,128)(2,1)S(1)} %collective-permute-done.1.refs_1_.lead_ref), channel_id=1, source_target_pairs={{0,4},{4,0},{8,12},{12,8},{1,5},{5,1},{9,13},{13,9},{2,6},{6,2},{1... | collective-permute-start | bytes 811016 | tf_op jit(solution)/shard_map/ppermute | solution.py:353
  31.8 13.3 %collective-permute-start.10 = (bf16[528,256]{1,0:T(8,128)(2,1)S(1)}, bf16[528,256]{1,0:T(8,128)(2,1)S(1)}, u32[]{:S(2)}, u32[]{:S(2)}) collective-permute-start(bf16[528,256]{1,0:T(8,128)(2,1)S(1)} %collective-permute-done.6.refs_3_), channel_id=1, source_target_pairs={{0,4},{4,0},{8,12},{12,8},{1,5},{5,1},{9,13},{13,9},{2,6},{6,2},{1... | collective-permute-start | bytes 811016 | tf_op jit(solution)/shard_map/ppermute | solution.py:353
  33.7 9.2 %collective-permute-start.11 = (bf16[2,16,16,256]{3,2,1,0:T(8,128)(2,1)S(1)}, bf16[2,16,16,256]{3,2,1,0:T(8,128)(2,1)S(1)}, u32[]{:S(2)}, u32[]{:S(2)}) collective-permute-start(bf16[2,16,16,256]{3,2,1,0:T(8,128)(2,1)S(1)} %get-tuple-element.69), channel_id=1, source_target_pairs={{0,2},{2,0},{1,3},{3,1},{4,6},{6,4},{5,7},{7,5},{8,10},{10,8},{9,1... | collective-permute-start | bytes 786440 | tf_op jit(solution)/shard_map/ppermute | solution.py:346
  40.6 6.3 %collective-permute-start.12 = (bf16[528,256]{1,0:T(8,128)(2,1)S(1)}, bf16[528,256]{1,0:T(8,128)(2,1)S(1)}, u32[]{:S(2)}, u32[]{:S(2)}) collective-permute-start(bf16[528,256]{1,0:T(8,128)(2,1)S(1)} %collective-permute-done.4.refs_0_.lead_ref), channel_id=1, source_target_pairs={{0,1},{1,0},{2,3},{3,2},{4,5},{5,4},{6,7},{7,6},{8,9},{9,8},{10,11... | collective-permute-start | bytes 811016 | tf_op jit(solution)/shard_map/ppermute | solution.py:350
  41.2 7.8 %collective-permute-start.14 = (bf16[1,16,16,256]{3,2,1,0:T(8,128)(2,1)S(1)}, bf16[1,16,16,256]{3,2,1,0:T(8,128)(2,1)S(1)}, u32[]{:S(2)}, u32[]{:S(2)}) collective-permute-start(bf16[1,16,16,256]{3,2,1,0:T(8,128)(2,1)S(1)} %get-tuple-element.80), channel_id=1, source_target_pairs={{0,2},{2,0},{1,3},{3,1},{4,6},{6,4},{5,7},{7,5},{8,10},{10,8},{9,1... | collective-permute-start | bytes 393224 | tf_op jit(solution)/shard_map/ppermute | solution.py:346
  45.5 6.2 %collective-permute-start.15 = (bf16[1,16,16,256]{3,2,1,0:T(8,128)(2,1)S(1)}, bf16[1,16,16,256]{3,2,1,0:T(8,128)(2,1)S(1)}, u32[]{:S(2)}, u32[]{:S(2)}) collective-permute-start(bf16[1,16,16,256]{3,2,1,0:T(8,128)(2,1)S(1)} %get-tuple-element.89), channel_id=1, source_target_pairs={{0,2},{2,0},{1,3},{3,1},{4,6},{6,4},{5,7},{7,5},{8,10},{10,8},{9,1... | collective-permute-start | bytes 393224 | tf_op jit(solution)/shard_map/ppermute | solution.py:346
  48.2 7.1 %collective-permute-start.13 = (bf16[272,256]{1,0:T(8,128)(2,1)S(1)}, bf16[272,256]{1,0:T(8,128)(2,1)S(1)}, u32[]{:S(2)}, u32[]{:S(2)}) collective-permute-start(bf16[272,256]{1,0:T(8,128)(2,1)S(1)} %get-tuple-element.86), channel_id=1, source_target_pairs={{0,2},{2,0},{1,3},{3,1},{4,6},{6,4},{5,7},{7,5},{8,10},{10,8},{9,1... | collective-permute-start | bytes 417800 | tf_op jit(solution)/shard_map/ppermute | solution.py:346
  52.6 1.4 %collective-permute-start.16 = (f32[16,16,128]{2,1,0:T(8,128)S(1)}, f32[16,16,128]{2,1,0:T(8,128)S(1)}, u32[]{:S(2)}, u32[]{:S(2)}) collective-permute-start(f32[16,16,128]{2,1,0:T(8,128)S(1)} %gram.1.mine_ref), channel_id=1, source_target_pairs={{0,1},{1,0},{2,3},{3,2},{4,5},{5,4},{6,7},{7,6},{8,9},{9,8},{10,11... | collective-permute-start | bytes 393224 | tf_op jit(solution)/shard_map/ppermute | solution.py:350
